TPU v7x, 512 devices: a whole 4x4x16 slice. The times are simulated.
512 devices in a mesh: ctx: 32 (over x_hi, z), head: 16 (over x_lo, y, core).
Axes of the slice: x: 4 (x_hi: 2, x_lo: 2; x = x_hi * 2 + x_lo), y: 4, z: 16, core: 2. Of those that a mesh axis runs over, the one named last changes fastest.
Arguments:
- queries: bfloat16 [4096, 2048], P('ctx', 'head'), may hold values from -6 to 6
- keys: bfloat16 [16384, 2048], P('ctx', 'head'), may hold values from -1.5 to 1.5
- values: bfloat16 [16384, 2048], P('ctx', 'head'), may hold values from -6 to 6
- d_out: bfloat16 [4096, 2048], P('ctx', 'head'), may hold values from -48 to 48
- key_weight: bfloat16 [2048, 2048], P(None, 'head'), may hold values from -0.1875 to 0.1875
- value_weight: bfloat16 [2048, 2048], P(None, 'head'), may hold values from -0.1875 to 0.1875
- block_lists: int32 [32, 64], replicated, may hold values from 0 to 127, all different within a row
Outputs:
- d_queries: bfloat16 [4096, 2048], P('ctx', 'head')
- d_memory: bfloat16 [16384, 2048], P('ctx', 'head')
Inputs may be any that keep to these rules, and one draw needn't show every extreme that they name: `block_lists`: each row names 64 different encoder blocks; every encoder block is named by some row.
All inputs are finite; a program needn't handle non-finite values.
Results may differ from a plain program's by a relative error of at most 0.024.
Values may be sent and summed in bfloat16 or wider, within the bound.
No kernel may reach another device: no remote copies, remote signals or barrier semaphores. Data moves between devices by JAX's collectives and lax.ppermute only.
A program may use at most 64 MiB of HBM per device.

v0:
```python
from functools import partial

import jax
import jax.numpy as jnp
from jax import lax
from jax.sharding import PartitionSpec as P

HEAD_DIM = 64
BLOCK = 128


masked_score = -1e30


def shortened(x):
    return jax.tree.map(lambda a: a.astype(jnp.bfloat16) if a.dtype == jnp.float32 else a, x)


def shifted(value, axis, steps):
    count = lax.axis_size(axis)
    pairs = [(source, (source + steps) % count) for source in range(count)]
    return lax.ppermute(value, axis, pairs)


def travel(payload, carry, local, visit):
    count = lax.axis_size("ctx")
    mine = lax.axis_index("ctx")
    width = len(carry)

    def turn(step, state):
        moving, moving_carry, kept = state
        moving_carry, kept = visit(moving, moving_carry, kept, (mine - step) % count)
        moving = jax.tree.map(
            lambda part, own: part.astype(own.dtype), shifted(shortened(moving), "ctx", 1), moving
        )
        moving_carry = shifted(moving_carry, "ctx", 1)
        return (moving, moving_carry, kept)

    moving, moving_carry, local = lax.fori_loop(0, count, turn, (payload, carry, local))
    return ([tuple(moving_carry[:width])], local)


def sweep(update, state, member):
    rows = member.shape[0] * BLOCK
    for index in range(member.shape[1]):
        column = jnp.broadcast_to(jnp.repeat(member[:, index], BLOCK)[:, None], (rows, BLOCK))
        state = lax.cond(
            jnp.any(member[:, index]),
            partial(update, start=index * BLOCK, count=BLOCK, mask=column),
            lambda unchanged: unchanged,
            state,
        )
    return state


def body(queries, keys, values, d_out, key_weight, value_weight, block_lists):
    tgt_rows = queries.shape[0]
    enc_rows = keys.shape[0]
    heads_here = keys.shape[1] // HEAD_DIM
    mine = lax.axis_index("ctx")
    query_heads = queries.reshape(tgt_rows, heads_here, HEAD_DIM)
    key_heads = keys.reshape(enc_rows, heads_here, HEAD_DIM)
    value_heads = values.reshape(enc_rows, heads_here, HEAD_DIM)
    out_heads = d_out.reshape(tgt_rows, heads_here, HEAD_DIM)
    query_count = tgt_rows // BLOCK
    key_count = enc_rows // BLOCK
    key_ids = mine * key_count + jnp.arange(key_count, dtype=jnp.int32)

    def members(source):
        listed = lax.dynamic_slice_in_dim(block_lists, source * query_count, query_count, 0)
        return jnp.any(listed[:, :, None] == key_ids[None, None, :], axis=1)

    def forward_visit(moving, carry, kept, source):
        visiting = moving[0]

        def update(state, start, count, mask):
            running, totals, weighted = state
            logits = jnp.einsum(
                "qhd,khd->hqk",
                visiting,
                key_heads[start : start + count],
                preferred_element_type=jnp.float32,
            )
            masked = jnp.where(mask[None], logits, masked_score)
            raised_peak = jnp.maximum(running, jnp.max(masked, axis=-1))
            raised = jnp.where(mask[None], jnp.exp(logits - raised_peak[..., None]), 0.0)
            fade = jnp.exp(running - raised_peak)
            totals = totals * fade + jnp.sum(raised, axis=-1)
            weighted = weighted * fade.T[:, :, None] + jnp.einsum(
                "hqk,khd->qhd",
                raised.astype(jnp.bfloat16),
                value_heads[start : start + count],
                preferred_element_type=jnp.float32,
            )
            return (raised_peak, totals, weighted)

        return (sweep(update, carry, members(source)), kept)

    start_running = jnp.full((heads_here, tgt_rows), masked_score, jnp.float32)
    start_totals = jnp.zeros((heads_here, tgt_rows), jnp.float32)
    start_weighted = jnp.zeros((tgt_rows, heads_here, HEAD_DIM), jnp.float32)
    pieces, unused = travel(
        (query_heads,), (start_running, start_totals, start_weighted), (), forward_visit
    )
    running = pieces[0][0]
    totals = jnp.zeros_like(start_totals)
    weighted = jnp.zeros_like(start_weighted)
    for piece in pieces:
        fade = jnp.exp(piece[0] - running)
        totals = piece[1] * fade
        weighted = piece[2] * fade.T[:, :, None]
    attended = weighted / totals.T[:, :, None]
    log_totals = running + jnp.log(totals)
    delta = jnp.sum(out_heads.astype(jnp.float32) * attended, axis=-1).T

    def backward_visit(moving, carry, kept, source):
        visiting, visiting_out = moving
        query_grad, visit_log, visit_delta = carry

        def update(state, start, count, mask):
            grad_query, grad_key, grad_value = state
            key_rows = key_heads[start : start + count]
            value_rows = value_heads[start : start + count]
            logits = jnp.einsum(
                "qhd,khd->hqk", visiting, key_rows, preferred_element_type=jnp.float32
            )
            chances = jnp.where(mask[None], jnp.exp(logits - visit_log[..., None]), 0.0)
            grad_value = grad_value.at[start : start + count].add(
                jnp.einsum(
                    "hqk,qhd->khd",
                    chances.astype(jnp.bfloat16),
                    visiting_out,
                    preferred_element_type=jnp.float32,
                )
            )
            grad_prob = jnp.einsum(
                "qhd,khd->hqk", visiting_out, value_rows, preferred_element_type=jnp.float32
            )
            grad_logits = (chances * (grad_prob - visit_delta[..., None])).astype(jnp.bfloat16)
            grad_query = grad_query + jnp.einsum(
                "hqk,khd->qhd", grad_logits, key_rows, preferred_element_type=jnp.float32
            )
            grad_key = grad_key.at[start : start + count].add(
                jnp.einsum(
                    "hqk,qhd->khd", grad_logits, visiting, preferred_element_type=jnp.float32
                )
            )
            return (grad_query, grad_key, grad_value)

        query_grad, grad_key, grad_value = sweep(
            update, (query_grad, kept[0], kept[1]), members(source)
        )
        return ((query_grad, visit_log, visit_delta), (grad_key, grad_value))

    empty_keys = jnp.zeros((enc_rows, heads_here, HEAD_DIM), jnp.float32)
    pieces, (grad_key, grad_value) = travel(
        (query_heads, out_heads),
        (jnp.zeros_like(start_weighted), log_totals, delta),
        (empty_keys, empty_keys),
        backward_visit,
    )
    query_grad = pieces[0][0]
    d_queries = query_grad.reshape(tgt_rows, heads_here * HEAD_DIM).astype(jnp.bfloat16)
    rounded_key = grad_key.reshape(enc_rows, heads_here * HEAD_DIM).astype(jnp.bfloat16)
    rounded_value = grad_value.reshape(enc_rows, heads_here * HEAD_DIM).astype(jnp.bfloat16)
    contract = (((1,), (1,)), ((), ()))
    memory_part = lax.dot_general(
        rounded_key, key_weight, contract, preferred_element_type=jnp.float32
    )
    memory_part = memory_part + lax.dot_general(
        rounded_value, value_weight, contract, preferred_element_type=jnp.float32
    )
    d_memory = lax.psum_scatter(
        memory_part.astype(jnp.bfloat16), "head", scatter_dimension=1, tiled=True
    )
    return (d_queries, d_memory)


def solution(mesh):
    placed = (
        P("ctx", "head"),
        P("ctx", "head"),
        P("ctx", "head"),
        P("ctx", "head"),
        P(None, "head"),
        P(None, "head"),
        P(),
    )
    return jax.shard_map(
        body,
        mesh=mesh,
        in_specs=placed,
        out_specs=(P("ctx", "head"), P("ctx", "head")),
        check_vma=False,
    )
```

profile of v0, /device:TPU:1, one launch (start us, length us, event | category | flops | bytes accessed | tf_op | source)
XLA Modules:
  0.0 1852.0 jit_solution(1281764762423033885)
XLA Ops:
  11.1 809.7 %while.58 = (s32[]{:T(128)}, bf16[128,2,64]{0,2,1:T(8,128)(2,1)S(1)}, f32[2,128]{1,0:T(2,128)S(1)}, f32[2,128]{1,0:T(2,128)S(1)}, f32[128,2,64]{0,2,1:T(8,128)S(...) while((s32[]{:T(128)}, ...), condition=%wide.region_18.19_spmd.clone, body=%wide.region_0.18_spmd.clone.sunk | while | flops 34737684 | bytes 3159422 | solution.py:39
  18.2 9.2 collective-permute-start.3
  32.4 6.4 collective-permute-start.1
  52.9 5.9 collective-permute-start.2
  58.8 4.3 collective-permute-start.1
  75.7 9.9 collective-permute-start
  125.0 4.9 conditional.27
  164.7 4.1 collective-permute-done.1
  175.7 4.9 conditional.27
  186.4 7.6 collective-permute-start.1
  201.9 4.9 conditional.27
  213.8 6.8 collective-permute-start.1
  232.1 6.3 collective-permute-start
  255.9 4.9 conditional.27
  290.0 4.8 collective-permute-done.2
  333.9 4.1 collective-permute-done.2
  353.6 7.4 collective-permute-start.1
  376.4 8.2 collective-permute-start.1
  393.0 7.0 collective-permute-start.3
  418.4 4.9 conditional.27
  443.9 4.9 conditional.27
  452.7 8.9 collective-permute-start.2
  463.6 6.2 collective-permute-done.1
  476.8 5.6 collective-permute-start.3
  502.5 4.9 conditional.27
  511.3 5.6 collective-permute-start.2
  516.8 4.6 collective-permute-start.1
  552.9 4.9 conditional.27
  565.5 4.1 collective-permute-done.2
  587.4 5.1 collective-permute-done.2
  610.5 6.7 collective-permute-start.1
  626.1 6.5 collective-permute-start.3
  660.3 4.1 collective-permute-done.2
  673.4 4.9 conditional.27
  699.2 4.9 conditional.27
  733.2 4.8 collective-permute-start.1
  748.8 5.1 collective-permute-start.3
  778.6 6.7 collective-permute-start.2
  788.5 5.0 collective-permute-done.1
  802.4 8.3 collective-permute-start
  820.9 829.1 %while.59 = (s32[]{:T(128)}, bf16[128,2,64]{0,2,1:T(8,128)(2,1)S(1)}, bf16[128,2,64]{0,2,1:T(8,128)(2,1)S(1)}, f32[128,2,64]{0,2,1:T(8,128)S(1)}, f32[2,128]{1,0...) while((s32[]{:T(128)}, ...), condition=%wide.region_30.31_spmd.clone, body=%wide.region_20.30_spmd.clone.sunk | while | flops 84869648 | bytes 5660324 | solution.py:39
  833.7 4.8 collective-permute-start.7
  838.5 6.1 collective-permute-start.8
  859.8 5.5 collective-permute-start.5
  883.4 5.1 collective-permute-start.4
  935.6 4.9 collective-permute-start.5
  940.5 4.8 collective-permute-start.7
  948.5 4.8 collective-permute-done.8
  1115.2 4.1 collective-permute-start.7
  1123.1 4.2 collective-permute-done.8
  1140.2 4.5 collective-permute-start.5
  1173.3 6.4 collective-permute-start.7
  1181.6 6.0 collective-permute-done.8
  1322.4 5.4 collective-permute-start.7
  1330.3 5.4 collective-permute-done.8
  1351.9 5.2 collective-permute-start.8
  1375.1 7.3 collective-permute-start.5
  1382.4 5.1 collective-permute-start.7
  1390.3 5.3 collective-permute-done.8
  1482.8 5.6 collective-permute-start.7
  1490.8 5.6 collective-permute-done.8
  1515.6 4.3 collective-permute-done.7
  1608.7 5.6 collective-permute-start.5
  1655.1 188.4 %reduce-scatter.4.cloned.1.call-done = bf16[128,512]{1,0:T(8,128)(2,1)} async-done(((bf16[2048,512]{1,0:T(8,128)(2,1)}), bf16[128,512]{1,0:T(8,128)(2,1)}) %reduce-scatter.4.cloned.1.call-update) | async-done | bytes 131088
  (2196 shorter events, 1286.3 us)
Async XLA Ops:
  7.2 1836.3 %reduce-scatter.4.cloned.1.call-start = ((), (), s32[]{:S(2)}) async-start(), calls=%async_computation.1 | async-start | bytes 2228224
  18.2 20.6 %collective-permute-start.3 = (f32[128,2,64]{0,2,1:T(8,128)S(1)}, f32[128,2,64]{0,2,1:T(8,128)S(1)}, u32[]{:S(2)}, u32[]{:S(2)}) collective-permute-start(f32[128,2,64]{0,2,1:T(8,128)S(1)} %get-tuple-element.1277), channel_id=1, source_target_pairs={{0,16},{16,32},{32,48},{48,64},{64,80},{80,96},{96,112},{112,128},... | collective-permute-start | bytes 196616 | tf_op jit(solution)/shard_map/while/body/eval_jaxpr/ppermute | solution.py:22
  48.0 15.1 collective-permute-start.3
  50.0 17.0 collective-permute-start
  73.5 20.0 %collective-permute-start.3 = (f32[128,2,64]{0,2,1:T(8,128)S(1)}, f32[128,2,64]{0,2,1:T(8,128)S(1)}, u32[]{:S(2)}, u32[]{:S(2)}) collective-permute-start(f32[128,2,64]{0,2,1:T(8,128)S(1)} %get-tuple-element.1277), channel_id=1, source_target_pairs={{0,16},{16,32},{32,48},{48,64},{64,80},{80,96},{96,112},{112,128},... | collective-permute-start | bytes 196616 | tf_op jit(solution)/shard_map/while/body/eval_jaxpr/ppermute | solution.py:22
  75.7 19.9 %collective-permute-start = (bf16[128,2,64]{0,2,1:T(8,128)(2,1)S(1)}, bf16[128,2,64]{0,2,1:T(8,128)(2,1)S(1)}, u32[]{:S(2)}, u32[]{:S(2)}) collective-permute-start(bf16[128,2,64]{0,2,1:T(8,128)(2,1)S(1)} %copy.113), channel_id=1, source_target_pairs={{0,16},{16,32},{32,48},{48,64},{64,80},{80,96},{96,112},{112,128},... | collective-permute-start | bytes 98312 | tf_op jit(solution)/shard_map/while/body/eval_jaxpr/ppermute | solution.py:22
  152.8 16.0 collective-permute-start
  229.0 17.4 collective-permute-start.3
  232.1 16.9 collective-permute-start
  368.9 15.7 collective-permute-start.3
  393.0 16.9 collective-permute-start.3
  448.9 14.7 collective-permute-start.3
  450.8 19.0 %collective-permute-start = (bf16[128,2,64]{0,2,1:T(8,128)(2,1)S(1)}, bf16[128,2,64]{0,2,1:T(8,128)(2,1)S(1)}, u32[]{:S(2)}, u32[]{:S(2)}) collective-permute-start(bf16[128,2,64]{0,2,1:T(8,128)(2,1)S(1)} %copy.113), channel_id=1, source_target_pairs={{0,16},{16,32},{32,48},{48,64},{64,80},{80,96},{96,112},{112,128},... | collective-permute-start | bytes 98312 | tf_op jit(solution)/shard_map/while/body/eval_jaxpr/ppermute | solution.py:22
  476.8 17.1 collective-permute-start.3
  482.4 14.2 collective-permute-start
  507.4 14.0 collective-permute-start.3
  509.3 15.6 collective-permute-start
  602.7 14.5 collective-permute-start.3
  626.1 16.3 collective-permute-start.3
  748.8 14.9 collective-permute-start.3
  773.4 15.1 collective-permute-start.3
  776.7 16.8 collective-permute-start
  800.5 18.1 collective-permute-start.3
  802.4 18.3 collective-permute-start
  827.9 16.7 collective-permute-start.6
  829.8 16.6 collective-permute-start.4
  831.8 14.7 collective-permute-start.5
  854.4 15.1 collective-permute-start.6
  856.3 19.1 %collective-permute-start.4 = (bf16[128,2,64]{0,2,1:T(8,128)(2,1)S(1)}, bf16[128,2,64]{0,2,1:T(8,128)(2,1)S(1)}, u32[]{:S(2)}, u32[]{:S(2)}) collective-permute-start(bf16[128,2,64]{0,2,1:T(8,128)(2,1)S(1)} %copy.131), channel_id=1, source_target_pairs={{0,16},{16,32},{32,48},{48,64},{64,80},{80,96},{96,112},{112,128},... | collective-permute-start | bytes 98312 | tf_op jit(solution)/shard_map/while/body/eval_jaxpr/ppermute | solution.py:22
  859.8 15.6 collective-permute-start.5
  883.4 17.1 collective-permute-start.4
  931.8 15.5 collective-permute-start.6
  933.7 19.6 %collective-permute-start.4 = (bf16[128,2,64]{0,2,1:T(8,128)(2,1)S(1)}, bf16[128,2,64]{0,2,1:T(8,128)(2,1)S(1)}, u32[]{:S(2)}, u32[]{:S(2)}) collective-permute-start(bf16[128,2,64]{0,2,1:T(8,128)(2,1)S(1)} %copy.131), channel_id=1, source_target_pairs={{0,16},{16,32},{32,48},{48,64},{64,80},{80,96},{96,112},{112,128},... | collective-permute-start | bytes 98312 | tf_op jit(solution)/shard_map/while/body/eval_jaxpr/ppermute | solution.py:22
  935.6 17.7 collective-permute-start.5
  962.2 14.1 collective-permute-start.4
  987.7 16.5 collective-permute-start.4
  989.6 14.6 collective-permute-start.5
  1063.4 15.0 collective-permute-start.4
  1088.3 14.2 collective-permute-start.4
  1111.3 15.9 collective-permute-start.4
  1135.2 15.4 collective-permute-start.6
  1137.1 18.7 %collective-permute-start.4 = (bf16[128,2,64]{0,2,1:T(8,128)(2,1)S(1)}, bf16[128,2,64]{0,2,1:T(8,128)(2,1)S(1)}, u32[]{:S(2)}, u32[]{:S(2)}) collective-permute-start(bf16[128,2,64]{0,2,1:T(8,128)(2,1)S(1)} %copy.131), channel_id=1, source_target_pairs={{0,16},{16,32},{32,48},{48,64},{64,80},{80,96},{96,112},{112,128},... | collective-permute-start | bytes 98312 | tf_op jit(solution)/shard_map/while/body/eval_jaxpr/ppermute | solution.py:22
  1140.2 15.7 collective-permute-start.5
  1163.8 17.8 collective-permute-start.6
  1166.1 21.5 %collective-permute-start.4 = (bf16[128,2,64]{0,2,1:T(8,128)(2,1)S(1)}, bf16[128,2,64]{0,2,1:T(8,128)(2,1)S(1)}, u32[]{:S(2)}, u32[]{:S(2)}) collective-permute-start(bf16[128,2,64]{0,2,1:T(8,128)(2,1)S(1)} %copy.131), channel_id=1, source_target_pairs={{0,16},{16,32},{32,48},{48,64},{64,80},{80,96},{96,112},{112,128},... | collective-permute-start | bytes 98312 | tf_op jit(solution)/shard_map/while/body/eval_jaxpr/ppermute | solution.py:22
  1169.4 18.2 collective-permute-start.5
  1196.5 14.5 collective-permute-start.4
  1220.8 15.5 collective-permute-start.4
  1246.9 15.0 collective-permute-start.4
  1318.2 17.5 collective-permute-start.4
  1320.1 15.6 collective-permute-start.5
  1342.7 14.3 collective-permute-start.6
  1344.6 15.2 collective-permute-start.4
  1369.3 20.2 %collective-permute-start.6 = (f32[128,2,64]{0,2,1:T(8,128)S(1)}, f32[128,2,64]{0,2,1:T(8,128)S(1)}, u32[]{:S(2)}, u32[]{:S(2)}) collective-permute-start(f32[128,2,64]{0,2,1:T(8,128)S(1)} %get-tuple-element.1304), channel_id=1, source_target_pairs={{0,16},{16,32},{32,48},{48,64},{64,80},{80,96},{96,112},{112,128},... | collective-permute-start | bytes 196616 | tf_op jit(solution)/shard_map/while/body/eval_jaxpr/ppermute | solution.py:22
  1371.2 24.4 %collective-permute-start.4 = (bf16[128,2,64]{0,2,1:T(8,128)(2,1)S(1)}, bf16[128,2,64]{0,2,1:T(8,128)(2,1)S(1)}, u32[]{:S(2)}, u32[]{:S(2)}) collective-permute-start(bf16[128,2,64]{0,2,1:T(8,128)(2,1)S(1)} %copy.131), channel_id=1, source_target_pairs={{0,16},{16,32},{32,48},{48,64},{64,80},{80,96},{96,112},{112,128},... | collective-permute-start | bytes 98312 | tf_op jit(solution)/shard_map/while/body/eval_jaxpr/ppermute | solution.py:22
  1375.1 20.5 %collective-permute-start.5 = (bf16[128,2,64]{0,2,1:T(8,128)(2,1)S(1)}, bf16[128,2,64]{0,2,1:T(8,128)(2,1)S(1)}, u32[]{:S(2)}, u32[]{:S(2)}) collective-permute-start(bf16[128,2,64]{0,2,1:T(8,128)(2,1)S(1)} %copy.132), channel_id=1, source_target_pairs={{0,16},{16,32},{32,48},{48,64},{64,80},{80,96},{96,112},{112,128},... | collective-permute-start | bytes 98312 | tf_op jit(solution)/shard_map/while/body/eval_jaxpr/ppermute | solution.py:22
  1479.0 17.4 collective-permute-start.4
  1480.9 15.5 collective-permute-start.5
  1557.5 14.6 collective-permute-start.4
  1581.9 15.1 collective-permute-start.4
  1604.9 14.7 collective-permute-start.6
  1606.8 19.0 %collective-permute-start.4 = (bf16[128,2,64]{0,2,1:T(8,128)(2,1)S(1)}, bf16[128,2,64]{0,2,1:T(8,128)(2,1)S(1)}, u32[]{:S(2)}, u32[]{:S(2)}) collective-permute-start(bf16[128,2,64]{0,2,1:T(8,128)(2,1)S(1)} %copy.131), channel_id=1, source_target_pairs={{0,16},{16,32},{32,48},{48,64},{64,80},{80,96},{96,112},{112,128},... | collective-permute-start | bytes 98312 | tf_op jit(solution)/shard_map/while/body/eval_jaxpr/ppermute | solution.py:22
  1608.7 17.1 collective-permute-start.5
  1634.8 15.2 collective-permute-start.4
  (227 other events, 3874.4 us)
Sparse Core Ops, SparseCore 0:
  1654.4 188.9 reduce-scatter.3
where the time goes:
time: 1870 us; the launch traced here: 1850 us
  starting transfers between devices  762 us (41%)
  waiting for transfers between devices  525 us (28%)
  local copies, waits for them, and re-layouts  228 us (12%)
  loops' own time  174 us (9%)
  matrix products  107 us (6%)
  other arithmetic  41.7 us (2%)
    ppermute x288, starting transfers between devices, shifted(): return lax.ppermute(value, axis, pairs)  762 us
    ppermute x288, waiting for transfers between devices, shifted(): return lax.ppermute(value, axis, pairs)  337 us
    unnamed x2, waiting for transfers between devices  188 us
    another operation x2, loops' own time, travel(): lax.fori_loop(0, count, turn, (payload, carry, local))  166 us
    reshape x192, local copies, waits for them, and re-layouts, sweep(): jnp.repeat(member[:, index], BLOCK)[:, None]  119 us
    dynamic_slice x64, local copies, waits for them, and re-layouts, members(): lax.dynamic_slice_in_dim(block_lists, source * query_count, query_count, 0)  44.4 us
    slice x64, local copies, waits for them, and re-layouts, sweep(): member[:, index]  42 us
  transfers between devices with their start and end apart: 289, of which 114 were waited for; matrix products, arithmetic and copies ran while one was open for 0% of the time, Pallas kernels for 0%

commit v1 on v0

v1 whole, which is shorter than its diff:
```python
from functools import partial

import jax
import jax.numpy as jnp
from jax import lax
from jax.experimental import pallas as pl
from jax.experimental.pallas import tpu as pltpu
from jax.sharding import Mesh, PartitionSpec as P

HEAD_DIM = 64
BLOCK = 128
AXES = ("xh", "z", "xl", "y", "core")
SIZES = (2, 16, 2, 4, 2)
CTX = ("xh", "z")
HEAD = ("xl", "y", "core")
BIG = 1e30

OWN = (4, 0, -4, 8)
LATER = (3, -1, -5, 7, 5, 1, -3, 9, 6, 2, -2, -6)
SLOTS = OWN + LATER

VMEM = pl.BlockSpec(memory_space=pltpu.VMEM)
SMEM = pl.BlockSpec(memory_space=pltpu.SMEM)
ROOM = pltpu.CompilerParams(vmem_limit_bytes=48 * 1024 * 1024)


def dot_nt(a, b):
    return lax.dot_general(a, b, (((1,), (1,)), ((), ())), preferred_element_type=jnp.float32)


def dot_nn(a, b):
    return lax.dot_general(a, b, (((1,), (0,)), ((), ())), preferred_element_type=jnp.float32)


def split_heads(rows):
    low = lax.broadcasted_iota(jnp.int32, rows.shape, 1) < HEAD_DIM
    zero = jnp.zeros_like(rows)
    return jnp.concatenate([jnp.where(low, rows, zero), jnp.where(low, zero, rows)], axis=0)


def load_keys(k_ref, v_ref, far_ref, keys, vals):
    rows = k_ref.shape[0]
    keys[:rows, :] = k_ref[...]
    vals[:rows, :] = v_ref[...]
    keys[rows:, :] = far_ref[:, :BLOCK]
    vals[rows:, :] = far_ref[:, BLOCK:]


def load_targets(pieces, held):
    at = 0
    for piece in pieces:
        held[at : at + piece.shape[0], :] = piece[...]
        at += piece.shape[0]


def away(member, first, second, block, blocks):
    seg = (lax.broadcasted_iota(jnp.int32, (1, 4 * BLOCK), 1) // BLOCK) % 2
    one = jnp.where(member[first * blocks + block] > 0, 0.0, BIG)
    two = jnp.where(member[second * blocks + block] > 0, 0.0, BIG)
    return jnp.where(seg == 0, one, two)


def forward_kernel(base, places, member, k_ref, v_ref, far_ref, *rest):
    *pieces, before, stats, keys, vals, held = rest
    load_keys(k_ref, v_ref, far_ref, keys, vals)
    load_targets(pieces, held)
    blocks = keys.shape[0] // BLOCK
    pairs = held.shape[0] // (2 * BLOCK)
    half = stats.shape[0] // 2
    if before is not None:
        stats[...] = before[...]

    def step(p, carry):
        rows = pl.ds(pl.multiple_of(p * 2 * BLOCK, 2 * BLOCK), 2 * BLOCK)
        first, second = places[base + 2 * p], places[base + 2 * p + 1]
        query = split_heads(held[rows, :BLOCK])
        out = split_heads(held[rows, BLOCK:])
        logits = dot_nt(keys[...], query)
        prob = dot_nt(vals[...], out)
        off = [away(member, first, second, b, blocks) for b in range(blocks)]
        peak = jnp.full((1, 4 * BLOCK), -1e3, jnp.float32)
        for b in range(blocks):
            part = logits[b * BLOCK : (b + 1) * BLOCK]
            peak = jnp.maximum(peak, jnp.max(part, axis=0, keepdims=True) - off[b])
        total = jnp.zeros((1, 4 * BLOCK), jnp.float32)
        weighted = jnp.zeros((1, 4 * BLOCK), jnp.float32)
        for b in range(blocks):
            part = slice(b * BLOCK, (b + 1) * BLOCK)
            raised = jnp.exp(logits[part] - (peak + off[b]))
            total = total + jnp.sum(raised, axis=0, keepdims=True)
            weighted = weighted + jnp.sum(raised * prob[part], axis=0, keepdims=True)
        some = total > 0.0
        log_total = jnp.where(some, peak + jnp.log(jnp.where(some, total, 1.0)), -BIG)
        mean = jnp.where(some, weighted / jnp.where(some, total, 1.0), 0.0)
        for h in range(2):
            for s, place in enumerate((first, second)):
                lanes = slice((2 * h + s) * BLOCK, (2 * h + s + 1) * BLOCK)
                stats[pl.ds(2 * place + h, 1), :] = log_total[:, lanes]
                stats[pl.ds(half + 2 * place + h, 1), :] = mean[:, lanes]
        return carry

    lax.fori_loop(0, pairs, step, 0)


def forward(base, places, member, k, v, far, pieces, before):
    count = len(SLOTS)
    rows = sum(p.shape[0] for p in pieces)
    enc = k.shape[0] + far.shape[0]
    given = [places, member, k, v, far, *pieces]
    specs = [SMEM, SMEM] + [VMEM] * (3 + len(pieces))
    if before is None:
        def kernel(*refs):
            ins, outs = refs[: len(given)], refs[len(given) :]
            forward_kernel(base, *ins, None, *outs)
    else:
        given.append(before)
        specs.append(VMEM)
        kernel = partial(forward_kernel, base)
    return pl.pallas_call(
        kernel,
        out_shape=jax.ShapeDtypeStruct((4 * count, BLOCK), jnp.float32),
        in_specs=specs,
        out_specs=VMEM,
        scratch_shapes=[
            pltpu.VMEM((enc, BLOCK), jnp.bfloat16),
            pltpu.VMEM((enc, BLOCK), jnp.bfloat16),
            pltpu.VMEM((rows, 2 * BLOCK), jnp.bfloat16),
        ],
        compiler_params=ROOM,
        name="forward",
    )(*given)


def backward_kernel(places, member, core, stats, k_ref, v_ref, far_ref, *rest):
    pieces = rest[:5]
    d_query, kept, to_core, to_half, to_both, keys, vals, held, turned, chances, slopes, d_key, d_value = rest[5:]
    load_keys(k_ref, v_ref, far_ref, keys, vals)
    load_targets(pieces, held)
    enc = keys.shape[0]
    blocks = enc // BLOCK
    pairs = held.shape[0] // (2 * BLOCK)
    half = stats.shape[0] // 2
    turned[...] = keys[...].T
    d_key[...] = jnp.zeros_like(d_key)
    d_value[...] = jnp.zeros_like(d_value)

    def step(p, carry):
        rows = pl.ds(pl.multiple_of(p * 2 * BLOCK, 2 * BLOCK), 2 * BLOCK)
        first, second = places[2 * p], places[2 * p + 1]
        query = split_heads(held[rows, :BLOCK])
        out = split_heads(held[rows, BLOCK:])
        spots = [2 * place + h for h in range(2) for place in (first, second)]
        log_total = jnp.concatenate([stats[pl.ds(s, 1), :] for s in spots], axis=1)
        delta = jnp.concatenate([stats[pl.ds(half + s, 1), :] for s in spots], axis=1)
        logits = dot_nt(keys[...], query)
        prob = dot_nt(vals[...], out)
        for b in range(blocks):
            part = slice(b * BLOCK, (b + 1) * BLOCK)
            chance = jnp.exp(logits[part] - (log_total + away(member, first, second, b, blocks)))
            chances[part, :] = chance.astype(jnp.bfloat16)
            slopes[part, :] = (chance * (prob[part] - delta)).astype(jnp.bfloat16)
        d_value[...] += dot_nn(chances[...], out)
        d_key[...] += dot_nn(slopes[...], query)
        both = dot_nn(turned[...], slopes[...]).T
        low = lax.broadcasted_iota(jnp.int32, (2 * BLOCK, BLOCK), 1) < HEAD_DIM
        grad = jnp.where(low, both[: 2 * BLOCK], both[2 * BLOCK :]).astype(jnp.bfloat16)
        d_query[first] = grad[:BLOCK]
        d_query[second] = grad[BLOCK:]
        return carry

    lax.fori_loop(0, pairs, step, 0)
    quarter = enc // 4
    mine = core[0]
    other = 1 - mine

    def put(target, start):
        start = pl.multiple_of(start, quarter)
        target[:, :BLOCK] = d_key[pl.ds(start, quarter), :].astype(target.dtype)
        target[:, BLOCK:] = d_value[pl.ds(start, quarter), :].astype(target.dtype)

    put(kept, mine * quarter)
    put(to_core, other * quarter)
    put(to_half, (2 + mine) * quarter)
    put(to_both, (2 + other) * quarter)


def backward(places, member, core, stats, k, v, far, pieces):
    count = len(SLOTS)
    rows = sum(p.shape[0] for p in pieces)
    enc = k.shape[0] + far.shape[0]
    quarter = (enc // 4, 2 * BLOCK)
    given = [places, member, core, stats, k, v, far, *pieces]
    return pl.pallas_call(
        backward_kernel,
        out_shape=(
            jax.ShapeDtypeStruct((count, BLOCK, BLOCK), jnp.bfloat16),
            jax.ShapeDtypeStruct(quarter, jnp.float32),
            jax.ShapeDtypeStruct(quarter, jnp.bfloat16),
            jax.ShapeDtypeStruct(quarter, jnp.bfloat16),
            jax.ShapeDtypeStruct(quarter, jnp.bfloat16),
        ),
        in_specs=[SMEM] * 3 + [VMEM] * (len(given) - 3),
        out_specs=(VMEM,) * 5,
        scratch_shapes=[
            pltpu.VMEM((enc, BLOCK), jnp.bfloat16),
            pltpu.VMEM((enc, BLOCK), jnp.bfloat16),
            pltpu.VMEM((rows, 2 * BLOCK), jnp.bfloat16),
            pltpu.VMEM((BLOCK, enc), jnp.bfloat16),
            pltpu.VMEM((enc, 4 * BLOCK), jnp.bfloat16),
            pltpu.VMEM((enc, 4 * BLOCK), jnp.bfloat16),
            pltpu.VMEM((enc, BLOCK), jnp.float32),
            pltpu.VMEM((enc, BLOCK), jnp.float32),
        ],
        compiler_params=ROOM,
        name="backward",
    )(*given)


def project_kernel(kept, from_half, from_core, from_both, kw, vw, far_kw, far_vw, memory):
    mine = (kept[...] + from_half[...].astype(jnp.float32)).astype(jnp.bfloat16)
    other = (from_core[...].astype(jnp.float32) + from_both[...].astype(jnp.float32)).astype(jnp.bfloat16)
    for j in range(memory.shape[0]):
        columns = slice(j * BLOCK, (j + 1) * BLOCK)
        total = dot_nt(mine[:, :BLOCK], kw[columns, :]) + dot_nt(mine[:, BLOCK:], vw[columns, :])
        total = total + dot_nt(other[:, :BLOCK], far_kw[columns, :])
        total = total + dot_nt(other[:, BLOCK:], far_vw[columns, :])
        memory[j] = total.astype(jnp.bfloat16)


def moved(value, axis, steps):
    count = lax.axis_size(axis)
    return lax.ppermute(value, axis, [(i, (i + steps) % count) for i in range(count)])


def merged(parts):
    half = parts[0].shape[0] // 2
    logs = [p[:half] for p in parts]
    top = logs[0]
    for log in logs[1:]:
        top = jnp.maximum(top, log)
    weights = [jnp.exp(log - top) for log in logs]
    total = sum(weights[1:], weights[0])
    mean = sum((w * p[half:] for w, p in zip(weights[1:], parts[1:])), weights[0] * parts[0][half:])
    return jnp.concatenate([top + jnp.log(total), mean / total], axis=0)


def body(queries, keys, values, d_out, key_weight, value_weight, block_lists):
    half = lax.axis_index("xh")
    place = lax.axis_index("z")
    core = lax.axis_index("core")
    depth = lax.axis_size("z")
    count = len(SLOTS)
    enc_blocks = keys.shape[0] // BLOCK

    near = jnp.concatenate([queries, d_out], axis=1)
    ahead = moved(near, "z", 4)
    behind = moved(near, "z", -4)
    across = moved(near, "z", 8)
    far = moved(jnp.concatenate([keys, values], axis=1), "xh", 1)

    places = (place + jnp.asarray(SLOTS, jnp.int32)) % depth
    listed = lax.dynamic_slice_in_dim(block_lists, half * count, count, 0)
    step = jnp.arange(enc_blocks, dtype=jnp.int32)
    ids = jnp.concatenate(
        [(half * depth + place) * enc_blocks + step, ((1 - half) * depth + place) * enc_blocks + step]
    )
    member = jnp.any(listed[:, :, None] == ids[None, None, :], axis=1).astype(jnp.int32).reshape(-1)

    bundle = jnp.concatenate([behind, near, ahead, across], axis=0)
    below = moved(bundle, "z", 1)
    above = moved(bundle, "z", -1)
    above2 = moved(bundle[: 2 * BLOCK], "z", -2)
    below2 = moved(bundle[BLOCK : 3 * BLOCK], "z", 2)
    far_kw = moved(key_weight, "core", 1)
    far_vw = moved(value_weight, "core", 1)

    early = forward(0, places, member, keys, values, far, [bundle], None)
    pieces = [below, above, above2, below2]
    stats = forward(len(OWN), places, member, keys, values, far, pieces, early)
    stats = merged([stats, moved(stats, "z", 4), moved(stats, "z", -4), moved(stats, "z", 8)])
    stats = merged([stats, moved(stats, "z", 1), moved(stats, "z", -1), moved(stats, "z", 2)])

    d_query, kept, to_core, to_half, to_both = backward(
        places, member, core[None], stats, keys, values, far, [bundle, *pieces]
    )
    from_half = moved(to_half, "xh", 1)
    from_core = moved(to_core, "core", 1)
    from_both = lax.ppermute(to_both, ("xh", "core"), [(0, 3), (1, 2), (2, 1), (3, 0)])

    chunks = key_weight.shape[0] // BLOCK
    memory = pl.pallas_call(
        project_kernel,
        out_shape=jax.ShapeDtypeStruct((chunks, kept.shape[0], BLOCK), jnp.bfloat16),
        in_specs=[VMEM] * 8,
        out_specs=VMEM,
        compiler_params=ROOM,
        name="project",
    )(kept, from_half, from_core, from_both, key_weight, value_weight, far_kw, far_vw)
    memory = lax.all_to_all(memory, HEAD, 0, 0, tiled=True)
    d_query = lax.all_to_all(d_query, "z", 0, 0, tiled=True)

    cores = lax.axis_size("core")
    memory = memory.reshape(chunks // cores, cores, *memory.shape[1:]).astype(jnp.float32)
    d_memory = jnp.sum(memory, axis=0).reshape(keys.shape).astype(jnp.bfloat16)
    d_queries = jnp.sum(d_query.astype(jnp.float32), axis=0).astype(jnp.bfloat16)
    return d_queries, d_memory


def solution(mesh):
    fine = Mesh(mesh.devices.reshape(SIZES), AXES)
    placed = P(CTX, HEAD)
    return jax.shard_map(
        body,
        mesh=fine,
        in_specs=(placed, placed, placed, placed, P(None, HEAD), P(None, HEAD), P()),
        out_specs=(placed, placed),
        check_vma=False,
    )
```

time: 1870 us -> 185 us (0.10)
  the two profiles are of different devices: /device:TPU:1 before, /device:TPU:2 now
where the time goes in v1:
time: 185 us; the launch traced here: 184 us
  starting transfers between devices  93.4 us (50%)
  waiting for transfers between devices  40.2 us (22%)
  Pallas kernels  24.8 us (13%)
  blocking collectives  20.9 us (11%)
  other arithmetic  3.16 us (2%)
    ppermute x18, starting transfers between devices, moved(): lax.ppermute(value, axis, [(i, (i + steps) % count) for i in range(count)])  81.4 us
    all_to_all x1, waiting for transfers between devices, body(): d_query = lax.all_to_all(d_query, 'z', 0, 0, tiled=True)  28.3 us
    all_to_all x1, blocking collectives, body(): memory = lax.all_to_all(memory, HEAD, 0, 0, tiled=True)  20.9 us
    pallas_call x1, Pallas kernels, backward(): pl.pallas_call(backward_kernel, out_shape=(jax.ShapeDtypeStruct((count, B...  13.6 us
    pallas_call x2, Pallas kernels, forward(): pl.pallas_call(kernel, out_shape=jax.ShapeDtypeStruct((4 * count, BLOCK),...  8.82 us
    all_to_all x1, starting transfers between devices, body(): d_query = lax.all_to_all(d_query, 'z', 0, 0, tiled=True)  8.26 us
    ppermute x18, waiting for transfers between devices, moved(): lax.ppermute(value, axis, [(i, (i + steps) % count) for i in range(count)])  7.15 us
    ppermute x1, waiting for transfers between devices, body(): lax.ppermute(to_both, ('xh', 'core'), [(0, 3), (1, 2), (2, 1), (3, 0)])  4.8 us
  transfers between devices with their start and end apart: 20, of which 6 were waited for; matrix products, arithmetic and copies ran while one was open for 1% of the time, Pallas kernels for 9%

profile of v1, /device:TPU:2, one launch (start us, length us, event | category | flops | bytes accessed | tf_op | source)
XLA Modules:
  0.0 184.4 jit_solution(10130413157342063002)
XLA Ops:
  0.6 0.0 copy-start
  0.6 0.0 copy-start.5
  0.7 0.8 constant_dynamic-update-slice_fusion.1
  1.4 0.0 copy-done.5
  1.5 15.7 %collective-permute-start.3 = (bf16[128,256]{1,0:T(8,128)(2,1)S(1)}, bf16[128,256]{1,0:T(8,128)(2,1)S(1)}, u32[]{:S(2)}, u32[]{:S(2)}) collective-permute-start(bf16[128,256]{1,0:T(8,128)(2,1)S(1)} %constant_dynamic-update-slice_fusion), channel_id=1, source_target_pairs={{0,128},{16,144},{32,160},{48,176},{64,192},{80,208},{96,224},{112... | collective-permute-start | bytes 196616 | tf_op jit(solution)/shard_map/ppermute | solution.py:232
  17.2 4.3 %collective-permute-start.2 = (bf16[128,256]{1,0:T(8,128)(2,1)S(1)}, bf16[128,256]{1,0:T(8,128)(2,1)S(1)}, u32[]{:S(2)}, u32[]{:S(2)}) collective-permute-start(bf16[128,256]{1,0:T(8,128)(2,1)S(1)} %constant_dynamic-update-slice_fusion), channel_id=1, source_target_pairs={{0,64},{16,80},{32,96},{48,112},{64,128},{80,144},{96,160},{112,17... | collective-permute-start | bytes 196616 | tf_op jit(solution)/shard_map/ppermute | solution.py:232
  21.5 5.5 %collective-permute-start.1 = (bf16[128,256]{1,0:T(8,128)(2,1)S(1)}, bf16[128,256]{1,0:T(8,128)(2,1)S(1)}, u32[]{:S(2)}, u32[]{:S(2)}) collective-permute-start(bf16[128,256]{1,0:T(8,128)(2,1)S(1)} %constant_dynamic-update-slice_fusion), channel_id=1, source_target_pairs={{0,192},{16,208},{32,224},{48,240},{64,0},{80,16},{96,32},{112,48}... | collective-permute-start | bytes 196616 | tf_op jit(solution)/shard_map/ppermute | solution.py:232
  27.0 1.0 pad_maximum_fusion
  28.0 4.0 %collective-permute-start = (bf16[512,256]{1,0:T(8,128)(2,1)S(1)}, bf16[512,256]{1,0:T(8,128)(2,1)S(1)}, u32[]{:S(2)}, u32[]{:S(2)}) collective-permute-start(bf16[512,256]{1,0:T(8,128)(2,1)S(1)} %pad_maximum_fusion), channel_id=1, source_target_pairs={{0,256},{256,0},{1,257},{257,1},{2,258},{258,2},{3,259},{259,3},{4... | collective-permute-start | bytes 786440 | tf_op jit(solution)/shard_map/ppermute | solution.py:232
  32.0 0.1 pad_add_fusion
  32.1 0.0 copy-done
  32.1 0.4 compare_reduce_fusion
  32.5 0.1 reshape.15.refs_1_.member
  32.6 0.0 collective-permute-done.3
  32.6 0.0 collective-permute-done.2
  32.7 2.0 %collective-permute-done.1 = bf16[128,256]{1,0:T(8,128)(2,1)S(1)} collective-permute-done((bf16[128,256]{1,0:T(8,128)(2,1)S(1)}, bf16[128,256]{1,0:T(8,128)(2,1)S(1)}, u32[]{:S(2)}, u32[]{:S(2)}) %collective-permute-start.1) | collective-permute-done | bytes 65568 | tf_op jit(solution)/shard_map/ppermute | solution.py:232
  34.7 0.0 copy-start.1
  34.7 0.0 copy-start.2
  34.7 4.1 %collective-permute-start.5 = (bf16[512,256]{1,0:T(8,128)(2,1)S(1)}, bf16[512,256]{1,0:T(8,128)(2,1)S(1)}, u32[]{:S(2)}, u32[]{:S(2)}) collective-permute-start(bf16[512,256]{1,0:T(8,128)(2,1)S(1)} %pad_maximum_fusion.1.refs_5_.rest_0_), channel_id=1, source_target_pairs={{0,240},{16,0},{32,16},{48,32},{64,48},{80,64},{96,80},{112,96},{1... | collective-permute-start | bytes 786440 | tf_op jit(solution)/shard_map/ppermute | solution.py:232
  38.8 1.9 %collective-permute-start.4 = (bf16[512,256]{1,0:T(8,128)(2,1)S(1)}, bf16[512,256]{1,0:T(8,128)(2,1)S(1)}, u32[]{:S(2)}, u32[]{:S(2)}) collective-permute-start(bf16[512,256]{1,0:T(8,128)(2,1)S(1)} %pad_maximum_fusion.1.refs_5_.rest_0_), channel_id=1, source_target_pairs={{0,16},{16,32},{32,48},{48,64},{64,80},{80,96},{96,112},{112,128},... | collective-permute-start | bytes 786440 | tf_op jit(solution)/shard_map/ppermute | solution.py:232
  40.8 0.0 copy-start.6
  40.8 2.3 %collective-permute-start.7 = (bf16[256,256]{1,0:T(8,128)(2,1)S(1)}, bf16[256,256]{1,0:T(8,128)(2,1)S(1)}, u32[]{:S(2)}, u32[]{:S(2)}) collective-permute-start(bf16[256,256]{1,0:T(8,128)(2,1)S(1)} %get-tuple-element.16), channel_id=1, source_target_pairs={{0,32},{16,48},{32,64},{48,80},{64,96},{80,112},{96,128},{112,144}... | collective-permute-start | bytes 393224 | tf_op jit(solution)/shard_map/ppermute | solution.py:232
  43.1 5.6 %collective-permute-start.6 = (bf16[256,256]{1,0:T(8,128)(2,1)S(1)}, bf16[256,256]{1,0:T(8,128)(2,1)S(1)}, u32[]{:S(2)}, u32[]{:S(2)}) collective-permute-start(bf16[256,256]{1,0:T(8,128)(2,1)S(1)} %get-tuple-element.17), channel_id=1, source_target_pairs={{0,224},{16,240},{32,0},{48,16},{64,32},{80,48},{96,64},{112,80},{... | collective-permute-start | bytes 393224 | tf_op jit(solution)/shard_map/ppermute | solution.py:232
  48.8 0.0 copy-done.6
  48.8 0.0 collective-permute-done.refs_4_.far_ref
  48.8 0.0 copy-done.1
  48.8 0.0 copy-done.2
  48.8 2.5 %forward.2.rest_4_ = f32[64,128]{1,0:T(8,128)S(1)} custom-call(s32[16]{0:T(128)S(1)} %and_select_fusion.refs_0_.places, s32[128]{0:T(128)S(1)} %reshape.15.refs_1_.member, bf16[512,128]{1,0:T(8,128)(2,1)S(1)} %copy-done.1, bf16[512,128]{1,0:T(8,128)(2,1)S(1)} %copy-done.2, bf16[512,256]{1,0:T(8,128)(2,1)S(1)} %collective-permute-done.refs_4_.far_ref, ...), custom_call_target="tpu_custom_call" | custom-call | tf_op jit(solution)/shard_map/forward/pallas_call | solution.py:119
  51.3 0.0 copy-start.3
  51.3 0.0 copy-start.4
  51.4 0.6 collective-permute-done.7.rest_3_.rest_4_
  51.9 0.7 collective-permute-done.6.rest_2_.rest_3_
  52.6 0.0 collective-permute-done.5.rest_1_.rest_2_
  52.6 0.0 collective-permute-done.4.rest_0_.rest_1_
  52.6 6.3 %forward.3 = f32[64,128]{1,0:T(8,128)S(1)} custom-call(s32[16]{0:T(128)S(1)} %and_select_fusion.refs_0_.places, s32[128]{0:T(128)S(1)} %reshape.15.refs_1_.member, bf16[512,128]{1,0:T(8,128)(2,1)S(1)} %copy-done.1, bf16[512,128]{1,0:T(8,128)(2,1)S(1)} %copy-done.2, bf16[512,256]{1,0:T(8,128)(2,1)S(1)} %collective-permute-done.refs_4_.far_ref, ...), custom_call_target="tpu_custom_call" | custom-call | tf_op jit(solution)/shard_map/forward/pallas_call | solution.py:119
  58.9 7.1 %collective-permute-start.10 = (f32[64,128]{1,0:T(8,128)S(1)}, f32[64,128]{1,0:T(8,128)S(1)}, u32[]{:S(2)}, u32[]{:S(2)}) collective-permute-start(f32[64,128]{1,0:T(8,128)S(1)} %forward.3), channel_id=1, source_target_pairs={{0,128},{16,144},{32,160},{48,176},{64,192},{80,208},{96,224},{112... | collective-permute-start | bytes 98312 | tf_op jit(solution)/shard_map/ppermute | solution.py:232
  66.0 4.1 %collective-permute-start.9 = (f32[64,128]{1,0:T(8,128)S(1)}, f32[64,128]{1,0:T(8,128)S(1)}, u32[]{:S(2)}, u32[]{:S(2)}) collective-permute-start(f32[64,128]{1,0:T(8,128)S(1)} %forward.3), channel_id=1, source_target_pairs={{0,192},{16,208},{32,224},{48,240},{64,0},{80,16},{96,32},{112,48}... | collective-permute-start | bytes 98312 | tf_op jit(solution)/shard_map/ppermute | solution.py:232
  70.2 5.6 %collective-permute-start.8 = (f32[64,128]{1,0:T(8,128)S(1)}, f32[64,128]{1,0:T(8,128)S(1)}, u32[]{:S(2)}, u32[]{:S(2)}) collective-permute-start(f32[64,128]{1,0:T(8,128)S(1)} %forward.3), channel_id=1, source_target_pairs={{0,64},{16,80},{32,96},{48,112},{64,128},{80,144},{96,160},{112,17... | collective-permute-start | bytes 98312 | tf_op jit(solution)/shard_map/ppermute | solution.py:232
  75.8 1.9 %collective-permute-start.17 = (bf16[2048,128]{1,0:T(8,128)(2,1)S(1)}, bf16[2048,128]{1,0:T(8,128)(2,1)S(1)}, u32[]{:S(2)}, u32[]{:S(2)}) collective-permute-start(bf16[2048,128]{1,0:T(8,128)(2,1)S(1)} %copy-done.3), channel_id=1, source_target_pairs={{0,1},{1,0},{2,3},{3,2},{4,5},{5,4},{6,7},{7,6},{8,9},{9,8},{10,11... | collective-permute-start | bytes 1572872 | tf_op jit(solution)/shard_map/ppermute | solution.py:232
  77.7 2.4 %collective-permute-start.18 = (bf16[2048,128]{1,0:T(8,128)(2,1)S(1)}, bf16[2048,128]{1,0:T(8,128)(2,1)}, u32[]{:S(2)}, u32[]{:S(2)}) collective-permute-start(bf16[2048,128]{1,0:T(8,128)(2,1)S(1)} %copy-done.4), channel_id=1, source_target_pairs={{0,1},{1,0},{2,3},{3,2},{4,5},{5,4},{6,7},{7,6},{8,9},{9,8},{10,11... | collective-permute-start | bytes 1572872 | tf_op jit(solution)/shard_map/ppermute | solution.py:232
  80.1 0.0 collective-permute-done.10
  80.2 0.0 collective-permute-done.9
  80.2 0.0 collective-permute-done.8
  80.3 5.3 %collective-permute-start.13 = (f32[64,128]{1,0:T(8,128)S(1)}, f32[64,128]{1,0:T(8,128)S(1)}, u32[]{:S(2)}, u32[]{:S(2)}) collective-permute-start(f32[64,128]{1,0:T(8,128)S(1)} %pad_maximum_fusion.4), channel_id=1, source_target_pairs={{0,32},{16,48},{32,64},{48,80},{64,96},{80,112},{96,128},{112,144}... | collective-permute-start | bytes 98312 | tf_op jit(solution)/shard_map/ppermute | solution.py:232
  85.6 2.7 %collective-permute-start.12 = (f32[64,128]{1,0:T(8,128)S(1)}, f32[64,128]{1,0:T(8,128)S(1)}, u32[]{:S(2)}, u32[]{:S(2)}) collective-permute-start(f32[64,128]{1,0:T(8,128)S(1)} %pad_maximum_fusion.4), channel_id=1, source_target_pairs={{0,240},{16,0},{32,16},{48,32},{64,48},{80,64},{96,80},{112,96},{1... | collective-permute-start | bytes 98312 | tf_op jit(solution)/shard_map/ppermute | solution.py:232
  88.3 3.1 %collective-permute-start.11 = (f32[64,128]{1,0:T(8,128)S(1)}, f32[64,128]{1,0:T(8,128)S(1)}, u32[]{:S(2)}, u32[]{:S(2)}) collective-permute-start(f32[64,128]{1,0:T(8,128)S(1)} %pad_maximum_fusion.4), channel_id=1, source_target_pairs={{0,16},{16,32},{32,48},{48,64},{64,80},{80,96},{96,112},{112,128},... | collective-permute-start | bytes 98312 | tf_op jit(solution)/shard_map/ppermute | solution.py:232
  91.4 0.0 collective-permute-done.13
  91.4 0.0 collective-permute-done.12
  91.4 3.9 %collective-permute-done.11 = f32[64,128]{1,0:T(8,128)S(1)} collective-permute-done((f32[64,128]{1,0:T(8,128)S(1)}, f32[64,128]{1,0:T(8,128)S(1)}, u32[]{:S(2)}, u32[]{:S(2)}) %collective-permute-start.11) | collective-permute-done | bytes 32800 | tf_op jit(solution)/shard_map/ppermute | solution.py:232
  95.3 13.6 %backward.1 = (bf16[16,128,128]{2,1,0:T(8,128)(2,1)}, f32[256,256]{1,0:T(8,128)S(1)}, bf16[256,256]{1,0:T(8,128)(2,1)S(1)}, bf16[256,256]{1,0:T(8,128)(2,1)S(1)}, bf16[256,256]{1,0:T(8,128)(2,1)S(1)}) custom-call(s32[16]{0:T(128)S(1)} %and_select_fusion.refs_0_.places, s32[128]{0:T(128)S(1)} %reshape.15.refs_1_.member, s32[1]{0:T(128)} %bitcast.core, ...), custom_call_target="tpu_custom_call" | custom-call | tf_op jit(solution)/shard_map/backward/pallas_call | solution.py:193
  109.0 3.7 %collective-permute-start.14 = (bf16[256,256]{1,0:T(8,128)(2,1)S(1)}, bf16[256,256]{1,0:T(8,128)(2,1)S(1)}, u32[]{:S(2)}, u32[]{:S(2)}) collective-permute-start(bf16[256,256]{1,0:T(8,128)(2,1)S(1)} %get-tuple-element.9), channel_id=1, source_target_pairs={{0,256},{256,0},{1,257},{257,1},{2,258},{258,2},{3,259},{259,3},{4... | collective-permute-start | bytes 393224 | tf_op jit(solution)/shard_map/ppermute | solution.py:232
  112.7 1.9 %collective-permute-start.15 = (bf16[256,256]{1,0:T(8,128)(2,1)S(1)}, bf16[256,256]{1,0:T(8,128)(2,1)S(1)}, u32[]{:S(2)}, u32[]{:S(2)}) collective-permute-start(bf16[256,256]{1,0:T(8,128)(2,1)S(1)} %get-tuple-element.10), channel_id=1, source_target_pairs={{0,1},{1,0},{2,3},{3,2},{4,5},{5,4},{6,7},{7,6},{8,9},{9,8},{10,11... | collective-permute-start | bytes 393224 | tf_op jit(solution)/shard_map/ppermute | solution.py:232
  114.6 3.7 %collective-permute-start.16 = (bf16[256,256]{1,0:T(8,128)(2,1)S(1)}, bf16[256,256]{1,0:T(8,128)(2,1)S(1)}, u32[]{:S(2)}, u32[]{:S(2)}) collective-permute-start(bf16[256,256]{1,0:T(8,128)(2,1)S(1)} %get-tuple-element.11), channel_id=1, source_target_pairs={{0,257},{1,256},{256,1},{257,0},{2,259},{3,258},{258,3},{259,2},{4... | collective-permute-start | bytes 393224 | tf_op jit(solution)/shard_map/ppermute | solution.py:288
  118.4 0.0 collective-permute-done.14.from_half
  118.4 0.0 collective-permute-done.15.from_core
  118.4 4.8 %collective-permute-done.16.from_both = bf16[256,256]{1,0:T(8,128)(2,1)S(1)} collective-permute-done((bf16[256,256]{1,0:T(8,128)(2,1)S(1)}, bf16[256,256]{1,0:T(8,128)(2,1)S(1)}, u32[]{:S(2)}, u32[]{:S(2)}) %collective-permute-start.16) | collective-permute-done | bytes 131104 | tf_op jit(solution)/shard_map/ppermute | solution.py:288
  123.2 0.0 collective-permute-done.17.far_kw
  123.2 0.0 collective-permute-done.18.far_vw
  123.2 2.3 %project.1 = bf16[16,256,128]{2,1,0:T(8,128)(2,1)S(1)} custom-call(f32[256,256]{1,0:T(8,128)S(1)} %get-tuple-element.8.kept, bf16[256,256]{1,0:T(8,128)(2,1)S(1)} %collective-permute-done.14.from_half, bf16[256,256]{1,0:T(8,128)(2,1)S(1)} %collective-permute-done.15.from_core, bf16[256,256]{1,0:T(8,128)(2,1)S(1)} %collective-permute-done.16.from_both, ...), custom_call_target="tpu_custom_call" | custom-call | tf_op jit(solution)/shard_map/project/pallas_call | solution.py:291
  125.5 20.9 %all_to_all.10 = bf16[16,256,128]{2,1,0:T(8,128)(2,1)S(1)} all-to-all(bf16[16,256,128]{2,1,0:T(8,128)(2,1)S(1)} %project.1), channel_id=1, replica_groups=mesh['xh'=2,'z'=16,'xl'=2,'y'=4,'core'=2] {'xl','y','core'}, dimensions={0} | all-to-all | bytes 2097152 | tf_op jit(solution)/shard_map/all_to_all | solution.py:299
  146.4 8.3 %all-to-all-start = ((bf16[16,128,128]{2,1,0:T(8,128)(2,1)}), bf16[16,128,128]{2,1,0:T(8,128)(2,1)S(1)}, u32[]{:S(2)}, u32[]{:S(2)}) async-start(bf16[16,128,128]{2,1,0:T(8,128)(2,1)} %get-tuple-element.7), calls=%async_computation | async-start | bytes 1048576 | tf_op jit(solution)/shard_map/all_to_all | solution.py:300
  154.7 0.8 reduce.1
  155.5 28.3 %all-to-all-done = bf16[16,128,128]{2,1,0:T(8,128)(2,1)S(1)} async-done(((bf16[16,128,128]{2,1,0:T(8,128)(2,1)}), bf16[16,128,128]{2,1,0:T(8,128)(2,1)S(1)}, u32[]{:S(2)}, u32[]{:S(2)}) %all-to-all-start) | async-done | bytes 524320 | tf_op jit(solution)/shard_map/all_to_all | solution.py:300
  183.8 0.7 reduce_sum.21
  (14 shorter events, 0.2 us)
Async XLA Ops:
  0.6 31.5 %copy-start = (s32[32,64]{1,0:T(8,128)S(1)}, s32[32,64]{1,0:T(8,128)}, u32[]{:S(2)}) copy-start(s32[32,64]{1,0:T(8,128)} %param.14) | copy-start | bytes 24580
  0.6 0.8 copy-start.5
  1.5 31.2 %collective-permute-start.3 = (bf16[128,256]{1,0:T(8,128)(2,1)S(1)}, bf16[128,256]{1,0:T(8,128)(2,1)S(1)}, u32[]{:S(2)}, u32[]{:S(2)}) collective-permute-start(bf16[128,256]{1,0:T(8,128)(2,1)S(1)} %constant_dynamic-update-slice_fusion), channel_id=1, source_target_pairs={{0,128},{16,144},{32,160},{48,176},{64,192},{80,208},{96,224},{112... | collective-permute-start | bytes 196616 | tf_op jit(solution)/shard_map/ppermute | solution.py:232
  17.2 15.5 %collective-permute-start.2 = (bf16[128,256]{1,0:T(8,128)(2,1)S(1)}, bf16[128,256]{1,0:T(8,128)(2,1)S(1)}, u32[]{:S(2)}, u32[]{:S(2)}) collective-permute-start(bf16[128,256]{1,0:T(8,128)(2,1)S(1)} %constant_dynamic-update-slice_fusion), channel_id=1, source_target_pairs={{0,64},{16,80},{32,96},{48,112},{64,128},{80,144},{96,160},{112,17... | collective-permute-start | bytes 196616 | tf_op jit(solution)/shard_map/ppermute | solution.py:232
  21.5 13.2 %collective-permute-start.1 = (bf16[128,256]{1,0:T(8,128)(2,1)S(1)}, bf16[128,256]{1,0:T(8,128)(2,1)S(1)}, u32[]{:S(2)}, u32[]{:S(2)}) collective-permute-start(bf16[128,256]{1,0:T(8,128)(2,1)S(1)} %constant_dynamic-update-slice_fusion), channel_id=1, source_target_pairs={{0,192},{16,208},{32,224},{48,240},{64,0},{80,16},{96,32},{112,48}... | collective-permute-start | bytes 196616 | tf_op jit(solution)/shard_map/ppermute | solution.py:232
  28.0 20.8 %collective-permute-start = (bf16[512,256]{1,0:T(8,128)(2,1)S(1)}, bf16[512,256]{1,0:T(8,128)(2,1)S(1)}, u32[]{:S(2)}, u32[]{:S(2)}) collective-permute-start(bf16[512,256]{1,0:T(8,128)(2,1)S(1)} %pad_maximum_fusion), channel_id=1, source_target_pairs={{0,256},{256,0},{1,257},{257,1},{2,258},{258,2},{3,259},{259,3},{4... | collective-permute-start | bytes 786440 | tf_op jit(solution)/shard_map/ppermute | solution.py:232
  34.7 14.1 %copy-start.1 = (bf16[512,128]{1,0:T(8,128)(2,1)S(1)}, bf16[512,128]{1,0:T(8,128)(2,1)}, u32[]{:S(2)}) copy-start(bf16[512,128]{1,0:T(8,128)(2,1)} %k_ref.3) | copy-start | bytes 393220
  34.7 14.1 %copy-start.2 = (bf16[512,128]{1,0:T(8,128)(2,1)S(1)}, bf16[512,128]{1,0:T(8,128)(2,1)}, u32[]{:S(2)}) copy-start(bf16[512,128]{1,0:T(8,128)(2,1)} %v_ref.3) | copy-start | bytes 393220
  34.7 17.9 %collective-permute-start.5 = (bf16[512,256]{1,0:T(8,128)(2,1)S(1)}, bf16[512,256]{1,0:T(8,128)(2,1)S(1)}, u32[]{:S(2)}, u32[]{:S(2)}) collective-permute-start(bf16[512,256]{1,0:T(8,128)(2,1)S(1)} %pad_maximum_fusion.1.refs_5_.rest_0_), channel_id=1, source_target_pairs={{0,240},{16,0},{32,16},{48,32},{64,48},{80,64},{96,80},{112,96},{1... | collective-permute-start | bytes 786440 | tf_op jit(solution)/shard_map/ppermute | solution.py:232
  38.8 13.8 %collective-permute-start.4 = (bf16[512,256]{1,0:T(8,128)(2,1)S(1)}, bf16[512,256]{1,0:T(8,128)(2,1)S(1)}, u32[]{:S(2)}, u32[]{:S(2)}) collective-permute-start(bf16[512,256]{1,0:T(8,128)(2,1)S(1)} %pad_maximum_fusion.1.refs_5_.rest_0_), channel_id=1, source_target_pairs={{0,16},{16,32},{32,48},{48,64},{64,80},{80,96},{96,112},{112,128},... | collective-permute-start | bytes 786440 | tf_op jit(solution)/shard_map/ppermute | solution.py:232
  40.8 8.0 %copy-start.6 = (s32[16]{0:T(128)S(1)}, s32[16]{0:T(128)}, u32[]{:S(2)}) copy-start(s32[16]{0:T(128)} %constant.43.clone) | copy-start | bytes 196
  40.8 11.1 %collective-permute-start.7 = (bf16[256,256]{1,0:T(8,128)(2,1)S(1)}, bf16[256,256]{1,0:T(8,128)(2,1)S(1)}, u32[]{:S(2)}, u32[]{:S(2)}) collective-permute-start(bf16[256,256]{1,0:T(8,128)(2,1)S(1)} %get-tuple-element.16), channel_id=1, source_target_pairs={{0,32},{16,48},{32,64},{48,80},{64,96},{80,112},{96,128},{112,144}... | collective-permute-start | bytes 393224 | tf_op jit(solution)/shard_map/ppermute | solution.py:232
  43.1 9.5 %collective-permute-start.6 = (bf16[256,256]{1,0:T(8,128)(2,1)S(1)}, bf16[256,256]{1,0:T(8,128)(2,1)S(1)}, u32[]{:S(2)}, u32[]{:S(2)}) collective-permute-start(bf16[256,256]{1,0:T(8,128)(2,1)S(1)} %get-tuple-element.17), channel_id=1, source_target_pairs={{0,224},{16,240},{32,0},{48,16},{64,32},{80,48},{96,64},{112,80},{... | collective-permute-start | bytes 393224 | tf_op jit(solution)/shard_map/ppermute | solution.py:232
  51.3 24.5 %copy-start.3 = (bf16[2048,128]{1,0:T(8,128)(2,1)S(1)}, bf16[2048,128]{1,0:T(8,128)(2,1)}, u32[]{:S(2)}) copy-start(bf16[2048,128]{1,0:T(8,128)(2,1)} %kw.1) | copy-start | bytes 1572868
  51.3 26.4 %copy-start.4 = (bf16[2048,128]{1,0:T(8,128)(2,1)S(1)}, bf16[2048,128]{1,0:T(8,128)(2,1)}, u32[]{:S(2)}) copy-start(bf16[2048,128]{1,0:T(8,128)(2,1)} %vw.1) | copy-start | bytes 1572868
  58.9 21.2 %collective-permute-start.10 = (f32[64,128]{1,0:T(8,128)S(1)}, f32[64,128]{1,0:T(8,128)S(1)}, u32[]{:S(2)}, u32[]{:S(2)}) collective-permute-start(f32[64,128]{1,0:T(8,128)S(1)} %forward.3), channel_id=1, source_target_pairs={{0,128},{16,144},{32,160},{48,176},{64,192},{80,208},{96,224},{112... | collective-permute-start | bytes 98312 | tf_op jit(solution)/shard_map/ppermute | solution.py:232
  66.0 14.1 %collective-permute-start.9 = (f32[64,128]{1,0:T(8,128)S(1)}, f32[64,128]{1,0:T(8,128)S(1)}, u32[]{:S(2)}, u32[]{:S(2)}) collective-permute-start(f32[64,128]{1,0:T(8,128)S(1)} %forward.3), channel_id=1, source_target_pairs={{0,192},{16,208},{32,224},{48,240},{64,0},{80,16},{96,32},{112,48}... | collective-permute-start | bytes 98312 | tf_op jit(solution)/shard_map/ppermute | solution.py:232
  70.2 10.0 %collective-permute-start.8 = (f32[64,128]{1,0:T(8,128)S(1)}, f32[64,128]{1,0:T(8,128)S(1)}, u32[]{:S(2)}, u32[]{:S(2)}) collective-permute-start(f32[64,128]{1,0:T(8,128)S(1)} %forward.3), channel_id=1, source_target_pairs={{0,64},{16,80},{32,96},{48,112},{64,128},{80,144},{96,160},{112,17... | collective-permute-start | bytes 98312 | tf_op jit(solution)/shard_map/ppermute | solution.py:232
  75.8 47.4 %collective-permute-start.17 = (bf16[2048,128]{1,0:T(8,128)(2,1)S(1)}, bf16[2048,128]{1,0:T(8,128)(2,1)S(1)}, u32[]{:S(2)}, u32[]{:S(2)}) collective-permute-start(bf16[2048,128]{1,0:T(8,128)(2,1)S(1)} %copy-done.3), channel_id=1, source_target_pairs={{0,1},{1,0},{2,3},{3,2},{4,5},{5,4},{6,7},{7,6},{8,9},{9,8},{10,11... | collective-permute-start | bytes 1572872 | tf_op jit(solution)/shard_map/ppermute | solution.py:232
  77.7 45.5 %collective-permute-start.18 = (bf16[2048,128]{1,0:T(8,128)(2,1)S(1)}, bf16[2048,128]{1,0:T(8,128)(2,1)}, u32[]{:S(2)}, u32[]{:S(2)}) collective-permute-start(bf16[2048,128]{1,0:T(8,128)(2,1)S(1)} %copy-done.4), channel_id=1, source_target_pairs={{0,1},{1,0},{2,3},{3,2},{4,5},{5,4},{6,7},{7,6},{8,9},{9,8},{10,11... | collective-permute-start | bytes 1572872 | tf_op jit(solution)/shard_map/ppermute | solution.py:232
  80.3 11.2 %collective-permute-start.13 = (f32[64,128]{1,0:T(8,128)S(1)}, f32[64,128]{1,0:T(8,128)S(1)}, u32[]{:S(2)}, u32[]{:S(2)}) collective-permute-start(f32[64,128]{1,0:T(8,128)S(1)} %pad_maximum_fusion.4), channel_id=1, source_target_pairs={{0,32},{16,48},{32,64},{48,80},{64,96},{80,112},{96,128},{112,144}... | collective-permute-start | bytes 98312 | tf_op jit(solution)/shard_map/ppermute | solution.py:232
  85.6 5.9 %collective-permute-start.12 = (f32[64,128]{1,0:T(8,128)S(1)}, f32[64,128]{1,0:T(8,128)S(1)}, u32[]{:S(2)}, u32[]{:S(2)}) collective-permute-start(f32[64,128]{1,0:T(8,128)S(1)} %pad_maximum_fusion.4), channel_id=1, source_target_pairs={{0,240},{16,0},{32,16},{48,32},{64,48},{80,64},{96,80},{112,96},{1... | collective-permute-start | bytes 98312 | tf_op jit(solution)/shard_map/ppermute | solution.py:232
  88.3 7.0 %collective-permute-start.11 = (f32[64,128]{1,0:T(8,128)S(1)}, f32[64,128]{1,0:T(8,128)S(1)}, u32[]{:S(2)}, u32[]{:S(2)}) collective-permute-start(f32[64,128]{1,0:T(8,128)S(1)} %pad_maximum_fusion.4), channel_id=1, source_target_pairs={{0,16},{16,32},{32,48},{48,64},{64,80},{80,96},{96,112},{112,128},... | collective-permute-start | bytes 98312 | tf_op jit(solution)/shard_map/ppermute | solution.py:232
  109.0 9.4 %collective-permute-start.14 = (bf16[256,256]{1,0:T(8,128)(2,1)S(1)}, bf16[256,256]{1,0:T(8,128)(2,1)S(1)}, u32[]{:S(2)}, u32[]{:S(2)}) collective-permute-start(bf16[256,256]{1,0:T(8,128)(2,1)S(1)} %get-tuple-element.9), channel_id=1, source_target_pairs={{0,256},{256,0},{1,257},{257,1},{2,258},{258,2},{3,259},{259,3},{4... | collective-permute-start | bytes 393224 | tf_op jit(solution)/shard_map/ppermute | solution.py:232
  112.7 5.7 %collective-permute-start.15 = (bf16[256,256]{1,0:T(8,128)(2,1)S(1)}, bf16[256,256]{1,0:T(8,128)(2,1)S(1)}, u32[]{:S(2)}, u32[]{:S(2)}) collective-permute-start(bf16[256,256]{1,0:T(8,128)(2,1)S(1)} %get-tuple-element.10), channel_id=1, source_target_pairs={{0,1},{1,0},{2,3},{3,2},{4,5},{5,4},{6,7},{7,6},{8,9},{9,8},{10,11... | collective-permute-start | bytes 393224 | tf_op jit(solution)/shard_map/ppermute | solution.py:232
  114.6 8.6 %collective-permute-start.16 = (bf16[256,256]{1,0:T(8,128)(2,1)S(1)}, bf16[256,256]{1,0:T(8,128)(2,1)S(1)}, u32[]{:S(2)}, u32[]{:S(2)}) collective-permute-start(bf16[256,256]{1,0:T(8,128)(2,1)S(1)} %get-tuple-element.11), channel_id=1, source_target_pairs={{0,257},{1,256},{256,1},{257,0},{2,259},{3,258},{258,3},{259,2},{4... | collective-permute-start | bytes 393224 | tf_op jit(solution)/shard_map/ppermute | solution.py:288
  146.4 37.3 %all-to-all-start = ((bf16[16,128,128]{2,1,0:T(8,128)(2,1)}), bf16[16,128,128]{2,1,0:T(8,128)(2,1)S(1)}, u32[]{:S(2)}, u32[]{:S(2)}) async-start(bf16[16,128,128]{2,1,0:T(8,128)(2,1)} %get-tuple-element.7), calls=%async_computation | async-start | bytes 1048576 | tf_op jit(solution)/shard_map/all_to_all | solution.py:300

commit v2 on v1

v2 whole, which is shorter than its diff:
```python
from functools import partial

import jax
import jax.numpy as jnp
from jax import lax
from jax.experimental import pallas as pl
from jax.experimental.pallas import tpu as pltpu
from jax.sharding import Mesh, PartitionSpec as P

HEAD_DIM = 64
BLOCK = 128
AXES = ("xh", "zh", "zl", "xl", "y", "core")
SIZES = (2, 4, 4, 2, 4, 2)
Z = ("zh", "zl")
CTX = ("xh", "zh", "zl")
HEAD = ("xl", "y", "core")
BIG = 1e30

VMEM = pl.BlockSpec(memory_space=pltpu.VMEM)
SMEM = pl.BlockSpec(memory_space=pltpu.SMEM)
ROOM = pltpu.CompilerParams(vmem_limit_bytes=48 * 1024 * 1024)


def cost(flops, exps):
    return pl.CostEstimate(flops=4 * flops, bytes_accessed=1 << 20, transcendentals=exps)


def dot_nt(a, b):
    return lax.dot_general(a, b, (((1,), (1,)), ((), ())), preferred_element_type=jnp.float32)


def dot_nn(a, b):
    return lax.dot_general(a, b, (((1,), (0,)), ((), ())), preferred_element_type=jnp.float32)


def split_heads(rows):
    low = lax.broadcasted_iota(jnp.int32, rows.shape, 1) < HEAD_DIM
    zero = jnp.zeros_like(rows)
    return jnp.concatenate([jnp.where(low, rows, zero), jnp.where(low, zero, rows)], axis=0)


def load_keys(near_ref, far_ref, keys, vals):
    rows = near_ref.shape[0]
    keys[:rows, :] = near_ref[:, :BLOCK]
    vals[:rows, :] = near_ref[:, BLOCK:]
    keys[rows:, :] = far_ref[:, :BLOCK]
    vals[rows:, :] = far_ref[:, BLOCK:]


def load_targets(pieces, held):
    at = 0
    for piece in pieces:
        held[at : at + piece.shape[0], :] = piece[...]
        at += piece.shape[0]


def away(member, first, second, block, blocks):
    seg = (lax.broadcasted_iota(jnp.int32, (1, 4 * BLOCK), 1) // BLOCK) % 2
    one = jnp.where(member[first * blocks + block] > 0, 0.0, BIG)
    two = jnp.where(member[second * blocks + block] > 0, 0.0, BIG)
    return jnp.where(seg == 0, one, two)


def forward_kernel(base, places, member, near_ref, far_ref, *rest):
    *pieces, before, stats, keys, vals, held = rest
    load_keys(near_ref, far_ref, keys, vals)
    load_targets(pieces, held)
    blocks = keys.shape[0] // BLOCK
    pairs = held.shape[0] // (2 * BLOCK)
    half = stats.shape[0] // 2
    if before is not None:
        stats[...] = before[...]

    def step(p, carry):
        rows = pl.ds(pl.multiple_of(p * 2 * BLOCK, 2 * BLOCK), 2 * BLOCK)
        first, second = places[base + 2 * p], places[base + 2 * p + 1]
        query = split_heads(held[rows, :BLOCK])
        out = split_heads(held[rows, BLOCK:])
        logits = dot_nt(keys[...], query)
        prob = dot_nt(vals[...], out)
        off = [away(member, first, second, b, blocks) for b in range(blocks)]
        peak = jnp.full((1, 4 * BLOCK), -1e3, jnp.float32)
        for b in range(blocks):
            part = logits[b * BLOCK : (b + 1) * BLOCK]
            peak = jnp.maximum(peak, jnp.max(part, axis=0, keepdims=True) - off[b])
        total = jnp.zeros((1, 4 * BLOCK), jnp.float32)
        weighted = jnp.zeros((1, 4 * BLOCK), jnp.float32)
        for b in range(blocks):
            part = slice(b * BLOCK, (b + 1) * BLOCK)
            raised = jnp.exp(logits[part] - (peak + off[b]))
            total = total + jnp.sum(raised, axis=0, keepdims=True)
            weighted = weighted + jnp.sum(raised * prob[part], axis=0, keepdims=True)
        some = total > 0.0
        log_total = jnp.where(some, peak + jnp.log(jnp.where(some, total, 1.0)), -BIG)
        mean = jnp.where(some, weighted / jnp.where(some, total, 1.0), 0.0)
        for h in range(2):
            for s, place in enumerate((first, second)):
                lanes = slice((2 * h + s) * BLOCK, (2 * h + s + 1) * BLOCK)
                stats[pl.ds(2 * place + h, 1), :] = log_total[:, lanes]
                stats[pl.ds(half + 2 * place + h, 1), :] = mean[:, lanes]
        return carry

    def two(i, carry):
        return step(2 * i + 1, step(2 * i, carry))

    lax.fori_loop(0, pairs // 2, two, 0)


def forward(base, places, member, near, far, pieces, before):
    count = places.shape[0]
    rows = sum(p.shape[0] for p in pieces)
    enc = near.shape[0] + far.shape[0]
    given = [places, member, near, far, *pieces]
    specs = [SMEM, SMEM] + [VMEM] * (2 + len(pieces))
    if before is None:
        def kernel(*refs):
            ins, outs = refs[: len(given)], refs[len(given) :]
            forward_kernel(base, *ins, None, *outs)
    else:
        given.append(before)
        specs.append(VMEM)
        kernel = partial(forward_kernel, base)
    return pl.pallas_call(
        kernel,
        out_shape=jax.ShapeDtypeStruct((4 * count, BLOCK), jnp.float32),
        in_specs=specs,
        out_specs=VMEM,
        scratch_shapes=[
            pltpu.VMEM((enc, BLOCK), jnp.bfloat16),
            pltpu.VMEM((enc, BLOCK), jnp.bfloat16),
            pltpu.VMEM((rows, 2 * BLOCK), jnp.bfloat16),
        ],
        compiler_params=ROOM,
        cost_estimate=cost(2 * rows * enc * 4 * BLOCK, rows * enc * 2),
        name="forward",
    )(*given)


def backward_kernel(base, places, member, core, stats, kv_ref, before, *rest):
    pieces = rest[:5]
    d_query, stay, leave, held, turned, chances, slopes, d_key, d_value = rest[5:]
    load_targets(pieces, held)
    enc = kv_ref.shape[0]
    blocks = enc // BLOCK
    pairs = held.shape[0] // (2 * BLOCK)
    half = stats.shape[0] // 2
    turned[...] = kv_ref[:, :BLOCK].T
    d_key[...] = jnp.zeros_like(d_key)
    d_value[...] = jnp.zeros_like(d_value)

    def step(p, u):
        rows = pl.ds(pl.multiple_of(p * 2 * BLOCK, 2 * BLOCK), 2 * BLOCK)
        first, second = places[2 * p], places[2 * p + 1]
        query = split_heads(held[rows, :BLOCK])
        out = split_heads(held[rows, BLOCK:])
        spots = [2 * place + h for h in range(2) for place in (first, second)]
        log_total = jnp.concatenate([stats[pl.ds(s, 1), :] for s in spots], axis=1)
        delta = jnp.concatenate([stats[pl.ds(half + s, 1), :] for s in spots], axis=1)
        logits = dot_nt(kv_ref[:, :BLOCK], query)
        prob = dot_nt(kv_ref[:, BLOCK:], out)
        for b in range(blocks):
            part = slice(b * BLOCK, (b + 1) * BLOCK)
            off = away(member, first, second, base + b, 2 * blocks)
            chance = jnp.exp(logits[part] - (log_total + off))
            chances[u, part, :] = chance.astype(jnp.bfloat16)
            slopes[u, part, :] = (chance * (prob[part] - delta)).astype(jnp.bfloat16)
        d_value[...] += dot_nn(chances[u], out)
        d_key[...] += dot_nn(slopes[u], query)
        both = dot_nn(turned[...], slopes[u]).T
        low = lax.broadcasted_iota(jnp.int32, (2 * BLOCK, BLOCK), 1) < HEAD_DIM
        grad = jnp.where(low, both[: 2 * BLOCK], both[2 * BLOCK :])
        for place, part in ((first, grad[:BLOCK]), (second, grad[BLOCK:])):
            if before is not None:
                part = part + before[place]
            d_query[place] = part.astype(d_query.dtype)

    def two(i, carry):
        step(2 * i, 0)
        step(2 * i + 1, 1)
        return carry

    lax.fori_loop(0, pairs // 2, two, 0)
    mine = core[0]
    for target, part in ((stay, mine), (leave, 1 - mine)):
        rows = pl.ds(pl.multiple_of(part * (enc // 2), enc // 2), enc // 2)
        target[:, :BLOCK] = d_key[rows, :].astype(target.dtype)
        target[:, BLOCK:] = d_value[rows, :].astype(target.dtype)


def backward(base, places, member, core, stats, kv, pieces, before, kinds):
    count = places.shape[0]
    rows = sum(p.shape[0] for p in pieces)
    enc = kv.shape[0]
    shape = (enc // 2, 2 * BLOCK)
    given = [places, member, core, stats, kv]
    fixed = len(given)
    if before is None:
        def kernel(*refs):
            backward_kernel(base, *refs[:fixed], None, *refs[fixed:])
    else:
        given.append(before)
        kernel = partial(backward_kernel, base)
    given += pieces
    return pl.pallas_call(
        kernel,
        out_shape=(
            jax.ShapeDtypeStruct((count, BLOCK, BLOCK), kinds[0]),
            jax.ShapeDtypeStruct(shape, kinds[1]),
            jax.ShapeDtypeStruct(shape, kinds[2]),
        ),
        in_specs=[SMEM] * 3 + [VMEM] * (len(given) - 3),
        out_specs=(VMEM,) * 3,
        scratch_shapes=[
            pltpu.VMEM((rows, 2 * BLOCK), jnp.bfloat16),
            pltpu.VMEM((BLOCK, enc), jnp.bfloat16),
            pltpu.VMEM((2, enc, 4 * BLOCK), jnp.bfloat16),
            pltpu.VMEM((2, enc, 4 * BLOCK), jnp.bfloat16),
            pltpu.VMEM((enc, BLOCK), jnp.float32),
            pltpu.VMEM((enc, BLOCK), jnp.float32),
        ],
        compiler_params=ROOM,
        cost_estimate=cost(5 * rows * enc * 4 * BLOCK, rows * enc * 2),
        name="backward",
    )(*given)


def project_kernel(part, kept, from_half, from_core, from_both, kw, vw, far, *rest):
    *before, memory = rest
    mine = (kept[...] + from_half[...].astype(jnp.float32)).astype(jnp.bfloat16)
    other = (from_core[...].astype(jnp.float32) + from_both[...].astype(jnp.float32)).astype(jnp.bfloat16)
    chunks = memory.shape[0]
    for j in range(chunks):
        rows = pl.ds(pl.multiple_of((part[0] * chunks + j) * BLOCK, BLOCK), BLOCK)
        total = dot_nt(mine[:, :BLOCK], kw[rows, :]) + dot_nt(mine[:, BLOCK:], vw[rows, :])
        total = total + dot_nt(other, far[rows, :])
        for piece in before:
            total = total + piece[j].astype(jnp.float32)
        memory[j] = total.astype(jnp.bfloat16)


def project(part, chunks, *given):
    return pl.pallas_call(
        project_kernel,
        out_shape=jax.ShapeDtypeStruct((chunks, given[0].shape[0], BLOCK), jnp.bfloat16),
        in_specs=[SMEM] + [VMEM] * len(given),
        out_specs=VMEM,
        compiler_params=ROOM,
        name="project",
    )(part[None], *given)


def moved(value, axis, steps):
    count = lax.axis_size(axis)
    return lax.ppermute(value, axis, [(i, (i + steps) % count) for i in range(count)])


def merged(parts):
    half = parts[0].shape[0] // 2
    logs = [p[:half] for p in parts]
    top = logs[0]
    for log in logs[1:]:
        top = jnp.maximum(top, log)
    weights = [jnp.exp(log - top) for log in logs]
    total = sum(weights[1:], weights[0])
    mean = sum((w * p[half:] for w, p in zip(weights[1:], parts[1:])), weights[0] * parts[0][half:])
    return jnp.concatenate([top + jnp.log(total), mean / total], axis=0)


def spread(value, axis):
    count = lax.axis_size(axis)
    return lax.all_to_all(jnp.broadcast_to(value, (count, *value.shape)), axis, 0, 0, tiled=True)


def body(queries, keys, values, d_out, key_weight, value_weight, block_lists):
    half = lax.axis_index("xh")
    place = lax.axis_index(Z)
    core = lax.axis_index("core")
    depth = lax.axis_size(Z)
    high, low = lax.axis_size("zh"), lax.axis_size("zl")
    enc_blocks = keys.shape[0] // BLOCK

    near = jnp.concatenate([queries, d_out], axis=1)
    bundle = spread(near, "zh").reshape(high * BLOCK, 2 * BLOCK)

    strides = low * jnp.arange(high, dtype=jnp.int32)
    places = jnp.concatenate([strides + (place + step) % low for step in (0, -1, 1, 2)])
    listed = lax.dynamic_slice_in_dim(block_lists, half * depth, depth, 0)
    step = jnp.arange(enc_blocks, dtype=jnp.int32)
    ids = jnp.concatenate(
        [(half * depth + place) * enc_blocks + step, ((1 - half) * depth + place) * enc_blocks + step]
    )
    member = jnp.any(listed[:, :, None] == ids[None, None, :], axis=1).astype(jnp.int32).reshape(-1)

    below = moved(bundle, Z, 1)
    above = moved(bundle, Z, -1)
    above2 = moved(bundle[: 2 * BLOCK], Z, -2)
    below2 = moved(bundle[2 * BLOCK :], Z, 2)
    own, bundle = lax.optimization_barrier((jnp.concatenate([keys, values], axis=1), bundle))
    far = moved(own, "xh", 1)

    early = forward(0, places, member, own, far, [bundle], None)
    pieces = [below, above, above2, below2]
    stats = forward(high, places, member, own, far, pieces, early)
    stats = merged(list(spread(stats, "zh")))
    stats = merged([stats, moved(stats, Z, 2)])
    stats = merged([stats, moved(stats, Z, 1)])

    weights, stats = lax.optimization_barrier((jnp.concatenate([key_weight, value_weight], axis=1), stats))
    pieces = [bundle, *pieces]
    f32, bf16 = jnp.float32, jnp.bfloat16
    d_query, to_half, to_both = backward(
        enc_blocks, places, member, core[None], stats, far, pieces, None, (f32, bf16, bf16)
    )
    from_half = moved(to_half, "xh", 1)
    from_both = lax.ppermute(to_both, ("xh", "core"), [(0, 3), (1, 2), (2, 1), (3, 0)])
    far_weights = moved(weights, "core", 1)
    d_query, kept, to_core = backward(
        0, places, member, core[None], stats, own, pieces, d_query, (bf16, f32, bf16)
    )
    d_query, to_core, from_half, from_both, far_weights = lax.optimization_barrier(
        (d_query, to_core, from_half, from_both, far_weights)
    )
    d_query = lax.all_to_all(d_query, Z, 0, 0, tiled=True)
    from_core = moved(to_core, "core", 1)

    side = lax.axis_index("xl")
    sides = lax.axis_size("xl")
    chunks = key_weight.shape[0] // (sides * BLOCK)
    given = (kept, from_half, from_core, from_both, key_weight, value_weight, far_weights)
    if sides > 1:
        given += (moved(project(1 - side, chunks, *given), "xl", 1),)
    memory, d_query = lax.optimization_barrier((project(side, chunks, *given), d_query))
    memory = lax.all_to_all(memory, ("y", "core"), 0, 0, tiled=True)

    cores = lax.axis_size("core")
    memory = memory.reshape(chunks // cores, cores, *memory.shape[1:]).astype(f32)
    d_memory = jnp.sum(memory, axis=0).reshape(keys.shape).astype(bf16)
    d_queries = jnp.sum(d_query.astype(f32), axis=0).astype(bf16)
    return d_queries, d_memory


def solution(mesh):
    fine = Mesh(mesh.devices.reshape(SIZES), AXES)
    placed = P(CTX, HEAD)
    return jax.shard_map(
        body,
        mesh=fine,
        in_specs=(placed, placed, placed, placed, P(None, HEAD), P(None, HEAD), P()),
        out_specs=(placed, placed),
        check_vma=False,
    )
```

time: 185 us -> 180 us (0.973)
  the two profiles are of different devices: /device:TPU:2 before, /device:TPU:1 now
where the time goes in v2:
time: 180 us; the launch traced here: 179 us
  starting transfers between devices  74.5 us (41%)
  waiting for transfers between devices  54.9 us (30%)
  Pallas kernels  24.6 us (14%)
  blocking collectives  15.6 us (9%)
  local copies, waits for them, and re-layouts  4.3 us (2%)
  other arithmetic  4.09 us (2%)
    ppermute x11, starting transfers between devices, moved(): lax.ppermute(value, axis, [(i, (i + steps) % count) for i in range(count)])  41 us
    ppermute x11, waiting for transfers between devices, moved(): lax.ppermute(value, axis, [(i, (i + steps) % count) for i in range(count)])  29.4 us
    all_to_all x1, starting transfers between devices, spread(): lax.all_to_all(jnp.broadcast_to(value, (count, *value.shape)), axis, 0, 0...  15.6 us
    all_to_all x1, blocking collectives, spread(): lax.all_to_all(jnp.broadcast_to(value, (count, *value.shape)), axis, 0, 0...  15.6 us
    pallas_call x2, Pallas kernels, backward(): pl.pallas_call(kernel, out_shape=(jax.ShapeDtypeStruct((count, BLOCK, BLO...  14.1 us
    all_to_all x1, waiting for transfers between devices, spread(): lax.all_to_all(jnp.broadcast_to(value, (count, *value.shape)), axis, 0, 0...  13.2 us
    all_to_all x1, starting transfers between devices, body(): memory = lax.all_to_all(memory, ('y', 'core'), 0, 0, tiled=True)  9.3 us
    all_to_all x1, waiting for transfers between devices, body(): memory = lax.all_to_all(memory, ('y', 'core'), 0, 0, tiled=True)  8.79 us
  transfers between devices with their start and end apart: 15, of which 9 were waited for; matrix products, arithmetic and copies ran while one was open for 1% of the time, Pallas kernels for 10%

profile of v2, /device:TPU:1, one launch (start us, length us, event | category | flops | bytes accessed | tf_op | source)
XLA Modules:
  0.0 179.0 jit_solution(7805226409013259129)
XLA Ops:
  0.6 0.0 copy-start
  0.6 0.0 copy-start.12
  0.7 0.0 copy-start.11
  0.7 0.8 pad_maximum_fusion.2
  1.5 0.7 broadcast_in_dim.20
  2.2 15.6 %all-to-all-start = ((bf16[4,128,256]{2,1,0:T(8,128)(2,1)}), bf16[4,128,256]{2,1,0:T(8,128)(2,1)S(1)}, u32[]{:S(2)}, u32[]{:S(2)}) async-start(bf16[4,128,256]{2,1,0:T(8,128)(2,1)} %broadcast_in_dim.20), calls=%async_computation | async-start | bytes 524288 | tf_op jit(solution)/shard_map/all_to_all | solution.py:271
  17.8 0.1 pad_add_fusion.1
  17.9 0.0 copy-done
  18.0 0.4 compare_reduce_fusion
  18.4 0.0 copy-done.12
  18.4 0.0 copy-done.11
  18.4 13.2 %all-to-all-done = bf16[4,128,256]{2,1,0:T(8,128)(2,1)S(1)} async-done(((bf16[4,128,256]{2,1,0:T(8,128)(2,1)}), bf16[4,128,256]{2,1,0:T(8,128)(2,1)S(1)}, u32[]{:S(2)}, u32[]{:S(2)}) %all-to-all-start) | async-done | bytes 262176 | tf_op jit(solution)/shard_map/all_to_all | solution.py:271
  31.6 4.6 %collective-permute-start = (bf16[512,256]{1,0:T(8,128)(2,1)S(1)}, bf16[512,256]{1,0:T(8,128)(2,1)S(1)}, u32[]{:S(2)}, u32[]{:S(2)}) collective-permute-start(bf16[512,256]{1,0:T(8,128)(2,1)S(1)} %pad_maximum_fusion.1.refs_2_.near_ref.kv_ref), channel_id=1, source_target_pairs={{0,256},{256,0},{1,257},{257,1},{2,258},{258,2},{3,259},{259,3},{4... | collective-permute-start | bytes 786440 | tf_op jit(solution)/shard_map/ppermute | solution.py:254
  36.3 0.1 pad_add_fusion.refs_0_.places
  36.3 0.1 reshape.29.refs_1_.member
  36.4 8.4 %collective-permute-start.1 = (bf16[512,256]{1,0:T(8,128)(2,1)S(1)}, bf16[512,256]{1,0:T(8,128)(2,1)S(1)}, u32[]{:S(2)}, u32[]{:S(2)}) collective-permute-start(bf16[512,256]{1,0:T(8,128)(2,1)S(1)} %bitcast.82), channel_id=1, source_target_pairs={{0,16},{16,32},{32,48},{48,64},{64,80},{80,96},{96,112},{112,128},... | collective-permute-start | bytes 786440 | tf_op jit(solution)/shard_map/ppermute | solution.py:254
  44.9 1.9 %collective-permute-start.2 = (bf16[512,256]{1,0:T(8,128)(2,1)S(1)}, bf16[512,256]{1,0:T(8,128)(2,1)S(1)}, u32[]{:S(2)}, u32[]{:S(2)}) collective-permute-start(bf16[512,256]{1,0:T(8,128)(2,1)S(1)} %bitcast.83), channel_id=1, source_target_pairs={{0,240},{16,0},{32,16},{48,32},{64,48},{80,64},{96,80},{112,96},{1... | collective-permute-start | bytes 786440 | tf_op jit(solution)/shard_map/ppermute | solution.py:254
  46.8 4.2 %collective-permute-start.3 = (bf16[256,256]{1,0:T(8,128)(2,1)S(1)}, bf16[256,256]{1,0:T(8,128)(2,1)S(1)}, u32[]{:S(2)}, u32[]{:S(2)}) collective-permute-start(bf16[256,256]{1,0:T(8,128)(2,1)S(1)} %bitcast.89), channel_id=1, source_target_pairs={{0,224},{16,240},{32,0},{48,16},{64,32},{80,48},{96,64},{112,80},{... | collective-permute-start | bytes 393224 | tf_op jit(solution)/shard_map/ppermute | solution.py:254
  51.1 2.0 %collective-permute-start.4 = (bf16[256,256]{1,0:T(8,128)(2,1)S(1)}, bf16[256,256]{1,0:T(8,128)(2,1)S(1)}, u32[]{:S(2)}, u32[]{:S(2)}) collective-permute-start(bf16[256,256]{1,0:T(8,128)(2,1)S(1)} %bitcast.88), channel_id=1, source_target_pairs={{0,32},{16,48},{32,64},{48,80},{64,96},{80,112},{96,128},{112,144}... | collective-permute-start | bytes 393224 | tf_op jit(solution)/shard_map/ppermute | solution.py:254
  53.0 0.0 collective-permute-done.refs_3_.far_ref.refs_4_
  53.0 2.3 %forward.2.rest_4_ = f32[64,128]{1,0:T(8,128)S(1)} custom-call(s32[16]{0:T(128)S(1)} %pad_add_fusion.refs_0_.places, s32[128]{0:T(128)S(1)} %reshape.29.refs_1_.member, bf16[512,256]{1,0:T(8,128)(2,1)S(1)} %pad_maximum_fusion.1.refs_2_.near_ref.kv_ref, bf16[512,256]{1,0:T(8,128)(2,1)S(1)} %collective-permute-done.refs_3_.far_ref.refs_4_, ...), custom_call_target="tpu_custom_call" | custom-call | flops 2147483648 | bytes 1048576 | tf_op jit(solution)/shard_map/forward/pallas_call | solution.py:123
  55.4 0.3 collective-permute-done.3.rest_2_.refs_8_.rest_3_
  55.6 7.0 %collective-permute-done.4.rest_3_.refs_9_.rest_4_ = bf16[256,256]{1,0:T(8,128)(2,1)S(1)} collective-permute-done((bf16[256,256]{1,0:T(8,128)(2,1)S(1)}, bf16[256,256]{1,0:T(8,128)(2,1)S(1)}, u32[]{:S(2)}, u32[]{:S(2)}) %collective-permute-start.4) | collective-permute-done | bytes 131104 | tf_op jit(solution)/shard_map/ppermute | solution.py:254
  62.6 0.0 collective-permute-done.1.rest_0_.refs_6_.rest_1_
  62.6 0.0 collective-permute-done.2.rest_1_.refs_7_.rest_2_
  62.6 0.0 copy-start.3
  62.6 0.0 copy-start.2
  62.6 5.9 %forward.3 = f32[64,128]{1,0:T(8,128)S(1)} custom-call(s32[16]{0:T(128)S(1)} %pad_add_fusion.refs_0_.places, s32[128]{0:T(128)S(1)} %reshape.29.refs_1_.member, bf16[512,256]{1,0:T(8,128)(2,1)S(1)} %pad_maximum_fusion.1.refs_2_.near_ref.kv_ref, bf16[512,256]{1,0:T(8,128)(2,1)S(1)} %collective-permute-done.refs_3_.far_ref.refs_4_, ...), custom_call_target="tpu_custom_call" | custom-call | flops 6442450944 | bytes 1048576 | tf_op jit(solution)/shard_map/forward/pallas_call | solution.py:123
  68.5 0.0 copy-done.5
  68.5 0.0 copy-start.1
  68.6 15.6 %all_to_all.20 = f32[4,64,128]{2,1,0:T(8,128)S(1)} all-to-all(f32[4,64,128]{2,1,0:T(8,128)S(1)} %broadcast_in_dim.21), channel_id=1, replica_groups=mesh['xh'=2,'zh'=4,'zl'=4,'xl'=2,'y'=4,'core'=2] {'zh'}, dimensions={0} | all-to-all | bytes 262144 | tf_op jit(solution)/shard_map/all_to_all | solution.py:271
  84.3 1.9 %collective-permute-start.5 = (f32[64,128]{1,0:T(8,128)S(1)}, f32[64,128]{1,0:T(8,128)S(1)}, u32[]{:S(2)}, u32[]{:S(2)}) collective-permute-start(f32[64,128]{1,0:T(8,128)S(1)} %pad_maximum_fusion.3), channel_id=1, source_target_pairs={{0,32},{16,48},{32,64},{48,80},{64,96},{80,112},{96,128},{112,144}... | collective-permute-start | bytes 98312 | tf_op jit(solution)/shard_map/ppermute | solution.py:254
  86.2 4.8 %collective-permute-done.5 = f32[64,128]{1,0:T(8,128)S(1)} collective-permute-done((f32[64,128]{1,0:T(8,128)S(1)}, f32[64,128]{1,0:T(8,128)S(1)}, u32[]{:S(2)}, u32[]{:S(2)}) %collective-permute-start.5) | collective-permute-done | bytes 32800 | tf_op jit(solution)/shard_map/ppermute | solution.py:254
  91.1 1.9 %collective-permute-start.6 = (f32[64,128]{1,0:T(8,128)S(1)}, f32[64,128]{1,0:T(8,128)S(1)}, u32[]{:S(2)}, u32[]{:S(2)}) collective-permute-start(f32[64,128]{1,0:T(8,128)S(1)} %pad_maximum_fusion.4), channel_id=1, source_target_pairs={{0,16},{16,32},{32,48},{48,64},{64,80},{80,96},{96,112},{112,128},... | collective-permute-start | bytes 98312 | tf_op jit(solution)/shard_map/ppermute | solution.py:254
  93.0 0.0 copy-done.2
  93.0 0.0 copy-done.1
  93.0 1.1 pad_maximum_fusion
  94.1 3.3 %collective-permute-done.6 = f32[64,128]{1,0:T(8,128)S(1)} collective-permute-done((f32[64,128]{1,0:T(8,128)S(1)}, f32[64,128]{1,0:T(8,128)S(1)}, u32[]{:S(2)}, u32[]{:S(2)}) %collective-permute-start.6) | collective-permute-done | bytes 32800 | tf_op jit(solution)/shard_map/ppermute | solution.py:254
  97.4 9.5 %collective-permute-start.9 = (bf16[2048,256]{1,0:T(8,128)(2,1)}, bf16[2048,256]{1,0:T(8,128)(2,1)S(1)}, u32[]{:S(2)}, u32[]{:S(2)}) collective-permute-start(bf16[2048,256]{1,0:T(8,128)(2,1)} %pad_maximum_fusion), channel_id=1, source_target_pairs={{0,1},{1,0},{2,3},{3,2},{4,5},{5,4},{6,7},{7,6},{8,9},{9,8},{10,11... | collective-permute-start | bytes 3145736 | tf_op jit(solution)/shard_map/ppermute | solution.py:254
  106.9 0.0 copy-done.3
  106.9 0.0 copy-start.6
  106.9 0.9 copy-done.6
  107.8 0.9 copy-done.8
  108.7 6.7 %backward.2 = (f32[16,128,128]{2,1,0:T(8,128)S(1)}, bf16[256,256]{1,0:T(8,128)(2,1)S(1)}, bf16[256,256]{1,0:T(8,128)(2,1)S(1)}) custom-call(s32[16]{0:T(128)S(1)} %pad_add_fusion.refs_0_.places, s32[128]{0:T(128)S(1)} %reshape.29.refs_1_.member, s32[1]{0:T(128)} %bitcast.1.refs_2_.core, f32[64,128]{1,0:T(8,128)S(1)} %pad_maximum_fusion.5.refs_3_.stats, ...), custom_call_target="tpu_custom_call" | custom-call | flops 10737418240 | bytes 1048576 | tf_op jit(solution)/shard_map/backward/pallas_call | solution.py:204
  115.4 2.1 %collective-permute-start.7 = (bf16[256,256]{1,0:T(8,128)(2,1)S(1)}, bf16[256,256]{1,0:T(8,128)(2,1)S(1)}, u32[]{:S(2)}, u32[]{:S(2)}) collective-permute-start(bf16[256,256]{1,0:T(8,128)(2,1)S(1)} %get-tuple-element.26), channel_id=1, source_target_pairs={{0,256},{256,0},{1,257},{257,1},{2,258},{258,2},{3,259},{259,3},{4... | collective-permute-start | bytes 393224 | tf_op jit(solution)/shard_map/ppermute | solution.py:254
  117.6 4.8 %collective-permute-start.8 = (bf16[256,256]{1,0:T(8,128)(2,1)S(1)}, bf16[256,256]{1,0:T(8,128)(2,1)S(1)}, u32[]{:S(2)}, u32[]{:S(2)}) collective-permute-start(bf16[256,256]{1,0:T(8,128)(2,1)S(1)} %get-tuple-element.27), channel_id=1, source_target_pairs={{0,257},{1,256},{256,1},{257,0},{2,259},{3,258},{258,3},{259,2},{4... | collective-permute-start | bytes 393224 | tf_op jit(solution)/shard_map/ppermute | solution.py:315
  122.4 0.9 copy-done.4
  123.3 7.5 %backward.3 = (bf16[16,128,128]{2,1,0:T(8,128)(2,1)}, f32[256,256]{1,0:T(8,128)S(1)}, bf16[256,256]{1,0:T(8,128)(2,1)S(1)}) custom-call(s32[16]{0:T(128)S(1)} %pad_add_fusion.refs_0_.places, s32[128]{0:T(128)S(1)} %reshape.29.refs_1_.member, s32[1]{0:T(128)} %bitcast.1.refs_2_.core, f32[64,128]{1,0:T(8,128)S(1)} %pad_maximum_fusion.5.refs_3_.stats, ...), custom_call_target="tpu_custom_call" | custom-call | flops 10737418240 | bytes 1048576 | tf_op jit(solution)/shard_map/backward/pallas_call | solution.py:204
  130.8 0.7 copy-done.9
  131.5 0.0 collective-permute-done.7.from_half
  131.5 0.0 collective-permute-done.8.from_both
  131.5 0.0 collective-permute-done.9.far
  131.5 3.7 %all-to-all-start.2 = ((bf16[16,128,128]{2,1,0:T(8,128)(2,1)}), bf16[16,128,128]{2,1,0:T(8,128)(2,1)S(1)}, u32[]{:S(2)}, u32[]{:S(2)}) async-start(bf16[16,128,128]{2,1,0:T(8,128)(2,1)} %get-tuple-element.33), calls=%async_computation.2 | async-start | bytes 1048576 | tf_op jit(solution)/shard_map/all_to_all | solution.py:323
  135.2 2.1 %collective-permute-start.10 = (bf16[256,256]{1,0:T(8,128)(2,1)S(1)}, bf16[256,256]{1,0:T(8,128)(2,1)S(1)}, u32[]{:S(2)}, u32[]{:S(2)}) collective-permute-start(bf16[256,256]{1,0:T(8,128)(2,1)S(1)} %copy-done.10), channel_id=1, source_target_pairs={{0,1},{1,0},{2,3},{3,2},{4,5},{5,4},{6,7},{7,6},{8,9},{9,8},{10,11... | collective-permute-start | bytes 393224 | tf_op jit(solution)/shard_map/ppermute | solution.py:254
  137.4 1.1 collective-permute-done.10.from_core
  138.5 0.7 project.2
  139.2 2.2 %collective-permute-start.11 = (bf16[8,256,128]{2,1,0:T(8,128)(2,1)S(1)}, bf16[8,256,128]{2,1,0:T(8,128)(2,1)S(1)}, u32[]{:S(2)}, u32[]{:S(2)}) collective-permute-start(bf16[8,256,128]{2,1,0:T(8,128)(2,1)S(1)} %project.2), channel_id=1, source_target_pairs={{0,8},{8,0},{1,9},{9,1},{2,10},{10,2},{3,11},{11,3},{4,12},{12,4},... | collective-permute-start | bytes 1572872 | tf_op jit(solution)/shard_map/ppermute | solution.py:254
  141.4 13.0 %collective-permute-done.11.rest_0_ = bf16[8,256,128]{2,1,0:T(8,128)(2,1)S(1)} collective-permute-done((bf16[8,256,128]{2,1,0:T(8,128)(2,1)S(1)}, bf16[8,256,128]{2,1,0:T(8,128)(2,1)S(1)}, u32[]{:S(2)}, u32[]{:S(2)}) %collective-permute-start.11) | collective-permute-done | bytes 524320 | tf_op jit(solution)/shard_map/ppermute | solution.py:254
  154.4 1.5 project.3
  155.9 3.5 %all-to-all-done.2 = bf16[16,128,128]{2,1,0:T(8,128)(2,1)S(1)} async-done(((bf16[16,128,128]{2,1,0:T(8,128)(2,1)}), bf16[16,128,128]{2,1,0:T(8,128)(2,1)S(1)}, u32[]{:S(2)}, u32[]{:S(2)}) %all-to-all-start.2) | async-done | bytes 524320 | tf_op jit(solution)/shard_map/all_to_all | solution.py:323
  159.5 9.3 %all-to-all-start.3 = ((bf16[8,256,128]{2,1,0:T(8,128)(2,1)}), bf16[8,256,128]{2,1,0:T(8,128)(2,1)S(1)}, u32[]{:S(2)}, u32[]{:S(2)}) async-start(bf16[8,256,128]{2,1,0:T(8,128)(2,1)} %project.3), calls=%async_computation.3 | async-start | bytes 1048576 | tf_op jit(solution)/shard_map/all_to_all | solution.py:333
  168.8 0.7 reduce_sum.21
  169.5 8.8 %all-to-all-done.3 = bf16[8,256,128]{2,1,0:T(8,128)(2,1)S(1)} async-done(((bf16[8,256,128]{2,1,0:T(8,128)(2,1)}), bf16[8,256,128]{2,1,0:T(8,128)(2,1)S(1)}, u32[]{:S(2)}, u32[]{:S(2)}) %all-to-all-start.3) | async-done | bytes 524320 | tf_op jit(solution)/shard_map/all_to_all | solution.py:333
  178.3 0.7 reduce.1
  (23 shorter events, 0.2 us)
Async XLA Ops:
  0.6 17.3 %copy-start = (s32[32,64]{1,0:T(8,128)S(1)}, s32[32,64]{1,0:T(8,128)}, u32[]{:S(2)}) copy-start(s32[32,64]{1,0:T(8,128)} %param.13) | copy-start | bytes 24580
  0.6 17.7 %copy-start.12 = (bf16[512,128]{1,0:T(8,128)(2,1)S(1)}, bf16[512,128]{1,0:T(8,128)(2,1)}, u32[]{:S(2)}) copy-start(bf16[512,128]{1,0:T(8,128)(2,1)} %param.8) | copy-start | bytes 393220
  0.7 17.7 %copy-start.11 = (bf16[512,128]{1,0:T(8,128)(2,1)S(1)}, bf16[512,128]{1,0:T(8,128)(2,1)}, u32[]{:S(2)}) copy-start(bf16[512,128]{1,0:T(8,128)(2,1)} %param.9) | copy-start | bytes 393220
  2.2 29.4 %all-to-all-start = ((bf16[4,128,256]{2,1,0:T(8,128)(2,1)}), bf16[4,128,256]{2,1,0:T(8,128)(2,1)S(1)}, u32[]{:S(2)}, u32[]{:S(2)}) async-start(bf16[4,128,256]{2,1,0:T(8,128)(2,1)} %broadcast_in_dim.20), calls=%async_computation | async-start | bytes 524288 | tf_op jit(solution)/shard_map/all_to_all | solution.py:271
  31.6 21.4 %collective-permute-start = (bf16[512,256]{1,0:T(8,128)(2,1)S(1)}, bf16[512,256]{1,0:T(8,128)(2,1)S(1)}, u32[]{:S(2)}, u32[]{:S(2)}) collective-permute-start(bf16[512,256]{1,0:T(8,128)(2,1)S(1)} %pad_maximum_fusion.1.refs_2_.near_ref.kv_ref), channel_id=1, source_target_pairs={{0,256},{256,0},{1,257},{257,1},{2,258},{258,2},{3,259},{259,3},{4... | collective-permute-start | bytes 786440 | tf_op jit(solution)/shard_map/ppermute | solution.py:254
  36.4 26.2 %collective-permute-start.1 = (bf16[512,256]{1,0:T(8,128)(2,1)S(1)}, bf16[512,256]{1,0:T(8,128)(2,1)S(1)}, u32[]{:S(2)}, u32[]{:S(2)}) collective-permute-start(bf16[512,256]{1,0:T(8,128)(2,1)S(1)} %bitcast.82), channel_id=1, source_target_pairs={{0,16},{16,32},{32,48},{48,64},{64,80},{80,96},{96,112},{112,128},... | collective-permute-start | bytes 786440 | tf_op jit(solution)/shard_map/ppermute | solution.py:254
  44.9 17.7 %collective-permute-start.2 = (bf16[512,256]{1,0:T(8,128)(2,1)S(1)}, bf16[512,256]{1,0:T(8,128)(2,1)S(1)}, u32[]{:S(2)}, u32[]{:S(2)}) collective-permute-start(bf16[512,256]{1,0:T(8,128)(2,1)S(1)} %bitcast.83), channel_id=1, source_target_pairs={{0,240},{16,0},{32,16},{48,32},{64,48},{80,64},{96,80},{112,96},{1... | collective-permute-start | bytes 786440 | tf_op jit(solution)/shard_map/ppermute | solution.py:254
  46.8 8.8 %collective-permute-start.3 = (bf16[256,256]{1,0:T(8,128)(2,1)S(1)}, bf16[256,256]{1,0:T(8,128)(2,1)S(1)}, u32[]{:S(2)}, u32[]{:S(2)}) collective-permute-start(bf16[256,256]{1,0:T(8,128)(2,1)S(1)} %bitcast.89), channel_id=1, source_target_pairs={{0,224},{16,240},{32,0},{48,16},{64,32},{80,48},{96,64},{112,80},{... | collective-permute-start | bytes 393224 | tf_op jit(solution)/shard_map/ppermute | solution.py:254
  51.1 11.5 %collective-permute-start.4 = (bf16[256,256]{1,0:T(8,128)(2,1)S(1)}, bf16[256,256]{1,0:T(8,128)(2,1)S(1)}, u32[]{:S(2)}, u32[]{:S(2)}) collective-permute-start(bf16[256,256]{1,0:T(8,128)(2,1)S(1)} %bitcast.88), channel_id=1, source_target_pairs={{0,32},{16,48},{32,64},{48,80},{64,96},{80,112},{96,128},{112,144}... | collective-permute-start | bytes 393224 | tf_op jit(solution)/shard_map/ppermute | solution.py:254
  55.6 12.9 %copy-start.5 = (bf16[256,256]{1,0:T(8,128)(2,1)}, bf16[256,256]{1,0:T(8,128)(2,1)S(1)}, u32[]{:S(2)}) copy-start(bf16[256,256]{1,0:T(8,128)(2,1)S(1)} %collective-permute-done.3.rest_2_.refs_8_.rest_3_) | copy-start | bytes 393220
  62.6 5.9 %copy-start.7 = (bf16[256,256]{1,0:T(8,128)(2,1)}, bf16[256,256]{1,0:T(8,128)(2,1)S(1)}, u32[]{:S(2)}) copy-start(bf16[256,256]{1,0:T(8,128)(2,1)S(1)} %collective-permute-done.4.rest_3_.refs_9_.rest_4_) | copy-start | bytes 393220
  62.6 44.3 %copy-start.3 = (bf16[512,256]{1,0:T(8,128)(2,1)}, bf16[512,256]{1,0:T(8,128)(2,1)S(1)}, u32[]{:S(2)}) copy-start(bf16[512,256]{1,0:T(8,128)(2,1)S(1)} %collective-permute-done.2.rest_1_.refs_7_.rest_2_) | copy-start | bytes 786436
  62.6 30.4 %copy-start.2 = (bf16[2048,128]{1,0:T(8,128)(2,1)S(1)}, bf16[2048,128]{1,0:T(8,128)(2,1)}, u32[]{:S(2)}) copy-start(bf16[2048,128]{1,0:T(8,128)(2,1)} %vw.3) | copy-start | bytes 1572868
  68.5 24.5 %copy-start.1 = (bf16[2048,128]{1,0:T(8,128)(2,1)S(1)}, bf16[2048,128]{1,0:T(8,128)(2,1)}, u32[]{:S(2)}) copy-start(bf16[2048,128]{1,0:T(8,128)(2,1)} %kw.3) | copy-start | bytes 1572868
  84.3 6.8 %collective-permute-start.5 = (f32[64,128]{1,0:T(8,128)S(1)}, f32[64,128]{1,0:T(8,128)S(1)}, u32[]{:S(2)}, u32[]{:S(2)}) collective-permute-start(f32[64,128]{1,0:T(8,128)S(1)} %pad_maximum_fusion.3), channel_id=1, source_target_pairs={{0,32},{16,48},{32,64},{48,80},{64,96},{80,112},{96,128},{112,144}... | collective-permute-start | bytes 98312 | tf_op jit(solution)/shard_map/ppermute | solution.py:254
  91.1 6.3 %collective-permute-start.6 = (f32[64,128]{1,0:T(8,128)S(1)}, f32[64,128]{1,0:T(8,128)S(1)}, u32[]{:S(2)}, u32[]{:S(2)}) collective-permute-start(f32[64,128]{1,0:T(8,128)S(1)} %pad_maximum_fusion.4), channel_id=1, source_target_pairs={{0,16},{16,32},{32,48},{48,64},{64,80},{80,96},{96,112},{112,128},... | collective-permute-start | bytes 98312 | tf_op jit(solution)/shard_map/ppermute | solution.py:254
  97.4 34.0 %collective-permute-start.9 = (bf16[2048,256]{1,0:T(8,128)(2,1)}, bf16[2048,256]{1,0:T(8,128)(2,1)S(1)}, u32[]{:S(2)}, u32[]{:S(2)}) collective-permute-start(bf16[2048,256]{1,0:T(8,128)(2,1)} %pad_maximum_fusion), channel_id=1, source_target_pairs={{0,1},{1,0},{2,3},{3,2},{4,5},{5,4},{6,7},{7,6},{8,9},{9,8},{10,11... | collective-permute-start | bytes 3145736 | tf_op jit(solution)/shard_map/ppermute | solution.py:254
  106.9 0.9 copy-start.6
  107.8 0.9 copy-start.8
  115.4 16.1 %collective-permute-start.7 = (bf16[256,256]{1,0:T(8,128)(2,1)S(1)}, bf16[256,256]{1,0:T(8,128)(2,1)S(1)}, u32[]{:S(2)}, u32[]{:S(2)}) collective-permute-start(bf16[256,256]{1,0:T(8,128)(2,1)S(1)} %get-tuple-element.26), channel_id=1, source_target_pairs={{0,256},{256,0},{1,257},{257,1},{2,258},{258,2},{3,259},{259,3},{4... | collective-permute-start | bytes 393224 | tf_op jit(solution)/shard_map/ppermute | solution.py:254
  117.6 13.9 %collective-permute-start.8 = (bf16[256,256]{1,0:T(8,128)(2,1)S(1)}, bf16[256,256]{1,0:T(8,128)(2,1)S(1)}, u32[]{:S(2)}, u32[]{:S(2)}) collective-permute-start(bf16[256,256]{1,0:T(8,128)(2,1)S(1)} %get-tuple-element.27), channel_id=1, source_target_pairs={{0,257},{1,256},{256,1},{257,0},{2,259},{3,258},{258,3},{259,2},{4... | collective-permute-start | bytes 393224 | tf_op jit(solution)/shard_map/ppermute | solution.py:315
  122.4 1.0 copy-start.4
  130.8 0.7 copy-start.9
  131.5 3.7 %copy-start.10 = (bf16[256,256]{1,0:T(8,128)(2,1)S(1)}, bf16[256,256]{1,0:T(8,128)(2,1)}, u32[]{:S(2)}) copy-start(bf16[256,256]{1,0:T(8,128)(2,1)} %copy-done.9) | copy-start | bytes 393220
  131.5 28.0 %all-to-all-start.2 = ((bf16[16,128,128]{2,1,0:T(8,128)(2,1)}), bf16[16,128,128]{2,1,0:T(8,128)(2,1)S(1)}, u32[]{:S(2)}, u32[]{:S(2)}) async-start(bf16[16,128,128]{2,1,0:T(8,128)(2,1)} %get-tuple-element.33), calls=%async_computation.2 | async-start | bytes 1048576 | tf_op jit(solution)/shard_map/all_to_all | solution.py:323
  135.2 3.2 %collective-permute-start.10 = (bf16[256,256]{1,0:T(8,128)(2,1)S(1)}, bf16[256,256]{1,0:T(8,128)(2,1)S(1)}, u32[]{:S(2)}, u32[]{:S(2)}) collective-permute-start(bf16[256,256]{1,0:T(8,128)(2,1)S(1)} %copy-done.10), channel_id=1, source_target_pairs={{0,1},{1,0},{2,3},{3,2},{4,5},{5,4},{6,7},{7,6},{8,9},{9,8},{10,11... | collective-permute-start | bytes 393224 | tf_op jit(solution)/shard_map/ppermute | solution.py:254
  139.2 15.2 %collective-permute-start.11 = (bf16[8,256,128]{2,1,0:T(8,128)(2,1)S(1)}, bf16[8,256,128]{2,1,0:T(8,128)(2,1)S(1)}, u32[]{:S(2)}, u32[]{:S(2)}) collective-permute-start(bf16[8,256,128]{2,1,0:T(8,128)(2,1)S(1)} %project.2), channel_id=1, source_target_pairs={{0,8},{8,0},{1,9},{9,1},{2,10},{10,2},{3,11},{11,3},{4,12},{12,4},... | collective-permute-start | bytes 1572872 | tf_op jit(solution)/shard_map/ppermute | solution.py:254
  159.5 18.8 %all-to-all-start.3 = ((bf16[8,256,128]{2,1,0:T(8,128)(2,1)}), bf16[8,256,128]{2,1,0:T(8,128)(2,1)S(1)}, u32[]{:S(2)}, u32[]{:S(2)}) async-start(bf16[8,256,128]{2,1,0:T(8,128)(2,1)} %project.3), calls=%async_computation.3 | async-start | bytes 1048576 | tf_op jit(solution)/shard_map/all_to_all | solution.py:333

commit v3 on v2

--- a/solution.py
+++ b/solution.py
@@ -9,12 +9,16 @@
 
 HEAD_DIM = 64
 BLOCK = 128
-AXES = ("xh", "zh", "zl", "xl", "y", "core")
-SIZES = (2, 4, 4, 2, 4, 2)
-Z = ("zh", "zl")
-CTX = ("xh", "zh", "zl")
+AXES = ("xh", "z", "xl", "y", "core")
+SIZES = (2, 16, 2, 4, 2)
+Z = "z"
+CTX = ("xh", "z")
 HEAD = ("xl", "y", "core")
 BIG = 1e30
+
+OWN = (4, 0, -4, 8)
+LATER = (3, -1, -5, 7, 5, 1, -3, 9, 6, 2, -2, -6)
+SLOTS = OWN + LATER
 
 VMEM = pl.BlockSpec(memory_space=pltpu.VMEM)
 SMEM = pl.BlockSpec(memory_space=pltpu.SMEM)
@@ -62,7 +66,7 @@
 
 
 def forward_kernel(base, places, member, near_ref, far_ref, *rest):
-    *pieces, before, stats, keys, vals, held = rest
+    *pieces, before, result, keys, vals, held, stats = rest
     load_keys(near_ref, far_ref, keys, vals)
     load_targets(pieces, held)
     blocks = keys.shape[0] // BLOCK
@@ -104,6 +108,14 @@
         return step(2 * i + 1, step(2 * i, carry))
 
     lax.fori_loop(0, pairs // 2, two, 0)
+    if before is None:
+        result[...] = stats[...]
+    else:
+        high = stats[:half, :].astype(jnp.bfloat16)
+        low = (stats[:half, :] - high.astype(jnp.float32)).astype(jnp.bfloat16)
+        message = jnp.concatenate([high, low, stats[half:, :].astype(jnp.bfloat16)], axis=0)
+        for peer in range(result.shape[0]):
+            result[peer] = message
 
 
 def forward(base, places, member, near, far, pieces, before):
@@ -112,6 +124,7 @@
     enc = near.shape[0] + far.shape[0]
     given = [places, member, near, far, *pieces]
     specs = [SMEM, SMEM] + [VMEM] * (2 + len(pieces))
+    shape = jax.ShapeDtypeStruct((4 * count, BLOCK), jnp.float32)
     if before is None:
         def kernel(*refs):
             ins, outs = refs[: len(given)], refs[len(given) :]
@@ -119,16 +132,18 @@
     else:
         given.append(before)
         specs.append(VMEM)
+        shape = jax.ShapeDtypeStruct((count, 6 * count, BLOCK), jnp.bfloat16)
         kernel = partial(forward_kernel, base)
     return pl.pallas_call(
         kernel,
-        out_shape=jax.ShapeDtypeStruct((4 * count, BLOCK), jnp.float32),
+        out_shape=shape,
         in_specs=specs,
         out_specs=VMEM,
         scratch_shapes=[
             pltpu.VMEM((enc, BLOCK), jnp.bfloat16),
             pltpu.VMEM((enc, BLOCK), jnp.bfloat16),
             pltpu.VMEM((rows, 2 * BLOCK), jnp.bfloat16),
+            pltpu.VMEM((4 * count, BLOCK), jnp.float32),
         ],
         compiler_params=ROOM,
         cost_estimate=cost(2 * rows * enc * 4 * BLOCK, rows * enc * 2),
@@ -136,9 +151,29 @@
     )(*given)
 
 
-def backward_kernel(base, places, member, core, stats, kv_ref, before, *rest):
+def merge_stats(parts, stats):
+    rows = stats.shape[0] // 2
+    logs = [
+        parts[i, :rows, :].astype(jnp.float32) + parts[i, rows : 2 * rows, :].astype(jnp.float32)
+        for i in range(parts.shape[0])
+    ]
+    top = logs[0]
+    for log in logs[1:]:
+        top = jnp.maximum(top, log)
+    total = jnp.zeros_like(top)
+    mean = jnp.zeros_like(top)
+    for i, log in enumerate(logs):
+        weight = jnp.exp(log - top)
+        total = total + weight
+        mean = mean + weight * parts[i, 2 * rows :, :].astype(jnp.float32)
+    stats[:rows, :] = top + jnp.log(total)
+    stats[rows:, :] = mean / total
+
+
+def backward_kernel(base, whole, places, member, core, parts, kv_ref, before, *rest):
     pieces = rest[:5]
-    d_query, stay, leave, held, turned, chances, slopes, d_key, d_value = rest[5:]
+    d_query, *sent, held, turned, chances, slopes, d_key, d_value, stats = rest[5:]
+    merge_stats(parts, stats)
     load_targets(pieces, held)
     enc = kv_ref.shape[0]
     blocks = enc // BLOCK
@@ -180,36 +215,38 @@
         return carry
 
     lax.fori_loop(0, pairs // 2, two, 0)
-    mine = core[0]
-    for target, part in ((stay, mine), (leave, 1 - mine)):
-        rows = pl.ds(pl.multiple_of(part * (enc // 2), enc // 2), enc // 2)
-        target[:, :BLOCK] = d_key[rows, :].astype(target.dtype)
-        target[:, BLOCK:] = d_value[rows, :].astype(target.dtype)
-
-
-def backward(base, places, member, core, stats, kv, pieces, before, kinds):
+    if whole:
+        sent[0][:, :BLOCK] = d_key[...].astype(jnp.bfloat16)
+        sent[0][:, BLOCK:] = d_value[...].astype(jnp.bfloat16)
+    else:
+        for target, part in zip(sent, (core[0], 1 - core[0]), strict=True):
+            rows = pl.ds(pl.multiple_of(part * (enc // 2), enc // 2), enc // 2)
+            target[:, :BLOCK] = d_key[rows, :]
+            target[:, BLOCK:] = d_value[rows, :]
+
+
+def backward(base, places, member, core, parts, kv, pieces, before):
+    whole = before is None
     count = places.shape[0]
     rows = sum(p.shape[0] for p in pieces)
     enc = kv.shape[0]
-    shape = (enc // 2, 2 * BLOCK)
-    given = [places, member, core, stats, kv]
+    given = [places, member, core, parts, kv]
     fixed = len(given)
-    if before is None:
+    if whole:
+        sent = [jax.ShapeDtypeStruct((enc, 2 * BLOCK), jnp.bfloat16)]
         def kernel(*refs):
-            backward_kernel(base, *refs[:fixed], None, *refs[fixed:])
+            backward_kernel(base, whole, *refs[:fixed], None, *refs[fixed:])
     else:
+        sent = [jax.ShapeDtypeStruct((enc // 2, 2 * BLOCK), jnp.float32)] * 2
         given.append(before)
-        kernel = partial(backward_kernel, base)
+        kernel = partial(backward_kernel, base, whole)
     given += pieces
+    kind = jnp.float32 if whole else jnp.bfloat16
     return pl.pallas_call(
         kernel,
-        out_shape=(
-            jax.ShapeDtypeStruct((count, BLOCK, BLOCK), kinds[0]),
-            jax.ShapeDtypeStruct(shape, kinds[1]),
-            jax.ShapeDtypeStruct(shape, kinds[2]),
-        ),
+        out_shape=[jax.ShapeDtypeStruct((count, BLOCK, BLOCK), kind), *sent],
         in_specs=[SMEM] * 3 + [VMEM] * (len(given) - 3),
-        out_specs=(VMEM,) * 3,
+        out_specs=[VMEM] * (1 + len(sent)),
         scratch_shapes=[
             pltpu.VMEM((rows, 2 * BLOCK), jnp.bfloat16),
             pltpu.VMEM((BLOCK, enc), jnp.bfloat16),
@@ -217,6 +254,7 @@
             pltpu.VMEM((2, enc, 4 * BLOCK), jnp.bfloat16),
             pltpu.VMEM((enc, BLOCK), jnp.float32),
             pltpu.VMEM((enc, BLOCK), jnp.float32),
+            pltpu.VMEM((4 * count, BLOCK), jnp.float32),
         ],
         compiler_params=ROOM,
         cost_estimate=cost(5 * rows * enc * 4 * BLOCK, rows * enc * 2),
@@ -224,29 +262,30 @@
     )(*given)
 
 
-def project_kernel(part, kept, from_half, from_core, from_both, kw, vw, far, *rest):
+def project_kernel(core, chunk, kept, from_half, from_core, kw, vw, far, *rest):
     *before, memory = rest
-    mine = (kept[...] + from_half[...].astype(jnp.float32)).astype(jnp.bfloat16)
-    other = (from_core[...].astype(jnp.float32) + from_both[...].astype(jnp.float32)).astype(jnp.bfloat16)
-    chunks = memory.shape[0]
-    for j in range(chunks):
-        rows = pl.ds(pl.multiple_of((part[0] * chunks + j) * BLOCK, BLOCK), BLOCK)
-        total = dot_nt(mine[:, :BLOCK], kw[rows, :]) + dot_nt(mine[:, BLOCK:], vw[rows, :])
-        total = total + dot_nt(other, far[rows, :])
+    rows = kept.shape[0]
+    half = from_half[pl.ds(pl.multiple_of(core[0] * rows, rows), rows), :]
+    mine = (kept[...] + half.astype(jnp.float32)).astype(jnp.bfloat16)
+    other = from_core[...]
+    for j in range(memory.shape[0]):
+        part = pl.ds(pl.multiple_of(chunk[j] * BLOCK, BLOCK), BLOCK)
+        total = dot_nt(mine[:, :BLOCK], kw[part, :]) + dot_nt(mine[:, BLOCK:], vw[part, :])
+        total = total + dot_nt(other, far[part, :])
         for piece in before:
             total = total + piece[j].astype(jnp.float32)
         memory[j] = total.astype(jnp.bfloat16)
 
 
-def project(part, chunks, *given):
+def project(core, chunk, *given):
     return pl.pallas_call(
         project_kernel,
-        out_shape=jax.ShapeDtypeStruct((chunks, given[0].shape[0], BLOCK), jnp.bfloat16),
-        in_specs=[SMEM] + [VMEM] * len(given),
+        out_shape=jax.ShapeDtypeStruct((chunk.shape[0], given[0].shape[0], BLOCK), jnp.bfloat16),
+        in_specs=[SMEM] * 2 + [VMEM] * len(given),
         out_specs=VMEM,
         compiler_params=ROOM,
         name="project",
-    )(part[None], *given)
+    )(core, chunk, *given)
 
 
 def moved(value, axis, steps):
@@ -254,36 +293,23 @@
     return lax.ppermute(value, axis, [(i, (i + steps) % count) for i in range(count)])
 
 
-def merged(parts):
-    half = parts[0].shape[0] // 2
-    logs = [p[:half] for p in parts]
-    top = logs[0]
-    for log in logs[1:]:
-        top = jnp.maximum(top, log)
-    weights = [jnp.exp(log - top) for log in logs]
-    total = sum(weights[1:], weights[0])
-    mean = sum((w * p[half:] for w, p in zip(weights[1:], parts[1:])), weights[0] * parts[0][half:])
-    return jnp.concatenate([top + jnp.log(total), mean / total], axis=0)
-
-
-def spread(value, axis):
-    count = lax.axis_size(axis)
-    return lax.all_to_all(jnp.broadcast_to(value, (count, *value.shape)), axis, 0, 0, tiled=True)
-
-
 def body(queries, keys, values, d_out, key_weight, value_weight, block_lists):
+    f32, bf16 = jnp.float32, jnp.bfloat16
     half = lax.axis_index("xh")
     place = lax.axis_index(Z)
     core = lax.axis_index("core")
     depth = lax.axis_size(Z)
-    high, low = lax.axis_size("zh"), lax.axis_size("zl")
-    enc_blocks = keys.shape[0] // BLOCK
+    enc_rows = keys.shape[0]
+    enc_blocks = enc_rows // BLOCK
 
     near = jnp.concatenate([queries, d_out], axis=1)
-    bundle = spread(near, "zh").reshape(high * BLOCK, 2 * BLOCK)
-
-    strides = low * jnp.arange(high, dtype=jnp.int32)
-    places = jnp.concatenate([strides + (place + step) % low for step in (0, -1, 1, 2)])
+    ahead = moved(near, Z, 4)
+    behind = moved(near, Z, -4)
+    across = moved(near, Z, 8)
+    own = jnp.concatenate([keys, values], axis=1)
+    far = moved(own, "xh", 1)
+
+    places = (place + jnp.asarray(SLOTS, jnp.int32)) % depth
     listed = lax.dynamic_slice_in_dim(block_lists, half * depth, depth, 0)
     step = jnp.arange(enc_blocks, dtype=jnp.int32)
     ids = jnp.concatenate(
@@ -291,50 +317,52 @@
     )
     member = jnp.any(listed[:, :, None] == ids[None, None, :], axis=1).astype(jnp.int32).reshape(-1)
 
+    bundle = jnp.concatenate([behind, near, ahead, across], axis=0)
+    above2 = moved(bundle[: 2 * BLOCK], Z, -2)
+    below2 = moved(bundle[BLOCK : 3 * BLOCK], Z, 2)
     below = moved(bundle, Z, 1)
     above = moved(bundle, Z, -1)
-    above2 = moved(bundle[: 2 * BLOCK], Z, -2)
-    below2 = moved(bundle[2 * BLOCK :], Z, 2)
-    own, bundle = lax.optimization_barrier((jnp.concatenate([keys, values], axis=1), bundle))
-    far = moved(own, "xh", 1)
 
     early = forward(0, places, member, own, far, [bundle], None)
     pieces = [below, above, above2, below2]
-    stats = forward(high, places, member, own, far, pieces, early)
-    stats = merged(list(spread(stats, "zh")))
-    stats = merged([stats, moved(stats, Z, 2)])
-    stats = merged([stats, moved(stats, Z, 1)])
-
-    weights, stats = lax.optimization_barrier((jnp.concatenate([key_weight, value_weight], axis=1), stats))
+    parts = forward(len(OWN), places, member, own, far, pieces, early)
+    weights, parts = lax.optimization_barrier(
+        (jnp.concatenate([key_weight, value_weight], axis=1), parts)
+    )
+    parts = lax.all_to_all(parts, Z, 0, 0, tiled=True)
+    far_weights = moved(weights, "core", 1)
+    parts, far_weights = lax.optimization_barrier((parts, far_weights))
+
     pieces = [bundle, *pieces]
-    f32, bf16 = jnp.float32, jnp.bfloat16
-    d_query, to_half, to_both = backward(
-        enc_blocks, places, member, core[None], stats, far, pieces, None, (f32, bf16, bf16)
+    here = core[None]
+    d_query, to_half = backward(enc_blocks, places, member, here, parts, far, pieces, None)
+    from_half = moved(to_half, "xh", 1)
+    d_query, kept, to_core = backward(0, places, member, here, parts, own, pieces, d_query)
+    d_query, to_core, from_half = lax.optimization_barrier((d_query, to_core, from_half))
+    d_query = lax.all_to_all(d_query, Z, 0, 0, tiled=True)
+    to_core = to_core + lax.dynamic_slice_in_dim(from_half, (1 - core) * (enc_rows // 2), enc_rows // 2, 0).astype(f32)
+    from_core = moved(to_core.astype(bf16), "core", 1)
+
+    sides, runs, cores = (lax.axis_size(axis) for axis in HEAD)
+    side = lax.axis_index("xl")
+    run = (lax.axis_index("y") + jnp.arange(runs, dtype=jnp.int32)) % runs
+    both = (core + jnp.arange(cores, dtype=jnp.int32)) % cores
+    chunk = (run[:, None] * cores + both[None, :]).reshape(-1)
+    given = (kept, from_half, from_core, key_weight, value_weight, far_weights)
+    if sides > 1:
+        sent = project(here, (1 - side) * runs * cores + chunk, *given)
+        given += (moved(sent, "xl", 1),)
+    memory = project(here, side * runs * cores + chunk, *given)
+    memory = memory.reshape(runs, cores, *memory.shape[1:])
+    total = memory[0].astype(f32)
+    for away_by in sorted(range(1, runs), key=lambda d: -min(d, runs - d)):
+        total = total + moved(memory[away_by], "y", away_by).astype(f32)
+    total = total.astype(bf16)
+    other = moved(total[1], "core", 1)
+    first = core == 0
+    d_memory = jnp.concatenate(
+        [jnp.where(first, total[0], other), jnp.where(first, other, total[0])], axis=0
     )
-    from_half = moved(to_half, "xh", 1)
-    from_both = lax.ppermute(to_both, ("xh", "core"), [(0, 3), (1, 2), (2, 1), (3, 0)])
-    far_weights = moved(weights, "core", 1)
-    d_query, kept, to_core = backward(
-        0, places, member, core[None], stats, own, pieces, d_query, (bf16, f32, bf16)
-    )
-    d_query, to_core, from_half, from_both, far_weights = lax.optimization_barrier(
-        (d_query, to_core, from_half, from_both, far_weights)
-    )
-    d_query = lax.all_to_all(d_query, Z, 0, 0, tiled=True)
-    from_core = moved(to_core, "core", 1)
-
-    side = lax.axis_index("xl")
-    sides = lax.axis_size("xl")
-    chunks = key_weight.shape[0] // (sides * BLOCK)
-    given = (kept, from_half, from_core, from_both, key_weight, value_weight, far_weights)
-    if sides > 1:
-        given += (moved(project(1 - side, chunks, *given), "xl", 1),)
-    memory, d_query = lax.optimization_barrier((project(side, chunks, *given), d_query))
-    memory = lax.all_to_all(memory, ("y", "core"), 0, 0, tiled=True)
-
-    cores = lax.axis_size("core")
-    memory = memory.reshape(chunks // cores, cores, *memory.shape[1:]).astype(f32)
-    d_memory = jnp.sum(memory, axis=0).reshape(keys.shape).astype(bf16)
     d_queries = jnp.sum(d_query.astype(f32), axis=0).astype(bf16)
     return d_queries, d_memory
 

time: 180 us -> 165 us (0.917)
  waiting for transfers between devices: 54.9 us -> 30.6 us
  starting transfers between devices: 74.5 us -> 92.7 us
  blocking collectives: 15.6 us -> 0 us
  other arithmetic: 4.09 us -> 7.14 us
  Pallas kernels: 24.6 us -> 26.6 us
  local copies, waits for them, and re-layouts: 4.3 us -> 6.29 us
    ppermute x11 -> x16, starting transfers between devices: 41 us -> 78 us  [moved(): lax.ppermute(value, axis, [(i, (i + steps) % count) for i in range(count)])]
    all_to_all x2 -> x1, starting transfers between devices: 24.9 us -> 8.48 us  [body(): parts = lax.all_to_all(parts, Z, 0, 0, tiled=True)]
    all_to_all x1 -> x0, blocking collectives: 15.6 us -> none  [spread(): lax.all_to_all(jnp.broadcast_to(value, (count, *value.shape)), axis, 0, 0...]
    all_to_all x2 -> x1, waiting for transfers between devices: 22 us -> 10.8 us  [body(): parts = lax.all_to_all(parts, Z, 0, 0, tiled=True)]
    ppermute x11 -> x16, waiting for transfers between devices: 29.4 us -> 19.8 us  [moved(): lax.ppermute(value, axis, [(i, (i + steps) % count) for i in range(count)])]
    ppermute x1 -> x0, starting transfers between devices: 4.82 us -> none  [body(): lax.ppermute(to_both, ('xh', 'core'), [(0, 3), (1, 2), (2, 1), (3, 0)])]
    all_to_all x1, waiting for transfers between devices: 3.54 us -> 0.01 us  [body(): d_query = lax.all_to_all(d_query, Z, 0, 0, tiled=True)]
    all_to_all x1, starting transfers between devices: 3.71 us -> 6.21 us  [body(): d_query = lax.all_to_all(d_query, Z, 0, 0, tiled=True)]
  transfers between devices with their start and end apart: 15 -> 18, of which waited for: 9 -> 8; matrix products, arithmetic and copies ran while one was open for 1% -> 5% of each run, Pallas kernels for 10% -> 8%
where the time goes in v3:
time: 165 us; the launch traced here: 164 us
  starting transfers between devices  92.7 us (56%)
  waiting for transfers between devices  30.6 us (19%)
  Pallas kernels  26.6 us (16%)
  other arithmetic  7.14 us (4%)
  local copies, waits for them, and re-layouts  6.29 us (4%)
    ppermute x16, starting transfers between devices, moved(): lax.ppermute(value, axis, [(i, (i + steps) % count) for i in range(count)])  78 us
    ppermute x16, waiting for transfers between devices, moved(): lax.ppermute(value, axis, [(i, (i + steps) % count) for i in range(count)])  19.8 us
    pallas_call x2, Pallas kernels, backward(): pl.pallas_call(kernel, out_shape=[jax.ShapeDtypeStruct((count, BLOCK, BLO...  14.3 us
    all_to_all x1, waiting for transfers between devices, body(): parts = lax.all_to_all(parts, Z, 0, 0, tiled=True)  10.8 us
    pallas_call x2, Pallas kernels, forward(): pl.pallas_call(kernel, out_shape=shape, in_specs=specs, out_specs=VMEM, s...  8.97 us
    all_to_all x1, starting transfers between devices, body(): parts = lax.all_to_all(parts, Z, 0, 0, tiled=True)  8.48 us
    all_to_all x1, starting transfers between devices, body(): d_query = lax.all_to_all(d_query, Z, 0, 0, tiled=True)  6.21 us
    unnamed x22, local copies, waits for them, and re-layouts  4.29 us
  transfers between devices with their start and end apart: 18, of which 8 were waited for; matrix products, arithmetic and copies ran while one was open for 5% of the time, Pallas kernels for 8%

profile of v3, /device:TPU:1, one launch (start us, length us, event | category | flops | bytes accessed | tf_op | source)
XLA Modules:
  0.0 164.3 jit_solution(14249589060608073825)
XLA Ops:
  0.6 0.0 copy-start
  0.7 0.8 constant_dynamic-update-slice_fusion.3
  1.5 0.8 constant_dynamic-update-slice_fusion.2
  2.2 13.3 %collective-permute-start.1 = (bf16[128,256]{1,0:T(8,128)(2,1)S(1)}, bf16[128,256]{1,0:T(8,128)(2,1)S(1)}, u32[]{:S(2)}, u32[]{:S(2)}) collective-permute-start(bf16[128,256]{1,0:T(8,128)(2,1)S(1)} %constant_dynamic-update-slice_fusion.2), channel_id=1, source_target_pairs={{0,192},{16,208},{32,224},{48,240},{64,0},{80,16},{96,32},{112,48}... | collective-permute-start | bytes 196616 | tf_op jit(solution)/shard_map/ppermute | solution.py:293
  15.5 1.9 %collective-permute-start.2 = (bf16[128,256]{1,0:T(8,128)(2,1)S(1)}, bf16[128,256]{1,0:T(8,128)(2,1)S(1)}, u32[]{:S(2)}, u32[]{:S(2)}) collective-permute-start(bf16[128,256]{1,0:T(8,128)(2,1)S(1)} %constant_dynamic-update-slice_fusion.2), channel_id=1, source_target_pairs={{0,64},{16,80},{32,96},{48,112},{64,128},{80,144},{96,160},{112,17... | collective-permute-start | bytes 196616 | tf_op jit(solution)/shard_map/ppermute | solution.py:293
  17.5 10.3 %collective-permute-start.3 = (bf16[128,256]{1,0:T(8,128)(2,1)S(1)}, bf16[128,256]{1,0:T(8,128)(2,1)S(1)}, u32[]{:S(2)}, u32[]{:S(2)}) collective-permute-start(bf16[128,256]{1,0:T(8,128)(2,1)S(1)} %constant_dynamic-update-slice_fusion.2), channel_id=1, source_target_pairs={{0,128},{16,144},{32,160},{48,176},{64,192},{80,208},{96,224},{112... | collective-permute-start | bytes 196616 | tf_op jit(solution)/shard_map/ppermute | solution.py:293
  27.7 0.9 constant_dynamic-update-slice_fusion.1
  28.7 0.9 constant_dynamic-update-slice_fusion.refs_2_.near_ref.kv_ref
  29.6 4.7 %collective-permute-start = (bf16[512,256]{1,0:T(8,128)(2,1)S(1)}, bf16[512,256]{1,0:T(8,128)(2,1)S(1)}, u32[]{:S(2)}, u32[]{:S(2)}) collective-permute-start(bf16[512,256]{1,0:T(8,128)(2,1)S(1)} %constant_dynamic-update-slice_fusion.refs_2_.near_ref.kv_ref), channel_id=1, source_target_pairs={{0,256},{256,0},{1,257},{257,1},{2,258},{258,2},{3,259},{259,3},{4... | collective-permute-start | bytes 786440 | tf_op jit(solution)/shard_map/ppermute | solution.py:293
  34.3 0.7 and_select_fusion.2.refs_0_.places
  34.9 0.1 pad_add_fusion
  35.0 2.1 %pad_maximum_fusion = bf16[2048,256]{1,0:T(8,128)(2,1)} fusion(bf16[2048,128]{1,0:T(8,128)(2,1)} %vw.3, bf16[2048,128]{1,0:T(8,128)(2,1)S(1)} %copy-done.1), kind=kLoop, calls=%fused_computation | loop fusion | flops 2097152 | bytes 2097152 | tf_op jit(solution)/shard_map/concatenate | solution.py:330
  37.2 0.4 compare_reduce_fusion
  37.6 0.1 reshape.59.refs_1_.member
  37.7 0.0 collective-permute-done.1
  37.7 0.0 collective-permute-done.2
  37.7 0.0 collective-permute-done.3
  37.8 2.6 %collective-permute-start.4 = (bf16[512,256]{1,0:T(8,128)(2,1)S(1)}, bf16[512,256]{1,0:T(8,128)(2,1)S(1)}, u32[]{:S(2)}, u32[]{:S(2)}) collective-permute-start(bf16[512,256]{1,0:T(8,128)(2,1)S(1)} %pad_maximum_fusion.1.refs_4_.refs_5_.rest_0_), channel_id=1, source_target_pairs={{0,16},{16,32},{32,48},{48,64},{64,80},{80,96},{96,112},{112,128},... | collective-permute-start | bytes 786440 | tf_op jit(solution)/shard_map/ppermute | solution.py:293
  40.4 3.8 %collective-permute-start.5 = (bf16[512,256]{1,0:T(8,128)(2,1)S(1)}, bf16[512,256]{1,0:T(8,128)(2,1)S(1)}, u32[]{:S(2)}, u32[]{:S(2)}) collective-permute-start(bf16[512,256]{1,0:T(8,128)(2,1)S(1)} %pad_maximum_fusion.1.refs_4_.refs_5_.rest_0_), channel_id=1, source_target_pairs={{0,240},{16,0},{32,16},{48,32},{64,48},{80,64},{96,80},{112,96},{1... | collective-permute-start | bytes 786440 | tf_op jit(solution)/shard_map/ppermute | solution.py:293
  44.3 2.0 %collective-permute-start.6 = (bf16[256,256]{1,0:T(8,128)(2,1)S(1)}, bf16[256,256]{1,0:T(8,128)(2,1)S(1)}, u32[]{:S(2)}, u32[]{:S(2)}) collective-permute-start(bf16[256,256]{1,0:T(8,128)(2,1)S(1)} %get-tuple-element.32), channel_id=1, source_target_pairs={{0,224},{16,240},{32,0},{48,16},{64,32},{80,48},{96,64},{112,80},{... | collective-permute-start | bytes 393224 | tf_op jit(solution)/shard_map/ppermute | solution.py:293
  46.3 4.1 %collective-permute-start.7 = (bf16[256,256]{1,0:T(8,128)(2,1)S(1)}, bf16[256,256]{1,0:T(8,128)(2,1)S(1)}, u32[]{:S(2)}, u32[]{:S(2)}) collective-permute-start(bf16[256,256]{1,0:T(8,128)(2,1)S(1)} %get-tuple-element.31), channel_id=1, source_target_pairs={{0,32},{16,48},{32,64},{48,80},{64,96},{80,112},{96,128},{112,144}... | collective-permute-start | bytes 393224 | tf_op jit(solution)/shard_map/ppermute | solution.py:293
  50.5 0.0 collective-permute-done.refs_3_.far_ref.refs_4_
  50.5 2.3 %forward.2.rest_4_ = f32[64,128]{1,0:T(8,128)S(1)} custom-call(s32[16]{0:T(128)S(1)} %and_select_fusion.2.refs_0_.places, s32[128]{0:T(128)S(1)} %reshape.59.refs_1_.member, bf16[512,256]{1,0:T(8,128)(2,1)S(1)} %constant_dynamic-update-slice_fusion.refs_2_.near_ref.kv_ref, bf16[512,256]{1,0:T(8,128)(2,1)S(1)} %collective-permute-done.refs_3_.far_ref.refs_4_, ...), custom_call_target="tpu_custom_call" | custom-call | flops 2147483648 | bytes 1048576 | tf_op jit(solution)/shard_map/forward/pallas_call | solution.py:137
  52.8 0.6 collective-permute-done.6.rest_2_.refs_8_.rest_3_
  53.4 2.0 %collective-permute-done.7.rest_3_.refs_9_.rest_4_ = bf16[256,256]{1,0:T(8,128)(2,1)S(1)} collective-permute-done((bf16[256,256]{1,0:T(8,128)(2,1)S(1)}, bf16[256,256]{1,0:T(8,128)(2,1)S(1)}, u32[]{:S(2)}, u32[]{:S(2)}) %collective-permute-start.7) | collective-permute-done | bytes 131104 | tf_op jit(solution)/shard_map/ppermute | solution.py:293
  55.4 0.0 collective-permute-done.4.rest_0_.refs_6_.rest_1_
  55.5 0.0 collective-permute-done.5.rest_1_.refs_7_.rest_2_
  55.5 6.7 %forward.3 = bf16[16,96,128]{2,1,0:T(8,128)(2,1)} custom-call(s32[16]{0:T(128)S(1)} %and_select_fusion.2.refs_0_.places, s32[128]{0:T(128)S(1)} %reshape.59.refs_1_.member, bf16[512,256]{1,0:T(8,128)(2,1)S(1)} %constant_dynamic-update-slice_fusion.refs_2_.near_ref.kv_ref, bf16[512,256]{1,0:T(8,128)(2,1)S(1)} %collective-permute-done.refs_3_.far_ref.refs_4_, ...), custom_call_target="tpu_custom_call" | custom-call | flops 6442450944 | bytes 1048576 | tf_op jit(solution)/shard_map/forward/pallas_call | solution.py:137
  62.1 0.7 copy-done.5
  62.8 8.5 %all-to-all-start = ((bf16[16,96,128]{2,1,0:T(8,128)(2,1)}), bf16[16,96,128]{2,1,0:T(8,128)(2,1)S(1)}, u32[]{:S(2)}, u32[]{:S(2)}) async-start(bf16[16,96,128]{2,1,0:T(8,128)(2,1)} %forward.3), calls=%async_computation | async-start | bytes 786432 | tf_op jit(solution)/shard_map/all_to_all | solution.py:332
  71.3 3.5 %collective-permute-start.8 = (bf16[2048,256]{1,0:T(8,128)(2,1)}, bf16[2048,256]{1,0:T(8,128)(2,1)S(1)}, u32[]{:S(2)}, u32[]{:S(2)}) collective-permute-start(bf16[2048,256]{1,0:T(8,128)(2,1)} %pad_maximum_fusion), channel_id=1, source_target_pairs={{0,1},{1,0},{2,3},{3,2},{4,5},{5,4},{6,7},{7,6},{8,9},{9,8},{10,11... | collective-permute-start | bytes 3145736 | tf_op jit(solution)/shard_map/ppermute | solution.py:293
  74.8 0.6 and_select_fusion
  75.4 0.6 fusion.1
  76.0 1.3 collective-permute-done.8.far
  77.3 10.8 %all-to-all-done.refs_3_.parts = bf16[16,96,128]{2,1,0:T(8,128)(2,1)S(1)} async-done(((bf16[16,96,128]{2,1,0:T(8,128)(2,1)}), bf16[16,96,128]{2,1,0:T(8,128)(2,1)S(1)}, u32[]{:S(2)}, u32[]{:S(2)}) %all-to-all-start) | async-done | bytes 393248 | tf_op jit(solution)/shard_map/all_to_all | solution.py:332
  88.0 0.0 copy-done.3
  88.0 0.9 copy-done.6
  89.0 6.7 %backward.2 = (f32[16,128,128]{2,1,0:T(8,128)S(1)}, bf16[512,256]{1,0:T(8,128)(2,1)S(1)}) custom-call(s32[16]{0:T(128)S(1)} %and_select_fusion.2.refs_0_.places, s32[128]{0:T(128)S(1)} %reshape.59.refs_1_.member, s32[1]{0:T(128)} %bitcast.refs_2_.core, bf16[16,96,128]{2,1,0:T(8,128)(2,1)S(1)} %all-to-all-done.refs_3_.parts, ...), custom_call_target="tpu_custom_call" | custom-call | flops 10737418240 | bytes 1048576 | tf_op jit(solution)/shard_map/backward/pallas_call | solution.py:245
  95.7 3.5 %collective-permute-start.9 = (bf16[512,256]{1,0:T(8,128)(2,1)S(1)}, bf16[512,256]{1,0:T(8,128)(2,1)S(1)}, u32[]{:S(2)}, u32[]{:S(2)}) collective-permute-start(bf16[512,256]{1,0:T(8,128)(2,1)S(1)} %get-tuple-element.20), channel_id=1, source_target_pairs={{0,256},{256,0},{1,257},{257,1},{2,258},{258,2},{3,259},{259,3},{4... | collective-permute-start | bytes 786440 | tf_op jit(solution)/shard_map/ppermute | solution.py:293
  99.2 0.9 copy-done.4
  100.1 7.5 %backward.3 = (bf16[16,128,128]{2,1,0:T(8,128)(2,1)}, f32[256,256]{1,0:T(8,128)S(1)}, f32[256,256]{1,0:T(8,128)S(1)}) custom-call(s32[16]{0:T(128)S(1)} %and_select_fusion.2.refs_0_.places, s32[128]{0:T(128)S(1)} %reshape.59.refs_1_.member, s32[1]{0:T(128)} %bitcast.refs_2_.core, bf16[16,96,128]{2,1,0:T(8,128)(2,1)S(1)} %all-to-all-done.refs_3_.parts, ...), custom_call_target="tpu_custom_call" | custom-call | flops 10737418240 | bytes 1048576 | tf_op jit(solution)/shard_map/backward/pallas_call | solution.py:245
  107.7 0.0 collective-permute-done.9.from_half
  107.7 10.3 %collective-permute-start.10 = (bf16[256,256]{1,0:T(8,128)(2,1)S(1)}, bf16[256,256]{1,0:T(8,128)(2,1)S(1)}, u32[]{:S(2)}, u32[]{:S(2)}) collective-permute-start(bf16[256,256]{1,0:T(8,128)(2,1)S(1)} %add_convert_fusion.1), channel_id=1, source_target_pairs={{0,1},{1,0},{2,3},{3,2},{4,5},{5,4},{6,7},{7,6},{8,9},{9,8},{10,11... | collective-permute-start | bytes 393224 | tf_op jit(solution)/shard_map/ppermute | solution.py:293
  118.1 6.2 %all-to-all-start.1 = ((bf16[16,128,128]{2,1,0:T(8,128)(2,1)}), bf16[16,128,128]{2,1,0:T(8,128)(2,1)}, u32[]{:S(2)}, u32[]{:S(2)}) async-start(bf16[16,128,128]{2,1,0:T(8,128)(2,1)} %get-tuple-element.21), calls=%async_computation.1 | async-start | bytes 1048576 | tf_op jit(solution)/shard_map/all_to_all | solution.py:342
  124.3 0.1 add_add_fusion
  124.4 0.1 add.145.chunk
  124.5 0.0 collective-permute-done.10.from_core
  124.5 2.1 %project.2 = bf16[8,256,128]{2,1,0:T(8,128)(2,1)} custom-call(s32[1]{0:T(128)} %bitcast.refs_2_.core, s32[8]{0:T(128)S(1)} %add.145.chunk, f32[256,256]{1,0:T(8,128)S(1)} %get-tuple-element.22.kept, bf16[512,256]{1,0:T(8,128)(2,1)S(1)} %collective-permute-done.9.from_half, bf16[256,256]{1,0:T(8,128)(2,1)S(1)} %collective-permute-done.10.from_core, ...), custom_call_target="tpu_custom_call" | custom-call | tf_op jit(solution)/shard_map/project/pallas_call | solution.py:281
  126.6 2.2 %collective-permute-start.11 = (bf16[8,256,128]{2,1,0:T(8,128)(2,1)}, bf16[8,256,128]{2,1,0:T(8,128)(2,1)S(1)}, u32[]{:S(2)}, u32[]{:S(2)}) collective-permute-start(bf16[8,256,128]{2,1,0:T(8,128)(2,1)} %project.2), channel_id=1, source_target_pairs={{0,8},{8,0},{1,9},{9,1},{2,10},{10,2},{3,11},{11,3},{4,12},{12,4},... | collective-permute-start | bytes 1572872 | tf_op jit(solution)/shard_map/ppermute | solution.py:293
  128.8 0.1 add.140.chunk
  128.9 13.1 %collective-permute-done.11.rest_0_ = bf16[8,256,128]{2,1,0:T(8,128)(2,1)S(1)} collective-permute-done((bf16[8,256,128]{2,1,0:T(8,128)(2,1)}, bf16[8,256,128]{2,1,0:T(8,128)(2,1)S(1)}, u32[]{:S(2)}, u32[]{:S(2)}) %collective-permute-start.11) | collective-permute-done | bytes 524320 | tf_op jit(solution)/shard_map/ppermute | solution.py:293
  142.0 1.3 project.3
  143.3 4.8 %collective-permute-start.12 = (bf16[2,256,128]{2,1,0:T(8,128)(2,1)S(1)}, bf16[2,256,128]{2,1,0:T(8,128)(2,1)S(1)}, u32[]{:S(2)}, u32[]{:S(2)}) collective-permute-start(bf16[2,256,128]{2,1,0:T(8,128)(2,1)S(1)} %get-tuple-element.26), channel_id=1, source_target_pairs={{0,4},{2,6},{4,0},{6,2},{1,5},{3,7},{5,1},{7,3},{8,12},{10,14},{12... | collective-permute-start | bytes 393224 | tf_op jit(solution)/shard_map/ppermute | solution.py:293
  148.1 2.3 %collective-permute-start.13 = (bf16[2,256,128]{2,1,0:T(8,128)(2,1)S(1)}, bf16[2,256,128]{2,1,0:T(8,128)(2,1)S(1)}, u32[]{:S(2)}, u32[]{:S(2)}) collective-permute-start(bf16[2,256,128]{2,1,0:T(8,128)(2,1)S(1)} %get-tuple-element.28), channel_id=1, source_target_pairs={{0,2},{2,4},{4,6},{6,0},{1,3},{3,5},{5,7},{7,1},{8,10},{10,12},{12... | collective-permute-start | bytes 393224 | tf_op jit(solution)/shard_map/ppermute | solution.py:293
  150.4 4.2 %collective-permute-start.14 = (bf16[2,256,128]{2,1,0:T(8,128)(2,1)S(1)}, bf16[2,256,128]{2,1,0:T(8,128)(2,1)S(1)}, u32[]{:S(2)}, u32[]{:S(2)}) collective-permute-start(bf16[2,256,128]{2,1,0:T(8,128)(2,1)S(1)} %get-tuple-element.27), channel_id=1, source_target_pairs={{0,6},{2,0},{4,2},{6,4},{1,7},{3,1},{5,3},{7,5},{8,14},{10,8},{12,... | collective-permute-start | bytes 393224 | tf_op jit(solution)/shard_map/ppermute | solution.py:293
  154.6 0.0 collective-permute-done.12
  154.6 0.4 collective-permute-done.13
  155.0 1.5 collective-permute-done.14
  156.6 0.1 add_convert_fusion
  156.6 4.3 %collective-permute-start.15 = (bf16[256,128]{1,0:T(8,128)(2,1)S(1)}, bf16[256,128]{1,0:T(8,128)(2,1)S(1)}, u32[]{:S(2)}, u32[]{:S(2)}) collective-permute-start(bf16[256,128]{1,0:T(8,128)(2,1)S(1)} %slice_bitcast_fusion), channel_id=1, source_target_pairs={{0,1},{1,0},{2,3},{3,2},{4,5},{5,4},{6,7},{7,6},{8,9},{9,8},{10,11... | collective-permute-start | bytes 196616 | tf_op jit(solution)/shard_map/ppermute | solution.py:293
  161.0 0.9 collective-permute-done.15
  161.9 0.7 pad_maximum_fusion.4
  162.5 0.0 all-to-all-done.1
  162.5 1.7 %reduce_sum.12 = bf16[128,128]{1,0:T(8,128)(2,1)} reduce(bf16[16,128,128]{2,1,0:T(8,128)(2,1)} %all-to-all-done.1, bf16[]{:T(256)} %constant.75.clone.1), dimensions={0}, to_apply=%region_1.2 | reduce | flops 245760 | bytes 557058 | tf_op jit(solution)/shard_map/reduce_sum | solution.py:366
  (24 shorter events, 0.2 us)
Async XLA Ops:
  0.6 34.4 %copy-start = (s32[32,64]{1,0:T(8,128)S(1)}, s32[32,64]{1,0:T(8,128)}, u32[]{:S(2)}) copy-start(s32[32,64]{1,0:T(8,128)} %param.14) | copy-start | bytes 24580
  0.6 34.4 %copy-start.1 = (bf16[2048,128]{1,0:T(8,128)(2,1)S(1)}, bf16[2048,128]{1,0:T(8,128)(2,1)}, u32[]{:S(2)}) copy-start(bf16[2048,128]{1,0:T(8,128)(2,1)} %kw.3) | copy-start | bytes 1572868
  2.2 35.5 %collective-permute-start.1 = (bf16[128,256]{1,0:T(8,128)(2,1)S(1)}, bf16[128,256]{1,0:T(8,128)(2,1)S(1)}, u32[]{:S(2)}, u32[]{:S(2)}) collective-permute-start(bf16[128,256]{1,0:T(8,128)(2,1)S(1)} %constant_dynamic-update-slice_fusion.2), channel_id=1, source_target_pairs={{0,192},{16,208},{32,224},{48,240},{64,0},{80,16},{96,32},{112,48}... | collective-permute-start | bytes 196616 | tf_op jit(solution)/shard_map/ppermute | solution.py:293
  15.5 22.2 %collective-permute-start.2 = (bf16[128,256]{1,0:T(8,128)(2,1)S(1)}, bf16[128,256]{1,0:T(8,128)(2,1)S(1)}, u32[]{:S(2)}, u32[]{:S(2)}) collective-permute-start(bf16[128,256]{1,0:T(8,128)(2,1)S(1)} %constant_dynamic-update-slice_fusion.2), channel_id=1, source_target_pairs={{0,64},{16,80},{32,96},{48,112},{64,128},{80,144},{96,160},{112,17... | collective-permute-start | bytes 196616 | tf_op jit(solution)/shard_map/ppermute | solution.py:293
  17.5 20.3 %collective-permute-start.3 = (bf16[128,256]{1,0:T(8,128)(2,1)S(1)}, bf16[128,256]{1,0:T(8,128)(2,1)S(1)}, u32[]{:S(2)}, u32[]{:S(2)}) collective-permute-start(bf16[128,256]{1,0:T(8,128)(2,1)S(1)} %constant_dynamic-update-slice_fusion.2), channel_id=1, source_target_pairs={{0,128},{16,144},{32,160},{48,176},{64,192},{80,208},{96,224},{112... | collective-permute-start | bytes 196616 | tf_op jit(solution)/shard_map/ppermute | solution.py:293
  29.6 20.9 %collective-permute-start = (bf16[512,256]{1,0:T(8,128)(2,1)S(1)}, bf16[512,256]{1,0:T(8,128)(2,1)S(1)}, u32[]{:S(2)}, u32[]{:S(2)}) collective-permute-start(bf16[512,256]{1,0:T(8,128)(2,1)S(1)} %constant_dynamic-update-slice_fusion.refs_2_.near_ref.kv_ref), channel_id=1, source_target_pairs={{0,256},{256,0},{1,257},{257,1},{2,258},{258,2},{3,259},{259,3},{4... | collective-permute-start | bytes 786440 | tf_op jit(solution)/shard_map/ppermute | solution.py:293
  37.8 17.7 %collective-permute-start.4 = (bf16[512,256]{1,0:T(8,128)(2,1)S(1)}, bf16[512,256]{1,0:T(8,128)(2,1)S(1)}, u32[]{:S(2)}, u32[]{:S(2)}) collective-permute-start(bf16[512,256]{1,0:T(8,128)(2,1)S(1)} %pad_maximum_fusion.1.refs_4_.refs_5_.rest_0_), channel_id=1, source_target_pairs={{0,16},{16,32},{32,48},{48,64},{64,80},{80,96},{96,112},{112,128},... | collective-permute-start | bytes 786440 | tf_op jit(solution)/shard_map/ppermute | solution.py:293
  40.4 15.0 %collective-permute-start.5 = (bf16[512,256]{1,0:T(8,128)(2,1)S(1)}, bf16[512,256]{1,0:T(8,128)(2,1)S(1)}, u32[]{:S(2)}, u32[]{:S(2)}) collective-permute-start(bf16[512,256]{1,0:T(8,128)(2,1)S(1)} %pad_maximum_fusion.1.refs_4_.refs_5_.rest_0_), channel_id=1, source_target_pairs={{0,240},{16,0},{32,16},{48,32},{64,48},{80,64},{96,80},{112,96},{1... | collective-permute-start | bytes 786440 | tf_op jit(solution)/shard_map/ppermute | solution.py:293
  44.3 9.1 %collective-permute-start.6 = (bf16[256,256]{1,0:T(8,128)(2,1)S(1)}, bf16[256,256]{1,0:T(8,128)(2,1)S(1)}, u32[]{:S(2)}, u32[]{:S(2)}) collective-permute-start(bf16[256,256]{1,0:T(8,128)(2,1)S(1)} %get-tuple-element.32), channel_id=1, source_target_pairs={{0,224},{16,240},{32,0},{48,16},{64,32},{80,48},{96,64},{112,80},{... | collective-permute-start | bytes 393224 | tf_op jit(solution)/shard_map/ppermute | solution.py:293
  46.3 9.1 %collective-permute-start.7 = (bf16[256,256]{1,0:T(8,128)(2,1)S(1)}, bf16[256,256]{1,0:T(8,128)(2,1)S(1)}, u32[]{:S(2)}, u32[]{:S(2)}) collective-permute-start(bf16[256,256]{1,0:T(8,128)(2,1)S(1)} %get-tuple-element.31), channel_id=1, source_target_pairs={{0,32},{16,48},{32,64},{48,80},{64,96},{80,112},{96,128},{112,144}... | collective-permute-start | bytes 393224 | tf_op jit(solution)/shard_map/ppermute | solution.py:293
  55.5 32.6 %copy-start.3 = (bf16[512,256]{1,0:T(8,128)(2,1)}, bf16[512,256]{1,0:T(8,128)(2,1)S(1)}, u32[]{:S(2)}) copy-start(bf16[512,256]{1,0:T(8,128)(2,1)S(1)} %collective-permute-done.5.rest_1_.refs_7_.rest_2_) | copy-start | bytes 786436
  62.1 0.7 copy-start.5
  62.8 25.3 %all-to-all-start = ((bf16[16,96,128]{2,1,0:T(8,128)(2,1)}), bf16[16,96,128]{2,1,0:T(8,128)(2,1)S(1)}, u32[]{:S(2)}, u32[]{:S(2)}) async-start(bf16[16,96,128]{2,1,0:T(8,128)(2,1)} %forward.3), calls=%async_computation | async-start | bytes 786432 | tf_op jit(solution)/shard_map/all_to_all | solution.py:332
  71.3 6.0 %collective-permute-start.8 = (bf16[2048,256]{1,0:T(8,128)(2,1)}, bf16[2048,256]{1,0:T(8,128)(2,1)S(1)}, u32[]{:S(2)}, u32[]{:S(2)}) collective-permute-start(bf16[2048,256]{1,0:T(8,128)(2,1)} %pad_maximum_fusion), channel_id=1, source_target_pairs={{0,1},{1,0},{2,3},{3,2},{4,5},{5,4},{6,7},{7,6},{8,9},{9,8},{10,11... | collective-permute-start | bytes 3145736 | tf_op jit(solution)/shard_map/ppermute | solution.py:293
  88.0 0.9 copy-start.6
  88.9 10.2 %copy-start.7 = (bf16[256,256]{1,0:T(8,128)(2,1)S(1)}, bf16[256,256]{1,0:T(8,128)(2,1)}, u32[]{:S(2)}) copy-start(bf16[256,256]{1,0:T(8,128)(2,1)} %copy-done.5) | copy-start | bytes 393220
  95.7 12.0 %collective-permute-start.9 = (bf16[512,256]{1,0:T(8,128)(2,1)S(1)}, bf16[512,256]{1,0:T(8,128)(2,1)S(1)}, u32[]{:S(2)}, u32[]{:S(2)}) collective-permute-start(bf16[512,256]{1,0:T(8,128)(2,1)S(1)} %get-tuple-element.20), channel_id=1, source_target_pairs={{0,256},{256,0},{1,257},{257,1},{2,258},{258,2},{3,259},{259,3},{4... | collective-permute-start | bytes 786440 | tf_op jit(solution)/shard_map/ppermute | solution.py:293
  99.2 1.0 copy-start.4
  107.7 16.6 %copy-start.8 = (s32[2]{0:T(128)S(1)}, s32[2]{0:T(128)}, u32[]{:S(2)}) copy-start(s32[2]{0:T(128)} %and_select_fusion) | copy-start | bytes 28
  107.7 16.6 %copy-start.9 = (s32[4]{0:T(128)S(1)}, s32[4]{0:T(128)}, u32[]{:S(2)}) copy-start(s32[4]{0:T(128)} %fusion.1) | copy-start | bytes 52
  107.7 16.8 %copy-start.2 = (bf16[2048,128]{1,0:T(8,128)(2,1)S(1)}, bf16[2048,128]{1,0:T(8,128)(2,1)}, u32[]{:S(2)}) copy-start(bf16[2048,128]{1,0:T(8,128)(2,1)} %vw.3) | copy-start | bytes 1572868
  107.7 16.8 %collective-permute-start.10 = (bf16[256,256]{1,0:T(8,128)(2,1)S(1)}, bf16[256,256]{1,0:T(8,128)(2,1)S(1)}, u32[]{:S(2)}, u32[]{:S(2)}) collective-permute-start(bf16[256,256]{1,0:T(8,128)(2,1)S(1)} %add_convert_fusion.1), channel_id=1, source_target_pairs={{0,1},{1,0},{2,3},{3,2},{4,5},{5,4},{6,7},{7,6},{8,9},{9,8},{10,11... | collective-permute-start | bytes 393224 | tf_op jit(solution)/shard_map/ppermute | solution.py:293
  118.1 44.5 %all-to-all-start.1 = ((bf16[16,128,128]{2,1,0:T(8,128)(2,1)}), bf16[16,128,128]{2,1,0:T(8,128)(2,1)}, u32[]{:S(2)}, u32[]{:S(2)}) async-start(bf16[16,128,128]{2,1,0:T(8,128)(2,1)} %get-tuple-element.21), calls=%async_computation.1 | async-start | bytes 1048576 | tf_op jit(solution)/shard_map/all_to_all | solution.py:342
  126.6 15.4 %collective-permute-start.11 = (bf16[8,256,128]{2,1,0:T(8,128)(2,1)}, bf16[8,256,128]{2,1,0:T(8,128)(2,1)S(1)}, u32[]{:S(2)}, u32[]{:S(2)}) collective-permute-start(bf16[8,256,128]{2,1,0:T(8,128)(2,1)} %project.2), channel_id=1, source_target_pairs={{0,8},{8,0},{1,9},{9,1},{2,10},{10,2},{3,11},{11,3},{4,12},{12,4},... | collective-permute-start | bytes 1572872 | tf_op jit(solution)/shard_map/ppermute | solution.py:293
  143.3 11.3 %collective-permute-start.12 = (bf16[2,256,128]{2,1,0:T(8,128)(2,1)S(1)}, bf16[2,256,128]{2,1,0:T(8,128)(2,1)S(1)}, u32[]{:S(2)}, u32[]{:S(2)}) collective-permute-start(bf16[2,256,128]{2,1,0:T(8,128)(2,1)S(1)} %get-tuple-element.26), channel_id=1, source_target_pairs={{0,4},{2,6},{4,0},{6,2},{1,5},{3,7},{5,1},{7,3},{8,12},{10,14},{12... | collective-permute-start | bytes 393224 | tf_op jit(solution)/shard_map/ppermute | solution.py:293
  148.1 6.9 %collective-permute-start.13 = (bf16[2,256,128]{2,1,0:T(8,128)(2,1)S(1)}, bf16[2,256,128]{2,1,0:T(8,128)(2,1)S(1)}, u32[]{:S(2)}, u32[]{:S(2)}) collective-permute-start(bf16[2,256,128]{2,1,0:T(8,128)(2,1)S(1)} %get-tuple-element.28), channel_id=1, source_target_pairs={{0,2},{2,4},{4,6},{6,0},{1,3},{3,5},{5,7},{7,1},{8,10},{10,12},{12... | collective-permute-start | bytes 393224 | tf_op jit(solution)/shard_map/ppermute | solution.py:293
  150.4 6.1 %collective-permute-start.14 = (bf16[2,256,128]{2,1,0:T(8,128)(2,1)S(1)}, bf16[2,256,128]{2,1,0:T(8,128)(2,1)S(1)}, u32[]{:S(2)}, u32[]{:S(2)}) collective-permute-start(bf16[2,256,128]{2,1,0:T(8,128)(2,1)S(1)} %get-tuple-element.27), channel_id=1, source_target_pairs={{0,6},{2,0},{4,2},{6,4},{1,7},{3,1},{5,3},{7,5},{8,14},{10,8},{12,... | collective-permute-start | bytes 393224 | tf_op jit(solution)/shard_map/ppermute | solution.py:293
  156.6 5.2 %collective-permute-start.15 = (bf16[256,128]{1,0:T(8,128)(2,1)S(1)}, bf16[256,128]{1,0:T(8,128)(2,1)S(1)}, u32[]{:S(2)}, u32[]{:S(2)}) collective-permute-start(bf16[256,128]{1,0:T(8,128)(2,1)S(1)} %slice_bitcast_fusion), channel_id=1, source_target_pairs={{0,1},{1,0},{2,3},{3,2},{4,5},{5,4},{6,7},{7,6},{8,9},{9,8},{10,11... | collective-permute-start | bytes 196616 | tf_op jit(solution)/shard_map/ppermute | solution.py:293

commit v4 on v3

v4 whole, which is shorter than its diff:
```python
from functools import partial

import jax
import jax.numpy as jnp
from jax import lax
from jax.experimental import pallas as pl
from jax.experimental.pallas import tpu as pltpu
from jax.sharding import Mesh, PartitionSpec as P

HEAD_DIM = 64
BLOCK = 128
AXES = ("xh", "z", "xl", "y", "core")
SIZES = (2, 16, 2, 4, 2)
Z = "z"
CTX = ("xh", "z")
HEAD = ("xl", "y", "core")
BIG = 1e30

OWN = (4, 0, -4, 8)
LATER = (3, -1, -5, 7, 5, 1, -3, 9, 6, 2, -2, -6)
SLOTS = OWN + LATER

VMEM = pl.BlockSpec(memory_space=pltpu.VMEM)
SMEM = pl.BlockSpec(memory_space=pltpu.SMEM)
ROOM = pltpu.CompilerParams(vmem_limit_bytes=48 * 1024 * 1024)


def cost(flops, exps):
    return pl.CostEstimate(flops=4 * flops, bytes_accessed=1 << 20, transcendentals=exps)


def dot_nt(a, b):
    return lax.dot_general(a, b, (((1,), (1,)), ((), ())), preferred_element_type=jnp.float32)


def dot_nn(a, b):
    return lax.dot_general(a, b, (((1,), (0,)), ((), ())), preferred_element_type=jnp.float32)


def split_heads(rows):
    low = lax.broadcasted_iota(jnp.int32, rows.shape, 1) < HEAD_DIM
    zero = jnp.zeros_like(rows)
    return jnp.concatenate([jnp.where(low, rows, zero), jnp.where(low, zero, rows)], axis=0)


def load_keys(near_ref, far_ref, keys, vals):
    rows = near_ref.shape[0]
    keys[:rows, :] = near_ref[:, :BLOCK]
    vals[:rows, :] = near_ref[:, BLOCK:]
    keys[rows:, :] = far_ref[:, :BLOCK]
    vals[rows:, :] = far_ref[:, BLOCK:]


def load_targets(pieces, held):
    at = 0
    for piece in pieces:
        held[at : at + piece.shape[0], :] = piece[...]
        at += piece.shape[0]


def away(member, first, second, block, blocks):
    seg = (lax.broadcasted_iota(jnp.int32, (1, 4 * BLOCK), 1) // BLOCK) % 2
    one = jnp.where(member[first * blocks + block] > 0, 0.0, BIG)
    two = jnp.where(member[second * blocks + block] > 0, 0.0, BIG)
    return jnp.where(seg == 0, one, two)


def forward_kernel(base, places, member, near_ref, far_ref, *rest):
    *pieces, before, result, stats, keys, vals, held = rest
    load_keys(near_ref, far_ref, keys, vals)
    load_targets(pieces, held)
    blocks = keys.shape[0] // BLOCK
    pairs = held.shape[0] // (2 * BLOCK)
    half = stats.shape[0] // 2
    if before is not None:
        stats[...] = before[...]

    def step(p, carry):
        rows = pl.ds(pl.multiple_of(p * 2 * BLOCK, 2 * BLOCK), 2 * BLOCK)
        first, second = places[base + 2 * p], places[base + 2 * p + 1]
        query = split_heads(held[rows, :BLOCK])
        out = split_heads(held[rows, BLOCK:])
        logits = dot_nt(keys[...], query)
        prob = dot_nt(vals[...], out)
        off = [away(member, first, second, b, blocks) for b in range(blocks)]
        peak = jnp.full((1, 4 * BLOCK), -1e3, jnp.float32)
        for b in range(blocks):
            part = logits[b * BLOCK : (b + 1) * BLOCK]
            peak = jnp.maximum(peak, jnp.max(part, axis=0, keepdims=True) - off[b])
        total = jnp.zeros((1, 4 * BLOCK), jnp.float32)
        weighted = jnp.zeros((1, 4 * BLOCK), jnp.float32)
        for b in range(blocks):
            part = slice(b * BLOCK, (b + 1) * BLOCK)
            raised = jnp.exp(logits[part] - (peak + off[b]))
            total = total + jnp.sum(raised, axis=0, keepdims=True)
            weighted = weighted + jnp.sum(raised * prob[part], axis=0, keepdims=True)
        some = total > 0.0
        log_total = jnp.where(some, peak + jnp.log(jnp.where(some, total, 1.0)), -BIG)
        mean = jnp.where(some, weighted / jnp.where(some, total, 1.0), 0.0)
        for h in range(2):
            for s, place in enumerate((first, second)):
                lanes = slice((2 * h + s) * BLOCK, (2 * h + s + 1) * BLOCK)
                stats[pl.ds(2 * place + h, 1), :] = log_total[:, lanes]
                stats[pl.ds(half + 2 * place + h, 1), :] = mean[:, lanes]
        return carry

    def two(i, carry):
        return step(2 * i + 1, step(2 * i, carry))

    lax.fori_loop(0, pairs // 2, two, 0)
    if result is not None:
        high = stats[:half, :].astype(jnp.bfloat16)
        low = (stats[:half, :] - high.astype(jnp.float32)).astype(jnp.bfloat16)
        message = jnp.concatenate([high, low, stats[half:, :].astype(jnp.bfloat16)], axis=0)
        for peer in range(result.shape[0]):
            result[peer] = message


def forward(base, places, member, near, far, pieces, before):
    count = places.shape[0]
    rows = sum(p.shape[0] for p in pieces)
    enc = near.shape[0] + far.shape[0]
    given = [places, member, near, far, *pieces]
    specs = [SMEM, SMEM] + [VMEM] * (2 + len(pieces))
    local = jax.ShapeDtypeStruct((4 * count, BLOCK), jnp.float32)
    if before is None:
        shapes = [local]
        def kernel(*refs):
            ins, outs = refs[: len(given)], refs[len(given) :]
            forward_kernel(base, *ins, None, None, *outs)
    else:
        given.append(before)
        specs.append(VMEM)
        shapes = [jax.ShapeDtypeStruct((count, 6 * count, BLOCK), jnp.bfloat16), local]
        kernel = partial(forward_kernel, base)
    return pl.pallas_call(
        kernel,
        out_shape=shapes,
        in_specs=specs,
        out_specs=[VMEM] * len(shapes),
        scratch_shapes=[
            pltpu.VMEM((enc, BLOCK), jnp.bfloat16),
            pltpu.VMEM((enc, BLOCK), jnp.bfloat16),
            pltpu.VMEM((rows, 2 * BLOCK), jnp.bfloat16),
        ],
        compiler_params=ROOM,
        cost_estimate=cost(2 * rows * enc * 4 * BLOCK, rows * enc * 2),
        name="forward",
    )(*given)


def merge_stats(parts, stats):
    rows = stats.shape[0] // 2
    logs = [
        parts[i, :rows, :].astype(jnp.float32) + parts[i, rows : 2 * rows, :].astype(jnp.float32)
        for i in range(parts.shape[0])
    ]
    top = logs[0]
    for log in logs[1:]:
        top = jnp.maximum(top, log)
    total = jnp.zeros_like(top)
    mean = jnp.zeros_like(top)
    for i, log in enumerate(logs):
        weight = jnp.exp(log - top)
        total = total + weight
        mean = mean + weight * parts[i, 2 * rows :, :].astype(jnp.float32)
    stats[:rows, :] = top + jnp.log(total)
    stats[rows:, :] = mean / total


def lanes_of(stats, first, second, start):
    spots = [start + 2 * place + h for h in range(2) for place in (first, second)]
    return jnp.concatenate([stats[pl.ds(s, 1), :] for s in spots], axis=1)


def local_kernel(places, member, stats, near_ref, far_ref, *rest):
    pieces = rest[:5]
    sums, near_chance, near_slope, far_chance, far_slope, keys, vals, held, turned = rest[5:]
    p = pl.program_id(0)

    @pl.when(p == 0)
    def _():
        load_keys(near_ref, far_ref, keys, vals)
        load_targets(pieces, held)
        turned[...] = keys[...].T

    enc = keys.shape[0]
    blocks = enc // BLOCK
    half = stats.shape[0] // 2
    rows = pl.ds(pl.multiple_of(p * 2 * BLOCK, 2 * BLOCK), 2 * BLOCK)
    first, second = places[2 * p], places[2 * p + 1]
    log_total = lanes_of(stats, first, second, 0)
    log_total = jnp.where(log_total > -0.5 * BIG, log_total, BIG)
    mean = lanes_of(stats, first, second, half)
    logits = dot_nt(keys[...], split_heads(held[rows, :BLOCK]))
    prob = dot_nt(vals[...], split_heads(held[rows, BLOCK:]))
    for b in range(blocks):
        part = slice(b * BLOCK, (b + 1) * BLOCK)
        chance = jnp.exp(logits[part] - (log_total + away(member, first, second, b, blocks)))
        slope = chance * (prob[part] - mean)
        if b < blocks // 2:
            near_chance[0, part, :] = chance.astype(jnp.bfloat16)
            near_slope[0, part, :] = slope.astype(jnp.bfloat16)
        else:
            part = slice((b - blocks // 2) * BLOCK, (b - blocks // 2 + 1) * BLOCK)
            far_chance[0, part, :] = chance.astype(jnp.bfloat16)
            far_slope[0, part, :] = slope.astype(jnp.bfloat16)
    for i, (near, far) in enumerate(((near_slope, far_slope), (near_chance, far_chance))):
        for h in range(2):
            dims = slice(h * HEAD_DIM, (h + 1) * HEAD_DIM)
            lanes = slice(2 * h * BLOCK, 2 * (h + 1) * BLOCK)
            total = dot_nn(turned[dims, : enc // 2], near[0, :, lanes])
            sums[0, i, dims, :] = total + dot_nn(turned[dims, enc // 2 :], far[0, :, lanes])


def local(places, member, stats, near, far, pieces):
    rows = sum(p.shape[0] for p in pieces)
    enc = near.shape[0] + far.shape[0]
    pairs = rows // (2 * BLOCK)
    table = jax.ShapeDtypeStruct((pairs, enc // 2, 4 * BLOCK), jnp.bfloat16)
    given = [places, member, stats, near, far, *pieces]
    return pl.pallas_call(
        local_kernel,
        grid=(pairs,),
        out_shape=[jax.ShapeDtypeStruct((pairs, 2, BLOCK, 2 * BLOCK), jnp.float32)] + [table] * 4,
        in_specs=[SMEM] * 2 + [VMEM] * (len(given) - 2),
        out_specs=[pl.BlockSpec((1, 2, BLOCK, 2 * BLOCK), lambda p: (p, 0, 0, 0))]
        + [pl.BlockSpec((1, enc // 2, 4 * BLOCK), lambda p: (p, 0, 0))] * 4,
        scratch_shapes=[
            pltpu.VMEM((enc, BLOCK), jnp.bfloat16),
            pltpu.VMEM((enc, BLOCK), jnp.bfloat16),
            pltpu.VMEM((rows, 2 * BLOCK), jnp.bfloat16),
            pltpu.VMEM((BLOCK, enc), jnp.bfloat16),
        ],
        compiler_params=ROOM,
        cost_estimate=cost(3 * rows * enc * 4 * BLOCK, rows * enc * 2),
        name="local",
    )(*given)


def scale_kernel(places, parts, stats, sums, *rest):
    pieces = rest[:5]
    d_query, scaled, held, whole = rest[5:]
    merge_stats(parts, whole)
    load_targets(pieces, held)
    half = stats.shape[0] // 2
    pairs = held.shape[0] // (2 * BLOCK)

    def step(p, carry):
        rows = pl.ds(pl.multiple_of(p * 2 * BLOCK, 2 * BLOCK), 2 * BLOCK)
        first, second = places[2 * p], places[2 * p + 1]
        share = jnp.exp(lanes_of(stats, first, second, 0) - lanes_of(whole, first, second, 0))
        shift = lanes_of(whole, first, second, half) - lanes_of(stats, first, second, half)

        def by_dim(row):
            head = (HEAD_DIM, 2 * BLOCK)
            return jnp.concatenate(
                [jnp.broadcast_to(row[:, h * 2 * BLOCK : (h + 1) * 2 * BLOCK], head) for h in range(2)], axis=0
            )

        share, shift = by_dim(share), by_dim(shift)
        grad = (share * (sums[p, 0] - shift * sums[p, 1])).T.astype(jnp.bfloat16)
        d_query[first] = grad[:BLOCK]
        d_query[second] = grad[BLOCK:]
        share, shift = share.T, shift.T
        query = held[rows, :BLOCK].astype(jnp.float32) * share
        out = held[rows, BLOCK:].astype(jnp.float32) * share
        scaled[rows, :BLOCK] = out.astype(jnp.bfloat16)
        scaled[rows, BLOCK : 2 * BLOCK] = (-shift * query).astype(jnp.bfloat16)
        scaled[rows, 2 * BLOCK :] = query.astype(jnp.bfloat16)
        return carry

    lax.fori_loop(0, pairs, step, 0)


def scale(places, parts, stats, sums, pieces):
    count = places.shape[0]
    rows = sum(p.shape[0] for p in pieces)
    given = [places, parts, stats, sums, *pieces]
    return pl.pallas_call(
        scale_kernel,
        out_shape=[
            jax.ShapeDtypeStruct((count, BLOCK, BLOCK), jnp.bfloat16),
            jax.ShapeDtypeStruct((rows, 3 * BLOCK), jnp.bfloat16),
        ],
        in_specs=[SMEM] + [VMEM] * (len(given) - 1),
        out_specs=[VMEM] * 2,
        scratch_shapes=[
            pltpu.VMEM((rows, 2 * BLOCK), jnp.bfloat16),
            pltpu.VMEM((4 * count, BLOCK), jnp.float32),
        ],
        compiler_params=ROOM,
        cost_estimate=cost(1 << 27, 1 << 16),
        name="scale",
    )(*given)


def gather_kernel(core, scaled, chance, slope, *rest):
    *sent, d_key, d_value = rest
    p = pl.program_id(0)
    rows = pl.ds(pl.multiple_of(p * 2 * BLOCK, 2 * BLOCK), 2 * BLOCK)
    out, lack, query = (split_heads(scaled[rows, i * BLOCK : (i + 1) * BLOCK]) for i in range(3))
    both = dot_nn(chance[0], jnp.concatenate([out, lack], axis=1))
    value, key = both[:, :BLOCK], both[:, BLOCK:] + dot_nn(slope[0], query)

    @pl.when(p == 0)
    def _():
        d_value[...] = value
        d_key[...] = key

    @pl.when(p > 0)
    def _():
        d_value[...] += value
        d_key[...] += key

    @pl.when(p == pl.num_programs(0) - 1)
    def _():
        if len(sent) == 1:
            sent[0][:, :BLOCK] = d_key[...].astype(jnp.bfloat16)
            sent[0][:, BLOCK:] = d_value[...].astype(jnp.bfloat16)
        else:
            half = d_key.shape[0] // 2
            for target, part in zip(sent, (core[0], 1 - core[0]), strict=True):
                at = pl.ds(pl.multiple_of(part * half, half), half)
                target[:, :BLOCK] = d_key[at, :]
                target[:, BLOCK:] = d_value[at, :]


def gather(core, scaled, chance, slope, whole):
    pairs, enc, lanes = chance.shape
    if whole:
        sent = [jax.ShapeDtypeStruct((enc, 2 * BLOCK), jnp.bfloat16)]
    else:
        sent = [jax.ShapeDtypeStruct((enc // 2, 2 * BLOCK), jnp.float32)] * 2
    table = pl.BlockSpec((1, enc, lanes), lambda p: (p, 0, 0))
    return pl.pallas_call(
        gather_kernel,
        grid=(pairs,),
        out_shape=sent,
        in_specs=[SMEM, VMEM, table, table],
        out_specs=[VMEM] * len(sent),
        scratch_shapes=[pltpu.VMEM((enc, BLOCK), jnp.float32)] * 2,
        compiler_params=ROOM,
        cost_estimate=cost(3 * pairs * enc * lanes * BLOCK, 0),
        name="gather",
    )(core, scaled, chance, slope)


def project_kernel(core, chunk, kept, from_half, from_core, kw, vw, far_kw, far_vw, memory):
    rows = kept.shape[0]
    half = from_half[pl.ds(pl.multiple_of(core[0] * rows, rows), rows), :]
    mine = (kept[...] + half.astype(jnp.float32)).astype(jnp.bfloat16)
    other = from_core[...]
    for j in range(memory.shape[0]):
        part = pl.ds(pl.multiple_of(chunk[j] * BLOCK, BLOCK), BLOCK)
        total = dot_nt(mine[:, :BLOCK], kw[part, :]) + dot_nt(mine[:, BLOCK:], vw[part, :])
        total = total + dot_nt(other[:, :BLOCK], far_kw[part, :]) + dot_nt(other[:, BLOCK:], far_vw[part, :])
        memory[j] = total.astype(jnp.bfloat16)


def project(core, chunk, *given):
    return pl.pallas_call(
        project_kernel,
        out_shape=jax.ShapeDtypeStruct((chunk.shape[0], given[0].shape[0], BLOCK), jnp.bfloat16),
        in_specs=[SMEM] * 2 + [VMEM] * len(given),
        out_specs=VMEM,
        compiler_params=ROOM,
        name="project",
    )(core, chunk, *given)


def moved(value, axis, steps):
    count = lax.axis_size(axis)
    return lax.ppermute(value, axis, [(i, (i + steps) % count) for i in range(count)])


def body(queries, keys, values, d_out, key_weight, value_weight, block_lists):
    f32, bf16 = jnp.float32, jnp.bfloat16
    half = lax.axis_index("xh")
    place = lax.axis_index(Z)
    core = lax.axis_index("core")
    depth = lax.axis_size(Z)
    enc_rows = keys.shape[0]
    enc_blocks = enc_rows // BLOCK

    near = jnp.concatenate([queries, d_out], axis=1)
    ahead = moved(near, Z, 4)
    behind = moved(near, Z, -4)
    across = moved(near, Z, 8)
    own = jnp.concatenate([keys, values], axis=1)
    far = moved(own, "xh", 1)

    places = (place + jnp.asarray(SLOTS, jnp.int32)) % depth
    listed = lax.dynamic_slice_in_dim(block_lists, half * depth, depth, 0)
    step = jnp.arange(enc_blocks, dtype=jnp.int32)
    ids = jnp.concatenate(
        [(half * depth + place) * enc_blocks + step, ((1 - half) * depth + place) * enc_blocks + step]
    )
    member = jnp.any(listed[:, :, None] == ids[None, None, :], axis=1).astype(jnp.int32).reshape(-1)

    bundle = jnp.concatenate([behind, near, ahead, across], axis=0)
    above2 = moved(bundle[: 2 * BLOCK], Z, -2)
    below2 = moved(bundle[BLOCK : 3 * BLOCK], Z, 2)
    below = moved(bundle, Z, 1)
    above = moved(bundle, Z, -1)

    (early,) = forward(0, places, member, own, far, [bundle], None)
    pieces = [below, above, above2, below2]
    parts, stats = forward(len(OWN), places, member, own, far, pieces, early)
    pieces = [bundle, *pieces]
    key_weight, value_weight, parts, stats = lax.optimization_barrier((key_weight, value_weight, parts, stats))
    parts = lax.all_to_all(parts, Z, 0, 0, tiled=True)
    far_key_weight = moved(key_weight, "core", 1)
    far_value_weight = moved(value_weight, "core", 1)
    sums, *tables = local(places, member, stats, own, far, pieces)
    parts, sums, tables, far_key_weight, far_value_weight = lax.optimization_barrier(
        (parts, sums, tables, far_key_weight, far_value_weight)
    )

    here = core[None]
    d_query, scaled = scale(places, parts, stats, sums, pieces)
    (to_half,) = gather(here, scaled, tables[2], tables[3], True)
    from_half = moved(to_half, "xh", 1)
    kept, to_core = gather(here, scaled, tables[0], tables[1], False)
    d_query = lax.all_to_all(d_query, Z, 0, 0, tiled=True)
    to_core, from_half = lax.optimization_barrier((to_core, from_half))
    to_core = to_core + lax.dynamic_slice_in_dim(from_half, (1 - core) * (enc_rows // 2), enc_rows // 2, 0).astype(f32)
    from_core = moved(to_core.astype(bf16), "core", 1)

    cores = lax.axis_size("core")
    chunk = jnp.arange(key_weight.shape[0] // BLOCK, dtype=jnp.int32)
    weights = (key_weight, value_weight, far_key_weight, far_value_weight)
    memory = project(here, chunk, kept, from_half, from_core, *weights)
    memory, d_query = lax.optimization_barrier((memory, d_query))
    memory = lax.all_to_all(memory, HEAD, 0, 0, tiled=True)
    memory = memory.reshape(-1, cores, *memory.shape[1:]).astype(f32)
    d_memory = jnp.sum(memory, axis=0).reshape(keys.shape).astype(bf16)
    d_queries = jnp.sum(d_query.astype(f32), axis=0).astype(bf16)
    return d_queries, d_memory


def solution(mesh):
    fine = Mesh(mesh.devices.reshape(SIZES), AXES)
    placed = P(CTX, HEAD)
    return jax.shard_map(
        body,
        mesh=fine,
        in_specs=(placed, placed, placed, placed, P(None, HEAD), P(None, HEAD), P()),
        out_specs=(placed, placed),
        check_vma=False,
    )
```

time: 165 us -> 169 us (1.024)
  local copies, waits for them, and re-layouts: 6.29 us -> 21.2 us
  Pallas kernels: 26.6 us -> 40.6 us
  starting transfers between devices: 92.7 us -> 79.3 us
  waiting for transfers between devices: 30.6 us -> 22.5 us
  other arithmetic: 7.14 us -> 2.76 us
    ppermute x16 -> x12, starting transfers between devices: 78 us -> 56.2 us  [moved(): lax.ppermute(value, axis, [(i, (i + steps) % count) for i in range(count)])]
    all_to_all x0 -> x1, waiting for transfers between devices: none -> 15.1 us  [body(): memory = lax.all_to_all(memory, HEAD, 0, 0, tiled=True)]
    unnamed x22 -> x62, local copies, waits for them, and re-layouts: 4.29 us -> 19.4 us
    pallas_call x4 -> x6, Pallas kernels: 23.2 us -> 37.3 us  [the longest x2 14.4 us: gather(): pl.pallas_call(gather_kernel, grid=(pairs,), out_shape=sent, in_specs=[SM...]
    ppermute x16 -> x12, waiting for transfers between devices: 19.8 us -> 7.36 us  [moved(): lax.ppermute(value, axis, [(i, (i + steps) % count) for i in range(count)])]
    all_to_all x1, waiting for transfers between devices: 10.8 us -> 0.01 us  [body(): parts = lax.all_to_all(parts, Z, 0, 0, tiled=True)]
    all_to_all x1, starting transfers between devices: 6.21 us -> 11.7 us  [body(): d_query = lax.all_to_all(d_query, Z, 0, 0, tiled=True)]
    all_to_all x0 -> x1, starting transfers between devices: none -> 5.19 us  [body(): memory = lax.all_to_all(memory, HEAD, 0, 0, tiled=True)]
  transfers between devices with their start and end apart: 18 -> 15, of which waited for: 8 -> 4; matrix products, arithmetic and copies ran while one was open for 5% -> 2% of each run, Pallas kernels for 8% -> 19%
where the time goes in v4:
time: 169 us; the launch traced here: 167 us
  starting transfers between devices  79.3 us (47%)
  Pallas kernels  40.6 us (24%)
  waiting for transfers between devices  22.5 us (13%)
  local copies, waits for them, and re-layouts  21.2 us (13%)
  other arithmetic  2.76 us (2%)
    ppermute x12, starting transfers between devices, moved(): lax.ppermute(value, axis, [(i, (i + steps) % count) for i in range(count)])  56.2 us
    unnamed x62, local copies, waits for them, and re-layouts  19.4 us
    all_to_all x1, waiting for transfers between devices, body(): memory = lax.all_to_all(memory, HEAD, 0, 0, tiled=True)  15.1 us
    pallas_call x2, Pallas kernels, gather(): pl.pallas_call(gather_kernel, grid=(pairs,), out_shape=sent, in_specs=[SM...  14.4 us
    all_to_all x1, starting transfers between devices, body(): d_query = lax.all_to_all(d_query, Z, 0, 0, tiled=True)  11.7 us
    pallas_call x1, Pallas kernels, local(): pl.pallas_call(local_kernel, grid=(pairs,), out_shape=[jax.ShapeDtypeStru...  11 us
    pallas_call x2, Pallas kernels, forward(): pl.pallas_call(kernel, out_shape=shapes, in_specs=specs, out_specs=[VMEM]...  8.97 us
    ppermute x12, waiting for transfers between devices, moved(): lax.ppermute(value, axis, [(i, (i + steps) % count) for i in range(count)])  7.36 us
  transfers between devices with their start and end apart: 15, of which 4 were waited for; matrix products, arithmetic and copies ran while one was open for 2% of the time, Pallas kernels for 19%

profile of v4, /device:TPU:1, one launch (start us, length us, event | category | flops | bytes accessed | tf_op | source)
XLA Modules:
  0.0 167.4 jit_solution(1424038442868902742)
XLA Ops:
  0.6 0.0 copy-start
  0.6 0.8 constant_dynamic-update-slice_fusion.3
  1.4 0.8 constant_dynamic-update-slice_fusion.2
  2.2 13.3 %collective-permute-start.1 = (bf16[128,256]{1,0:T(8,128)(2,1)S(1)}, bf16[128,256]{1,0:T(8,128)(2,1)S(1)}, u32[]{:S(2)}, u32[]{:S(2)}) collective-permute-start(bf16[128,256]{1,0:T(8,128)(2,1)S(1)} %constant_dynamic-update-slice_fusion.2), channel_id=1, source_target_pairs={{0,192},{16,208},{32,224},{48,240},{64,0},{80,16},{96,32},{112,48}... | collective-permute-start | bytes 196616 | tf_op jit(solution)/shard_map/ppermute | solution.py:374
  15.5 1.9 %collective-permute-start.2 = (bf16[128,256]{1,0:T(8,128)(2,1)S(1)}, bf16[128,256]{1,0:T(8,128)(2,1)S(1)}, u32[]{:S(2)}, u32[]{:S(2)}) collective-permute-start(bf16[128,256]{1,0:T(8,128)(2,1)S(1)} %constant_dynamic-update-slice_fusion.2), channel_id=1, source_target_pairs={{0,64},{16,80},{32,96},{48,112},{64,128},{80,144},{96,160},{112,17... | collective-permute-start | bytes 196616 | tf_op jit(solution)/shard_map/ppermute | solution.py:374
  17.4 10.3 %collective-permute-start.3 = (bf16[128,256]{1,0:T(8,128)(2,1)S(1)}, bf16[128,256]{1,0:T(8,128)(2,1)S(1)}, u32[]{:S(2)}, u32[]{:S(2)}) collective-permute-start(bf16[128,256]{1,0:T(8,128)(2,1)S(1)} %constant_dynamic-update-slice_fusion.2), channel_id=1, source_target_pairs={{0,128},{16,144},{32,160},{48,176},{64,192},{80,208},{96,224},{112... | collective-permute-start | bytes 196616 | tf_op jit(solution)/shard_map/ppermute | solution.py:374
  27.7 0.9 constant_dynamic-update-slice_fusion.1
  28.6 0.9 constant_dynamic-update-slice_fusion.refs_2_.near_ref
  29.5 4.7 %collective-permute-start = (bf16[512,256]{1,0:T(8,128)(2,1)S(1)}, bf16[512,256]{1,0:T(8,128)(2,1)S(1)}, u32[]{:S(2)}, u32[]{:S(2)}) collective-permute-start(bf16[512,256]{1,0:T(8,128)(2,1)S(1)} %constant_dynamic-update-slice_fusion.refs_2_.near_ref), channel_id=1, source_target_pairs={{0,256},{256,0},{1,257},{257,1},{2,258},{258,2},{3,259},{259,3},{4... | collective-permute-start | bytes 786440 | tf_op jit(solution)/shard_map/ppermute | solution.py:374
  34.2 0.7 and_select_fusion.refs_0_.places
  34.9 0.1 pad_add_fusion
  35.0 0.4 compare_reduce_fusion
  35.4 0.1 reshape.15.refs_1_.member
  35.5 0.0 collective-permute-done.1
  35.5 0.0 collective-permute-done.2
  35.5 0.0 collective-permute-done.3
  35.6 2.6 %collective-permute-start.4 = (bf16[512,256]{1,0:T(8,128)(2,1)S(1)}, bf16[512,256]{1,0:T(8,128)(2,1)S(1)}, u32[]{:S(2)}, u32[]{:S(2)}) collective-permute-start(bf16[512,256]{1,0:T(8,128)(2,1)S(1)} %pad_maximum_fusion.refs_4_.rest_0_), channel_id=1, source_target_pairs={{0,16},{16,32},{32,48},{48,64},{64,80},{80,96},{96,112},{112,128},... | collective-permute-start | bytes 786440 | tf_op jit(solution)/shard_map/ppermute | solution.py:374
  38.2 4.9 %collective-permute-start.5 = (bf16[512,256]{1,0:T(8,128)(2,1)S(1)}, bf16[512,256]{1,0:T(8,128)(2,1)S(1)}, u32[]{:S(2)}, u32[]{:S(2)}) collective-permute-start(bf16[512,256]{1,0:T(8,128)(2,1)S(1)} %pad_maximum_fusion.refs_4_.rest_0_), channel_id=1, source_target_pairs={{0,240},{16,0},{32,16},{48,32},{64,48},{80,64},{96,80},{112,96},{1... | collective-permute-start | bytes 786440 | tf_op jit(solution)/shard_map/ppermute | solution.py:374
  43.2 3.1 %collective-permute-start.6 = (bf16[256,256]{1,0:T(8,128)(2,1)S(1)}, bf16[256,256]{1,0:T(8,128)(2,1)S(1)}, u32[]{:S(2)}, u32[]{:S(2)}) collective-permute-start(bf16[256,256]{1,0:T(8,128)(2,1)S(1)} %get-tuple-element.57), channel_id=1, source_target_pairs={{0,224},{16,240},{32,0},{48,16},{64,32},{80,48},{96,64},{112,80},{... | collective-permute-start | bytes 393224 | tf_op jit(solution)/shard_map/ppermute | solution.py:374
  46.3 3.1 %collective-permute-start.7 = (bf16[256,256]{1,0:T(8,128)(2,1)S(1)}, bf16[256,256]{1,0:T(8,128)(2,1)S(1)}, u32[]{:S(2)}, u32[]{:S(2)}) collective-permute-start(bf16[256,256]{1,0:T(8,128)(2,1)S(1)} %get-tuple-element.56), channel_id=1, source_target_pairs={{0,32},{16,48},{32,64},{48,80},{64,96},{80,112},{96,128},{112,144}... | collective-permute-start | bytes 393224 | tf_op jit(solution)/shard_map/ppermute | solution.py:374
  49.4 0.0 collective-permute-done.refs_3_.far_ref
  49.4 2.3 %forward.2.rest_4_ = f32[64,128]{1,0:T(8,128)S(1)} custom-call(s32[16]{0:T(128)S(1)} %and_select_fusion.refs_0_.places, s32[128]{0:T(128)S(1)} %reshape.15.refs_1_.member, bf16[512,256]{1,0:T(8,128)(2,1)S(1)} %constant_dynamic-update-slice_fusion.refs_2_.near_ref, bf16[512,256]{1,0:T(8,128)(2,1)S(1)} %collective-permute-done.refs_3_.far_ref, ...), custom_call_target="tpu_custom_call" | custom-call | flops 2147483648 | bytes 1048576 | tf_op jit(solution)/shard_map/forward/pallas_call | solution.py:136
  51.7 0.0 copy-start.1
  51.7 1.5 collective-permute-done.6.rest_2_.rest_3_
  53.2 4.9 %collective-permute-done.7.rest_3_.rest_4_ = bf16[256,256]{1,0:T(8,128)(2,1)S(1)} collective-permute-done((bf16[256,256]{1,0:T(8,128)(2,1)S(1)}, bf16[256,256]{1,0:T(8,128)(2,1)S(1)}, u32[]{:S(2)}, u32[]{:S(2)}) %collective-permute-start.7) | collective-permute-done | bytes 131104 | tf_op jit(solution)/shard_map/ppermute | solution.py:374
  58.1 0.0 collective-permute-done.5.rest_1_.rest_2_
  58.2 6.7 %forward.3 = (bf16[16,96,128]{2,1,0:T(8,128)(2,1)}, f32[64,128]{1,0:T(8,128)S(1)}) custom-call(s32[16]{0:T(128)S(1)} %and_select_fusion.refs_0_.places, s32[128]{0:T(128)S(1)} %reshape.15.refs_1_.member, bf16[512,256]{1,0:T(8,128)(2,1)S(1)} %constant_dynamic-update-slice_fusion.refs_2_.near_ref, bf16[512,256]{1,0:T(8,128)(2,1)S(1)} %collective-permute-done.refs_3_.far_ref, ...), custom_call_target="tpu_custom_call" | custom-call | flops 6442450944 | bytes 1048576 | tf_op jit(solution)/shard_map/forward/pallas_call | solution.py:136
  64.8 0.0 copy-start.17
  64.9 0.6 copy-done.17
  65.5 6.1 %all-to-all-start = ((bf16[16,96,128]{2,1,0:T(8,128)(2,1)}), bf16[16,96,128]{2,1,0:T(8,128)(2,1)S(1)}, u32[]{:S(2)}, u32[]{:S(2)}) async-start(bf16[16,96,128]{2,1,0:T(8,128)(2,1)} %get-tuple-element.31), calls=%async_computation | async-start | bytes 786432 | tf_op jit(solution)/shard_map/all_to_all | solution.py:412
  71.6 3.0 %collective-permute-start.8 = (bf16[2048,128]{1,0:T(8,128)(2,1)S(1)}, bf16[2048,128]{1,0:T(8,128)(2,1)S(1)}, u32[]{:S(2)}, u32[]{:S(2)}) collective-permute-start(bf16[2048,128]{1,0:T(8,128)(2,1)S(1)} %copy-done.1), channel_id=1, source_target_pairs={{0,1},{1,0},{2,3},{3,2},{4,5},{5,4},{6,7},{7,6},{8,9},{9,8},{10,11... | collective-permute-start | bytes 1572872 | tf_op jit(solution)/shard_map/ppermute | solution.py:374
  74.6 1.9 %collective-permute-start.9 = (bf16[2048,128]{1,0:T(8,128)(2,1)}, bf16[2048,128]{1,0:T(8,128)(2,1)S(1)}, u32[]{:S(2)}, u32[]{:S(2)}) collective-permute-start(bf16[2048,128]{1,0:T(8,128)(2,1)} %vw), channel_id=1, source_target_pairs={{0,1},{1,0},{2,3},{3,2},{4,5},{5,4},{6,7},{7,6},{8,9},{9,8},{10,11... | collective-permute-start | bytes 1572872 | tf_op jit(solution)/shard_map/ppermute | solution.py:374
  76.5 0.9 copy-done.7
  77.5 0.9 copy-done.10
  78.4 0.9 copy-done.13
  79.3 0.9 copy-done.16
  80.2 0.8 copy-done.18
  81.0 0.6 copy-done.21
  81.6 0.6 copy-done.23
  82.2 0.9 copy-done.28
  83.1 11.0 %local.1 = (f32[8,2,128,256]{3,2,1,0:T(8,128)S(1)}, bf16[8,512,512]{2,1,0:T(8,128)(2,1)}, bf16[8,512,512]{2,1,0:T(8,128)(2,1)}, bf16[8,512,512]{2,1,0:T(8,128)(2,1)}, bf16[8,512,512]{2,1,0:T(8,128)(2,1)}) custom-call(s32[16]{0:T(128)S(1)} %copy-done.23, s32[128]{0:T(128)S(1)} %copy-done.21, f32[64,128]{1,0:T(8,128)S(1)} %copy-done.18, ...), custom_call_target="tpu_custom_call" | custom-call | flops 12884901888 | bytes 1048576 | tf_op jit(solution)/shard_map/local/pallas_call | solution.py:222
  94.1 0.0 collective-permute-done.8.far_kw
  94.1 0.8 copy-done.2
  94.9 0.8 copy-done.4
  95.7 0.9 copy-done.8
  96.7 0.9 copy-done.11
  97.6 0.9 copy-done.14
  98.5 0.8 copy-done.19
  99.3 0.6 copy-done.24
  99.8 2.9 %scale.1 = (bf16[16,128,128]{2,1,0:T(8,128)(2,1)}, bf16[2048,384]{1,0:T(8,128)(2,1)S(1)}) custom-call(s32[16]{0:T(128)S(1)} %copy-done.24, bf16[16,96,128]{2,1,0:T(8,128)(2,1)S(1)} %all-to-all-done.parts, f32[64,128]{1,0:T(8,128)S(1)} %copy-done.19, f32[8,2,128,256]{3,2,1,0:T(8,128)S(1)} %get-tuple-element.41.sums, ...), custom_call_target="tpu_custom_call" | custom-call | flops 536870912 | bytes 1048576 | tf_op jit(solution)/shard_map/scale/pallas_call | solution.py:280
  102.8 1.2 copy-done.25
  103.9 11.7 %all-to-all-start.1 = ((bf16[16,128,128]{2,1,0:T(8,128)(2,1)}), bf16[16,128,128]{2,1,0:T(8,128)(2,1)S(1)}, u32[]{:S(2)}, u32[]{:S(2)}) async-start(bf16[16,128,128]{2,1,0:T(8,128)(2,1)} %get-tuple-element.53), calls=%async_computation.1 | async-start | bytes 1048576 | tf_op jit(solution)/shard_map/all_to_all | solution.py:425
  115.7 1.4 copy-done.26
  117.1 2.2 %copy-done.29 = bf16[8,512,512]{2,1,0:T(8,128)(2,1)S(1)} copy-done((bf16[8,512,512]{2,1,0:T(8,128)(2,1)S(1)}, bf16[8,512,512]{2,1,0:T(8,128)(2,1)}, u32[]{:S(2)}) %copy-start.29) | copy-done | bytes 4194328
  119.3 6.8 %gather.3 = bf16[512,256]{1,0:T(8,128)(2,1)S(1)} custom-call(s32[1]{0:T(128)} %bitcast.core, bf16[2048,384]{1,0:T(8,128)(2,1)S(1)} %copy-done.26, bf16[8,512,512]{2,1,0:T(8,128)(2,1)S(1)} %copy-done.29, bf16[8,512,512]{2,1,0:T(8,128)(2,1)} %get-tuple-element.48.slope), custom_call_target="tpu_custom_call" | custom-call | flops 3221225472 | bytes 1048576 | tf_op jit(solution)/shard_map/gather/pallas_call | solution.py:336
  126.1 4.5 %collective-permute-start.10 = (bf16[512,256]{1,0:T(8,128)(2,1)S(1)}, bf16[512,256]{1,0:T(8,128)(2,1)S(1)}, u32[]{:S(2)}, u32[]{:S(2)}) collective-permute-start(bf16[512,256]{1,0:T(8,128)(2,1)S(1)} %gather.3), channel_id=1, source_target_pairs={{0,256},{256,0},{1,257},{257,1},{2,258},{258,2},{3,259},{259,3},{4... | collective-permute-start | bytes 786440 | tf_op jit(solution)/shard_map/ppermute | solution.py:374
  130.6 7.6 %gather.2 = (f32[256,256]{1,0:T(8,128)S(1)}, f32[256,256]{1,0:T(8,128)S(1)}) custom-call(s32[1]{0:T(128)} %bitcast.core, bf16[2048,384]{1,0:T(8,128)(2,1)S(1)} %copy-done.26, bf16[8,512,512]{2,1,0:T(8,128)(2,1)} %get-tuple-element.43.chance, bf16[8,512,512]{2,1,0:T(8,128)(2,1)} %get-tuple-element.44.slope), custom_call_target="tpu_custom_call" | custom-call | flops 3221225472 | bytes 1048576 | tf_op jit(solution)/shard_map/gather/pallas_call | solution.py:336
  138.3 3.0 %collective-permute-start.11 = (bf16[256,256]{1,0:T(8,128)(2,1)S(1)}, bf16[256,256]{1,0:T(8,128)(2,1)S(1)}, u32[]{:S(2)}, u32[]{:S(2)}) collective-permute-start(bf16[256,256]{1,0:T(8,128)(2,1)S(1)} %add_convert_fusion), channel_id=1, source_target_pairs={{0,1},{1,0},{2,3},{3,2},{4,5},{5,4},{6,7},{7,6},{8,9},{9,8},{10,11... | collective-permute-start | bytes 393224 | tf_op jit(solution)/shard_map/ppermute | solution.py:374
  141.3 1.0 collective-permute-done.11.from_core
  142.2 3.3 %project.1 = bf16[16,256,128]{2,1,0:T(8,128)(2,1)} custom-call(s32[1]{0:T(128)} %bitcast.core, s32[16]{0:T(128)S(1)} %iota.8.chunk, f32[256,256]{1,0:T(8,128)S(1)} %get-tuple-element.45.kept, bf16[512,256]{1,0:T(8,128)(2,1)S(1)} %collective-permute-done.10.from_half, bf16[256,256]{1,0:T(8,128)(2,1)S(1)} %collective-permute-done.11.from_core, ...), custom_call_target="tpu_custom_call" | custom-call | tf_op jit(solution)/shard_map/project/pallas_call | solution.py:362
  145.6 5.2 %all-to-all-start.2 = ((bf16[16,256,128]{2,1,0:T(8,128)(2,1)}), bf16[16,256,128]{2,1,0:T(8,128)(2,1)S(1)}, u32[]{:S(2)}, u32[]{:S(2)}) async-start(bf16[16,256,128]{2,1,0:T(8,128)(2,1)} %project.1), calls=%async_computation.2 | async-start | bytes 2097152 | tf_op jit(solution)/shard_map/all_to_all | solution.py:435
  150.8 0.7 reduce_sum.21
  151.5 15.1 %all-to-all-done.2 = bf16[16,256,128]{2,1,0:T(8,128)(2,1)S(1)} async-done(((bf16[16,256,128]{2,1,0:T(8,128)(2,1)}), bf16[16,256,128]{2,1,0:T(8,128)(2,1)S(1)}, u32[]{:S(2)}, u32[]{:S(2)}) %all-to-all-start.2) | async-done | bytes 1048608 | tf_op jit(solution)/shard_map/all_to_all | solution.py:435
  166.6 0.8 reduce.1
  (50 shorter events, 0.2 us)
Async XLA Ops:
  0.6 34.4 %copy-start = (s32[32,64]{1,0:T(8,128)S(1)}, s32[32,64]{1,0:T(8,128)}, u32[]{:S(2)}) copy-start(s32[32,64]{1,0:T(8,128)} %param.14) | copy-start | bytes 24580
  2.2 33.3 %collective-permute-start.1 = (bf16[128,256]{1,0:T(8,128)(2,1)S(1)}, bf16[128,256]{1,0:T(8,128)(2,1)S(1)}, u32[]{:S(2)}, u32[]{:S(2)}) collective-permute-start(bf16[128,256]{1,0:T(8,128)(2,1)S(1)} %constant_dynamic-update-slice_fusion.2), channel_id=1, source_target_pairs={{0,192},{16,208},{32,224},{48,240},{64,0},{80,16},{96,32},{112,48}... | collective-permute-start | bytes 196616 | tf_op jit(solution)/shard_map/ppermute | solution.py:374
  15.5 20.1 %collective-permute-start.2 = (bf16[128,256]{1,0:T(8,128)(2,1)S(1)}, bf16[128,256]{1,0:T(8,128)(2,1)S(1)}, u32[]{:S(2)}, u32[]{:S(2)}) collective-permute-start(bf16[128,256]{1,0:T(8,128)(2,1)S(1)} %constant_dynamic-update-slice_fusion.2), channel_id=1, source_target_pairs={{0,64},{16,80},{32,96},{48,112},{64,128},{80,144},{96,160},{112,17... | collective-permute-start | bytes 196616 | tf_op jit(solution)/shard_map/ppermute | solution.py:374
  17.4 18.1 %collective-permute-start.3 = (bf16[128,256]{1,0:T(8,128)(2,1)S(1)}, bf16[128,256]{1,0:T(8,128)(2,1)S(1)}, u32[]{:S(2)}, u32[]{:S(2)}) collective-permute-start(bf16[128,256]{1,0:T(8,128)(2,1)S(1)} %constant_dynamic-update-slice_fusion.2), channel_id=1, source_target_pairs={{0,128},{16,144},{32,160},{48,176},{64,192},{80,208},{96,224},{112... | collective-permute-start | bytes 196616 | tf_op jit(solution)/shard_map/ppermute | solution.py:374
  29.5 28.6 %copy-start.15 = (bf16[512,256]{1,0:T(8,128)(2,1)}, bf16[512,256]{1,0:T(8,128)(2,1)S(1)}, u32[]{:S(2)}) copy-start(bf16[512,256]{1,0:T(8,128)(2,1)S(1)} %constant_dynamic-update-slice_fusion.refs_2_.near_ref) | copy-start | bytes 786436
  29.5 19.8 %collective-permute-start = (bf16[512,256]{1,0:T(8,128)(2,1)S(1)}, bf16[512,256]{1,0:T(8,128)(2,1)S(1)}, u32[]{:S(2)}, u32[]{:S(2)}) collective-permute-start(bf16[512,256]{1,0:T(8,128)(2,1)S(1)} %constant_dynamic-update-slice_fusion.refs_2_.near_ref), channel_id=1, source_target_pairs={{0,256},{256,0},{1,257},{257,1},{2,258},{258,2},{3,259},{259,3},{4... | collective-permute-start | bytes 786440 | tf_op jit(solution)/shard_map/ppermute | solution.py:374
  34.9 23.2 %copy-start.22 = (s32[16]{0:T(128)}, s32[16]{0:T(128)S(1)}, u32[]{:S(2)}) copy-start(s32[16]{0:T(128)S(1)} %and_select_fusion.refs_0_.places) | copy-start | bytes 196
  35.5 22.6 %copy-start.20 = (s32[128]{0:T(128)}, s32[128]{0:T(128)S(1)}, u32[]{:S(2)}) copy-start(s32[128]{0:T(128)S(1)} %reshape.15.refs_1_.member) | copy-start | bytes 1540
  35.6 22.5 %collective-permute-start.4 = (bf16[512,256]{1,0:T(8,128)(2,1)S(1)}, bf16[512,256]{1,0:T(8,128)(2,1)S(1)}, u32[]{:S(2)}, u32[]{:S(2)}) collective-permute-start(bf16[512,256]{1,0:T(8,128)(2,1)S(1)} %pad_maximum_fusion.refs_4_.rest_0_), channel_id=1, source_target_pairs={{0,16},{16,32},{32,48},{48,64},{64,80},{80,96},{96,112},{112,128},... | collective-permute-start | bytes 786440 | tf_op jit(solution)/shard_map/ppermute | solution.py:374
  38.2 19.9 %collective-permute-start.5 = (bf16[512,256]{1,0:T(8,128)(2,1)S(1)}, bf16[512,256]{1,0:T(8,128)(2,1)S(1)}, u32[]{:S(2)}, u32[]{:S(2)}) collective-permute-start(bf16[512,256]{1,0:T(8,128)(2,1)S(1)} %pad_maximum_fusion.refs_4_.rest_0_), channel_id=1, source_target_pairs={{0,240},{16,0},{32,16},{48,32},{64,48},{80,64},{96,80},{112,96},{1... | collective-permute-start | bytes 786440 | tf_op jit(solution)/shard_map/ppermute | solution.py:374
  43.2 10.0 %collective-permute-start.6 = (bf16[256,256]{1,0:T(8,128)(2,1)S(1)}, bf16[256,256]{1,0:T(8,128)(2,1)S(1)}, u32[]{:S(2)}, u32[]{:S(2)}) collective-permute-start(bf16[256,256]{1,0:T(8,128)(2,1)S(1)} %get-tuple-element.57), channel_id=1, source_target_pairs={{0,224},{16,240},{32,0},{48,16},{64,32},{80,48},{96,64},{112,80},{... | collective-permute-start | bytes 393224 | tf_op jit(solution)/shard_map/ppermute | solution.py:374
  46.3 11.8 %collective-permute-start.7 = (bf16[256,256]{1,0:T(8,128)(2,1)S(1)}, bf16[256,256]{1,0:T(8,128)(2,1)S(1)}, u32[]{:S(2)}, u32[]{:S(2)}) collective-permute-start(bf16[256,256]{1,0:T(8,128)(2,1)S(1)} %get-tuple-element.56), channel_id=1, source_target_pairs={{0,32},{16,48},{32,64},{48,80},{64,96},{80,112},{96,128},{112,144}... | collective-permute-start | bytes 393224 | tf_op jit(solution)/shard_map/ppermute | solution.py:374
  49.4 15.4 %copy-start.27 = (bf16[512,256]{1,0:T(8,128)(2,1)}, bf16[512,256]{1,0:T(8,128)(2,1)S(1)}, u32[]{:S(2)}) copy-start(bf16[512,256]{1,0:T(8,128)(2,1)S(1)} %collective-permute-done.refs_3_.far_ref) | copy-start | bytes 786436
  51.7 19.9 %copy-start.1 = (bf16[2048,128]{1,0:T(8,128)(2,1)S(1)}, bf16[2048,128]{1,0:T(8,128)(2,1)}, u32[]{:S(2)}) copy-start(bf16[2048,128]{1,0:T(8,128)(2,1)} %kw) | copy-start | bytes 1572868
  53.2 11.6 %copy-start.9 = (bf16[256,256]{1,0:T(8,128)(2,1)}, bf16[256,256]{1,0:T(8,128)(2,1)S(1)}, u32[]{:S(2)}) copy-start(bf16[256,256]{1,0:T(8,128)(2,1)S(1)} %collective-permute-done.6.rest_2_.rest_3_) | copy-start | bytes 393220
  58.1 6.7 %copy-start.12 = (bf16[256,256]{1,0:T(8,128)(2,1)}, bf16[256,256]{1,0:T(8,128)(2,1)S(1)}, u32[]{:S(2)}) copy-start(bf16[256,256]{1,0:T(8,128)(2,1)S(1)} %collective-permute-done.7.rest_3_.rest_4_) | copy-start | bytes 393220
  58.1 6.7 %copy-start.6 = (bf16[512,256]{1,0:T(8,128)(2,1)}, bf16[512,256]{1,0:T(8,128)(2,1)S(1)}, u32[]{:S(2)}) copy-start(bf16[512,256]{1,0:T(8,128)(2,1)S(1)} %collective-permute-done.5.rest_1_.rest_2_) | copy-start | bytes 786436
  64.8 0.6 copy-start.17
  65.5 30.3 %all-to-all-start = ((bf16[16,96,128]{2,1,0:T(8,128)(2,1)}), bf16[16,96,128]{2,1,0:T(8,128)(2,1)S(1)}, u32[]{:S(2)}, u32[]{:S(2)}) async-start(bf16[16,96,128]{2,1,0:T(8,128)(2,1)} %get-tuple-element.31), calls=%async_computation | async-start | bytes 786432 | tf_op jit(solution)/shard_map/all_to_all | solution.py:412
  71.6 22.5 %collective-permute-start.8 = (bf16[2048,128]{1,0:T(8,128)(2,1)S(1)}, bf16[2048,128]{1,0:T(8,128)(2,1)S(1)}, u32[]{:S(2)}, u32[]{:S(2)}) collective-permute-start(bf16[2048,128]{1,0:T(8,128)(2,1)S(1)} %copy-done.1), channel_id=1, source_target_pairs={{0,1},{1,0},{2,3},{3,2},{4,5},{5,4},{6,7},{7,6},{8,9},{9,8},{10,11... | collective-permute-start | bytes 1572872 | tf_op jit(solution)/shard_map/ppermute | solution.py:374
  74.6 20.3 %collective-permute-start.9 = (bf16[2048,128]{1,0:T(8,128)(2,1)}, bf16[2048,128]{1,0:T(8,128)(2,1)S(1)}, u32[]{:S(2)}, u32[]{:S(2)}) collective-permute-start(bf16[2048,128]{1,0:T(8,128)(2,1)} %vw), channel_id=1, source_target_pairs={{0,1},{1,0},{2,3},{3,2},{4,5},{5,4},{6,7},{7,6},{8,9},{9,8},{10,11... | collective-permute-start | bytes 1572872 | tf_op jit(solution)/shard_map/ppermute | solution.py:374
  76.5 1.0 copy-start.7
  77.5 0.9 copy-start.10
  78.4 0.9 copy-start.13
  79.3 0.9 copy-start.16
  80.2 0.8 copy-start.18
  81.0 0.6 copy-start.21
  81.6 0.6 copy-start.23
  82.2 0.9 copy-start.28
  94.1 0.8 copy-start.2
  94.9 0.8 copy-start.4
  95.7 1.0 copy-start.8
  96.7 0.9 copy-start.11
  97.6 0.9 copy-start.14
  98.5 0.8 copy-start.19
  99.3 0.6 copy-start.24
  102.8 1.2 copy-start.25
  103.9 41.6 %all-to-all-start.1 = ((bf16[16,128,128]{2,1,0:T(8,128)(2,1)}), bf16[16,128,128]{2,1,0:T(8,128)(2,1)S(1)}, u32[]{:S(2)}, u32[]{:S(2)}) async-start(bf16[16,128,128]{2,1,0:T(8,128)(2,1)} %get-tuple-element.53), calls=%async_computation.1 | async-start | bytes 1048576 | tf_op jit(solution)/shard_map/all_to_all | solution.py:425
  115.7 1.4 copy-start.26
  117.1 2.2 %copy-start.29 = (bf16[8,512,512]{2,1,0:T(8,128)(2,1)S(1)}, bf16[8,512,512]{2,1,0:T(8,128)(2,1)}, u32[]{:S(2)}) copy-start(bf16[8,512,512]{2,1,0:T(8,128)(2,1)} %get-tuple-element.47.chance) | copy-start | bytes 12582916
  126.1 16.1 %copy-start.3 = (bf16[2048,128]{1,0:T(8,128)(2,1)S(1)}, bf16[2048,128]{1,0:T(8,128)(2,1)}, u32[]{:S(2)}) copy-start(bf16[2048,128]{1,0:T(8,128)(2,1)} %copy-done.2) | copy-start | bytes 1572868
  126.1 16.1 %copy-start.5 = (bf16[2048,128]{1,0:T(8,128)(2,1)S(1)}, bf16[2048,128]{1,0:T(8,128)(2,1)}, u32[]{:S(2)}) copy-start(bf16[2048,128]{1,0:T(8,128)(2,1)} %copy-done.4) | copy-start | bytes 1572868
  126.1 12.1 %collective-permute-start.10 = (bf16[512,256]{1,0:T(8,128)(2,1)S(1)}, bf16[512,256]{1,0:T(8,128)(2,1)S(1)}, u32[]{:S(2)}, u32[]{:S(2)}) collective-permute-start(bf16[512,256]{1,0:T(8,128)(2,1)S(1)} %gather.3), channel_id=1, source_target_pairs={{0,256},{256,0},{1,257},{257,1},{2,258},{258,2},{3,259},{259,3},{4... | collective-permute-start | bytes 786440 | tf_op jit(solution)/shard_map/ppermute | solution.py:374
  138.3 3.9 %collective-permute-start.11 = (bf16[256,256]{1,0:T(8,128)(2,1)S(1)}, bf16[256,256]{1,0:T(8,128)(2,1)S(1)}, u32[]{:S(2)}, u32[]{:S(2)}) collective-permute-start(bf16[256,256]{1,0:T(8,128)(2,1)S(1)} %add_convert_fusion), channel_id=1, source_target_pairs={{0,1},{1,0},{2,3},{3,2},{4,5},{5,4},{6,7},{7,6},{8,9},{9,8},{10,11... | collective-permute-start | bytes 393224 | tf_op jit(solution)/shard_map/ppermute | solution.py:374
  145.6 21.0 %all-to-all-start.2 = ((bf16[16,256,128]{2,1,0:T(8,128)(2,1)}), bf16[16,256,128]{2,1,0:T(8,128)(2,1)S(1)}, u32[]{:S(2)}, u32[]{:S(2)}) async-start(bf16[16,256,128]{2,1,0:T(8,128)(2,1)} %project.1), calls=%async_computation.2 | async-start | bytes 2097152 | tf_op jit(solution)/shard_map/all_to_all | solution.py:435

commit v5 on v4

--- a/solution.py
+++ b/solution.py
@@ -21,8 +21,8 @@
 SLOTS = OWN + LATER
 
 VMEM = pl.BlockSpec(memory_space=pltpu.VMEM)
+ANY = pl.BlockSpec(memory_space=pl.ANY)
 SMEM = pl.BlockSpec(memory_space=pltpu.SMEM)
-ROOM = pltpu.CompilerParams(vmem_limit_bytes=48 * 1024 * 1024)
 
 
 def cost(flops, exps):
@@ -41,6 +41,47 @@
     low = lax.broadcasted_iota(jnp.int32, rows.shape, 1) < HEAD_DIM
     zero = jnp.zeros_like(rows)
     return jnp.concatenate([jnp.where(low, rows, zero), jnp.where(low, zero, rows)], axis=0)
+
+
+def room(mib):
+    return pltpu.CompilerParams(vmem_limit_bytes=mib << 20)
+
+
+def in_hbm(*arrays):
+    return [pltpu.with_memory_space_constraint(x, pltpu.HBM) for x in arrays]
+
+
+def fetch(pairs, sems):
+    copies = [pltpu.make_async_copy(source, target, sems.at[i]) for i, (source, target) in enumerate(pairs)]
+    for copy in copies:
+        copy.start()
+    return copies
+
+
+def stacked(pieces, held):
+    at, pairs = 0, []
+    for piece in pieces:
+        pairs.append((piece, held.at[pl.ds(at, piece.shape[0])]))
+        at += piece.shape[0]
+    return pairs
+
+
+def join_kernel(left, right, out, sems):
+    width = left.shape[1]
+    for copy in fetch([(left, out.at[:, pl.ds(0, width)]), (right, out.at[:, pl.ds(width, width)])], sems):
+        copy.wait()
+
+
+def join(left, right):
+    return pl.pallas_call(
+        join_kernel,
+        out_shape=jax.ShapeDtypeStruct((left.shape[0], 2 * left.shape[1]), left.dtype),
+        in_specs=[ANY] * 2,
+        out_specs=VMEM,
+        scratch_shapes=[pltpu.SemaphoreType.DMA((2,))],
+        compiler_params=room(4),
+        name="join",
+    )(*in_hbm(left, right))
 
 
 def load_keys(near_ref, far_ref, keys, vals):
@@ -143,7 +184,7 @@
             pltpu.VMEM((enc, BLOCK), jnp.bfloat16),
             pltpu.VMEM((rows, 2 * BLOCK), jnp.bfloat16),
         ],
-        compiler_params=ROOM,
+        compiler_params=room(16),
         cost_estimate=cost(2 * rows * enc * 4 * BLOCK, rows * enc * 2),
         name="forward",
     )(*given)
@@ -173,18 +214,19 @@
     return jnp.concatenate([stats[pl.ds(s, 1), :] for s in spots], axis=1)
 
 
-def local_kernel(places, member, stats, near_ref, far_ref, *rest):
+def local_kernel(places, member, stats_ref, near_ref, far_ref, *rest):
     pieces = rest[:5]
-    sums, near_chance, near_slope, far_chance, far_slope, keys, vals, held, turned = rest[5:]
+    sums, near_chance, near_slope, far_chance, far_slope, kv, held, stats, turned, sems = rest[5:]
     p = pl.program_id(0)
 
     @pl.when(p == 0)
     def _():
-        load_keys(near_ref, far_ref, keys, vals)
-        load_targets(pieces, held)
-        turned[...] = keys[...].T
-
-    enc = keys.shape[0]
+        pairs = stacked((near_ref, far_ref), kv) + stacked(pieces, held) + [(stats_ref, stats)]
+        for copy in fetch(pairs, sems):
+            copy.wait()
+        turned[...] = kv[:, :BLOCK].T
+
+    enc = kv.shape[0]
     blocks = enc // BLOCK
     half = stats.shape[0] // 2
     rows = pl.ds(pl.multiple_of(p * 2 * BLOCK, 2 * BLOCK), 2 * BLOCK)
@@ -192,8 +234,8 @@
     log_total = lanes_of(stats, first, second, 0)
     log_total = jnp.where(log_total > -0.5 * BIG, log_total, BIG)
     mean = lanes_of(stats, first, second, half)
-    logits = dot_nt(keys[...], split_heads(held[rows, :BLOCK]))
-    prob = dot_nt(vals[...], split_heads(held[rows, BLOCK:]))
+    logits = dot_nt(kv[:, :BLOCK], split_heads(held[rows, :BLOCK]))
+    prob = dot_nt(kv[:, BLOCK:], split_heads(held[rows, BLOCK:]))
     for b in range(blocks):
         part = slice(b * BLOCK, (b + 1) * BLOCK)
         chance = jnp.exp(logits[part] - (log_total + away(member, first, second, b, blocks)))
@@ -217,32 +259,35 @@
     rows = sum(p.shape[0] for p in pieces)
     enc = near.shape[0] + far.shape[0]
     pairs = rows // (2 * BLOCK)
-    table = jax.ShapeDtypeStruct((pairs, enc // 2, 4 * BLOCK), jnp.bfloat16)
-    given = [places, member, stats, near, far, *pieces]
+    table = pltpu.HBM((pairs, enc // 2, 4 * BLOCK), jnp.bfloat16)
+    given = in_hbm(places, member, stats, near, far, *pieces)
     return pl.pallas_call(
         local_kernel,
         grid=(pairs,),
-        out_shape=[jax.ShapeDtypeStruct((pairs, 2, BLOCK, 2 * BLOCK), jnp.float32)] + [table] * 4,
-        in_specs=[SMEM] * 2 + [VMEM] * (len(given) - 2),
+        out_shape=[pltpu.HBM((pairs, 2, BLOCK, 2 * BLOCK), jnp.float32)] + [table] * 4,
+        in_specs=[SMEM] * 2 + [ANY] * (len(given) - 2),
         out_specs=[pl.BlockSpec((1, 2, BLOCK, 2 * BLOCK), lambda p: (p, 0, 0, 0))]
         + [pl.BlockSpec((1, enc // 2, 4 * BLOCK), lambda p: (p, 0, 0))] * 4,
         scratch_shapes=[
-            pltpu.VMEM((enc, BLOCK), jnp.bfloat16),
-            pltpu.VMEM((enc, BLOCK), jnp.bfloat16),
+            pltpu.VMEM((enc, 2 * BLOCK), jnp.bfloat16),
             pltpu.VMEM((rows, 2 * BLOCK), jnp.bfloat16),
+            pltpu.VMEM(stats.shape, stats.dtype),
             pltpu.VMEM((BLOCK, enc), jnp.bfloat16),
+            pltpu.SemaphoreType.DMA((len(given) - 2,)),
         ],
-        compiler_params=ROOM,
+        compiler_params=room(16),
         cost_estimate=cost(3 * rows * enc * 4 * BLOCK, rows * enc * 2),
         name="local",
     )(*given)
 
 
-def scale_kernel(places, parts, stats, sums, *rest):
+def scale_kernel(places, parts, stats_ref, sums_ref, *rest):
     pieces = rest[:5]
-    d_query, scaled, held, whole = rest[5:]
+    d_query, scaled, held, whole, stats, sums, sems = rest[5:]
+    copies = fetch(stacked(pieces, held) + [(stats_ref, stats), (sums_ref, sums)], sems)
     merge_stats(parts, whole)
-    load_targets(pieces, held)
+    for copy in copies:
+        copy.wait()
     half = stats.shape[0] // 2
     pairs = held.shape[0] // (2 * BLOCK)
 
@@ -276,20 +321,23 @@
 def scale(places, parts, stats, sums, pieces):
     count = places.shape[0]
     rows = sum(p.shape[0] for p in pieces)
-    given = [places, parts, stats, sums, *pieces]
+    given = [*in_hbm(places), parts, *in_hbm(stats, sums, *pieces)]
     return pl.pallas_call(
         scale_kernel,
         out_shape=[
-            jax.ShapeDtypeStruct((count, BLOCK, BLOCK), jnp.bfloat16),
-            jax.ShapeDtypeStruct((rows, 3 * BLOCK), jnp.bfloat16),
+            pltpu.HBM((count, BLOCK, BLOCK), jnp.bfloat16),
+            pltpu.HBM((rows, 3 * BLOCK), jnp.bfloat16),
         ],
-        in_specs=[SMEM] + [VMEM] * (len(given) - 1),
+        in_specs=[SMEM, VMEM] + [ANY] * (len(given) - 2),
         out_specs=[VMEM] * 2,
         scratch_shapes=[
             pltpu.VMEM((rows, 2 * BLOCK), jnp.bfloat16),
             pltpu.VMEM((4 * count, BLOCK), jnp.float32),
+            pltpu.VMEM(stats.shape, stats.dtype),
+            pltpu.VMEM(sums.shape, sums.dtype),
+            pltpu.SemaphoreType.DMA((len(given) - 2,)),
         ],
-        compiler_params=ROOM,
+        compiler_params=room(16),
         cost_estimate=cost(1 << 27, 1 << 16),
         name="scale",
     )(*given)
@@ -298,10 +346,13 @@
 def gather_kernel(core, scaled, chance, slope, *rest):
     *sent, d_key, d_value = rest
     p = pl.program_id(0)
-    rows = pl.ds(pl.multiple_of(p * 2 * BLOCK, 2 * BLOCK), 2 * BLOCK)
-    out, lack, query = (split_heads(scaled[rows, i * BLOCK : (i + 1) * BLOCK]) for i in range(3))
-    both = dot_nn(chance[0], jnp.concatenate([out, lack], axis=1))
-    value, key = both[:, :BLOCK], both[:, BLOCK:] + dot_nn(slope[0], query)
+    value = key = None
+    for i in range(chance.shape[0]):
+        rows = slice(2 * i * BLOCK, 2 * (i + 1) * BLOCK)
+        out, lack, query = (split_heads(scaled[rows, j * BLOCK : (j + 1) * BLOCK]) for j in range(3))
+        both = dot_nn(chance[i], jnp.concatenate([out, lack], axis=1))
+        more, least = both[:, :BLOCK], both[:, BLOCK:] + dot_nn(slope[i], query)
+        value, key = (more, least) if value is None else (value + more, key + least)
 
     @pl.when(p == 0)
     def _():
@@ -332,18 +383,20 @@
         sent = [jax.ShapeDtypeStruct((enc, 2 * BLOCK), jnp.bfloat16)]
     else:
         sent = [jax.ShapeDtypeStruct((enc // 2, 2 * BLOCK), jnp.float32)] * 2
-    table = pl.BlockSpec((1, enc, lanes), lambda p: (p, 0, 0))
+    step = 2
+    table = pl.BlockSpec((step, enc, lanes), lambda p: (p, 0, 0))
+    given = in_hbm(scaled, chance, slope)
     return pl.pallas_call(
         gather_kernel,
-        grid=(pairs,),
+        grid=(pairs // step,),
         out_shape=sent,
-        in_specs=[SMEM, VMEM, table, table],
+        in_specs=[SMEM, pl.BlockSpec((step * 2 * BLOCK, scaled.shape[1]), lambda p: (p, 0)), table, table],
         out_specs=[VMEM] * len(sent),
         scratch_shapes=[pltpu.VMEM((enc, BLOCK), jnp.float32)] * 2,
-        compiler_params=ROOM,
+        compiler_params=room(16),
         cost_estimate=cost(3 * pairs * enc * lanes * BLOCK, 0),
         name="gather",
-    )(core, scaled, chance, slope)
+    )(core, *given)
 
 
 def project_kernel(core, chunk, kept, from_half, from_core, kw, vw, far_kw, far_vw, memory):
@@ -364,7 +417,7 @@
         out_shape=jax.ShapeDtypeStruct((chunk.shape[0], given[0].shape[0], BLOCK), jnp.bfloat16),
         in_specs=[SMEM] * 2 + [VMEM] * len(given),
         out_specs=VMEM,
-        compiler_params=ROOM,
+        compiler_params=room(8),
         name="project",
     )(core, chunk, *given)
 
@@ -383,11 +436,11 @@
     enc_rows = keys.shape[0]
     enc_blocks = enc_rows // BLOCK
 
-    near = jnp.concatenate([queries, d_out], axis=1)
+    near = join(queries, d_out)
     ahead = moved(near, Z, 4)
     behind = moved(near, Z, -4)
     across = moved(near, Z, 8)
-    own = jnp.concatenate([keys, values], axis=1)
+    own = join(keys, values)
     far = moved(own, "xh", 1)
 
     places = (place + jnp.asarray(SLOTS, jnp.int32)) % depth

time: 169 us -> 158 us (0.935)
  local copies, waits for them, and re-layouts: 21.2 us -> 0.76 us
  starting transfers between devices: 79.3 us -> 86.9 us
  Pallas kernels: 40.6 us -> 43.4 us
    unnamed x62 -> x26, local copies, waits for them, and re-layouts: 19.4 us -> 0.67 us
    all_to_all x1, starting transfers between devices: 5.19 us -> 11.3 us  [body(): memory = lax.all_to_all(memory, HEAD, 0, 0, tiled=True)]
    pallas_call x4 -> x6, Pallas kernels: 28.3 us -> 31.6 us  [the longest x1 12.7 us: local(): pl.pallas_call(local_kernel, grid=(pairs,), out_shape=[pltpu.HBM((pairs,...]
    ppermute x12, starting transfers between devices: 56.2 us -> 58 us  [moved(): lax.ppermute(value, axis, [(i, (i + steps) % count) for i in range(count)])]
    concatenate x2 -> x0, local copies, waits for them, and re-layouts: 1.71 us -> none  [the longest x1 0.94 us: body(): own = jnp.concatenate([keys, values], axis=1)]
  transfers between devices with their start and end apart: 15 -> 15, of which waited for: 4 -> 5; matrix products, arithmetic and copies ran while one was open for 2% -> 1% of each run, Pallas kernels for 19% -> 19%
where the time goes in v5:
time: 158 us; the launch traced here: 157 us
  starting transfers between devices  86.9 us (55%)
  Pallas kernels  43.4 us (27%)
  waiting for transfers between devices  22.6 us (14%)
  other arithmetic  2.75 us (2%)
    ppermute x12, starting transfers between devices, moved(): lax.ppermute(value, axis, [(i, (i + steps) % count) for i in range(count)])  58 us
    all_to_all x1, waiting for transfers between devices, body(): memory = lax.all_to_all(memory, HEAD, 0, 0, tiled=True)  15.1 us
    pallas_call x1, Pallas kernels, local(): pl.pallas_call(local_kernel, grid=(pairs,), out_shape=[pltpu.HBM((pairs,...  12.7 us
    pallas_call x2, Pallas kernels, gather(): pl.pallas_call(gather_kernel, grid=(pairs // step,), out_shape=sent, in_s...  11.8 us
    all_to_all x1, starting transfers between devices, body(): d_query = lax.all_to_all(d_query, Z, 0, 0, tiled=True)  11.6 us
    all_to_all x1, starting transfers between devices, body(): memory = lax.all_to_all(memory, HEAD, 0, 0, tiled=True)  11.3 us
    pallas_call x2, Pallas kernels, forward(): pl.pallas_call(kernel, out_shape=shapes, in_specs=specs, out_specs=[VMEM]...  8.97 us
    ppermute x12, waiting for transfers between devices, moved(): lax.ppermute(value, axis, [(i, (i + steps) % count) for i in range(count)])  7.34 us
  transfers between devices with their start and end apart: 15, of which 5 were waited for; matrix products, arithmetic and copies ran while one was open for 1% of the time, Pallas kernels for 19%

profile of v5, /device:TPU:1, one launch (start us, length us, event | category | flops | bytes accessed | tf_op | source)
XLA Modules:
  0.0 157.5 jit_solution(2008201790219569584)
XLA Ops:
  0.6 0.0 copy-start
  0.6 0.8 join.3
  1.4 13.3 %collective-permute-start.1 = (bf16[128,256]{1,0:T(8,128)(2,1)S(1)}, bf16[128,256]{1,0:T(8,128)(2,1)S(1)}, u32[]{:S(2)}, u32[]{:S(2)}) collective-permute-start(bf16[128,256]{1,0:T(8,128)(2,1)S(1)} %join.3), channel_id=1, source_target_pairs={{0,192},{16,208},{32,224},{48,240},{64,0},{80,16},{96,32},{112,48}... | collective-permute-start | bytes 196616 | tf_op jit(solution)/shard_map/ppermute | solution.py:427
  14.7 1.9 %collective-permute-start.2 = (bf16[128,256]{1,0:T(8,128)(2,1)S(1)}, bf16[128,256]{1,0:T(8,128)(2,1)S(1)}, u32[]{:S(2)}, u32[]{:S(2)}) collective-permute-start(bf16[128,256]{1,0:T(8,128)(2,1)S(1)} %join.3), channel_id=1, source_target_pairs={{0,64},{16,80},{32,96},{48,112},{64,128},{80,144},{96,160},{112,17... | collective-permute-start | bytes 196616 | tf_op jit(solution)/shard_map/ppermute | solution.py:427
  16.7 10.3 %collective-permute-start.3 = (bf16[128,256]{1,0:T(8,128)(2,1)S(1)}, bf16[128,256]{1,0:T(8,128)(2,1)S(1)}, u32[]{:S(2)}, u32[]{:S(2)}) collective-permute-start(bf16[128,256]{1,0:T(8,128)(2,1)S(1)} %join.3), channel_id=1, source_target_pairs={{0,128},{16,144},{32,160},{48,176},{64,192},{80,208},{96,224},{112... | collective-permute-start | bytes 196616 | tf_op jit(solution)/shard_map/ppermute | solution.py:427
  26.9 1.0 join.2.refs_2_.near_ref
  27.9 0.0 copy-start.4
  27.9 4.7 %collective-permute-start = (bf16[512,256]{1,0:T(8,128)(2,1)S(1)}, bf16[512,256]{1,0:T(8,128)(2,1)S(1)}, u32[]{:S(2)}, u32[]{:S(2)}) collective-permute-start(bf16[512,256]{1,0:T(8,128)(2,1)S(1)} %join.2.refs_2_.near_ref), channel_id=1, source_target_pairs={{0,256},{256,0},{1,257},{257,1},{2,258},{258,2},{3,259},{259,3},{4... | collective-permute-start | bytes 786440 | tf_op jit(solution)/shard_map/ppermute | solution.py:427
  32.6 0.7 and_select_fusion.refs_0_.places
  33.3 0.1 pad_add_fusion
  33.4 0.0 copy-done
  33.4 0.4 compare_reduce_fusion
  33.8 0.1 reshape.15.refs_1_.member
  33.9 0.0 copy-start.10
  33.9 0.0 collective-permute-done.1
  33.9 0.0 collective-permute-done.2
  33.9 0.0 collective-permute-done.3
  34.0 0.0 copy-start.1
  34.0 2.6 %collective-permute-start.4 = (bf16[512,256]{1,0:T(8,128)(2,1)S(1)}, bf16[512,256]{1,0:T(8,128)(2,1)S(1)}, u32[]{:S(2)}, u32[]{:S(2)}) collective-permute-start(bf16[512,256]{1,0:T(8,128)(2,1)S(1)} %pad_maximum_fusion.refs_4_.rest_0_), channel_id=1, source_target_pairs={{0,16},{16,32},{32,48},{48,64},{64,80},{80,96},{96,112},{112,128},... | collective-permute-start | bytes 786440 | tf_op jit(solution)/shard_map/ppermute | solution.py:427
  36.6 5.8 %collective-permute-start.5 = (bf16[512,256]{1,0:T(8,128)(2,1)S(1)}, bf16[512,256]{1,0:T(8,128)(2,1)S(1)}, u32[]{:S(2)}, u32[]{:S(2)}) collective-permute-start(bf16[512,256]{1,0:T(8,128)(2,1)S(1)} %pad_maximum_fusion.refs_4_.rest_0_), channel_id=1, source_target_pairs={{0,240},{16,0},{32,16},{48,32},{64,48},{80,64},{96,80},{112,96},{1... | collective-permute-start | bytes 786440 | tf_op jit(solution)/shard_map/ppermute | solution.py:427
  42.5 3.1 %collective-permute-start.6 = (bf16[256,256]{1,0:T(8,128)(2,1)S(1)}, bf16[256,256]{1,0:T(8,128)(2,1)S(1)}, u32[]{:S(2)}, u32[]{:S(2)}) collective-permute-start(bf16[256,256]{1,0:T(8,128)(2,1)S(1)} %get-tuple-element.57), channel_id=1, source_target_pairs={{0,224},{16,240},{32,0},{48,16},{64,32},{80,48},{96,64},{112,80},{... | collective-permute-start | bytes 393224 | tf_op jit(solution)/shard_map/ppermute | solution.py:427
  45.6 3.1 %collective-permute-start.7 = (bf16[256,256]{1,0:T(8,128)(2,1)S(1)}, bf16[256,256]{1,0:T(8,128)(2,1)S(1)}, u32[]{:S(2)}, u32[]{:S(2)}) collective-permute-start(bf16[256,256]{1,0:T(8,128)(2,1)S(1)} %get-tuple-element.56), channel_id=1, source_target_pairs={{0,32},{16,48},{32,64},{48,80},{64,96},{80,112},{96,128},{112,144}... | collective-permute-start | bytes 393224 | tf_op jit(solution)/shard_map/ppermute | solution.py:427
  48.7 0.0 collective-permute-done.refs_3_.far_ref
  48.7 0.0 copy-start.12
  48.7 2.3 %forward.2.rest_4_ = f32[64,128]{1,0:T(8,128)S(1)} custom-call(s32[16]{0:T(128)S(1)} %and_select_fusion.refs_0_.places, s32[128]{0:T(128)S(1)} %reshape.15.refs_1_.member, bf16[512,256]{1,0:T(8,128)(2,1)S(1)} %join.2.refs_2_.near_ref, bf16[512,256]{1,0:T(8,128)(2,1)S(1)} %collective-permute-done.refs_3_.far_ref, ...), custom_call_target="tpu_custom_call" | custom-call | flops 2147483648 | bytes 1048576 | tf_op jit(solution)/shard_map/forward/pallas_call | solution.py:177
  51.0 0.0 copy-done.1
  51.0 0.0 copy-start.2
  51.0 0.0 copy-start.3
  51.0 2.0 %collective-permute-done.6.rest_2_.rest_3_ = bf16[256,256]{1,0:T(8,128)(2,1)S(1)} collective-permute-done((bf16[256,256]{1,0:T(8,128)(2,1)S(1)}, bf16[256,256]{1,0:T(8,128)(2,1)S(1)}, u32[]{:S(2)}, u32[]{:S(2)}) %collective-permute-start.6) | collective-permute-done | bytes 131104 | tf_op jit(solution)/shard_map/ppermute | solution.py:427
  53.1 4.3 %collective-permute-done.7.rest_3_.rest_4_ = bf16[256,256]{1,0:T(8,128)(2,1)S(1)} collective-permute-done((bf16[256,256]{1,0:T(8,128)(2,1)S(1)}, bf16[256,256]{1,0:T(8,128)(2,1)S(1)}, u32[]{:S(2)}, u32[]{:S(2)}) %collective-permute-start.7) | collective-permute-done | bytes 131104 | tf_op jit(solution)/shard_map/ppermute | solution.py:427
  57.4 0.0 collective-permute-done.4.rest_0_.rest_1_
  57.4 0.0 collective-permute-done.5.rest_1_.rest_2_
  57.4 0.0 copy-done.4
  57.4 0.0 copy-done.11
  57.4 0.0 copy-done.10
  57.4 0.0 copy-start.6
  57.4 6.7 %forward.3 = (bf16[16,96,128]{2,1,0:T(8,128)(2,1)}, f32[64,128]{1,0:T(8,128)S(1)}) custom-call(s32[16]{0:T(128)S(1)} %and_select_fusion.refs_0_.places, s32[128]{0:T(128)S(1)} %reshape.15.refs_1_.member, bf16[512,256]{1,0:T(8,128)(2,1)S(1)} %join.2.refs_2_.near_ref, bf16[512,256]{1,0:T(8,128)(2,1)S(1)} %collective-permute-done.refs_3_.far_ref, ...), custom_call_target="tpu_custom_call" | custom-call | flops 6442450944 | bytes 1048576 | tf_op jit(solution)/shard_map/forward/pallas_call | solution.py:177
  64.1 0.0 copy-done.12
  64.1 0.0 copy-done.8
  64.1 0.0 copy-done.5
  64.1 0.0 copy-done.6
  64.1 0.0 copy-start.9
  64.2 0.6 copy-done.9
  64.8 5.9 %all-to-all-start = ((bf16[16,96,128]{2,1,0:T(8,128)(2,1)}), bf16[16,96,128]{2,1,0:T(8,128)(2,1)S(1)}, u32[]{:S(2)}, u32[]{:S(2)}) async-start(bf16[16,96,128]{2,1,0:T(8,128)(2,1)} %get-tuple-element.31), calls=%async_computation | async-start | bytes 786432 | tf_op jit(solution)/shard_map/all_to_all | solution.py:465
  70.7 3.2 %collective-permute-start.8 = (bf16[2048,128]{1,0:T(8,128)(2,1)S(1)}, bf16[2048,128]{1,0:T(8,128)(2,1)S(1)}, u32[]{:S(2)}, u32[]{:S(2)}) collective-permute-start(bf16[2048,128]{1,0:T(8,128)(2,1)S(1)} %copy-done.2), channel_id=1, source_target_pairs={{0,1},{1,0},{2,3},{3,2},{4,5},{5,4},{6,7},{7,6},{8,9},{9,8},{10,11... | collective-permute-start | bytes 1572872 | tf_op jit(solution)/shard_map/ppermute | solution.py:427
  73.9 1.9 %collective-permute-start.9 = (bf16[2048,128]{1,0:T(8,128)(2,1)S(1)}, bf16[2048,128]{1,0:T(8,128)(2,1)S(1)}, u32[]{:S(2)}, u32[]{:S(2)}) collective-permute-start(bf16[2048,128]{1,0:T(8,128)(2,1)S(1)} %copy-done.3), channel_id=1, source_target_pairs={{0,1},{1,0},{2,3},{3,2},{4,5},{5,4},{6,7},{7,6},{8,9},{9,8},{10,11... | collective-permute-start | bytes 1572872 | tf_op jit(solution)/shard_map/ppermute | solution.py:427
  75.8 12.7 %local.1 = (f32[8,2,128,256]{3,2,1,0:T(8,128)}, bf16[8,512,512]{2,1,0:T(8,128)(2,1)}, bf16[8,512,512]{2,1,0:T(8,128)(2,1)}, bf16[8,512,512]{2,1,0:T(8,128)(2,1)}, bf16[8,512,512]{2,1,0:T(8,128)(2,1)}) custom-call(s32[16]{0:T(128)} %copy-done.11, s32[128]{0:T(128)} %copy-done.10, f32[64,128]{1,0:T(8,128)} %copy-done.9, bf16[512,256]{1,0:T(8,128)(2,1)} %copy-done.4, ...), custom_call_target="tpu_custom_call" | custom-call | flops 12884901888 | bytes 1048576 | tf_op jit(solution)/shard_map/local/pallas_call | solution.py:264
  88.5 0.0 collective-permute-done.8.far_kw
  88.5 0.0 collective-permute-done.9.far_vw
  88.5 0.1 all-to-all-done.parts
  88.7 5.4 %scale.1 = (bf16[16,128,128]{2,1,0:T(8,128)(2,1)}, bf16[2048,384]{1,0:T(8,128)(2,1)}) custom-call(s32[16]{0:T(128)} %copy-done.11, bf16[16,96,128]{2,1,0:T(8,128)(2,1)S(1)} %all-to-all-done.parts, f32[64,128]{1,0:T(8,128)} %copy-done.9, f32[8,2,128,256]{3,2,1,0:T(8,128)} %get-tuple-element.41.sums_ref, bf16[512,256]{1,0:T(8,128)(2,1)} %copy-done.1, ...), custom_call_target="tpu_custom_call" | custom-call | flops 536870912 | bytes 1048576 | tf_op jit(solution)/shard_map/scale/pallas_call | solution.py:325
  94.1 11.6 %all-to-all-start.1 = ((bf16[16,128,128]{2,1,0:T(8,128)(2,1)}), bf16[16,128,128]{2,1,0:T(8,128)(2,1)S(1)}, u32[]{:S(2)}, u32[]{:S(2)}) async-start(bf16[16,128,128]{2,1,0:T(8,128)(2,1)} %get-tuple-element.53), calls=%async_computation.1 | async-start | bytes 1048576 | tf_op jit(solution)/shard_map/all_to_all | solution.py:478
  105.7 5.9 %gather.3 = bf16[512,256]{1,0:T(8,128)(2,1)S(1)} custom-call(s32[1]{0:T(128)} %bitcast.core, bf16[2048,384]{1,0:T(8,128)(2,1)} %get-tuple-element.42.scaled, bf16[8,512,512]{2,1,0:T(8,128)(2,1)} %get-tuple-element.47.chance, bf16[8,512,512]{2,1,0:T(8,128)(2,1)} %get-tuple-element.48.slope), custom_call_target="tpu_custom_call" | custom-call | flops 3221225472 | bytes 1048576 | tf_op jit(solution)/shard_map/gather/pallas_call | solution.py:389
  111.6 4.4 %collective-permute-start.10 = (bf16[512,256]{1,0:T(8,128)(2,1)S(1)}, bf16[512,256]{1,0:T(8,128)(2,1)S(1)}, u32[]{:S(2)}, u32[]{:S(2)}) collective-permute-start(bf16[512,256]{1,0:T(8,128)(2,1)S(1)} %gather.3), channel_id=1, source_target_pairs={{0,256},{256,0},{1,257},{257,1},{2,258},{258,2},{3,259},{259,3},{4... | collective-permute-start | bytes 786440 | tf_op jit(solution)/shard_map/ppermute | solution.py:427
  116.0 5.9 %gather.2 = (f32[256,256]{1,0:T(8,128)S(1)}, f32[256,256]{1,0:T(8,128)S(1)}) custom-call(s32[1]{0:T(128)} %bitcast.core, bf16[2048,384]{1,0:T(8,128)(2,1)} %get-tuple-element.42.scaled, bf16[8,512,512]{2,1,0:T(8,128)(2,1)} %get-tuple-element.43.chance, bf16[8,512,512]{2,1,0:T(8,128)(2,1)} %get-tuple-element.44.slope), custom_call_target="tpu_custom_call" | custom-call | flops 3221225472 | bytes 1048576 | tf_op jit(solution)/shard_map/gather/pallas_call | solution.py:389
  121.9 0.0 collective-permute-done.10.from_half
  122.0 3.7 %collective-permute-start.11 = (bf16[256,256]{1,0:T(8,128)(2,1)S(1)}, bf16[256,256]{1,0:T(8,128)(2,1)S(1)}, u32[]{:S(2)}, u32[]{:S(2)}) collective-permute-start(bf16[256,256]{1,0:T(8,128)(2,1)S(1)} %add_convert_fusion), channel_id=1, source_target_pairs={{0,1},{1,0},{2,3},{3,2},{4,5},{5,4},{6,7},{7,6},{8,9},{9,8},{10,11... | collective-permute-start | bytes 393224 | tf_op jit(solution)/shard_map/ppermute | solution.py:427
  125.7 1.0 collective-permute-done.11.from_core
  126.7 2.8 %project.1 = bf16[16,256,128]{2,1,0:T(8,128)(2,1)} custom-call(s32[1]{0:T(128)} %bitcast.core, s32[16]{0:T(128)S(1)} %iota.8.chunk, f32[256,256]{1,0:T(8,128)S(1)} %get-tuple-element.45.kept, bf16[512,256]{1,0:T(8,128)(2,1)S(1)} %collective-permute-done.10.from_half, bf16[256,256]{1,0:T(8,128)(2,1)S(1)} %collective-permute-done.11.from_core, ...), custom_call_target="tpu_custom_call" | custom-call | tf_op jit(solution)/shard_map/project/pallas_call | solution.py:415
  129.5 0.0 all-to-all-done.1
  129.5 11.3 %all-to-all-start.2 = ((bf16[16,256,128]{2,1,0:T(8,128)(2,1)}), bf16[16,256,128]{2,1,0:T(8,128)(2,1)S(1)}, u32[]{:S(2)}, u32[]{:S(2)}) async-start(bf16[16,256,128]{2,1,0:T(8,128)(2,1)} %project.1), calls=%async_computation.2 | async-start | bytes 2097152 | tf_op jit(solution)/shard_map/all_to_all | solution.py:488
  140.8 0.7 reduce_sum.21
  141.5 15.1 %all-to-all-done.2 = bf16[16,256,128]{2,1,0:T(8,128)(2,1)S(1)} async-done(((bf16[16,256,128]{2,1,0:T(8,128)(2,1)}), bf16[16,256,128]{2,1,0:T(8,128)(2,1)S(1)}, u32[]{:S(2)}, u32[]{:S(2)}) %all-to-all-start.2) | async-done | bytes 1048608 | tf_op jit(solution)/shard_map/all_to_all | solution.py:488
  156.6 0.8 reduce.1
  (14 shorter events, 0.1 us)
Async XLA Ops:
  0.6 32.7 %copy-start = (s32[32,64]{1,0:T(8,128)S(1)}, s32[32,64]{1,0:T(8,128)}, u32[]{:S(2)}) copy-start(s32[32,64]{1,0:T(8,128)} %param.14) | copy-start | bytes 24580
  1.4 32.5 %collective-permute-start.1 = (bf16[128,256]{1,0:T(8,128)(2,1)S(1)}, bf16[128,256]{1,0:T(8,128)(2,1)S(1)}, u32[]{:S(2)}, u32[]{:S(2)}) collective-permute-start(bf16[128,256]{1,0:T(8,128)(2,1)S(1)} %join.3), channel_id=1, source_target_pairs={{0,192},{16,208},{32,224},{48,240},{64,0},{80,16},{96,32},{112,48}... | collective-permute-start | bytes 196616 | tf_op jit(solution)/shard_map/ppermute | solution.py:427
  14.7 19.2 %collective-permute-start.2 = (bf16[128,256]{1,0:T(8,128)(2,1)S(1)}, bf16[128,256]{1,0:T(8,128)(2,1)S(1)}, u32[]{:S(2)}, u32[]{:S(2)}) collective-permute-start(bf16[128,256]{1,0:T(8,128)(2,1)S(1)} %join.3), channel_id=1, source_target_pairs={{0,64},{16,80},{32,96},{48,112},{64,128},{80,144},{96,160},{112,17... | collective-permute-start | bytes 196616 | tf_op jit(solution)/shard_map/ppermute | solution.py:427
  16.7 17.3 %collective-permute-start.3 = (bf16[128,256]{1,0:T(8,128)(2,1)S(1)}, bf16[128,256]{1,0:T(8,128)(2,1)S(1)}, u32[]{:S(2)}, u32[]{:S(2)}) collective-permute-start(bf16[128,256]{1,0:T(8,128)(2,1)S(1)} %join.3), channel_id=1, source_target_pairs={{0,128},{16,144},{32,160},{48,176},{64,192},{80,208},{96,224},{112... | collective-permute-start | bytes 196616 | tf_op jit(solution)/shard_map/ppermute | solution.py:427
  27.9 29.5 %copy-start.4 = (bf16[512,256]{1,0:T(8,128)(2,1)}, bf16[512,256]{1,0:T(8,128)(2,1)S(1)}, u32[]{:S(2)}) copy-start(bf16[512,256]{1,0:T(8,128)(2,1)S(1)} %join.2.refs_2_.near_ref) | copy-start | bytes 786436
  27.9 20.7 %collective-permute-start = (bf16[512,256]{1,0:T(8,128)(2,1)S(1)}, bf16[512,256]{1,0:T(8,128)(2,1)S(1)}, u32[]{:S(2)}, u32[]{:S(2)}) collective-permute-start(bf16[512,256]{1,0:T(8,128)(2,1)S(1)} %join.2.refs_2_.near_ref), channel_id=1, source_target_pairs={{0,256},{256,0},{1,257},{257,1},{2,258},{258,2},{3,259},{259,3},{4... | collective-permute-start | bytes 786440 | tf_op jit(solution)/shard_map/ppermute | solution.py:427
  33.3 24.1 %copy-start.11 = (s32[16]{0:T(128)}, s32[16]{0:T(128)S(1)}, u32[]{:S(2)}) copy-start(s32[16]{0:T(128)S(1)} %and_select_fusion.refs_0_.places) | copy-start | bytes 196
  33.9 23.5 %copy-start.10 = (s32[128]{0:T(128)}, s32[128]{0:T(128)S(1)}, u32[]{:S(2)}) copy-start(s32[128]{0:T(128)S(1)} %reshape.15.refs_1_.member) | copy-start | bytes 1540
  34.0 17.0 %copy-start.1 = (bf16[512,256]{1,0:T(8,128)(2,1)}, bf16[512,256]{1,0:T(8,128)(2,1)S(1)}, u32[]{:S(2)}) copy-start(bf16[512,256]{1,0:T(8,128)(2,1)S(1)} %pad_maximum_fusion.refs_4_.rest_0_) | copy-start | bytes 786436
  34.0 23.4 %collective-permute-start.4 = (bf16[512,256]{1,0:T(8,128)(2,1)S(1)}, bf16[512,256]{1,0:T(8,128)(2,1)S(1)}, u32[]{:S(2)}, u32[]{:S(2)}) collective-permute-start(bf16[512,256]{1,0:T(8,128)(2,1)S(1)} %pad_maximum_fusion.refs_4_.rest_0_), channel_id=1, source_target_pairs={{0,16},{16,32},{32,48},{48,64},{64,80},{80,96},{96,112},{112,128},... | collective-permute-start | bytes 786440 | tf_op jit(solution)/shard_map/ppermute | solution.py:427
  36.6 20.8 %collective-permute-start.5 = (bf16[512,256]{1,0:T(8,128)(2,1)S(1)}, bf16[512,256]{1,0:T(8,128)(2,1)S(1)}, u32[]{:S(2)}, u32[]{:S(2)}) collective-permute-start(bf16[512,256]{1,0:T(8,128)(2,1)S(1)} %pad_maximum_fusion.refs_4_.rest_0_), channel_id=1, source_target_pairs={{0,240},{16,0},{32,16},{48,32},{64,48},{80,64},{96,80},{112,96},{1... | collective-permute-start | bytes 786440 | tf_op jit(solution)/shard_map/ppermute | solution.py:427
  42.5 10.6 %collective-permute-start.6 = (bf16[256,256]{1,0:T(8,128)(2,1)S(1)}, bf16[256,256]{1,0:T(8,128)(2,1)S(1)}, u32[]{:S(2)}, u32[]{:S(2)}) collective-permute-start(bf16[256,256]{1,0:T(8,128)(2,1)S(1)} %get-tuple-element.57), channel_id=1, source_target_pairs={{0,224},{16,240},{32,0},{48,16},{64,32},{80,48},{96,64},{112,80},{... | collective-permute-start | bytes 393224 | tf_op jit(solution)/shard_map/ppermute | solution.py:427
  45.6 11.8 %collective-permute-start.7 = (bf16[256,256]{1,0:T(8,128)(2,1)S(1)}, bf16[256,256]{1,0:T(8,128)(2,1)S(1)}, u32[]{:S(2)}, u32[]{:S(2)}) collective-permute-start(bf16[256,256]{1,0:T(8,128)(2,1)S(1)} %get-tuple-element.56), channel_id=1, source_target_pairs={{0,32},{16,48},{32,64},{48,80},{64,96},{80,112},{96,128},{112,144}... | collective-permute-start | bytes 393224 | tf_op jit(solution)/shard_map/ppermute | solution.py:427
  48.7 15.4 %copy-start.12 = (bf16[512,256]{1,0:T(8,128)(2,1)}, bf16[512,256]{1,0:T(8,128)(2,1)S(1)}, u32[]{:S(2)}) copy-start(bf16[512,256]{1,0:T(8,128)(2,1)S(1)} %collective-permute-done.refs_3_.far_ref) | copy-start | bytes 786436
  51.0 19.6 %copy-start.2 = (bf16[2048,128]{1,0:T(8,128)(2,1)S(1)}, bf16[2048,128]{1,0:T(8,128)(2,1)}, u32[]{:S(2)}) copy-start(bf16[2048,128]{1,0:T(8,128)(2,1)} %kw) | copy-start | bytes 1572868
  51.0 22.9 %copy-start.3 = (bf16[2048,128]{1,0:T(8,128)(2,1)S(1)}, bf16[2048,128]{1,0:T(8,128)(2,1)}, u32[]{:S(2)}) copy-start(bf16[2048,128]{1,0:T(8,128)(2,1)} %vw) | copy-start | bytes 1572868
  53.1 11.0 %copy-start.7 = (bf16[256,256]{1,0:T(8,128)(2,1)}, bf16[256,256]{1,0:T(8,128)(2,1)S(1)}, u32[]{:S(2)}) copy-start(bf16[256,256]{1,0:T(8,128)(2,1)S(1)} %collective-permute-done.6.rest_2_.rest_3_) | copy-start | bytes 393220
  57.4 6.7 %copy-start.8 = (bf16[256,256]{1,0:T(8,128)(2,1)}, bf16[256,256]{1,0:T(8,128)(2,1)S(1)}, u32[]{:S(2)}) copy-start(bf16[256,256]{1,0:T(8,128)(2,1)S(1)} %collective-permute-done.7.rest_3_.rest_4_) | copy-start | bytes 393220
  57.4 6.7 %copy-start.5 = (bf16[512,256]{1,0:T(8,128)(2,1)}, bf16[512,256]{1,0:T(8,128)(2,1)S(1)}, u32[]{:S(2)}) copy-start(bf16[512,256]{1,0:T(8,128)(2,1)S(1)} %collective-permute-done.4.rest_0_.rest_1_) | copy-start | bytes 786436
  57.4 6.7 %copy-start.6 = (bf16[512,256]{1,0:T(8,128)(2,1)}, bf16[512,256]{1,0:T(8,128)(2,1)S(1)}, u32[]{:S(2)}) copy-start(bf16[512,256]{1,0:T(8,128)(2,1)S(1)} %collective-permute-done.5.rest_1_.rest_2_) | copy-start | bytes 786436
  64.1 0.6 copy-start.9
  64.8 23.9 %all-to-all-start = ((bf16[16,96,128]{2,1,0:T(8,128)(2,1)}), bf16[16,96,128]{2,1,0:T(8,128)(2,1)S(1)}, u32[]{:S(2)}, u32[]{:S(2)}) async-start(bf16[16,96,128]{2,1,0:T(8,128)(2,1)} %get-tuple-element.31), calls=%async_computation | async-start | bytes 786432 | tf_op jit(solution)/shard_map/all_to_all | solution.py:465
  70.7 17.9 %collective-permute-start.8 = (bf16[2048,128]{1,0:T(8,128)(2,1)S(1)}, bf16[2048,128]{1,0:T(8,128)(2,1)S(1)}, u32[]{:S(2)}, u32[]{:S(2)}) collective-permute-start(bf16[2048,128]{1,0:T(8,128)(2,1)S(1)} %copy-done.2), channel_id=1, source_target_pairs={{0,1},{1,0},{2,3},{3,2},{4,5},{5,4},{6,7},{7,6},{8,9},{9,8},{10,11... | collective-permute-start | bytes 1572872 | tf_op jit(solution)/shard_map/ppermute | solution.py:427
  73.9 14.6 %collective-permute-start.9 = (bf16[2048,128]{1,0:T(8,128)(2,1)S(1)}, bf16[2048,128]{1,0:T(8,128)(2,1)S(1)}, u32[]{:S(2)}, u32[]{:S(2)}) collective-permute-start(bf16[2048,128]{1,0:T(8,128)(2,1)S(1)} %copy-done.3), channel_id=1, source_target_pairs={{0,1},{1,0},{2,3},{3,2},{4,5},{5,4},{6,7},{7,6},{8,9},{9,8},{10,11... | collective-permute-start | bytes 1572872 | tf_op jit(solution)/shard_map/ppermute | solution.py:427
  94.1 35.4 %all-to-all-start.1 = ((bf16[16,128,128]{2,1,0:T(8,128)(2,1)}), bf16[16,128,128]{2,1,0:T(8,128)(2,1)S(1)}, u32[]{:S(2)}, u32[]{:S(2)}) async-start(bf16[16,128,128]{2,1,0:T(8,128)(2,1)} %get-tuple-element.53), calls=%async_computation.1 | async-start | bytes 1048576 | tf_op jit(solution)/shard_map/all_to_all | solution.py:478
  111.6 10.3 %collective-permute-start.10 = (bf16[512,256]{1,0:T(8,128)(2,1)S(1)}, bf16[512,256]{1,0:T(8,128)(2,1)S(1)}, u32[]{:S(2)}, u32[]{:S(2)}) collective-permute-start(bf16[512,256]{1,0:T(8,128)(2,1)S(1)} %gather.3), channel_id=1, source_target_pairs={{0,256},{256,0},{1,257},{257,1},{2,258},{258,2},{3,259},{259,3},{4... | collective-permute-start | bytes 786440 | tf_op jit(solution)/shard_map/ppermute | solution.py:427
  122.0 4.7 %collective-permute-start.11 = (bf16[256,256]{1,0:T(8,128)(2,1)S(1)}, bf16[256,256]{1,0:T(8,128)(2,1)S(1)}, u32[]{:S(2)}, u32[]{:S(2)}) collective-permute-start(bf16[256,256]{1,0:T(8,128)(2,1)S(1)} %add_convert_fusion), channel_id=1, source_target_pairs={{0,1},{1,0},{2,3},{3,2},{4,5},{5,4},{6,7},{7,6},{8,9},{9,8},{10,11... | collective-permute-start | bytes 393224 | tf_op jit(solution)/shard_map/ppermute | solution.py:427
  129.5 27.2 %all-to-all-start.2 = ((bf16[16,256,128]{2,1,0:T(8,128)(2,1)}), bf16[16,256,128]{2,1,0:T(8,128)(2,1)S(1)}, u32[]{:S(2)}, u32[]{:S(2)}) async-start(bf16[16,256,128]{2,1,0:T(8,128)(2,1)} %project.1), calls=%async_computation.2 | async-start | bytes 2097152 | tf_op jit(solution)/shard_map/all_to_all | solution.py:488

commit v6 on v5

v6 whole, which is shorter than its diff:
```python
from functools import partial

import jax
import jax.numpy as jnp
from jax import lax
from jax.experimental import pallas as pl
from jax.experimental.pallas import tpu as pltpu
from jax.sharding import Mesh, PartitionSpec as P

HEAD_DIM = 64
BLOCK = 128
AXES = ("xh", "zh", "par", "xl", "y", "core")
SIZES = (2, 8, 2, 2, 4, 2)
Z = ("zh", "par")
CTX = ("xh", "zh", "par")
HEAD = ("xl", "y", "core")
BIG = 1e30

OWN = (2, 0, -2, 4)
LATER = (3, 1, -1, -3)
SLOTS = OWN + LATER

VMEM = pl.BlockSpec(memory_space=pltpu.VMEM)
ANY = pl.BlockSpec(memory_space=pl.ANY)
SMEM = pl.BlockSpec(memory_space=pltpu.SMEM)


def cost(flops, exps):
    return pl.CostEstimate(flops=4 * flops, bytes_accessed=1 << 20, transcendentals=exps)


def dot_nt(a, b):
    return lax.dot_general(a, b, (((1,), (1,)), ((), ())), preferred_element_type=jnp.float32)


def dot_nn(a, b):
    return lax.dot_general(a, b, (((1,), (0,)), ((), ())), preferred_element_type=jnp.float32)


def split_heads(rows):
    low = lax.broadcasted_iota(jnp.int32, rows.shape, 1) < HEAD_DIM
    zero = jnp.zeros_like(rows)
    return jnp.concatenate([jnp.where(low, rows, zero), jnp.where(low, zero, rows)], axis=0)


def room(mib):
    return pltpu.CompilerParams(vmem_limit_bytes=mib << 20)


def in_hbm(*arrays):
    return [pltpu.with_memory_space_constraint(x, pltpu.HBM) for x in arrays]


def fetch(pairs, sems):
    copies = [pltpu.make_async_copy(source, target, sems.at[i]) for i, (source, target) in enumerate(pairs)]
    for copy in copies:
        copy.start()
    return copies


def stacked(pieces, held):
    at, pairs = 0, []
    for piece in pieces:
        pairs.append((piece, held.at[pl.ds(at, piece.shape[0])]))
        at += piece.shape[0]
    return pairs


def join_kernel(left, right, out, sems):
    width = left.shape[1]
    for copy in fetch([(left, out.at[:, pl.ds(0, width)]), (right, out.at[:, pl.ds(width, width)])], sems):
        copy.wait()


def join(left, right):
    return pl.pallas_call(
        join_kernel,
        out_shape=jax.ShapeDtypeStruct((left.shape[0], 2 * left.shape[1]), left.dtype),
        in_specs=[ANY] * 2,
        out_specs=VMEM,
        scratch_shapes=[pltpu.SemaphoreType.DMA((2,))],
        compiler_params=room(4),
        name="join",
    )(*in_hbm(left, right))


def load_targets(pieces, held):
    at = 0
    for piece in pieces:
        held[at : at + piece.shape[0], :] = piece[...]
        at += piece.shape[0]


def away(member, first, second, block, blocks):
    seg = (lax.broadcasted_iota(jnp.int32, (1, 4 * BLOCK), 1) // BLOCK) % 2
    one = jnp.where(member[first * blocks + block] > 0, 0.0, BIG)
    two = jnp.where(member[second * blocks + block] > 0, 0.0, BIG)
    return jnp.where(seg == 0, one, two)


def part_stats(kv, query, out, member, first, second, base, blocks):
    logits = dot_nt(kv[:, :BLOCK], query)
    prob = dot_nt(kv[:, BLOCK:], out)
    here = kv.shape[0] // BLOCK
    off = [away(member, first, second, base + b, blocks) for b in range(here)]
    peak = jnp.full((1, 4 * BLOCK), -1e3, jnp.float32)
    for b in range(here):
        part = logits[b * BLOCK : (b + 1) * BLOCK]
        peak = jnp.maximum(peak, jnp.max(part, axis=0, keepdims=True) - off[b])
    total = jnp.zeros((1, 4 * BLOCK), jnp.float32)
    weighted = jnp.zeros((1, 4 * BLOCK), jnp.float32)
    for b in range(here):
        part = slice(b * BLOCK, (b + 1) * BLOCK)
        raised = jnp.exp(logits[part] - (peak + off[b]))
        total = total + jnp.sum(raised, axis=0, keepdims=True)
        weighted = weighted + jnp.sum(raised * prob[part], axis=0, keepdims=True)
    some = total > 0.0
    log_total = jnp.where(some, peak + jnp.log(jnp.where(some, total, 1.0)), -BIG)
    mean = jnp.where(some, weighted / jnp.where(some, total, 1.0), 0.0)
    return log_total, mean


def union(parts):
    top = parts[0][0]
    for log, _ in parts[1:]:
        top = jnp.maximum(top, log)
    total = jnp.zeros_like(top)
    mean = jnp.zeros_like(top)
    for log, part in parts:
        weight = jnp.exp(log - top)
        total = total + weight
        mean = mean + weight * part
    return top + jnp.log(total), mean / total


def forward_kernel(base, places, member, near_ref, far_ref, *rest):
    *pieces, before, result, stats, held = rest
    load_targets(pieces, held)
    blocks = (near_ref.shape[0] + far_ref.shape[0]) // BLOCK
    pairs = held.shape[0] // (2 * BLOCK)
    half = stats.shape[0] // 2
    if before is not None:
        stats[...] = before[...]

    def step(p, carry):
        rows = pl.ds(pl.multiple_of(p * 2 * BLOCK, 2 * BLOCK), 2 * BLOCK)
        first, second = places[base + 2 * p], places[base + 2 * p + 1]
        query = split_heads(held[rows, :BLOCK])
        out = split_heads(held[rows, BLOCK:])
        log_total, mean = union(
            [
                part_stats(near_ref, query, out, member, first, second, 0, blocks),
                part_stats(far_ref, query, out, member, first, second, blocks // 2, blocks),
            ]
        )
        for h in range(2):
            for s, place in enumerate((first, second)):
                lanes = slice((2 * h + s) * BLOCK, (2 * h + s + 1) * BLOCK)
                stats[pl.ds(2 * place + h, 1), :] = log_total[:, lanes]
                stats[pl.ds(half + 2 * place + h, 1), :] = mean[:, lanes]
        return carry

    lax.fori_loop(0, pairs, step, 0)
    if result is not None:
        high = stats[:half, :].astype(jnp.bfloat16)
        low = (stats[:half, :] - high.astype(jnp.float32)).astype(jnp.bfloat16)
        message = jnp.concatenate([high, low, stats[half:, :].astype(jnp.bfloat16)], axis=0)
        for peer in range(result.shape[0]):
            result[peer] = message


def forward(base, places, member, near, far, pieces, before):
    count = places.shape[0]
    rows = sum(p.shape[0] for p in pieces)
    enc = near.shape[0] + far.shape[0]
    given = [places, member, near, far, *pieces]
    local = jax.ShapeDtypeStruct((4 * count, BLOCK), jnp.float32)
    if before is None:
        shapes = [local]
        def kernel(*refs):
            ins, outs = refs[: len(given)], refs[len(given) :]
            forward_kernel(base, *ins, None, None, *outs)
    else:
        given.append(before)
        shapes = [jax.ShapeDtypeStruct((count, 6 * count, BLOCK), jnp.bfloat16), local]
        kernel = partial(forward_kernel, base)
    return pl.pallas_call(
        kernel,
        out_shape=shapes,
        in_specs=[SMEM] * 2 + [VMEM] * (len(given) - 2),
        out_specs=[VMEM] * len(shapes),
        scratch_shapes=[pltpu.VMEM((rows, 2 * BLOCK), jnp.bfloat16)],
        compiler_params=room(20),
        cost_estimate=cost(2 * rows * enc * 4 * BLOCK, rows * enc * 2),
        name="forward",
    )(*given)


def merge_stats(parts, stats):
    rows = stats.shape[0] // 2
    given = []
    for i in range(parts.shape[0]):
        part = parts[i].astype(jnp.float32)
        given.append((part[:rows] + part[rows : 2 * rows], part[2 * rows :]))
    stats[:rows, :], stats[rows:, :] = union(given)


def lanes_of(stats, first, second, start):
    spots = [start + 2 * place + h for h in range(2) for place in (first, second)]
    return jnp.concatenate([stats[pl.ds(s, 1), :] for s in spots], axis=1)


def local_kernel(places, member, stats_ref, near_ref, far_ref, *rest):
    pieces = rest[:3]
    sums, chances, slopes, kv, held, stats, turned, sems = rest[3:]
    side, p = pl.program_id(0), pl.program_id(1)
    enc = near_ref.shape[0]

    @pl.when((side == 0) & (p == 0))
    def _():
        pairs = [(near_ref, kv.at[0]), (far_ref, kv.at[1]), *stacked(pieces, held), (stats_ref, stats)]
        for copy in fetch(pairs, sems):
            copy.wait()

    @pl.when(p == 0)
    def _():
        turned[...] = kv[side, :, :BLOCK].T

    blocks = enc // BLOCK
    half = stats.shape[0] // 2
    rows = pl.ds(pl.multiple_of(p * 2 * BLOCK, 2 * BLOCK), 2 * BLOCK)
    first, second = places[2 * p], places[2 * p + 1]
    log_total = lanes_of(stats, first, second, 0)
    log_total = jnp.where(log_total > -0.5 * BIG, log_total, BIG)
    mean = lanes_of(stats, first, second, half)
    logits = dot_nt(kv[side, :, :BLOCK], split_heads(held[rows, :BLOCK]))
    prob = dot_nt(kv[side, :, BLOCK:], split_heads(held[rows, BLOCK:]))
    for b in range(blocks):
        part = slice(b * BLOCK, (b + 1) * BLOCK)
        off = away(member, first, second, side * blocks + b, 2 * blocks)
        chance = jnp.exp(logits[part] - (log_total + off))
        chances[0, part, :] = chance.astype(jnp.bfloat16)
        slopes[0, part, :] = (chance * (prob[part] - mean)).astype(jnp.bfloat16)
    for i, table in enumerate((slopes, chances)):
        for h in range(2):
            dims = slice(h * HEAD_DIM, (h + 1) * HEAD_DIM)
            lanes = slice(2 * h * BLOCK, 2 * (h + 1) * BLOCK)
            sums[0, i, dims, :] = dot_nn(turned[dims, :], table[0, :, lanes])


def local(places, member, stats, near, far, pieces):
    rows = sum(p.shape[0] for p in pieces)
    enc = near.shape[0]
    pairs = rows // (2 * BLOCK)
    table = pltpu.HBM((2 * pairs, enc, 4 * BLOCK), jnp.bfloat16)
    given = in_hbm(places, member, stats, near, far, *pieces)
    return pl.pallas_call(
        local_kernel,
        grid=(2, pairs),
        out_shape=[pltpu.HBM((2 * pairs, 2, BLOCK, 2 * BLOCK), jnp.float32)] + [table] * 2,
        in_specs=[SMEM] * 2 + [ANY] * (len(given) - 2),
        out_specs=[pl.BlockSpec((1, 2, BLOCK, 2 * BLOCK), lambda side, p: (side * pairs + p, 0, 0, 0))]
        + [pl.BlockSpec((1, enc, 4 * BLOCK), lambda side, p: (side * pairs + p, 0, 0))] * 2,
        scratch_shapes=[
            pltpu.VMEM((2, enc, 2 * BLOCK), jnp.bfloat16),
            pltpu.VMEM((rows, 2 * BLOCK), jnp.bfloat16),
            pltpu.VMEM(stats.shape, stats.dtype),
            pltpu.VMEM((BLOCK, enc), jnp.bfloat16),
            pltpu.SemaphoreType.DMA((len(given) - 2,)),
        ],
        compiler_params=room(20),
        cost_estimate=cost(3 * rows * 2 * enc * 4 * BLOCK, rows * enc * 4),
        name="local",
    )(*given)


def scale_kernel(places, parts, stats_ref, sums_ref, *rest):
    pieces = rest[:3]
    d_query, scaled, held, whole, stats, sums, sems = rest[3:]
    copies = fetch(stacked(pieces, held) + [(stats_ref, stats), (sums_ref, sums)], sems)
    merge_stats(parts, whole)
    for copy in copies:
        copy.wait()
    half = stats.shape[0] // 2
    pairs = held.shape[0] // (2 * BLOCK)

    def step(p, carry):
        rows = pl.ds(pl.multiple_of(p * 2 * BLOCK, 2 * BLOCK), 2 * BLOCK)
        first, second = places[2 * p], places[2 * p + 1]
        share = jnp.exp(lanes_of(stats, first, second, 0) - lanes_of(whole, first, second, 0))
        shift = lanes_of(whole, first, second, half) - lanes_of(stats, first, second, half)

        def by_dim(row):
            head = (HEAD_DIM, 2 * BLOCK)
            return jnp.concatenate(
                [jnp.broadcast_to(row[:, h * 2 * BLOCK : (h + 1) * 2 * BLOCK], head) for h in range(2)], axis=0
            )

        share, shift = by_dim(share), by_dim(shift)
        slope = sums[p, 0] + sums[pairs + p, 0]
        chance = sums[p, 1] + sums[pairs + p, 1]
        grad = (share * (slope - shift * chance)).T.astype(jnp.bfloat16)
        d_query[first] = grad[:BLOCK]
        d_query[second] = grad[BLOCK:]
        share, shift = share.T, shift.T
        query = held[rows, :BLOCK].astype(jnp.float32) * share
        out = held[rows, BLOCK:].astype(jnp.float32) * share
        scaled[rows, :BLOCK] = out.astype(jnp.bfloat16)
        scaled[rows, BLOCK : 2 * BLOCK] = (-shift * query).astype(jnp.bfloat16)
        scaled[rows, 2 * BLOCK :] = query.astype(jnp.bfloat16)
        return carry

    lax.fori_loop(0, pairs, step, 0)


def scale(places, parts, stats, sums, pieces):
    count = places.shape[0]
    rows = sum(p.shape[0] for p in pieces)
    given = [*in_hbm(places), parts, *in_hbm(stats, sums, *pieces)]
    return pl.pallas_call(
        scale_kernel,
        out_shape=[
            pltpu.HBM((count, BLOCK, BLOCK), jnp.bfloat16),
            pltpu.HBM((rows, 3 * BLOCK), jnp.bfloat16),
        ],
        in_specs=[SMEM, VMEM] + [ANY] * (len(given) - 2),
        out_specs=[VMEM] * 2,
        scratch_shapes=[
            pltpu.VMEM((rows, 2 * BLOCK), jnp.bfloat16),
            pltpu.VMEM((4 * count, BLOCK), jnp.float32),
            pltpu.VMEM(stats.shape, stats.dtype),
            pltpu.VMEM(sums.shape, sums.dtype),
            pltpu.SemaphoreType.DMA((len(given) - 2,)),
        ],
        compiler_params=room(16),
        cost_estimate=cost(1 << 27, 1 << 16),
        name="scale",
    )(*given)


def gather_kernel(scaled, chance, slope, sent, d_key, d_value):
    p = pl.program_id(0)
    value = key = None
    for i in range(chance.shape[0]):
        rows = slice(2 * i * BLOCK, 2 * (i + 1) * BLOCK)
        out, lack, query = (split_heads(scaled[rows, j * BLOCK : (j + 1) * BLOCK]) for j in range(3))
        both = dot_nn(chance[i], jnp.concatenate([out, lack], axis=1))
        more, least = both[:, :BLOCK], both[:, BLOCK:] + dot_nn(slope[i], query)
        value, key = (more, least) if value is None else (value + more, key + least)

    @pl.when(p == 0)
    def _():
        d_value[...] = value
        d_key[...] = key

    @pl.when(p > 0)
    def _():
        d_value[...] += value
        d_key[...] += key

    @pl.when(p == pl.num_programs(0) - 1)
    def _():
        sent[:, :BLOCK] = d_key[...].astype(sent.dtype)
        sent[:, BLOCK:] = d_value[...].astype(sent.dtype)


def gather(scaled, chance, slope, side, kind):
    pairs, enc, lanes = chance.shape
    pairs, step = pairs // 2, 2
    steps = pairs // step
    table = pl.BlockSpec((step, enc, lanes), lambda p: (side * steps + p, 0, 0))
    given = in_hbm(scaled, chance, slope)
    return pl.pallas_call(
        gather_kernel,
        grid=(steps,),
        out_shape=jax.ShapeDtypeStruct((enc, 2 * BLOCK), kind),
        in_specs=[pl.BlockSpec((step * 2 * BLOCK, scaled.shape[1]), lambda p: (p, 0)), table, table],
        out_specs=VMEM,
        scratch_shapes=[pltpu.VMEM((enc, BLOCK), jnp.float32)] * 2,
        compiler_params=room(20),
        cost_estimate=cost(3 * pairs * enc * lanes * BLOCK, 0),
        name="gather",
    )(*given)


def project_kernel(core, chunk, grads, from_core, kw, vw, far_kw, far_vw, memory):
    rows = from_core.shape[0]
    mine = grads[pl.ds(pl.multiple_of(core[0] * rows, rows), rows), :]
    other = from_core[...]
    for j in range(memory.shape[0]):
        part = pl.ds(pl.multiple_of(chunk[j] * BLOCK, BLOCK), BLOCK)
        total = dot_nt(mine[:, :BLOCK], kw[part, :]) + dot_nt(mine[:, BLOCK:], vw[part, :])
        total = total + dot_nt(other[:, :BLOCK], far_kw[part, :]) + dot_nt(other[:, BLOCK:], far_vw[part, :])
        memory[j] = total.astype(jnp.bfloat16)


def project(core, chunk, *given):
    return pl.pallas_call(
        project_kernel,
        out_shape=jax.ShapeDtypeStruct((chunk.shape[0], given[1].shape[0], BLOCK), jnp.bfloat16),
        in_specs=[SMEM] * 2 + [VMEM] * len(given),
        out_specs=VMEM,
        compiler_params=room(8),
        name="project",
    )(core, chunk, *given)


def moved(value, axis, steps):
    count = lax.axis_size(axis)
    return lax.ppermute(value, axis, [(i, (i + steps) % count) for i in range(count)])


def body(queries, keys, values, d_out, key_weight, value_weight, block_lists):
    f32, bf16 = jnp.float32, jnp.bfloat16
    half = lax.axis_index("xh")
    place = lax.axis_index("zh")
    parity = lax.axis_index("par")
    core = lax.axis_index("core")
    depth = lax.axis_size(Z)
    enc_rows = keys.shape[0]
    enc_blocks = enc_rows // BLOCK

    near = join(queries, d_out)
    own = join(keys, values)
    ahead = moved(near, Z, 4)
    behind = moved(near, Z, -4)
    across = moved(near, Z, 8)
    own = jnp.concatenate([own, moved(own, "xh", 1)], axis=0)
    far = moved(own, "par", 1)

    count = lax.axis_size("zh")
    places = (place + jnp.asarray(SLOTS, jnp.int32)) % count
    listed = lax.dynamic_slice_in_dim(block_lists, half * depth, depth, 0).reshape(count, depth // count, -1)
    listed = lax.dynamic_index_in_dim(listed, parity, 1, keepdims=False)
    step = jnp.arange(enc_blocks, dtype=jnp.int32)
    ids = jnp.concatenate(
        [((h * count + place) * 2 + p) * enc_blocks + step for p in (parity, 1 - parity) for h in (half, 1 - half)]
    )
    member = jnp.any(listed[:, :, None] == ids[None, None, :], axis=1).astype(jnp.int32).reshape(-1)

    bundle = jnp.concatenate([behind, near, ahead, across], axis=0)
    above = moved(bundle[: 2 * BLOCK], Z, -2)
    below = moved(bundle[BLOCK : 3 * BLOCK], Z, 2)

    (early,) = forward(0, places, member, own, far, [bundle], None)
    parts, stats = forward(len(OWN), places, member, own, far, [above, below], early)
    pieces = [bundle, above, below]
    parts = lax.all_to_all(parts, "zh", 0, 0, tiled=True)
    sums, chances, slopes = local(places, member, stats, own, far, pieces)
    parts, sums, chances, slopes = lax.optimization_barrier((parts, sums, chances, slopes))

    d_query, scaled = scale(places, parts, stats, sums, pieces)
    from_next = moved(gather(scaled, chances, slopes, 1, bf16), "par", 1)
    grads = gather(scaled, chances, slopes, 0, f32)
    d_query = lax.all_to_all(d_query, "zh", 0, 0, tiled=True)
    grads, from_next, key_weight, value_weight = lax.optimization_barrier(
        (grads, from_next, key_weight, value_weight)
    )
    far_key_weight = moved(key_weight, "core", 1)
    far_value_weight = moved(value_weight, "core", 1)
    from_half = moved((grads[enc_rows:] + from_next[enc_rows:].astype(f32)).astype(bf16), "xh", 1)
    grads = grads[:enc_rows] + from_next[:enc_rows].astype(f32) + from_half.astype(f32)
    grads = grads.astype(bf16)
    from_core = moved(lax.dynamic_slice_in_dim(grads, (1 - core) * (enc_rows // 2), enc_rows // 2, 0), "core", 1)

    cores = lax.axis_size("core")
    chunk = jnp.arange(key_weight.shape[0] // BLOCK, dtype=jnp.int32)
    weights = (key_weight, value_weight, far_key_weight, far_value_weight)
    memory = project(core[None], chunk, grads, from_core, *weights)
    memory, d_query = lax.optimization_barrier((memory, d_query))
    memory = lax.all_to_all(memory, HEAD, 0, 0, tiled=True)
    memory = memory.reshape(-1, cores, *memory.shape[1:]).astype(f32)
    d_memory = jnp.sum(memory, axis=0).reshape(keys.shape).astype(bf16)
    d_queries = jnp.sum(d_query.astype(f32), axis=0).astype(bf16)
    return d_queries, d_memory


def solution(mesh):
    fine = Mesh(mesh.devices.reshape(SIZES), AXES)
    placed = P(CTX, HEAD)
    return jax.shard_map(
        body,
        mesh=fine,
        in_specs=(placed, placed, placed, placed, P(None, HEAD), P(None, HEAD), P()),
        out_specs=(placed, placed),
        check_vma=False,
    )
```

time: 158 us -> 154 us (0.975)
  starting transfers between devices: 86.9 us -> 80.8 us
  waiting for transfers between devices: 22.6 us -> 26.9 us
  Pallas kernels: 43.4 us -> 40.1 us
  other arithmetic: 2.75 us -> 4.56 us
    all_to_all x1, starting transfers between devices: 11.3 us -> 5.78 us  [body(): memory = lax.all_to_all(memory, HEAD, 0, 0, tiled=True)]
    ppermute x12, waiting for transfers between devices: 7.34 us -> 11.5 us  [moved(): lax.ppermute(value, axis, [(i, (i + steps) % count) for i in range(count)])]
    pallas_call x5, Pallas kernels: 33.4 us -> 31.3 us  [the longest x1 12.2 us: local(): pl.pallas_call(local_kernel, grid=(2, pairs), out_shape=[pltpu.HBM((2 * p...]
    convert_element_type x1 -> x2, other arithmetic: 0.03 us -> 1.97 us  [the longest x1 1.11 us: body(): grads = grads.astype(bf16)]
  transfers between devices with their start and end apart: 15 -> 15, of which waited for: 5 -> 5; matrix products, arithmetic and copies ran while one was open for 1% -> 3% of each run, Pallas kernels for 19% -> 16%
where the time goes in v6:
time: 154 us
  starting transfers between devices  80.8 us (52%)
  Pallas kernels  40.1 us (26%)
  waiting for transfers between devices  26.9 us (17%)
  other arithmetic  4.56 us (3%)
    ppermute x12, starting transfers between devices, moved(): lax.ppermute(value, axis, [(i, (i + steps) % count) for i in range(count)])  58.4 us
    all_to_all x1, waiting for transfers between devices, body(): memory = lax.all_to_all(memory, HEAD, 0, 0, tiled=True)  15.2 us
    pallas_call x1, Pallas kernels, local(): pl.pallas_call(local_kernel, grid=(2, pairs), out_shape=[pltpu.HBM((2 * p...  12.2 us
    ppermute x12, waiting for transfers between devices, moved(): lax.ppermute(value, axis, [(i, (i + steps) % count) for i in range(count)])  11.5 us
    all_to_all x1, starting transfers between devices, body(): d_query = lax.all_to_all(d_query, 'zh', 0, 0, tiled=True)  11.3 us
    pallas_call x2, Pallas kernels, gather(): pl.pallas_call(gather_kernel, grid=(steps,), out_shape=jax.ShapeDtypeStru...  10.4 us
    pallas_call x2, Pallas kernels, forward(): pl.pallas_call(kernel, out_shape=shapes, in_specs=[SMEM] * 2 + [VMEM] * (...  8.73 us
    all_to_all x1, starting transfers between devices, body(): memory = lax.all_to_all(memory, HEAD, 0, 0, tiled=True)  5.78 us
  transfers between devices with their start and end apart: 15, of which 5 were waited for; matrix products, arithmetic and copies ran while one was open for 3% of the time, Pallas kernels for 16%

profile of v6, /device:TPU:1, one launch (start us, length us, event | category | flops | bytes accessed | tf_op | source)
XLA Modules:
  0.0 153.6 jit_solution(12615795587439811496)
XLA Ops:
  0.6 0.0 copy-start
  0.6 0.8 join.3
  1.4 13.3 %collective-permute-start.2 = (bf16[128,256]{1,0:T(8,128)(2,1)S(1)}, bf16[128,256]{1,0:T(8,128)(2,1)S(1)}, u32[]{:S(2)}, u32[]{:S(2)}) collective-permute-start(bf16[128,256]{1,0:T(8,128)(2,1)S(1)} %join.3), channel_id=1, source_target_pairs={{0,192},{16,208},{32,224},{48,240},{64,0},{80,16},{96,32},{112,48}... | collective-permute-start | bytes 196616 | tf_op jit(solution)/shard_map/ppermute | solution.py:410
  14.7 1.9 %collective-permute-start.4 = (bf16[128,256]{1,0:T(8,128)(2,1)S(1)}, bf16[128,256]{1,0:T(8,128)(2,1)S(1)}, u32[]{:S(2)}, u32[]{:S(2)}) collective-permute-start(bf16[128,256]{1,0:T(8,128)(2,1)S(1)} %join.3), channel_id=1, source_target_pairs={{0,64},{16,80},{32,96},{48,112},{64,128},{80,144},{96,160},{112,17... | collective-permute-start | bytes 196616 | tf_op jit(solution)/shard_map/ppermute | solution.py:410
  16.7 10.3 %collective-permute-start.6 = (bf16[128,256]{1,0:T(8,128)(2,1)S(1)}, bf16[128,256]{1,0:T(8,128)(2,1)S(1)}, u32[]{:S(2)}, u32[]{:S(2)}) collective-permute-start(bf16[128,256]{1,0:T(8,128)(2,1)S(1)} %join.3), channel_id=1, source_target_pairs={{0,128},{16,144},{32,160},{48,176},{64,192},{80,208},{96,224},{112... | collective-permute-start | bytes 196616 | tf_op jit(solution)/shard_map/ppermute | solution.py:410
  26.9 1.0 join.2
  27.9 4.7 %collective-permute-start = (bf16[512,256]{1,0:T(8,128)(2,1)S(1)}, bf16[512,256]{1,0:T(8,128)(2,1)S(1)}, u32[]{:S(2)}, u32[]{:S(2)}) collective-permute-start(bf16[512,256]{1,0:T(8,128)(2,1)S(1)} %join.2), channel_id=1, source_target_pairs={{0,256},{256,0},{1,257},{257,1},{2,258},{258,2},{3,259},{259,3},{4... | collective-permute-start | bytes 786440 | tf_op jit(solution)/shard_map/ppermute | solution.py:410
  32.6 0.1 pad_add_fusion
  32.7 0.0 copy-done
  32.7 4.9 %collective-permute-done = bf16[512,256]{1,0:T(8,128)(2,1)S(1)} collective-permute-done((bf16[512,256]{1,0:T(8,128)(2,1)S(1)}, bf16[512,256]{1,0:T(8,128)(2,1)S(1)}, u32[]{:S(2)}, u32[]{:S(2)}) %collective-permute-start) | collective-permute-done | bytes 262176 | tf_op jit(solution)/shard_map/ppermute | solution.py:410
  37.6 0.0 copy-start.2
  37.7 2.6 %collective-permute-start.1 = (bf16[1024,256]{1,0:T(8,128)(2,1)S(1)}, bf16[1024,256]{1,0:T(8,128)(2,1)S(1)}, u32[]{:S(2)}, u32[]{:S(2)}) collective-permute-start(bf16[1024,256]{1,0:T(8,128)(2,1)S(1)} %pad_maximum_fusion.refs_2_.near_ref), channel_id=1, source_target_pairs={{0,16},{16,0},{1,17},{17,1},{2,18},{18,2},{3,19},{19,3},{4,20},{20... | collective-permute-start | bytes 1572872 | tf_op jit(solution)/shard_map/ppermute | solution.py:410
  40.3 0.7 and_select_fusion.refs_0_.places
  41.0 0.3 compare_reduce_fusion
  41.3 0.1 reshape.20.refs_1_.member
  41.4 0.0 collective-permute-done.2
  41.4 0.0 collective-permute-done.4
  41.4 2.2 %collective-permute-start.3 = (bf16[256,256]{1,0:T(8,128)(2,1)S(1)}, bf16[256,256]{1,0:T(8,128)(2,1)S(1)}, u32[]{:S(2)}, u32[]{:S(2)}) collective-permute-start(bf16[256,256]{1,0:T(8,128)(2,1)S(1)} %get-tuple-element.37), channel_id=1, source_target_pairs={{0,224},{16,240},{32,0},{48,16},{64,32},{80,48},{96,64},{112,80},{... | collective-permute-start | bytes 393224 | tf_op jit(solution)/shard_map/ppermute | solution.py:410
  43.6 4.0 %collective-permute-start.5 = (bf16[256,256]{1,0:T(8,128)(2,1)S(1)}, bf16[256,256]{1,0:T(8,128)(2,1)S(1)}, u32[]{:S(2)}, u32[]{:S(2)}) collective-permute-start(bf16[256,256]{1,0:T(8,128)(2,1)S(1)} %get-tuple-element.36), channel_id=1, source_target_pairs={{0,32},{16,48},{32,64},{48,80},{64,96},{80,112},{96,128},{112,144}... | collective-permute-start | bytes 393224 | tf_op jit(solution)/shard_map/ppermute | solution.py:410
  47.6 0.0 collective-permute-done.6
  47.6 0.0 copy-start.1
  47.7 5.7 %collective-permute-done.1.refs_3_.far_ref = bf16[1024,256]{1,0:T(8,128)(2,1)S(1)} collective-permute-done((bf16[1024,256]{1,0:T(8,128)(2,1)S(1)}, bf16[1024,256]{1,0:T(8,128)(2,1)S(1)}, u32[]{:S(2)}, u32[]{:S(2)}) %collective-permute-start.1) | collective-permute-done | bytes 524320 | tf_op jit(solution)/shard_map/ppermute | solution.py:410
  53.3 4.0 %forward.2.rest_2_ = f32[32,128]{1,0:T(8,128)S(1)} custom-call(s32[8]{0:T(128)S(1)} %and_select_fusion.refs_0_.places, s32[128]{0:T(128)S(1)} %reshape.20.refs_1_.member, bf16[1024,256]{1,0:T(8,128)(2,1)S(1)} %pad_maximum_fusion.refs_2_.near_ref, bf16[1024,256]{1,0:T(8,128)(2,1)S(1)} %collective-permute-done.1.refs_3_.far_ref, ...), custom_call_target="tpu_custom_call" | custom-call | flops 4294967296 | bytes 1048576 | tf_op jit(solution)/shard_map/forward/pallas_call | solution.py:187
  57.4 0.0 collective-permute-done.3.rest_0_.rest_1_
  57.4 0.0 copy-start.5
  57.4 0.0 collective-permute-done.5.rest_1_.rest_2_
  57.4 0.0 copy-done.2
  57.4 0.0 copy-done.8
  57.4 0.0 copy-done.9
  57.4 0.0 copy-start.6
  57.5 4.7 %forward.3 = (bf16[8,48,128]{2,1,0:T(8,128)(2,1)}, f32[32,128]{1,0:T(8,128)S(1)}) custom-call(s32[8]{0:T(128)S(1)} %and_select_fusion.refs_0_.places, s32[128]{0:T(128)S(1)} %reshape.20.refs_1_.member, bf16[1024,256]{1,0:T(8,128)(2,1)S(1)} %pad_maximum_fusion.refs_2_.near_ref, bf16[1024,256]{1,0:T(8,128)(2,1)S(1)} %collective-permute-done.1.refs_3_.far_ref, ...), custom_call_target="tpu_custom_call" | custom-call | flops 4294967296 | bytes 1048576 | tf_op jit(solution)/shard_map/forward/pallas_call | solution.py:187
  62.2 0.0 copy-done.1
  62.2 0.0 copy-done.10
  62.2 5.3 %all-to-all-start = ((bf16[8,48,128]{2,1,0:T(8,128)(2,1)}), bf16[8,48,128]{2,1,0:T(8,128)(2,1)S(1)}, u32[]{:S(2)}, u32[]{:S(2)}) async-start(bf16[8,48,128]{2,1,0:T(8,128)(2,1)} %get-tuple-element.19), calls=%async_computation | async-start | bytes 196608 | tf_op jit(solution)/shard_map/all_to_all | solution.py:448
  67.4 0.0 copy-done.5
  67.4 0.0 copy-done.6
  67.5 0.0 copy-done.7
  67.5 12.2 %local.1 = (f32[8,2,128,256]{3,2,1,0:T(8,128)}, bf16[8,1024,512]{2,1,0:T(8,128)(2,1)}, bf16[8,1024,512]{2,1,0:T(8,128)(2,1)}) custom-call(s32[8]{0:T(128)} %copy-done.8, s32[128]{0:T(128)} %copy-done.9, f32[32,128]{1,0:T(8,128)} %copy-done.7, bf16[1024,256]{1,0:T(8,128)(2,1)} %copy-done.2, bf16[1024,256]{1,0:T(8,128)(2,1)} %copy-done.10, ...), custom_call_target="tpu_custom_call" | custom-call | flops 12884901888 | bytes 1048576 | tf_op jit(solution)/shard_map/local/pallas_call | solution.py:257
  79.6 0.2 all-to-all-done.parts
  79.8 4.2 %scale.1 = (bf16[8,128,128]{2,1,0:T(8,128)(2,1)}, bf16[1024,384]{1,0:T(8,128)(2,1)}) custom-call(s32[8]{0:T(128)} %copy-done.8, bf16[8,48,128]{2,1,0:T(8,128)(2,1)S(1)} %all-to-all-done.parts, f32[32,128]{1,0:T(8,128)} %copy-done.7, f32[8,2,128,256]{3,2,1,0:T(8,128)} %get-tuple-element.25.sums_ref, bf16[512,256]{1,0:T(8,128)(2,1)} %copy-done.1, ...), custom_call_target="tpu_custom_call" | custom-call | flops 536870912 | bytes 1048576 | tf_op jit(solution)/shard_map/scale/pallas_call | solution.py:320
  84.0 5.2 %gather.3 = bf16[1024,256]{1,0:T(8,128)(2,1)S(1)} custom-call(bf16[1024,384]{1,0:T(8,128)(2,1)} %get-tuple-element.26.scaled, bf16[8,1024,512]{2,1,0:T(8,128)(2,1)} %get-tuple-element.27.chance, bf16[8,1024,512]{2,1,0:T(8,128)(2,1)} %get-tuple-element.28.slope), custom_call_target="tpu_custom_call" | custom-call | flops 3221225472 | bytes 1048576 | tf_op jit(solution)/shard_map/gather/pallas_call | solution.py:373
  89.2 1.9 %collective-permute-start.7 = (bf16[1024,256]{1,0:T(8,128)(2,1)S(1)}, bf16[1024,256]{1,0:T(8,128)(2,1)S(1)}, u32[]{:S(2)}, u32[]{:S(2)}) collective-permute-start(bf16[1024,256]{1,0:T(8,128)(2,1)S(1)} %gather.3), channel_id=1, source_target_pairs={{0,16},{16,0},{1,17},{17,1},{2,18},{18,2},{3,19},{19,3},{4,20},{20... | collective-permute-start | bytes 1572872 | tf_op jit(solution)/shard_map/ppermute | solution.py:410
  91.2 11.3 %all-to-all-start.1 = ((bf16[8,128,128]{2,1,0:T(8,128)(2,1)}), bf16[8,128,128]{2,1,0:T(8,128)(2,1)S(1)}, u32[]{:S(2)}, u32[]{:S(2)}) async-start(bf16[8,128,128]{2,1,0:T(8,128)(2,1)} %get-tuple-element.33), calls=%async_computation.1 | async-start | bytes 524288 | tf_op jit(solution)/shard_map/all_to_all | solution.py:455
  102.4 0.0 copy-start.4
  102.5 5.2 %gather.2 = f32[1024,256]{1,0:T(8,128)S(1)} custom-call(bf16[1024,384]{1,0:T(8,128)(2,1)} %get-tuple-element.26.scaled, bf16[8,1024,512]{2,1,0:T(8,128)(2,1)} %get-tuple-element.27.chance, bf16[8,1024,512]{2,1,0:T(8,128)(2,1)} %get-tuple-element.28.slope), custom_call_target="tpu_custom_call" | custom-call | flops 3221225472 | bytes 1048576 | tf_op jit(solution)/shard_map/gather/pallas_call | solution.py:373
  107.7 0.0 collective-permute-done.7
  107.7 0.9 add_convert_fusion.1
  108.6 4.6 %collective-permute-start.8 = (bf16[512,256]{1,0:T(8,128)(2,1)}, bf16[512,256]{1,0:T(8,128)(2,1)}, u32[]{:S(2)}, u32[]{:S(2)}) collective-permute-start(bf16[512,256]{1,0:T(8,128)(2,1)} %add_convert_fusion.1), channel_id=1, source_target_pairs={{0,256},{256,0},{1,257},{257,1},{2,258},{258,2},{3,259},{259,3},{4... | collective-permute-start | bytes 786440 | tf_op jit(solution)/shard_map/ppermute | solution.py:410
  113.2 0.0 copy-done.11
  113.2 0.0 copy-done.3
  113.2 7.8 %collective-permute-start.10 = (bf16[2048,128]{1,0:T(8,128)(2,1)S(1)}, bf16[2048,128]{1,0:T(8,128)(2,1)S(1)}, u32[]{:S(2)}, u32[]{:S(2)}) collective-permute-start(bf16[2048,128]{1,0:T(8,128)(2,1)S(1)} %copy-done.3), channel_id=1, source_target_pairs={{0,1},{1,0},{2,3},{3,2},{4,5},{5,4},{6,7},{7,6},{8,9},{9,8},{10,11... | collective-permute-start | bytes 1572872 | tf_op jit(solution)/shard_map/ppermute | solution.py:410
  121.1 1.9 %collective-permute-start.11 = (bf16[2048,128]{1,0:T(8,128)(2,1)S(1)}, bf16[2048,128]{1,0:T(8,128)(2,1)S(1)}, u32[]{:S(2)}, u32[]{:S(2)}) collective-permute-start(bf16[2048,128]{1,0:T(8,128)(2,1)S(1)} %copy-done.4), channel_id=1, source_target_pairs={{0,1},{1,0},{2,3},{3,2},{4,5},{5,4},{6,7},{7,6},{8,9},{9,8},{10,11... | collective-permute-start | bytes 1572872 | tf_op jit(solution)/shard_map/ppermute | solution.py:410
  123.0 0.0 collective-permute-done.8
  123.0 1.1 add_convert_fusion.grads
  124.2 3.2 %collective-permute-start.9 = (bf16[256,256]{1,0:T(8,128)(2,1)S(1)}, bf16[256,256]{1,0:T(8,128)(2,1)S(1)}, u32[]{:S(2)}, u32[]{:S(2)}) collective-permute-start(bf16[256,256]{1,0:T(8,128)(2,1)S(1)} %constant_dynamic-slice_fusion), channel_id=1, source_target_pairs={{0,1},{1,0},{2,3},{3,2},{4,5},{5,4},{6,7},{7,6},{8,9},{9,8},{10,11... | collective-permute-start | bytes 393224 | tf_op jit(solution)/shard_map/ppermute | solution.py:410
  127.3 1.0 collective-permute-done.9.from_core
  128.3 0.0 collective-permute-done.10.far_kw
  128.3 0.0 collective-permute-done.11.far_vw
  128.3 2.8 %project.1 = bf16[16,256,128]{2,1,0:T(8,128)(2,1)} custom-call(s32[1]{0:T(128)} %bitcast.core, s32[16]{0:T(128)S(1)} %iota.12.chunk, bf16[512,256]{1,0:T(8,128)(2,1)S(1)} %add_convert_fusion.grads, bf16[256,256]{1,0:T(8,128)(2,1)S(1)} %collective-permute-done.9.from_core, bf16[2048,128]{1,0:T(8,128)(2,1)S(1)} %copy-done.3, bf16[2048,128]{1,0:T(8,128)(2,1)S(1)} %copy-done.4, ...), custom_call_target="tpu_custom_call" | custom-call | tf_op jit(solution)/shard_map/project/pallas_call | solution.py:398
  131.2 0.0 all-to-all-done.1
  131.2 5.8 %all-to-all-start.2 = ((bf16[16,256,128]{2,1,0:T(8,128)(2,1)}), bf16[16,256,128]{2,1,0:T(8,128)(2,1)S(1)}, u32[]{:S(2)}, u32[]{:S(2)}) async-start(bf16[16,256,128]{2,1,0:T(8,128)(2,1)} %project.1), calls=%async_computation.2 | async-start | bytes 2097152 | tf_op jit(solution)/shard_map/all_to_all | solution.py:471
  136.9 0.7 reduce_sum.21
  137.6 15.2 %all-to-all-done.2 = bf16[16,256,128]{2,1,0:T(8,128)(2,1)S(1)} async-done(((bf16[16,256,128]{2,1,0:T(8,128)(2,1)}), bf16[16,256,128]{2,1,0:T(8,128)(2,1)S(1)}, u32[]{:S(2)}, u32[]{:S(2)}) %all-to-all-start.2) | async-done | bytes 1048608 | tf_op jit(solution)/shard_map/all_to_all | solution.py:471
  152.8 0.8 reduce.1
  (17 shorter events, 0.1 us)
Async XLA Ops:
  0.6 32.1 %copy-start = (s32[32,64]{1,0:T(8,128)S(1)}, s32[32,64]{1,0:T(8,128)}, u32[]{:S(2)}) copy-start(s32[32,64]{1,0:T(8,128)} %param.14) | copy-start | bytes 24580
  1.4 39.9 %collective-permute-start.2 = (bf16[128,256]{1,0:T(8,128)(2,1)S(1)}, bf16[128,256]{1,0:T(8,128)(2,1)S(1)}, u32[]{:S(2)}, u32[]{:S(2)}) collective-permute-start(bf16[128,256]{1,0:T(8,128)(2,1)S(1)} %join.3), channel_id=1, source_target_pairs={{0,192},{16,208},{32,224},{48,240},{64,0},{80,16},{96,32},{112,48}... | collective-permute-start | bytes 196616 | tf_op jit(solution)/shard_map/ppermute | solution.py:410
  14.7 26.6 %collective-permute-start.4 = (bf16[128,256]{1,0:T(8,128)(2,1)S(1)}, bf16[128,256]{1,0:T(8,128)(2,1)S(1)}, u32[]{:S(2)}, u32[]{:S(2)}) collective-permute-start(bf16[128,256]{1,0:T(8,128)(2,1)S(1)} %join.3), channel_id=1, source_target_pairs={{0,64},{16,80},{32,96},{48,112},{64,128},{80,144},{96,160},{112,17... | collective-permute-start | bytes 196616 | tf_op jit(solution)/shard_map/ppermute | solution.py:410
  16.7 30.9 %collective-permute-start.6 = (bf16[128,256]{1,0:T(8,128)(2,1)S(1)}, bf16[128,256]{1,0:T(8,128)(2,1)S(1)}, u32[]{:S(2)}, u32[]{:S(2)}) collective-permute-start(bf16[128,256]{1,0:T(8,128)(2,1)S(1)} %join.3), channel_id=1, source_target_pairs={{0,128},{16,144},{32,160},{48,176},{64,192},{80,208},{96,224},{112... | collective-permute-start | bytes 196616 | tf_op jit(solution)/shard_map/ppermute | solution.py:410
  27.9 9.7 %collective-permute-start = (bf16[512,256]{1,0:T(8,128)(2,1)S(1)}, bf16[512,256]{1,0:T(8,128)(2,1)S(1)}, u32[]{:S(2)}, u32[]{:S(2)}) collective-permute-start(bf16[512,256]{1,0:T(8,128)(2,1)S(1)} %join.2), channel_id=1, source_target_pairs={{0,256},{256,0},{1,257},{257,1},{2,258},{258,2},{3,259},{259,3},{4... | collective-permute-start | bytes 786440 | tf_op jit(solution)/shard_map/ppermute | solution.py:410
  37.6 19.8 %copy-start.2 = (bf16[1024,256]{1,0:T(8,128)(2,1)}, bf16[1024,256]{1,0:T(8,128)(2,1)S(1)}, u32[]{:S(2)}) copy-start(bf16[1024,256]{1,0:T(8,128)(2,1)S(1)} %pad_maximum_fusion.refs_2_.near_ref) | copy-start | bytes 1572868
  37.7 15.7 %collective-permute-start.1 = (bf16[1024,256]{1,0:T(8,128)(2,1)S(1)}, bf16[1024,256]{1,0:T(8,128)(2,1)S(1)}, u32[]{:S(2)}, u32[]{:S(2)}) collective-permute-start(bf16[1024,256]{1,0:T(8,128)(2,1)S(1)} %pad_maximum_fusion.refs_2_.near_ref), channel_id=1, source_target_pairs={{0,16},{16,0},{1,17},{17,1},{2,18},{18,2},{3,19},{19,3},{4,20},{20... | collective-permute-start | bytes 1572872 | tf_op jit(solution)/shard_map/ppermute | solution.py:410
  41.0 16.4 %copy-start.8 = (s32[8]{0:T(128)}, s32[8]{0:T(128)S(1)}, u32[]{:S(2)}) copy-start(s32[8]{0:T(128)S(1)} %and_select_fusion.refs_0_.places) | copy-start | bytes 100
  41.4 16.1 %copy-start.9 = (s32[128]{0:T(128)}, s32[128]{0:T(128)S(1)}, u32[]{:S(2)}) copy-start(s32[128]{0:T(128)S(1)} %reshape.20.refs_1_.member) | copy-start | bytes 1540
  41.4 16.0 %collective-permute-start.3 = (bf16[256,256]{1,0:T(8,128)(2,1)S(1)}, bf16[256,256]{1,0:T(8,128)(2,1)S(1)}, u32[]{:S(2)}, u32[]{:S(2)}) collective-permute-start(bf16[256,256]{1,0:T(8,128)(2,1)S(1)} %get-tuple-element.37), channel_id=1, source_target_pairs={{0,224},{16,240},{32,0},{48,16},{64,32},{80,48},{96,64},{112,80},{... | collective-permute-start | bytes 393224 | tf_op jit(solution)/shard_map/ppermute | solution.py:410
  43.6 13.8 %collective-permute-start.5 = (bf16[256,256]{1,0:T(8,128)(2,1)S(1)}, bf16[256,256]{1,0:T(8,128)(2,1)S(1)}, u32[]{:S(2)}, u32[]{:S(2)}) collective-permute-start(bf16[256,256]{1,0:T(8,128)(2,1)S(1)} %get-tuple-element.36), channel_id=1, source_target_pairs={{0,32},{16,48},{32,64},{48,80},{64,96},{80,112},{96,128},{112,144}... | collective-permute-start | bytes 393224 | tf_op jit(solution)/shard_map/ppermute | solution.py:410
  47.6 14.5 %copy-start.1 = (bf16[512,256]{1,0:T(8,128)(2,1)}, bf16[512,256]{1,0:T(8,128)(2,1)S(1)}, u32[]{:S(2)}) copy-start(bf16[512,256]{1,0:T(8,128)(2,1)S(1)} %pad_maximum_fusion.1.refs_4_.rest_0_) | copy-start | bytes 786436
  53.3 8.8 %copy-start.10 = (bf16[1024,256]{1,0:T(8,128)(2,1)}, bf16[1024,256]{1,0:T(8,128)(2,1)S(1)}, u32[]{:S(2)}) copy-start(bf16[1024,256]{1,0:T(8,128)(2,1)S(1)} %collective-permute-done.1.refs_3_.far_ref) | copy-start | bytes 1572868
  57.4 10.0 %copy-start.5 = (bf16[256,256]{1,0:T(8,128)(2,1)}, bf16[256,256]{1,0:T(8,128)(2,1)S(1)}, u32[]{:S(2)}) copy-start(bf16[256,256]{1,0:T(8,128)(2,1)S(1)} %collective-permute-done.3.rest_0_.rest_1_) | copy-start | bytes 393220
  57.4 10.0 %copy-start.6 = (bf16[256,256]{1,0:T(8,128)(2,1)}, bf16[256,256]{1,0:T(8,128)(2,1)S(1)}, u32[]{:S(2)}) copy-start(bf16[256,256]{1,0:T(8,128)(2,1)S(1)} %collective-permute-done.5.rest_1_.rest_2_) | copy-start | bytes 393220
  62.2 5.3 %copy-start.7 = (f32[32,128]{1,0:T(8,128)}, f32[32,128]{1,0:T(8,128)S(1)}, u32[]{:S(2)}) copy-start(f32[32,128]{1,0:T(8,128)S(1)} %get-tuple-element.20.stats_ref) | copy-start | bytes 49156
  62.2 17.7 %all-to-all-start = ((bf16[8,48,128]{2,1,0:T(8,128)(2,1)}), bf16[8,48,128]{2,1,0:T(8,128)(2,1)S(1)}, u32[]{:S(2)}, u32[]{:S(2)}) async-start(bf16[8,48,128]{2,1,0:T(8,128)(2,1)} %get-tuple-element.19), calls=%async_computation | async-start | bytes 196608 | tf_op jit(solution)/shard_map/all_to_all | solution.py:448
  89.2 18.5 %collective-permute-start.7 = (bf16[1024,256]{1,0:T(8,128)(2,1)S(1)}, bf16[1024,256]{1,0:T(8,128)(2,1)S(1)}, u32[]{:S(2)}, u32[]{:S(2)}) collective-permute-start(bf16[1024,256]{1,0:T(8,128)(2,1)S(1)} %gather.3), channel_id=1, source_target_pairs={{0,16},{16,0},{1,17},{17,1},{2,18},{18,2},{3,19},{19,3},{4,20},{20... | collective-permute-start | bytes 1572872 | tf_op jit(solution)/shard_map/ppermute | solution.py:410
  91.2 40.0 %all-to-all-start.1 = ((bf16[8,128,128]{2,1,0:T(8,128)(2,1)}), bf16[8,128,128]{2,1,0:T(8,128)(2,1)S(1)}, u32[]{:S(2)}, u32[]{:S(2)}) async-start(bf16[8,128,128]{2,1,0:T(8,128)(2,1)} %get-tuple-element.33), calls=%async_computation.1 | async-start | bytes 524288 | tf_op jit(solution)/shard_map/all_to_all | solution.py:455
  102.4 10.8 %copy-start.3 = (bf16[2048,128]{1,0:T(8,128)(2,1)S(1)}, bf16[2048,128]{1,0:T(8,128)(2,1)}, u32[]{:S(2)}) copy-start(bf16[2048,128]{1,0:T(8,128)(2,1)} %kw) | copy-start | bytes 1572868
  102.4 18.6 %copy-start.4 = (bf16[2048,128]{1,0:T(8,128)(2,1)S(1)}, bf16[2048,128]{1,0:T(8,128)(2,1)}, u32[]{:S(2)}) copy-start(bf16[2048,128]{1,0:T(8,128)(2,1)} %vw) | copy-start | bytes 1572868
  107.7 5.5 %copy-start.11 = (bf16[1024,256]{1,0:T(8,128)(2,1)}, bf16[1024,256]{1,0:T(8,128)(2,1)S(1)}, u32[]{:S(2)}) copy-start(bf16[1024,256]{1,0:T(8,128)(2,1)S(1)} %collective-permute-done.7) | copy-start | bytes 1572868
  108.6 14.4 %collective-permute-start.8 = (bf16[512,256]{1,0:T(8,128)(2,1)}, bf16[512,256]{1,0:T(8,128)(2,1)}, u32[]{:S(2)}, u32[]{:S(2)}) collective-permute-start(bf16[512,256]{1,0:T(8,128)(2,1)} %add_convert_fusion.1), channel_id=1, source_target_pairs={{0,256},{256,0},{1,257},{257,1},{2,258},{258,2},{3,259},{259,3},{4... | collective-permute-start | bytes 786440 | tf_op jit(solution)/shard_map/ppermute | solution.py:410
  113.2 15.1 %collective-permute-start.10 = (bf16[2048,128]{1,0:T(8,128)(2,1)S(1)}, bf16[2048,128]{1,0:T(8,128)(2,1)S(1)}, u32[]{:S(2)}, u32[]{:S(2)}) collective-permute-start(bf16[2048,128]{1,0:T(8,128)(2,1)S(1)} %copy-done.3), channel_id=1, source_target_pairs={{0,1},{1,0},{2,3},{3,2},{4,5},{5,4},{6,7},{7,6},{8,9},{9,8},{10,11... | collective-permute-start | bytes 1572872 | tf_op jit(solution)/shard_map/ppermute | solution.py:410
  121.1 7.2 %collective-permute-start.11 = (bf16[2048,128]{1,0:T(8,128)(2,1)S(1)}, bf16[2048,128]{1,0:T(8,128)(2,1)S(1)}, u32[]{:S(2)}, u32[]{:S(2)}) collective-permute-start(bf16[2048,128]{1,0:T(8,128)(2,1)S(1)} %copy-done.4), channel_id=1, source_target_pairs={{0,1},{1,0},{2,3},{3,2},{4,5},{5,4},{6,7},{7,6},{8,9},{9,8},{10,11... | collective-permute-start | bytes 1572872 | tf_op jit(solution)/shard_map/ppermute | solution.py:410
  124.2 4.1 %collective-permute-start.9 = (bf16[256,256]{1,0:T(8,128)(2,1)S(1)}, bf16[256,256]{1,0:T(8,128)(2,1)S(1)}, u32[]{:S(2)}, u32[]{:S(2)}) collective-permute-start(bf16[256,256]{1,0:T(8,128)(2,1)S(1)} %constant_dynamic-slice_fusion), channel_id=1, source_target_pairs={{0,1},{1,0},{2,3},{3,2},{4,5},{5,4},{6,7},{7,6},{8,9},{9,8},{10,11... | collective-permute-start | bytes 393224 | tf_op jit(solution)/shard_map/ppermute | solution.py:410
  131.2 21.6 %all-to-all-start.2 = ((bf16[16,256,128]{2,1,0:T(8,128)(2,1)}), bf16[16,256,128]{2,1,0:T(8,128)(2,1)S(1)}, u32[]{:S(2)}, u32[]{:S(2)}) async-start(bf16[16,256,128]{2,1,0:T(8,128)(2,1)} %project.1), calls=%async_computation.2 | async-start | bytes 2097152 | tf_op jit(solution)/shard_map/all_to_all | solution.py:471

commit v7 on v6

--- a/solution.py
+++ b/solution.py
@@ -133,10 +133,13 @@
     return top + jnp.log(total), mean / total
 
 
-def forward_kernel(base, places, member, near_ref, far_ref, *rest):
-    *pieces, before, result, stats, held = rest
+def forward_kernel(base, places, member, *rest):
+    tables = rest[:4]
+    *pieces, before, result, stats, held, kv = rest[4:]
     load_targets(pieces, held)
-    blocks = (near_ref.shape[0] + far_ref.shape[0]) // BLOCK
+    load_targets(tables[:2], kv.at[0])
+    load_targets(tables[2:], kv.at[1])
+    blocks = 2 * kv.shape[1] // BLOCK
     pairs = held.shape[0] // (2 * BLOCK)
     half = stats.shape[0] // 2
     if before is not None:
@@ -149,8 +152,8 @@
         out = split_heads(held[rows, BLOCK:])
         log_total, mean = union(
             [
-                part_stats(near_ref, query, out, member, first, second, 0, blocks),
-                part_stats(far_ref, query, out, member, first, second, blocks // 2, blocks),
+                part_stats(kv.at[0], query, out, member, first, second, 0, blocks),
+                part_stats(kv.at[1], query, out, member, first, second, blocks // 2, blocks),
             ]
         )
         for h in range(2):
@@ -169,11 +172,11 @@
             result[peer] = message
 
 
-def forward(base, places, member, near, far, pieces, before):
+def forward(base, places, member, tables, pieces, before):
     count = places.shape[0]
     rows = sum(p.shape[0] for p in pieces)
-    enc = near.shape[0] + far.shape[0]
-    given = [places, member, near, far, *pieces]
+    enc = sum(t.shape[0] for t in tables)
+    given = [places, member, *tables, *pieces]
     local = jax.ShapeDtypeStruct((4 * count, BLOCK), jnp.float32)
     if before is None:
         shapes = [local]
@@ -189,7 +192,10 @@
         out_shape=shapes,
         in_specs=[SMEM] * 2 + [VMEM] * (len(given) - 2),
         out_specs=[VMEM] * len(shapes),
-        scratch_shapes=[pltpu.VMEM((rows, 2 * BLOCK), jnp.bfloat16)],
+        scratch_shapes=[
+            pltpu.VMEM((rows, 2 * BLOCK), jnp.bfloat16),
+            pltpu.VMEM((2, enc // 2, 2 * BLOCK), jnp.bfloat16),
+        ],
         compiler_params=room(20),
         cost_estimate=cost(2 * rows * enc * 4 * BLOCK, rows * enc * 2),
         name="forward",
@@ -210,15 +216,16 @@
     return jnp.concatenate([stats[pl.ds(s, 1), :] for s in spots], axis=1)
 
 
-def local_kernel(places, member, stats_ref, near_ref, far_ref, *rest):
-    pieces = rest[:3]
-    sums, chances, slopes, kv, held, stats, turned, sems = rest[3:]
+def local_kernel(places, member, stats_ref, *rest):
+    tables, pieces = rest[:4], rest[4:7]
+    sums, chances, slopes, kv, held, stats, turned, sems = rest[7:]
     side, p = pl.program_id(0), pl.program_id(1)
-    enc = near_ref.shape[0]
+    enc = kv.shape[1]
 
     @pl.when((side == 0) & (p == 0))
     def _():
-        pairs = [(near_ref, kv.at[0]), (far_ref, kv.at[1]), *stacked(pieces, held), (stats_ref, stats)]
+        pairs = stacked(tables[:2], kv.at[0]) + stacked(tables[2:], kv.at[1])
+        pairs += stacked(pieces, held) + [(stats_ref, stats)]
         for copy in fetch(pairs, sems):
             copy.wait()
 
@@ -248,12 +255,12 @@
             sums[0, i, dims, :] = dot_nn(turned[dims, :], table[0, :, lanes])
 
 
-def local(places, member, stats, near, far, pieces):
+def local(places, member, stats, tables, pieces):
     rows = sum(p.shape[0] for p in pieces)
-    enc = near.shape[0]
+    enc = sum(t.shape[0] for t in tables) // 2
     pairs = rows // (2 * BLOCK)
     table = pltpu.HBM((2 * pairs, enc, 4 * BLOCK), jnp.bfloat16)
-    given = in_hbm(places, member, stats, near, far, *pieces)
+    given = in_hbm(places, member, stats, *tables, *pieces)
     return pl.pallas_call(
         local_kernel,
         grid=(2, pairs),
@@ -421,12 +428,17 @@
     enc_blocks = enc_rows // BLOCK
 
     near = join(queries, d_out)
-    own = join(keys, values)
     ahead = moved(near, Z, 4)
     behind = moved(near, Z, -4)
     across = moved(near, Z, 8)
-    own = jnp.concatenate([own, moved(own, "xh", 1)], axis=0)
-    far = moved(own, "par", 1)
+    own = join(keys, values)
+    late, ahead, behind = lax.optimization_barrier((own, ahead, behind))
+    tables = [
+        own,
+        moved(own, "xh", 1),
+        moved(own, "par", 1),
+        lax.ppermute(late, ("xh", "par"), [(0, 3), (1, 2), (2, 1), (3, 0)]),
+    ]
 
     count = lax.axis_size("zh")
     places = (place + jnp.asarray(SLOTS, jnp.int32)) % count
@@ -442,16 +454,17 @@
     above = moved(bundle[: 2 * BLOCK], Z, -2)
     below = moved(bundle[BLOCK : 3 * BLOCK], Z, 2)
 
-    (early,) = forward(0, places, member, own, far, [bundle], None)
-    parts, stats = forward(len(OWN), places, member, own, far, [above, below], early)
+    (early,) = forward(0, places, member, tables, [bundle], None)
+    parts, stats = forward(len(OWN), places, member, tables, [above, below], early)
     pieces = [bundle, above, below]
     parts = lax.all_to_all(parts, "zh", 0, 0, tiled=True)
-    sums, chances, slopes = local(places, member, stats, own, far, pieces)
+    sums, chances, slopes = local(places, member, stats, tables, pieces)
     parts, sums, chances, slopes = lax.optimization_barrier((parts, sums, chances, slopes))
 
     d_query, scaled = scale(places, parts, stats, sums, pieces)
     from_next = moved(gather(scaled, chances, slopes, 1, bf16), "par", 1)
     grads = gather(scaled, chances, slopes, 0, f32)
+    d_query, grads = lax.optimization_barrier((d_query, grads))
     d_query = lax.all_to_all(d_query, "zh", 0, 0, tiled=True)
     grads, from_next, key_weight, value_weight = lax.optimization_barrier(
         (grads, from_next, key_weight, value_weight)

time: 154 us -> 150 us (0.974)
  waiting for transfers between devices: 26.9 us -> 20 us
  starting transfers between devices: 80.8 us -> 83.3 us
    ppermute x12, waiting for transfers between devices: 11.5 us -> 0.99 us  [moved(): lax.ppermute(value, axis, [(i, (i + steps) % count) for i in range(count)])]
    ppermute x0 -> x1, waiting for transfers between devices: none -> 3.49 us  [body(): lax.ppermute(late, ('xh', 'par'), [(0, 3), (1, 2), (2, 1), (3, 0)])]
    ppermute x0 -> x1, starting transfers between devices: none -> 2.57 us  [body(): lax.ppermute(late, ('xh', 'par'), [(0, 3), (1, 2), (2, 1), (3, 0)])]
  transfers between devices with their start and end apart: 15 -> 16, of which waited for: 5 -> 4; matrix products, arithmetic and copies ran while one was open for 3% -> 3% of each run, Pallas kernels for 16% -> 17%
where the time goes in v7:
time: 150 us; the launch traced here: 149 us
  starting transfers between devices  83.3 us (56%)
  Pallas kernels  40.3 us (27%)
  waiting for transfers between devices  20 us (13%)
  other arithmetic  4.52 us (3%)
    ppermute x12, starting transfers between devices, moved(): lax.ppermute(value, axis, [(i, (i + steps) % count) for i in range(count)])  56.9 us
    all_to_all x1, waiting for transfers between devices, body(): memory = lax.all_to_all(memory, HEAD, 0, 0, tiled=True)  15.2 us
    pallas_call x1, Pallas kernels, local(): pl.pallas_call(local_kernel, grid=(2, pairs), out_shape=[pltpu.HBM((2 * p...  12.2 us
    all_to_all x1, starting transfers between devices, body(): d_query = lax.all_to_all(d_query, 'zh', 0, 0, tiled=True)  11.1 us
    pallas_call x2, Pallas kernels, gather(): pl.pallas_call(gather_kernel, grid=(steps,), out_shape=jax.ShapeDtypeStru...  10.3 us
    pallas_call x2, Pallas kernels, forward(): pl.pallas_call(kernel, out_shape=shapes, in_specs=[SMEM] * 2 + [VMEM] * (...  8.92 us
    all_to_all x1, starting transfers between devices, body(): parts = lax.all_to_all(parts, 'zh', 0, 0, tiled=True)  6.77 us
    all_to_all x1, starting transfers between devices, body(): memory = lax.all_to_all(memory, HEAD, 0, 0, tiled=True)  5.95 us
  transfers between devices with their start and end apart: 16, of which 4 were waited for; matrix products, arithmetic and copies ran while one was open for 3% of the time, Pallas kernels for 17%

profile of v7, /device:TPU:1, one launch (start us, length us, event | category | flops | bytes accessed | tf_op | source)
XLA Modules:
  0.0 149.4 jit_solution(10321925688339712582)
XLA Ops:
  0.6 0.0 copy-start
  0.6 0.8 join.3
  1.4 9.6 %collective-permute-start.2 = (bf16[128,256]{1,0:T(8,128)(2,1)S(1)}, bf16[128,256]{1,0:T(8,128)(2,1)S(1)}, u32[]{:S(2)}, u32[]{:S(2)}) collective-permute-start(bf16[128,256]{1,0:T(8,128)(2,1)S(1)} %join.3), channel_id=1, source_target_pairs={{0,64},{16,80},{32,96},{48,112},{64,128},{80,144},{96,160},{112,17... | collective-permute-start | bytes 196616 | tf_op jit(solution)/shard_map/ppermute | solution.py:417
  11.1 5.6 %collective-permute-start.3 = (bf16[128,256]{1,0:T(8,128)(2,1)S(1)}, bf16[128,256]{1,0:T(8,128)(2,1)S(1)}, u32[]{:S(2)}, u32[]{:S(2)}) collective-permute-start(bf16[128,256]{1,0:T(8,128)(2,1)S(1)} %join.3), channel_id=1, source_target_pairs={{0,192},{16,208},{32,224},{48,240},{64,0},{80,16},{96,32},{112,48}... | collective-permute-start | bytes 196616 | tf_op jit(solution)/shard_map/ppermute | solution.py:417
  16.7 10.3 %collective-permute-start.7 = (bf16[128,256]{1,0:T(8,128)(2,1)S(1)}, bf16[128,256]{1,0:T(8,128)(2,1)S(1)}, u32[]{:S(2)}, u32[]{:S(2)}) collective-permute-start(bf16[128,256]{1,0:T(8,128)(2,1)S(1)} %join.3), channel_id=1, source_target_pairs={{0,128},{16,144},{32,160},{48,176},{64,192},{80,208},{96,224},{112... | collective-permute-start | bytes 196616 | tf_op jit(solution)/shard_map/ppermute | solution.py:417
  26.9 1.0 join.2.refs_2_.rest_0_
  27.9 0.0 copy-start.4
  27.9 4.7 %collective-permute-start = (bf16[512,256]{1,0:T(8,128)(2,1)S(1)}, bf16[512,256]{1,0:T(8,128)(2,1)S(1)}, u32[]{:S(2)}, u32[]{:S(2)}) collective-permute-start(bf16[512,256]{1,0:T(8,128)(2,1)S(1)} %join.2.refs_2_.rest_0_), channel_id=1, source_target_pairs={{0,256},{256,0},{1,257},{257,1},{2,258},{258,2},{3,259},{259,3},{4... | collective-permute-start | bytes 786440 | tf_op jit(solution)/shard_map/ppermute | solution.py:417
  32.6 2.6 %collective-permute-start.1 = (bf16[512,256]{1,0:T(8,128)(2,1)S(1)}, bf16[512,256]{1,0:T(8,128)(2,1)S(1)}, u32[]{:S(2)}, u32[]{:S(2)}) collective-permute-start(bf16[512,256]{1,0:T(8,128)(2,1)S(1)} %join.2.refs_2_.rest_0_), channel_id=1, source_target_pairs={{0,16},{16,0},{1,17},{17,1},{2,18},{18,2},{3,19},{19,3},{4,20},{20... | collective-permute-start | bytes 786440 | tf_op jit(solution)/shard_map/ppermute | solution.py:417
  35.3 0.7 and_select_fusion.refs_0_.places
  36.0 0.0 copy-done
  36.0 0.1 pad_add_fusion
  36.1 0.0 collective-permute-done.2
  36.1 0.0 collective-permute-done.3
  36.1 2.6 %collective-permute-start.4 = (bf16[512,256]{1,0:T(8,128)(2,1)S(1)}, bf16[512,256]{1,0:T(8,128)(2,1)S(1)}, u32[]{:S(2)}, u32[]{:S(2)}) collective-permute-start(bf16[512,256]{1,0:T(8,128)(2,1)S(1)} %join.2.refs_2_.rest_0_), channel_id=1, source_target_pairs={{0,272},{16,256},{256,16},{272,0},{1,273},{17,257},{257,17},{273,1... | collective-permute-start | bytes 786440 | tf_op jit(solution)/shard_map/ppermute | solution.py:440
  38.7 0.3 compare_reduce_fusion
  39.0 0.1 reshape.20.refs_1_.member
  39.1 1.9 %collective-permute-start.5 = (bf16[256,256]{1,0:T(8,128)(2,1)S(1)}, bf16[256,256]{1,0:T(8,128)(2,1)S(1)}, u32[]{:S(2)}, u32[]{:S(2)}) collective-permute-start(bf16[256,256]{1,0:T(8,128)(2,1)S(1)} %get-tuple-element.47), channel_id=1, source_target_pairs={{0,224},{16,240},{32,0},{48,16},{64,32},{80,48},{96,64},{112,80},{... | collective-permute-start | bytes 393224 | tf_op jit(solution)/shard_map/ppermute | solution.py:417
  41.0 0.0 collective-permute-done.7
  41.0 4.3 %collective-permute-start.6 = (bf16[256,256]{1,0:T(8,128)(2,1)S(1)}, bf16[256,256]{1,0:T(8,128)(2,1)S(1)}, u32[]{:S(2)}, u32[]{:S(2)}) collective-permute-start(bf16[256,256]{1,0:T(8,128)(2,1)S(1)} %get-tuple-element.46), channel_id=1, source_target_pairs={{0,32},{16,48},{32,64},{48,80},{64,96},{80,112},{96,128},{112,144}... | collective-permute-start | bytes 393224 | tf_op jit(solution)/shard_map/ppermute | solution.py:417
  45.3 0.0 copy-start.1
  45.3 0.0 collective-permute-done.refs_3_.rest_1_
  45.3 0.0 copy-start.10
  45.4 0.0 collective-permute-done.1.refs_4_.rest_2_
  45.4 0.0 copy-start.11
  45.4 3.5 %collective-permute-done.4.refs_5_.rest_3_ = bf16[512,256]{1,0:T(8,128)(2,1)S(1)} collective-permute-done((bf16[512,256]{1,0:T(8,128)(2,1)S(1)}, bf16[512,256]{1,0:T(8,128)(2,1)S(1)}, u32[]{:S(2)}, u32[]{:S(2)}) %collective-permute-start.4) | collective-permute-done | bytes 262176 | tf_op jit(solution)/shard_map/ppermute | solution.py:440
  48.9 4.1 %forward.2.rest_6_ = f32[32,128]{1,0:T(8,128)S(1)} custom-call(s32[8]{0:T(128)S(1)} %and_select_fusion.refs_0_.places, s32[128]{0:T(128)S(1)} %reshape.20.refs_1_.member, bf16[512,256]{1,0:T(8,128)(2,1)S(1)} %join.2.refs_2_.rest_0_, bf16[512,256]{1,0:T(8,128)(2,1)S(1)} %collective-permute-done.refs_3_.rest_1_, ...), custom_call_target="tpu_custom_call" | custom-call | flops 4294967296 | bytes 1048576 | tf_op jit(solution)/shard_map/forward/pallas_call | solution.py:190
  53.0 0.0 collective-permute-done.5.rest_4_.rest_5_.rest_1_
  53.0 0.0 copy-start.5
  53.0 0.0 collective-permute-done.6.rest_5_.rest_6_.rest_2_
  53.0 0.0 copy-done.4
  53.0 0.0 copy-done.8
  53.1 4.8 %forward.3 = (bf16[8,48,128]{2,1,0:T(8,128)(2,1)}, f32[32,128]{1,0:T(8,128)S(1)}) custom-call(s32[8]{0:T(128)S(1)} %and_select_fusion.refs_0_.places, s32[128]{0:T(128)S(1)} %reshape.20.refs_1_.member, bf16[512,256]{1,0:T(8,128)(2,1)S(1)} %join.2.refs_2_.rest_0_, bf16[512,256]{1,0:T(8,128)(2,1)S(1)} %collective-permute-done.refs_3_.rest_1_, ...), custom_call_target="tpu_custom_call" | custom-call | flops 4294967296 | bytes 1048576 | tf_op jit(solution)/shard_map/forward/pallas_call | solution.py:190
  57.9 0.0 copy-done.10
  57.9 0.0 copy-start.7
  57.9 6.8 %all-to-all-start = ((bf16[8,48,128]{2,1,0:T(8,128)(2,1)}), bf16[8,48,128]{2,1,0:T(8,128)(2,1)S(1)}, u32[]{:S(2)}, u32[]{:S(2)}) async-start(bf16[8,48,128]{2,1,0:T(8,128)(2,1)} %get-tuple-element.27), calls=%async_computation | async-start | bytes 196608 | tf_op jit(solution)/shard_map/all_to_all | solution.py:460
  64.7 0.0 copy-done.6
  64.7 0.0 copy-done.7
  64.7 12.2 %local.1 = (f32[8,2,128,256]{3,2,1,0:T(8,128)}, bf16[8,1024,512]{2,1,0:T(8,128)(2,1)}, bf16[8,1024,512]{2,1,0:T(8,128)(2,1)}) custom-call(s32[8]{0:T(128)} %copy-done.8, s32[128]{0:T(128)} %copy-done.9, f32[32,128]{1,0:T(8,128)} %copy-done.7, bf16[512,256]{1,0:T(8,128)(2,1)} %copy-done.4, bf16[512,256]{1,0:T(8,128)(2,1)} %copy-done.10, ...), custom_call_target="tpu_custom_call" | custom-call | flops 12884901888 | bytes 1048576 | tf_op jit(solution)/shard_map/local/pallas_call | solution.py:264
  76.9 0.3 all-to-all-done.parts
  77.3 4.2 %scale.1 = (bf16[8,128,128]{2,1,0:T(8,128)(2,1)}, bf16[1024,384]{1,0:T(8,128)(2,1)}) custom-call(s32[8]{0:T(128)} %copy-done.8, bf16[8,48,128]{2,1,0:T(8,128)(2,1)S(1)} %all-to-all-done.parts, f32[32,128]{1,0:T(8,128)} %copy-done.7, f32[8,2,128,256]{3,2,1,0:T(8,128)} %get-tuple-element.33.sums_ref, bf16[512,256]{1,0:T(8,128)(2,1)} %copy-done.1, ...), custom_call_target="tpu_custom_call" | custom-call | flops 536870912 | bytes 1048576 | tf_op jit(solution)/shard_map/scale/pallas_call | solution.py:327
  81.5 5.2 %gather.3 = bf16[1024,256]{1,0:T(8,128)(2,1)S(1)} custom-call(bf16[1024,384]{1,0:T(8,128)(2,1)} %get-tuple-element.35.scaled, bf16[8,1024,512]{2,1,0:T(8,128)(2,1)} %get-tuple-element.36.chance, bf16[8,1024,512]{2,1,0:T(8,128)(2,1)} %get-tuple-element.37.slope), custom_call_target="tpu_custom_call" | custom-call | flops 3221225472 | bytes 1048576 | tf_op jit(solution)/shard_map/gather/pallas_call | solution.py:380
  86.7 0.0 copy-start.2
  86.7 0.0 copy-start.3
  86.7 2.1 %collective-permute-start.8 = (bf16[1024,256]{1,0:T(8,128)(2,1)S(1)}, bf16[1024,256]{1,0:T(8,128)(2,1)S(1)}, u32[]{:S(2)}, u32[]{:S(2)}) collective-permute-start(bf16[1024,256]{1,0:T(8,128)(2,1)S(1)} %gather.3), channel_id=1, source_target_pairs={{0,16},{16,0},{1,17},{17,1},{2,18},{18,2},{3,19},{19,3},{4,20},{20... | collective-permute-start | bytes 1572872 | tf_op jit(solution)/shard_map/ppermute | solution.py:417
  88.7 5.2 %gather.2 = f32[1024,256]{1,0:T(8,128)S(1)} custom-call(bf16[1024,384]{1,0:T(8,128)(2,1)} %get-tuple-element.35.scaled, bf16[8,1024,512]{2,1,0:T(8,128)(2,1)} %get-tuple-element.36.chance, bf16[8,1024,512]{2,1,0:T(8,128)(2,1)} %get-tuple-element.37.slope), custom_call_target="tpu_custom_call" | custom-call | flops 3221225472 | bytes 1048576 | tf_op jit(solution)/shard_map/gather/pallas_call | solution.py:380
  93.9 11.1 %all-to-all-start.1 = ((bf16[8,128,128]{2,1,0:T(8,128)(2,1)}), bf16[8,128,128]{2,1,0:T(8,128)(2,1)S(1)}, u32[]{:S(2)}, u32[]{:S(2)}) async-start(bf16[8,128,128]{2,1,0:T(8,128)(2,1)} %get-tuple-element.43), calls=%async_computation.1 | async-start | bytes 524288 | tf_op jit(solution)/shard_map/all_to_all | solution.py:468
  105.0 0.0 collective-permute-done.8
  105.1 0.9 add_convert_fusion.1
  105.9 3.4 %collective-permute-start.9 = (bf16[512,256]{1,0:T(8,128)(2,1)}, bf16[512,256]{1,0:T(8,128)(2,1)}, u32[]{:S(2)}, u32[]{:S(2)}) collective-permute-start(bf16[512,256]{1,0:T(8,128)(2,1)} %add_convert_fusion.1), channel_id=1, source_target_pairs={{0,256},{256,0},{1,257},{257,1},{2,258},{258,2},{3,259},{259,3},{4... | collective-permute-start | bytes 786440 | tf_op jit(solution)/shard_map/ppermute | solution.py:417
  109.3 7.1 %collective-permute-start.11 = (bf16[2048,128]{1,0:T(8,128)(2,1)S(1)}, bf16[2048,128]{1,0:T(8,128)(2,1)S(1)}, u32[]{:S(2)}, u32[]{:S(2)}) collective-permute-start(bf16[2048,128]{1,0:T(8,128)(2,1)S(1)} %copy-done.2), channel_id=1, source_target_pairs={{0,1},{1,0},{2,3},{3,2},{4,5},{5,4},{6,7},{7,6},{8,9},{9,8},{10,11... | collective-permute-start | bytes 1572872 | tf_op jit(solution)/shard_map/ppermute | solution.py:417
  116.4 1.9 %collective-permute-start.12 = (bf16[2048,128]{1,0:T(8,128)(2,1)S(1)}, bf16[2048,128]{1,0:T(8,128)(2,1)S(1)}, u32[]{:S(2)}, u32[]{:S(2)}) collective-permute-start(bf16[2048,128]{1,0:T(8,128)(2,1)S(1)} %copy-done.3), channel_id=1, source_target_pairs={{0,1},{1,0},{2,3},{3,2},{4,5},{5,4},{6,7},{7,6},{8,9},{9,8},{10,11... | collective-permute-start | bytes 1572872 | tf_op jit(solution)/shard_map/ppermute | solution.py:417
  118.4 0.0 collective-permute-done.9
  118.4 1.1 add_convert_fusion.grads
  119.5 3.5 %collective-permute-start.10 = (bf16[256,256]{1,0:T(8,128)(2,1)S(1)}, bf16[256,256]{1,0:T(8,128)(2,1)S(1)}, u32[]{:S(2)}, u32[]{:S(2)}) collective-permute-start(bf16[256,256]{1,0:T(8,128)(2,1)S(1)} %constant_dynamic-slice_fusion), channel_id=1, source_target_pairs={{0,1},{1,0},{2,3},{3,2},{4,5},{5,4},{6,7},{7,6},{8,9},{9,8},{10,11... | collective-permute-start | bytes 393224 | tf_op jit(solution)/shard_map/ppermute | solution.py:417
  123.1 1.0 collective-permute-done.10.from_core
  124.0 0.0 collective-permute-done.11.far_kw
  124.0 0.0 collective-permute-done.12.far_vw
  124.0 2.8 %project.1 = bf16[16,256,128]{2,1,0:T(8,128)(2,1)} custom-call(s32[1]{0:T(128)} %bitcast.core, s32[16]{0:T(128)S(1)} %iota.12.chunk, bf16[512,256]{1,0:T(8,128)(2,1)S(1)} %add_convert_fusion.grads, bf16[256,256]{1,0:T(8,128)(2,1)S(1)} %collective-permute-done.10.from_core, bf16[2048,128]{1,0:T(8,128)(2,1)S(1)} %copy-done.2, bf16[2048,128]{1,0:T(8,128)(2,1)S(1)} %copy-done.3, ...), custom_call_target="tpu_custom_call" | custom-call | tf_op jit(solution)/shard_map/project/pallas_call | solution.py:405
  126.8 0.0 all-to-all-done.1
  126.8 6.0 %all-to-all-start.2 = ((bf16[16,256,128]{2,1,0:T(8,128)(2,1)}), bf16[16,256,128]{2,1,0:T(8,128)(2,1)S(1)}, u32[]{:S(2)}, u32[]{:S(2)}) async-start(bf16[16,256,128]{2,1,0:T(8,128)(2,1)} %project.1), calls=%async_computation.2 | async-start | bytes 2097152 | tf_op jit(solution)/shard_map/all_to_all | solution.py:484
  132.8 0.7 reduce_sum.21
  133.4 15.2 %all-to-all-done.2 = bf16[16,256,128]{2,1,0:T(8,128)(2,1)S(1)} async-done(((bf16[16,256,128]{2,1,0:T(8,128)(2,1)}), bf16[16,256,128]{2,1,0:T(8,128)(2,1)S(1)}, u32[]{:S(2)}, u32[]{:S(2)}) %all-to-all-start.2) | async-done | bytes 1048608 | tf_op jit(solution)/shard_map/all_to_all | solution.py:484
  148.6 0.8 reduce.1
  (22 shorter events, 0.1 us)
Async XLA Ops:
  0.6 35.3 %copy-start = (s32[32,64]{1,0:T(8,128)S(1)}, s32[32,64]{1,0:T(8,128)}, u32[]{:S(2)}) copy-start(s32[32,64]{1,0:T(8,128)} %param.14) | copy-start | bytes 24580
  1.4 34.6 %collective-permute-start.2 = (bf16[128,256]{1,0:T(8,128)(2,1)S(1)}, bf16[128,256]{1,0:T(8,128)(2,1)S(1)}, u32[]{:S(2)}, u32[]{:S(2)}) collective-permute-start(bf16[128,256]{1,0:T(8,128)(2,1)S(1)} %join.3), channel_id=1, source_target_pairs={{0,64},{16,80},{32,96},{48,112},{64,128},{80,144},{96,160},{112,17... | collective-permute-start | bytes 196616 | tf_op jit(solution)/shard_map/ppermute | solution.py:417
  11.1 25.0 %collective-permute-start.3 = (bf16[128,256]{1,0:T(8,128)(2,1)S(1)}, bf16[128,256]{1,0:T(8,128)(2,1)S(1)}, u32[]{:S(2)}, u32[]{:S(2)}) collective-permute-start(bf16[128,256]{1,0:T(8,128)(2,1)S(1)} %join.3), channel_id=1, source_target_pairs={{0,192},{16,208},{32,224},{48,240},{64,0},{80,16},{96,32},{112,48}... | collective-permute-start | bytes 196616 | tf_op jit(solution)/shard_map/ppermute | solution.py:417
  16.7 24.3 %collective-permute-start.7 = (bf16[128,256]{1,0:T(8,128)(2,1)S(1)}, bf16[128,256]{1,0:T(8,128)(2,1)S(1)}, u32[]{:S(2)}, u32[]{:S(2)}) collective-permute-start(bf16[128,256]{1,0:T(8,128)(2,1)S(1)} %join.3), channel_id=1, source_target_pairs={{0,128},{16,144},{32,160},{48,176},{64,192},{80,208},{96,224},{112... | collective-permute-start | bytes 196616 | tf_op jit(solution)/shard_map/ppermute | solution.py:417
  27.9 25.1 %copy-start.4 = (bf16[512,256]{1,0:T(8,128)(2,1)}, bf16[512,256]{1,0:T(8,128)(2,1)S(1)}, u32[]{:S(2)}) copy-start(bf16[512,256]{1,0:T(8,128)(2,1)S(1)} %join.2.refs_2_.rest_0_) | copy-start | bytes 786436
  27.9 17.4 %collective-permute-start = (bf16[512,256]{1,0:T(8,128)(2,1)S(1)}, bf16[512,256]{1,0:T(8,128)(2,1)S(1)}, u32[]{:S(2)}, u32[]{:S(2)}) collective-permute-start(bf16[512,256]{1,0:T(8,128)(2,1)S(1)} %join.2.refs_2_.rest_0_), channel_id=1, source_target_pairs={{0,256},{256,0},{1,257},{257,1},{2,258},{258,2},{3,259},{259,3},{4... | collective-permute-start | bytes 786440 | tf_op jit(solution)/shard_map/ppermute | solution.py:417
  32.6 12.8 %collective-permute-start.1 = (bf16[512,256]{1,0:T(8,128)(2,1)S(1)}, bf16[512,256]{1,0:T(8,128)(2,1)S(1)}, u32[]{:S(2)}, u32[]{:S(2)}) collective-permute-start(bf16[512,256]{1,0:T(8,128)(2,1)S(1)} %join.2.refs_2_.rest_0_), channel_id=1, source_target_pairs={{0,16},{16,0},{1,17},{17,1},{2,18},{18,2},{3,19},{19,3},{4,20},{20... | collective-permute-start | bytes 786440 | tf_op jit(solution)/shard_map/ppermute | solution.py:417
  35.9 17.1 %copy-start.8 = (s32[8]{0:T(128)}, s32[8]{0:T(128)S(1)}, u32[]{:S(2)}) copy-start(s32[8]{0:T(128)S(1)} %and_select_fusion.refs_0_.places) | copy-start | bytes 100
  36.1 12.8 %collective-permute-start.4 = (bf16[512,256]{1,0:T(8,128)(2,1)S(1)}, bf16[512,256]{1,0:T(8,128)(2,1)S(1)}, u32[]{:S(2)}, u32[]{:S(2)}) collective-permute-start(bf16[512,256]{1,0:T(8,128)(2,1)S(1)} %join.2.refs_2_.rest_0_), channel_id=1, source_target_pairs={{0,272},{16,256},{256,16},{272,0},{1,273},{17,257},{257,17},{273,1... | collective-permute-start | bytes 786440 | tf_op jit(solution)/shard_map/ppermute | solution.py:440
  39.1 14.0 %copy-start.9 = (s32[128]{0:T(128)}, s32[128]{0:T(128)S(1)}, u32[]{:S(2)}) copy-start(s32[128]{0:T(128)S(1)} %reshape.20.refs_1_.member) | copy-start | bytes 1540
  39.1 13.9 %collective-permute-start.5 = (bf16[256,256]{1,0:T(8,128)(2,1)S(1)}, bf16[256,256]{1,0:T(8,128)(2,1)S(1)}, u32[]{:S(2)}, u32[]{:S(2)}) collective-permute-start(bf16[256,256]{1,0:T(8,128)(2,1)S(1)} %get-tuple-element.47), channel_id=1, source_target_pairs={{0,224},{16,240},{32,0},{48,16},{64,32},{80,48},{96,64},{112,80},{... | collective-permute-start | bytes 393224 | tf_op jit(solution)/shard_map/ppermute | solution.py:417
  41.0 12.0 %collective-permute-start.6 = (bf16[256,256]{1,0:T(8,128)(2,1)S(1)}, bf16[256,256]{1,0:T(8,128)(2,1)S(1)}, u32[]{:S(2)}, u32[]{:S(2)}) collective-permute-start(bf16[256,256]{1,0:T(8,128)(2,1)S(1)} %get-tuple-element.46), channel_id=1, source_target_pairs={{0,32},{16,48},{32,64},{48,80},{64,96},{80,112},{96,128},{112,144}... | collective-permute-start | bytes 393224 | tf_op jit(solution)/shard_map/ppermute | solution.py:417
  45.3 12.5 %copy-start.1 = (bf16[512,256]{1,0:T(8,128)(2,1)}, bf16[512,256]{1,0:T(8,128)(2,1)S(1)}, u32[]{:S(2)}) copy-start(bf16[512,256]{1,0:T(8,128)(2,1)S(1)} %pad_maximum_fusion.refs_6_.rest_4_.rest_0_) | copy-start | bytes 786436
  45.3 12.5 %copy-start.10 = (bf16[512,256]{1,0:T(8,128)(2,1)}, bf16[512,256]{1,0:T(8,128)(2,1)S(1)}, u32[]{:S(2)}) copy-start(bf16[512,256]{1,0:T(8,128)(2,1)S(1)} %collective-permute-done.refs_3_.rest_1_) | copy-start | bytes 786436
  45.4 12.5 %copy-start.11 = (bf16[512,256]{1,0:T(8,128)(2,1)}, bf16[512,256]{1,0:T(8,128)(2,1)S(1)}, u32[]{:S(2)}) copy-start(bf16[512,256]{1,0:T(8,128)(2,1)S(1)} %collective-permute-done.1.refs_4_.rest_2_) | copy-start | bytes 786436
  48.9 9.0 %copy-start.12 = (bf16[512,256]{1,0:T(8,128)(2,1)}, bf16[512,256]{1,0:T(8,128)(2,1)S(1)}, u32[]{:S(2)}) copy-start(bf16[512,256]{1,0:T(8,128)(2,1)S(1)} %collective-permute-done.4.refs_5_.rest_3_) | copy-start | bytes 786436
  53.0 11.7 %copy-start.5 = (bf16[256,256]{1,0:T(8,128)(2,1)}, bf16[256,256]{1,0:T(8,128)(2,1)S(1)}, u32[]{:S(2)}) copy-start(bf16[256,256]{1,0:T(8,128)(2,1)S(1)} %collective-permute-done.5.rest_4_.rest_5_.rest_1_) | copy-start | bytes 393220
  53.1 11.6 %copy-start.6 = (bf16[256,256]{1,0:T(8,128)(2,1)}, bf16[256,256]{1,0:T(8,128)(2,1)S(1)}, u32[]{:S(2)}) copy-start(bf16[256,256]{1,0:T(8,128)(2,1)S(1)} %collective-permute-done.6.rest_5_.rest_6_.rest_2_) | copy-start | bytes 393220
  57.9 6.8 %copy-start.7 = (f32[32,128]{1,0:T(8,128)}, f32[32,128]{1,0:T(8,128)S(1)}, u32[]{:S(2)}) copy-start(f32[32,128]{1,0:T(8,128)S(1)} %get-tuple-element.28.stats_ref) | copy-start | bytes 49156
  57.9 19.4 %all-to-all-start = ((bf16[8,48,128]{2,1,0:T(8,128)(2,1)}), bf16[8,48,128]{2,1,0:T(8,128)(2,1)S(1)}, u32[]{:S(2)}, u32[]{:S(2)}) async-start(bf16[8,48,128]{2,1,0:T(8,128)(2,1)} %get-tuple-element.27), calls=%async_computation | async-start | bytes 196608 | tf_op jit(solution)/shard_map/all_to_all | solution.py:460
  86.7 22.7 %copy-start.2 = (bf16[2048,128]{1,0:T(8,128)(2,1)S(1)}, bf16[2048,128]{1,0:T(8,128)(2,1)}, u32[]{:S(2)}) copy-start(bf16[2048,128]{1,0:T(8,128)(2,1)} %kw) | copy-start | bytes 1572868
  86.7 29.8 %copy-start.3 = (bf16[2048,128]{1,0:T(8,128)(2,1)S(1)}, bf16[2048,128]{1,0:T(8,128)(2,1)}, u32[]{:S(2)}) copy-start(bf16[2048,128]{1,0:T(8,128)(2,1)} %vw) | copy-start | bytes 1572868
  86.7 18.4 %collective-permute-start.8 = (bf16[1024,256]{1,0:T(8,128)(2,1)S(1)}, bf16[1024,256]{1,0:T(8,128)(2,1)S(1)}, u32[]{:S(2)}, u32[]{:S(2)}) collective-permute-start(bf16[1024,256]{1,0:T(8,128)(2,1)S(1)} %gather.3), channel_id=1, source_target_pairs={{0,16},{16,0},{1,17},{17,1},{2,18},{18,2},{3,19},{19,3},{4,20},{20... | collective-permute-start | bytes 1572872 | tf_op jit(solution)/shard_map/ppermute | solution.py:417
  93.9 32.9 %all-to-all-start.1 = ((bf16[8,128,128]{2,1,0:T(8,128)(2,1)}), bf16[8,128,128]{2,1,0:T(8,128)(2,1)S(1)}, u32[]{:S(2)}, u32[]{:S(2)}) async-start(bf16[8,128,128]{2,1,0:T(8,128)(2,1)} %get-tuple-element.43), calls=%async_computation.1 | async-start | bytes 524288 | tf_op jit(solution)/shard_map/all_to_all | solution.py:468
  105.1 4.3 %copy-start.13 = (bf16[1024,256]{1,0:T(8,128)(2,1)}, bf16[1024,256]{1,0:T(8,128)(2,1)S(1)}, u32[]{:S(2)}) copy-start(bf16[1024,256]{1,0:T(8,128)(2,1)S(1)} %collective-permute-done.8) | copy-start | bytes 1572868
  105.9 12.5 %collective-permute-start.9 = (bf16[512,256]{1,0:T(8,128)(2,1)}, bf16[512,256]{1,0:T(8,128)(2,1)}, u32[]{:S(2)}, u32[]{:S(2)}) collective-permute-start(bf16[512,256]{1,0:T(8,128)(2,1)} %add_convert_fusion.1), channel_id=1, source_target_pairs={{0,256},{256,0},{1,257},{257,1},{2,258},{258,2},{3,259},{259,3},{4... | collective-permute-start | bytes 786440 | tf_op jit(solution)/shard_map/ppermute | solution.py:417
  109.3 14.7 %collective-permute-start.11 = (bf16[2048,128]{1,0:T(8,128)(2,1)S(1)}, bf16[2048,128]{1,0:T(8,128)(2,1)S(1)}, u32[]{:S(2)}, u32[]{:S(2)}) collective-permute-start(bf16[2048,128]{1,0:T(8,128)(2,1)S(1)} %copy-done.2), channel_id=1, source_target_pairs={{0,1},{1,0},{2,3},{3,2},{4,5},{5,4},{6,7},{7,6},{8,9},{9,8},{10,11... | collective-permute-start | bytes 1572872 | tf_op jit(solution)/shard_map/ppermute | solution.py:417
  116.4 7.6 %collective-permute-start.12 = (bf16[2048,128]{1,0:T(8,128)(2,1)S(1)}, bf16[2048,128]{1,0:T(8,128)(2,1)S(1)}, u32[]{:S(2)}, u32[]{:S(2)}) collective-permute-start(bf16[2048,128]{1,0:T(8,128)(2,1)S(1)} %copy-done.3), channel_id=1, source_target_pairs={{0,1},{1,0},{2,3},{3,2},{4,5},{5,4},{6,7},{7,6},{8,9},{9,8},{10,11... | collective-permute-start | bytes 1572872 | tf_op jit(solution)/shard_map/ppermute | solution.py:417
  119.5 4.5 %collective-permute-start.10 = (bf16[256,256]{1,0:T(8,128)(2,1)S(1)}, bf16[256,256]{1,0:T(8,128)(2,1)S(1)}, u32[]{:S(2)}, u32[]{:S(2)}) collective-permute-start(bf16[256,256]{1,0:T(8,128)(2,1)S(1)} %constant_dynamic-slice_fusion), channel_id=1, source_target_pairs={{0,1},{1,0},{2,3},{3,2},{4,5},{5,4},{6,7},{7,6},{8,9},{9,8},{10,11... | collective-permute-start | bytes 393224 | tf_op jit(solution)/shard_map/ppermute | solution.py:417
  126.8 21.8 %all-to-all-start.2 = ((bf16[16,256,128]{2,1,0:T(8,128)(2,1)}), bf16[16,256,128]{2,1,0:T(8,128)(2,1)S(1)}, u32[]{:S(2)}, u32[]{:S(2)}) async-start(bf16[16,256,128]{2,1,0:T(8,128)(2,1)} %project.1), calls=%async_computation.2 | async-start | bytes 2097152 | tf_op jit(solution)/shard_map/all_to_all | solution.py:484

commit v8 on v7

--- a/solution.py
+++ b/solution.py
@@ -9,10 +9,11 @@
 
 HEAD_DIM = 64
 BLOCK = 128
-AXES = ("xh", "zh", "par", "xl", "y", "core")
-SIZES = (2, 8, 2, 2, 4, 2)
-Z = ("zh", "par")
-CTX = ("xh", "zh", "par")
+AXES = ("xh", "z2", "z4", "par", "xl", "y", "core")
+SIZES = (2, 2, 4, 2, 2, 4, 2)
+ZH = ("z2", "z4")
+Z = ("z2", "z4", "par")
+CTX = ("xh", "z2", "z4", "par")
 HEAD = ("xl", "y", "core")
 BIG = 1e30
 
@@ -133,69 +134,89 @@
     return top + jnp.log(total), mean / total
 
 
-def forward_kernel(base, places, member, *rest):
-    tables = rest[:4]
-    *pieces, before, result, stats, held, kv = rest[4:]
+def store_stats(stats, first, second, given):
+    half = stats.shape[0] // 2
+    for start, row in zip((0, half), given, strict=True):
+        for h in range(2):
+            for s, place in enumerate((first, second)):
+                stats[pl.ds(start + 2 * place + h, 1), :] = row[:, (2 * h + s) * BLOCK : (2 * h + s + 1) * BLOCK]
+
+
+def early_kernel(places, member, near_ref, side_ref, piece, stats, kv):
+    load_targets((near_ref, side_ref), kv)
+    blocks = 2 * kv.shape[0] // BLOCK
+
+    def step(p, carry):
+        rows = pl.ds(pl.multiple_of(p * 2 * BLOCK, 2 * BLOCK), 2 * BLOCK)
+        first, second = places[2 * p], places[2 * p + 1]
+        query, out = split_heads(piece[rows, :BLOCK]), split_heads(piece[rows, BLOCK:])
+        store_stats(stats, first, second, part_stats(kv, query, out, member, first, second, 0, blocks))
+        return carry
+
+    lax.fori_loop(0, piece.shape[0] // (2 * BLOCK), step, 0)
+
+
+def forward_kernel(places, member, *rest):
+    tables, pieces = rest[:4], rest[4:7]
+    before, result, stats, held, kv = rest[7:]
     load_targets(pieces, held)
     load_targets(tables[:2], kv.at[0])
     load_targets(tables[2:], kv.at[1])
     blocks = 2 * kv.shape[1] // BLOCK
     pairs = held.shape[0] // (2 * BLOCK)
+    known = pieces[0].shape[0] // (2 * BLOCK)
     half = stats.shape[0] // 2
-    if before is not None:
-        stats[...] = before[...]
-
-    def step(p, carry):
+
+    def step(p, done):
         rows = pl.ds(pl.multiple_of(p * 2 * BLOCK, 2 * BLOCK), 2 * BLOCK)
-        first, second = places[base + 2 * p], places[base + 2 * p + 1]
-        query = split_heads(held[rows, :BLOCK])
-        out = split_heads(held[rows, BLOCK:])
-        log_total, mean = union(
-            [
-                part_stats(kv.at[0], query, out, member, first, second, 0, blocks),
-                part_stats(kv.at[1], query, out, member, first, second, blocks // 2, blocks),
-            ]
-        )
-        for h in range(2):
-            for s, place in enumerate((first, second)):
-                lanes = slice((2 * h + s) * BLOCK, (2 * h + s + 1) * BLOCK)
-                stats[pl.ds(2 * place + h, 1), :] = log_total[:, lanes]
-                stats[pl.ds(half + 2 * place + h, 1), :] = mean[:, lanes]
+        first, second = places[2 * p], places[2 * p + 1]
+        query, out = split_heads(held[rows, :BLOCK]), split_heads(held[rows, BLOCK:])
+        if done:
+            one = lanes_of(before, first, second, 0), lanes_of(before, first, second, half)
+        else:
+            one = part_stats(kv.at[0], query, out, member, first, second, 0, blocks)
+        two = part_stats(kv.at[1], query, out, member, first, second, blocks // 2, blocks)
+        store_stats(stats, first, second, union([one, two]))
+
+    def step_known(p, carry):
+        step(p, True)
         return carry
 
-    lax.fori_loop(0, pairs, step, 0)
-    if result is not None:
-        high = stats[:half, :].astype(jnp.bfloat16)
-        low = (stats[:half, :] - high.astype(jnp.float32)).astype(jnp.bfloat16)
-        message = jnp.concatenate([high, low, stats[half:, :].astype(jnp.bfloat16)], axis=0)
-        for peer in range(result.shape[0]):
-            result[peer] = message
-
-
-def forward(base, places, member, tables, pieces, before):
+    def step_new(p, carry):
+        step(p, False)
+        return carry
+
+    lax.fori_loop(0, known, step_known, 0)
+    lax.fori_loop(known, pairs, step_new, 0)
+    high = stats[:half, :].astype(jnp.bfloat16)
+    low = (stats[:half, :] - high.astype(jnp.float32)).astype(jnp.bfloat16)
+    message = jnp.concatenate([high, low, stats[half:, :].astype(jnp.bfloat16)], axis=0)
+    for peer in range(result.shape[0]):
+        result[peer] = message
+
+
+def forward(places, member, tables, pieces, before):
     count = places.shape[0]
     rows = sum(p.shape[0] for p in pieces)
     enc = sum(t.shape[0] for t in tables)
-    given = [places, member, *tables, *pieces]
     local = jax.ShapeDtypeStruct((4 * count, BLOCK), jnp.float32)
     if before is None:
-        shapes = [local]
-        def kernel(*refs):
-            ins, outs = refs[: len(given)], refs[len(given) :]
-            forward_kernel(base, *ins, None, None, *outs)
+        kernel, shapes = early_kernel, local
+        scratch = [pltpu.VMEM((enc, 2 * BLOCK), jnp.bfloat16)]
+        given = [places, member, *tables, *pieces]
     else:
-        given.append(before)
-        shapes = [jax.ShapeDtypeStruct((count, 6 * count, BLOCK), jnp.bfloat16), local]
-        kernel = partial(forward_kernel, base)
+        kernel, shapes = forward_kernel, [jax.ShapeDtypeStruct((count, 6 * count, BLOCK), jnp.bfloat16), local]
+        scratch = [
+            pltpu.VMEM((rows, 2 * BLOCK), jnp.bfloat16),
+            pltpu.VMEM((2, enc // 2, 2 * BLOCK), jnp.bfloat16),
+        ]
+        given = [places, member, *tables, *pieces, before]
     return pl.pallas_call(
         kernel,
         out_shape=shapes,
         in_specs=[SMEM] * 2 + [VMEM] * (len(given) - 2),
-        out_specs=[VMEM] * len(shapes),
-        scratch_shapes=[
-            pltpu.VMEM((rows, 2 * BLOCK), jnp.bfloat16),
-            pltpu.VMEM((2, enc // 2, 2 * BLOCK), jnp.bfloat16),
-        ],
+        out_specs=VMEM if before is None else [VMEM] * 2,
+        scratch_shapes=scratch,
         compiler_params=room(20),
         cost_estimate=cost(2 * rows * enc * 4 * BLOCK, rows * enc * 2),
         name="forward",
@@ -306,9 +327,10 @@
         share, shift = by_dim(share), by_dim(shift)
         slope = sums[p, 0] + sums[pairs + p, 0]
         chance = sums[p, 1] + sums[pairs + p, 1]
-        grad = (share * (slope - shift * chance)).T.astype(jnp.bfloat16)
-        d_query[first] = grad[:BLOCK]
-        d_query[second] = grad[BLOCK:]
+        grad = (share * (slope - shift * chance)).T
+        far = d_query.shape[0] // 2
+        for place, part in ((first, grad[:BLOCK]), (second, grad[BLOCK:])):
+            d_query[2 * (place % far) + place // far] = part
         share, shift = share.T, shift.T
         query = held[rows, :BLOCK].astype(jnp.float32) * share
         out = held[rows, BLOCK:].astype(jnp.float32) * share
@@ -327,7 +349,7 @@
     return pl.pallas_call(
         scale_kernel,
         out_shape=[
-            pltpu.HBM((count, BLOCK, BLOCK), jnp.bfloat16),
+            pltpu.HBM((count, BLOCK, BLOCK), jnp.float32),
             pltpu.HBM((rows, 3 * BLOCK), jnp.bfloat16),
         ],
         in_specs=[SMEM, VMEM] + [ANY] * (len(given) - 2),
@@ -345,7 +367,8 @@
     )(*given)
 
 
-def gather_kernel(scaled, chance, slope, sent, d_key, d_value):
+def gather_kernel(scaled, chance, slope, *rest):
+    *sent, d_key, d_value = rest
     p = pl.program_id(0)
     value = key = None
     for i in range(chance.shape[0]):
@@ -367,8 +390,11 @@
 
     @pl.when(p == pl.num_programs(0) - 1)
     def _():
-        sent[:, :BLOCK] = d_key[...].astype(sent.dtype)
-        sent[:, BLOCK:] = d_value[...].astype(sent.dtype)
+        half = d_key.shape[0] // 2
+        for i, target in enumerate(sent):
+            rows = slice(i * half, (i + 1) * half)
+            target[:, :BLOCK] = d_key[rows, :].astype(target.dtype)
+            target[:, BLOCK:] = d_value[rows, :].astype(target.dtype)
 
 
 def gather(scaled, chance, slope, side, kind):
@@ -380,9 +406,9 @@
     return pl.pallas_call(
         gather_kernel,
         grid=(steps,),
-        out_shape=jax.ShapeDtypeStruct((enc, 2 * BLOCK), kind),
+        out_shape=[jax.ShapeDtypeStruct((enc // 2, 2 * BLOCK), kind)] * 2,
         in_specs=[pl.BlockSpec((step * 2 * BLOCK, scaled.shape[1]), lambda p: (p, 0)), table, table],
-        out_specs=VMEM,
+        out_specs=[VMEM] * 2,
         scratch_shapes=[pltpu.VMEM((enc, BLOCK), jnp.float32)] * 2,
         compiler_params=room(20),
         cost_estimate=cost(3 * pairs * enc * lanes * BLOCK, 0),
@@ -390,26 +416,27 @@
     )(*given)
 
 
-def project_kernel(core, chunk, grads, from_core, kw, vw, far_kw, far_vw, memory):
+def project_kernel(core, grads, from_core, kw, vw, far_kw, far_vw, memory):
     rows = from_core.shape[0]
     mine = grads[pl.ds(pl.multiple_of(core[0] * rows, rows), rows), :]
     other = from_core[...]
-    for j in range(memory.shape[0]):
-        part = pl.ds(pl.multiple_of(chunk[j] * BLOCK, BLOCK), BLOCK)
+    for j in range(0, memory.shape[0], 2):
+        part = slice(j * BLOCK, (j + 2) * BLOCK)
         total = dot_nt(mine[:, :BLOCK], kw[part, :]) + dot_nt(mine[:, BLOCK:], vw[part, :])
         total = total + dot_nt(other[:, :BLOCK], far_kw[part, :]) + dot_nt(other[:, BLOCK:], far_vw[part, :])
-        memory[j] = total.astype(jnp.bfloat16)
-
-
-def project(core, chunk, *given):
+        memory[j] = total[:, :BLOCK].astype(jnp.bfloat16)
+        memory[j + 1] = total[:, BLOCK:].astype(jnp.bfloat16)
+
+
+def project(core, *given):
     return pl.pallas_call(
         project_kernel,
-        out_shape=jax.ShapeDtypeStruct((chunk.shape[0], given[1].shape[0], BLOCK), jnp.bfloat16),
-        in_specs=[SMEM] * 2 + [VMEM] * len(given),
+        out_shape=jax.ShapeDtypeStruct((given[2].shape[0] // BLOCK, given[1].shape[0], BLOCK), jnp.bfloat16),
+        in_specs=[SMEM] + [VMEM] * len(given),
         out_specs=VMEM,
         compiler_params=room(8),
         name="project",
-    )(core, chunk, *given)
+    )(core, *given)
 
 
 def moved(value, axis, steps):
@@ -420,27 +447,24 @@
 def body(queries, keys, values, d_out, key_weight, value_weight, block_lists):
     f32, bf16 = jnp.float32, jnp.bfloat16
     half = lax.axis_index("xh")
-    place = lax.axis_index("zh")
+    place = lax.axis_index(ZH)
     parity = lax.axis_index("par")
     core = lax.axis_index("core")
     depth = lax.axis_size(Z)
     enc_rows = keys.shape[0]
     enc_blocks = enc_rows // BLOCK
 
-    near = join(queries, d_out)
+    own = join(keys, values)
+    side = moved(own, "xh", 1)
+    next_ = moved(own, "par", 1)
+    near, own = lax.optimization_barrier((join(queries, d_out), own))
     ahead = moved(near, Z, 4)
     behind = moved(near, Z, -4)
     across = moved(near, Z, 8)
-    own = join(keys, values)
     late, ahead, behind = lax.optimization_barrier((own, ahead, behind))
-    tables = [
-        own,
-        moved(own, "xh", 1),
-        moved(own, "par", 1),
-        lax.ppermute(late, ("xh", "par"), [(0, 3), (1, 2), (2, 1), (3, 0)]),
-    ]
-
-    count = lax.axis_size("zh")
+    tables = [own, side, next_, lax.ppermute(late, ("xh", "par"), [(0, 3), (1, 2), (2, 1), (3, 0)])]
+
+    count = lax.axis_size(ZH)
     places = (place + jnp.asarray(SLOTS, jnp.int32)) % count
     listed = lax.dynamic_slice_in_dim(block_lists, half * depth, depth, 0).reshape(count, depth // count, -1)
     listed = lax.dynamic_index_in_dim(listed, parity, 1, keepdims=False)
@@ -454,37 +478,34 @@
     above = moved(bundle[: 2 * BLOCK], Z, -2)
     below = moved(bundle[BLOCK : 3 * BLOCK], Z, 2)
 
-    (early,) = forward(0, places, member, tables, [bundle], None)
-    parts, stats = forward(len(OWN), places, member, tables, [above, below], early)
+    early = forward(places, member, tables[:2], [bundle], None)
     pieces = [bundle, above, below]
-    parts = lax.all_to_all(parts, "zh", 0, 0, tiled=True)
+    parts, stats = forward(places, member, tables, pieces, early)
+    parts = lax.all_to_all(parts, ZH, 0, 0, tiled=True)
     sums, chances, slopes = local(places, member, stats, tables, pieces)
     parts, sums, chances, slopes = lax.optimization_barrier((parts, sums, chances, slopes))
 
     d_query, scaled = scale(places, parts, stats, sums, pieces)
-    from_next = moved(gather(scaled, chances, slopes, 1, bf16), "par", 1)
-    grads = gather(scaled, chances, slopes, 0, f32)
-    d_query, grads = lax.optimization_barrier((d_query, grads))
-    d_query = lax.all_to_all(d_query, "zh", 0, 0, tiled=True)
-    grads, from_next, key_weight, value_weight = lax.optimization_barrier(
-        (grads, from_next, key_weight, value_weight)
-    )
+    d_query = lax.psum_scatter(d_query.reshape(-1, BLOCK), "z4", scatter_dimension=0, tiled=True)
+    onward, next_ = (moved(part, "par", 1) for part in reversed(gather(scaled, chances, slopes, 1, bf16)))
+    grads, side = gather(scaled, chances, slopes, 0, f32)
+    side, onward = lax.optimization_barrier((side, onward))
+    from_half = moved((side + onward.astype(f32)).astype(bf16), "xh", 1)
+    grads, key_weight, value_weight = lax.optimization_barrier((grads, key_weight, value_weight))
     far_key_weight = moved(key_weight, "core", 1)
     far_value_weight = moved(value_weight, "core", 1)
-    from_half = moved((grads[enc_rows:] + from_next[enc_rows:].astype(f32)).astype(bf16), "xh", 1)
-    grads = grads[:enc_rows] + from_next[:enc_rows].astype(f32) + from_half.astype(f32)
-    grads = grads.astype(bf16)
+    grads = (grads + next_.astype(f32) + from_half.astype(f32)).astype(bf16)
     from_core = moved(lax.dynamic_slice_in_dim(grads, (1 - core) * (enc_rows // 2), enc_rows // 2, 0), "core", 1)
 
     cores = lax.axis_size("core")
-    chunk = jnp.arange(key_weight.shape[0] // BLOCK, dtype=jnp.int32)
     weights = (key_weight, value_weight, far_key_weight, far_value_weight)
-    memory = project(core[None], chunk, grads, from_core, *weights)
-    memory, d_query = lax.optimization_barrier((memory, d_query))
+    from_core, d_query = lax.optimization_barrier((from_core, d_query))
+    memory = project(core[None], grads, from_core, *weights)
+    d_query = lax.psum_scatter(d_query, "z2", scatter_dimension=0, tiled=True)
     memory = lax.all_to_all(memory, HEAD, 0, 0, tiled=True)
     memory = memory.reshape(-1, cores, *memory.shape[1:]).astype(f32)
     d_memory = jnp.sum(memory, axis=0).reshape(keys.shape).astype(bf16)
-    d_queries = jnp.sum(d_query.astype(f32), axis=0).astype(bf16)
+    d_queries = d_query.astype(bf16)
     return d_queries, d_memory
 
 

time: 150 us -> 198 us (1.32)
  waiting for transfers between devices: 20 us -> 60.9 us
  between operations: 1.1 us -> 14.5 us
  starting transfers between devices: 83.3 us -> 76.1 us
    reduce_scatter x0 -> x2, waiting for transfers between devices: none -> 53.9 us  [the longest x1 33.6 us: body(): d_query = lax.psum_scatter(d_query, 'z2', scatter_dimension=0, tiled=True)]
    all_to_all x1, waiting for transfers between devices: 15.2 us -> 0.01 us  [body(): memory = lax.all_to_all(memory, HEAD, 0, 0, tiled=True)]
    all_to_all x2 -> x1, starting transfers between devices: 17.9 us -> 6.51 us  [body(): parts = lax.all_to_all(parts, ZH, 0, 0, tiled=True)]
    ppermute x12 -> x13, starting transfers between devices: 56.9 us -> 60.3 us  [moved(): lax.ppermute(value, axis, [(i, (i + steps) % count) for i in range(count)])]
  transfers between devices with their start and end apart: 16 -> 18, of which waited for: 4 -> 6; matrix products, arithmetic and copies ran while one was open for 3% -> 2% of each run, Pallas kernels for 17% -> 10%
where the time goes in v8:
time: 198 us; the launch traced here: 197 us
  starting transfers between devices  76.1 us (38%)
  waiting for transfers between devices  60.9 us (31%)
  Pallas kernels  40.1 us (20%)
  between operations  14.5 us (7%)
  other arithmetic  4.17 us (2%)
    ppermute x13, starting transfers between devices, moved(): lax.ppermute(value, axis, [(i, (i + steps) % count) for i in range(count)])  60.3 us
    reduce_scatter x1, waiting for transfers between devices, body(): d_query = lax.psum_scatter(d_query, 'z2', scatter_dimension=0, tiled=True)  33.6 us
    reduce_scatter x1, waiting for transfers between devices, body(): lax.psum_scatter(d_query.reshape(-1, BLOCK), 'z4', scatter_dimension=0, t...  20.2 us
    pallas_call x1, Pallas kernels, local(): pl.pallas_call(local_kernel, grid=(2, pairs), out_shape=[pltpu.HBM((2 * p...  12.2 us
    pallas_call x2, Pallas kernels, gather(): pl.pallas_call(gather_kernel, grid=(steps,), out_shape=[jax.ShapeDtypeStr...  10.4 us
    pallas_call x2, Pallas kernels, forward(): pl.pallas_call(kernel, out_shape=shapes, in_specs=[SMEM] * 2 + [VMEM] * (...  9.07 us
    all_to_all x1, starting transfers between devices, body(): memory = lax.all_to_all(memory, HEAD, 0, 0, tiled=True)  6.66 us
    all_to_all x1, starting transfers between devices, body(): parts = lax.all_to_all(parts, ZH, 0, 0, tiled=True)  6.51 us
  transfers between devices with their start and end apart: 18, of which 6 were waited for; matrix products, arithmetic and copies ran while one was open for 2% of the time, Pallas kernels for 10%

profile of v8, /device:TPU:1, one launch (start us, length us, event | category | flops | bytes accessed | tf_op | source)
XLA Modules:
  0.0 196.6 jit_solution(5906395615246751349)
XLA Ops:
  7.2 0.0 copy-start
  7.2 1.0 join.3.near_ref.rest_0_
  8.2 0.0 copy-start.4
  8.2 0.9 join.2
  9.1 9.6 %collective-permute-start.2 = (bf16[128,256]{1,0:T(8,128)(2,1)S(1)}, bf16[128,256]{1,0:T(8,128)(2,1)S(1)}, u32[]{:S(2)}, u32[]{:S(2)}) collective-permute-start(bf16[128,256]{1,0:T(8,128)(2,1)S(1)} %join.2), channel_id=1, source_target_pairs={{0,64},{16,80},{32,96},{48,112},{64,128},{80,144},{96,160},{112,17... | collective-permute-start | bytes 196616 | tf_op jit(solution)/shard_map/ppermute | solution.py:444
  18.7 5.6 %collective-permute-start.3 = (bf16[128,256]{1,0:T(8,128)(2,1)S(1)}, bf16[128,256]{1,0:T(8,128)(2,1)S(1)}, u32[]{:S(2)}, u32[]{:S(2)}) collective-permute-start(bf16[128,256]{1,0:T(8,128)(2,1)S(1)} %join.2), channel_id=1, source_target_pairs={{0,192},{16,208},{32,224},{48,240},{64,0},{80,16},{96,32},{112,48}... | collective-permute-start | bytes 196616 | tf_op jit(solution)/shard_map/ppermute | solution.py:444
  24.3 10.3 %collective-permute-start.5 = (bf16[128,256]{1,0:T(8,128)(2,1)S(1)}, bf16[128,256]{1,0:T(8,128)(2,1)S(1)}, u32[]{:S(2)}, u32[]{:S(2)}) collective-permute-start(bf16[128,256]{1,0:T(8,128)(2,1)S(1)} %join.2), channel_id=1, source_target_pairs={{0,128},{16,144},{32,160},{48,176},{64,192},{80,208},{96,224},{112... | collective-permute-start | bytes 196616 | tf_op jit(solution)/shard_map/ppermute | solution.py:444
  34.5 4.7 %collective-permute-start = (bf16[512,256]{1,0:T(8,128)(2,1)S(1)}, bf16[512,256]{1,0:T(8,128)(2,1)S(1)}, u32[]{:S(2)}, u32[]{:S(2)}) collective-permute-start(bf16[512,256]{1,0:T(8,128)(2,1)S(1)} %join.3.near_ref.rest_0_), channel_id=1, source_target_pairs={{0,256},{256,0},{1,257},{257,1},{2,258},{258,2},{3,259},{259,3},{4... | collective-permute-start | bytes 786440 | tf_op jit(solution)/shard_map/ppermute | solution.py:444
  39.2 2.6 %collective-permute-start.1 = (bf16[512,256]{1,0:T(8,128)(2,1)S(1)}, bf16[512,256]{1,0:T(8,128)(2,1)S(1)}, u32[]{:S(2)}, u32[]{:S(2)}) collective-permute-start(bf16[512,256]{1,0:T(8,128)(2,1)S(1)} %join.3.near_ref.rest_0_), channel_id=1, source_target_pairs={{0,16},{16,0},{1,17},{17,1},{2,18},{18,2},{3,19},{19,3},{4,20},{20... | collective-permute-start | bytes 786440 | tf_op jit(solution)/shard_map/ppermute | solution.py:444
  41.9 0.7 and_select_fusion.places
  42.6 0.0 copy-done
  42.6 0.1 pad_add_fusion
  42.7 0.3 compare_reduce_fusion
  43.0 0.1 reshape.24.member
  43.1 0.0 collective-permute-done.2
  43.1 0.0 collective-permute-done.3
  43.2 2.2 %collective-permute-start.6 = (bf16[256,256]{1,0:T(8,128)(2,1)S(1)}, bf16[256,256]{1,0:T(8,128)(2,1)S(1)}, u32[]{:S(2)}, u32[]{:S(2)}) collective-permute-start(bf16[256,256]{1,0:T(8,128)(2,1)S(1)} %get-tuple-element.57), channel_id=1, source_target_pairs={{0,224},{16,240},{32,0},{48,16},{64,32},{80,48},{96,64},{112,80},{... | collective-permute-start | bytes 393224 | tf_op jit(solution)/shard_map/ppermute | solution.py:444
  45.4 4.0 %collective-permute-start.7 = (bf16[256,256]{1,0:T(8,128)(2,1)S(1)}, bf16[256,256]{1,0:T(8,128)(2,1)S(1)}, u32[]{:S(2)}, u32[]{:S(2)}) collective-permute-start(bf16[256,256]{1,0:T(8,128)(2,1)S(1)} %get-tuple-element.56), channel_id=1, source_target_pairs={{0,32},{16,48},{32,64},{48,80},{64,96},{80,112},{96,128},{112,144}... | collective-permute-start | bytes 393224 | tf_op jit(solution)/shard_map/ppermute | solution.py:444
  49.4 0.0 collective-permute-done.5
  49.4 2.6 %collective-permute-start.4 = (bf16[512,256]{1,0:T(8,128)(2,1)S(1)}, bf16[512,256]{1,0:T(8,128)(2,1)S(1)}, u32[]{:S(2)}, u32[]{:S(2)}) collective-permute-start(bf16[512,256]{1,0:T(8,128)(2,1)S(1)} %join.3.near_ref.rest_0_), channel_id=1, source_target_pairs={{0,272},{16,256},{256,16},{272,0},{1,273},{17,257},{257,17},{273,1... | collective-permute-start | bytes 786440 | tf_op jit(solution)/shard_map/ppermute | solution.py:465
  52.0 0.0 copy-start.3
  52.0 0.0 collective-permute-done.side_ref.rest_1_
  52.0 2.5 %forward.2.rest_7_ = f32[32,128]{1,0:T(8,128)S(1)} custom-call(s32[8]{0:T(128)S(1)} %and_select_fusion.places, s32[128]{0:T(128)S(1)} %reshape.24.member, bf16[512,256]{1,0:T(8,128)(2,1)S(1)} %join.3.near_ref.rest_0_, bf16[512,256]{1,0:T(8,128)(2,1)S(1)} %collective-permute-done.side_ref.rest_1_, ...), custom_call_target="tpu_custom_call" | custom-call | flops 2147483648 | bytes 1048576 | tf_op jit(solution)/shard_map/forward/pallas_call | solution.py:214
  54.5 0.0 collective-permute-done.6.rest_5_.rest_1_
  54.5 0.0 copy-start.5
  54.5 1.8 collective-permute-done.7.rest_6_.rest_2_
  56.3 0.0 collective-permute-done.1.rest_2_
  56.3 3.2 %collective-permute-done.4.rest_3_ = bf16[512,256]{1,0:T(8,128)(2,1)S(1)} collective-permute-done((bf16[512,256]{1,0:T(8,128)(2,1)S(1)}, bf16[512,256]{1,0:T(8,128)(2,1)S(1)}, u32[]{:S(2)}, u32[]{:S(2)}) %collective-permute-start.4) | collective-permute-done | bytes 262176 | tf_op jit(solution)/shard_map/ppermute | solution.py:465
  59.6 6.6 %forward.3 = (bf16[8,48,128]{2,1,0:T(8,128)(2,1)}, f32[32,128]{1,0:T(8,128)S(1)}) custom-call(s32[8]{0:T(128)S(1)} %and_select_fusion.places, s32[128]{0:T(128)S(1)} %reshape.24.member, bf16[512,256]{1,0:T(8,128)(2,1)S(1)} %join.3.near_ref.rest_0_, bf16[512,256]{1,0:T(8,128)(2,1)S(1)} %collective-permute-done.side_ref.rest_1_, ...), custom_call_target="tpu_custom_call" | custom-call | flops 8589934592 | bytes 1048576 | tf_op jit(solution)/shard_map/forward/pallas_call | solution.py:214
  66.3 0.0 copy-start.7
  66.3 0.6 copy-done.7
  66.9 6.5 %all-to-all-start = ((bf16[8,48,128]{2,1,0:T(8,128)(2,1)}), bf16[8,48,128]{2,1,0:T(8,128)(2,1)S(1)}, u32[]{:S(2)}, u32[]{:S(2)}) async-start(bf16[8,48,128]{2,1,0:T(8,128)(2,1)} %get-tuple-element.34), calls=%async_computation | async-start | bytes 196608 | tf_op jit(solution)/shard_map/all_to_all | solution.py:484
  73.4 0.0 reduce-scatter.3.cloned.1.call-start
  73.4 12.2 %local.1 = (f32[8,2,128,256]{3,2,1,0:T(8,128)}, bf16[8,1024,512]{2,1,0:T(8,128)(2,1)}, bf16[8,1024,512]{2,1,0:T(8,128)(2,1)}) custom-call(s32[8]{0:T(128)} %copy-done.8, s32[128]{0:T(128)} %copy-done.9, f32[32,128]{1,0:T(8,128)} %copy-done.7, bf16[512,256]{1,0:T(8,128)(2,1)} %copy-done.4, bf16[512,256]{1,0:T(8,128)(2,1)} %copy-done.10, ...), custom_call_target="tpu_custom_call" | custom-call | flops 12884901888 | bytes 1048576 | tf_op jit(solution)/shard_map/local/pallas_call | solution.py:285
  85.7 0.2 all-to-all-done.parts
  85.9 4.3 %scale.1 = (f32[8,128,128]{2,1,0:T(8,128)}, bf16[1024,384]{1,0:T(8,128)(2,1)}) custom-call(s32[8]{0:T(128)} %copy-done.8, bf16[8,48,128]{2,1,0:T(8,128)(2,1)S(1)} %all-to-all-done.parts, f32[32,128]{1,0:T(8,128)} %copy-done.7, f32[8,2,128,256]{3,2,1,0:T(8,128)} %get-tuple-element.40.sums_ref, bf16[512,256]{1,0:T(8,128)(2,1)} %copy-done.3, ...), custom_call_target="tpu_custom_call" | custom-call | flops 536870912 | bytes 1048576 | tf_op jit(solution)/shard_map/scale/pallas_call | solution.py:349
  90.2 5.2 %gather.3 = (bf16[512,256]{1,0:T(8,128)(2,1)S(1)}, bf16[512,256]{1,0:T(8,128)(2,1)S(1)}) custom-call(bf16[1024,384]{1,0:T(8,128)(2,1)} %get-tuple-element.41.scaled, bf16[8,1024,512]{2,1,0:T(8,128)(2,1)} %get-tuple-element.42.chance, bf16[8,1024,512]{2,1,0:T(8,128)(2,1)} %get-tuple-element.43.slope), custom_call_target="tpu_custom_call" | custom-call | flops 3221225472 | bytes 1048576 | tf_op jit(solution)/shard_map/gather/pallas_call | solution.py:406
  95.4 4.6 %collective-permute-start.9 = (bf16[512,256]{1,0:T(8,128)(2,1)S(1)}, bf16[512,256]{1,0:T(8,128)(2,1)S(1)}, u32[]{:S(2)}, u32[]{:S(2)}) collective-permute-start(bf16[512,256]{1,0:T(8,128)(2,1)S(1)} %get-tuple-element.48), channel_id=1, source_target_pairs={{0,16},{16,0},{1,17},{17,1},{2,18},{18,2},{3,19},{19,3},{4,20},{20... | collective-permute-start | bytes 786440 | tf_op jit(solution)/shard_map/ppermute | solution.py:444
  100.0 0.0 reduce-scatter.3.cloned.1.call-update
  100.0 0.0 copy-start.1
  100.0 0.0 copy-start.2
  100.0 5.2 %gather.2 = (f32[512,256]{1,0:T(8,128)S(1)}, f32[512,256]{1,0:T(8,128)S(1)}) custom-call(bf16[1024,384]{1,0:T(8,128)(2,1)} %get-tuple-element.41.scaled, bf16[8,1024,512]{2,1,0:T(8,128)(2,1)} %get-tuple-element.42.chance, bf16[8,1024,512]{2,1,0:T(8,128)(2,1)} %get-tuple-element.43.slope), custom_call_target="tpu_custom_call" | custom-call | flops 3221225472 | bytes 1048576 | tf_op jit(solution)/shard_map/gather/pallas_call | solution.py:406
  105.3 1.9 collective-permute-start.8
  107.2 0.0 collective-permute-done.9
  107.2 0.7 add_convert_fusion.1
  108.0 3.9 %collective-permute-start.10 = (bf16[512,256]{1,0:T(8,128)(2,1)}, bf16[512,256]{1,0:T(8,128)(2,1)S(1)}, u32[]{:S(2)}, u32[]{:S(2)}) collective-permute-start(bf16[512,256]{1,0:T(8,128)(2,1)} %add_convert_fusion.1), channel_id=1, source_target_pairs={{0,256},{256,0},{1,257},{257,1},{2,258},{258,2},{3,259},{259,3},{4... | collective-permute-start | bytes 786440 | tf_op jit(solution)/shard_map/ppermute | solution.py:444
  111.9 5.6 %collective-permute-start.12 = (bf16[2048,128]{1,0:T(8,128)(2,1)S(1)}, bf16[2048,128]{1,0:T(8,128)(2,1)S(1)}, u32[]{:S(2)}, u32[]{:S(2)}) collective-permute-start(bf16[2048,128]{1,0:T(8,128)(2,1)S(1)} %copy-done.1), channel_id=1, source_target_pairs={{0,1},{1,0},{2,3},{3,2},{4,5},{5,4},{6,7},{7,6},{8,9},{9,8},{10,11... | collective-permute-start | bytes 1572872 | tf_op jit(solution)/shard_map/ppermute | solution.py:444
  117.5 1.9 collective-permute-start.13
  119.4 0.0 collective-permute-done.8
  119.4 0.0 collective-permute-done.10
  119.4 0.1 add_convert_fusion.grads
  119.6 3.5 %collective-permute-start.11 = (bf16[256,256]{1,0:T(8,128)(2,1)S(1)}, bf16[256,256]{1,0:T(8,128)(2,1)S(1)}, u32[]{:S(2)}, u32[]{:S(2)}) collective-permute-start(bf16[256,256]{1,0:T(8,128)(2,1)S(1)} %constant_dynamic-slice_fusion), channel_id=1, source_target_pairs={{0,1},{1,0},{2,3},{3,2},{4,5},{5,4},{6,7},{7,6},{8,9},{9,8},{10,11... | collective-permute-start | bytes 393224 | tf_op jit(solution)/shard_map/ppermute | solution.py:444
  123.0 1.0 collective-permute-done.11.from_core
  124.0 20.2 %reduce-scatter.3.cloned.1.call-done = f32[256,128]{1,0:T(8,128)} async-done(((f32[1024,128]{1,0:T(8,128)}), f32[256,128]{1,0:T(8,128)}) %reduce-scatter.3.cloned.1.call-update) | async-done | bytes 131088 | tf_op jit(solution)/shard_map/reduce_scatter | solution.py:489
  144.2 0.0 collective-permute-done.12.far_kw
  144.2 0.0 collective-permute-done.13.far_vw
  144.2 2.2 %project.1 = bf16[16,256,128]{2,1,0:T(8,128)(2,1)} custom-call(s32[1]{0:T(128)} %bitcast.3.core, bf16[512,256]{1,0:T(8,128)(2,1)S(1)} %add_convert_fusion.grads, bf16[256,256]{1,0:T(8,128)(2,1)S(1)} %collective-permute-done.11.from_core, bf16[2048,128]{1,0:T(8,128)(2,1)S(1)} %copy-done.1, bf16[2048,128]{1,0:T(8,128)(2,1)S(1)} %copy-done.2, ...), custom_call_target="tpu_custom_call" | custom-call | tf_op jit(solution)/shard_map/project/pallas_call | solution.py:432
  146.5 6.7 %all-to-all-start.1 = ((bf16[16,256,128]{2,1,0:T(8,128)(2,1)}), bf16[16,256,128]{2,1,0:T(8,128)(2,1)S(1)}, u32[]{:S(2)}, u32[]{:S(2)}) async-start(bf16[16,256,128]{2,1,0:T(8,128)(2,1)} %project.1), calls=%async_computation.3 | async-start | bytes 2097152 | tf_op jit(solution)/shard_map/all_to_all | solution.py:505
  153.1 0.0 reduce-scatter.5.cloned.1.call-start
  153.2 0.7 reduce-scatter.5.cloned.1.call-update
  153.9 33.6 %reduce-scatter.5.cloned.1.call-done = f32[128,128]{1,0:T(8,128)} async-done(((f32[256,128]{1,0:T(8,128)}), f32[128,128]{1,0:T(8,128)}) %reduce-scatter.5.cloned.1.call-update) | async-done | bytes 65552 | tf_op jit(solution)/shard_map/reduce_scatter | solution.py:504
  187.5 1.5 convert_element_type.44
  189.0 0.0 all-to-all-done.1
  189.0 0.8 reduce
  (28 shorter events, 0.1 us)
Async XLA Ops:
  7.2 35.4 %copy-start = (s32[32,64]{1,0:T(8,128)S(1)}, s32[32,64]{1,0:T(8,128)}, u32[]{:S(2)}) copy-start(s32[32,64]{1,0:T(8,128)} %param.14) | copy-start | bytes 24580
  8.2 58.0 %copy-start.4 = (bf16[512,256]{1,0:T(8,128)(2,1)}, bf16[512,256]{1,0:T(8,128)(2,1)S(1)}, u32[]{:S(2)}) copy-start(bf16[512,256]{1,0:T(8,128)(2,1)S(1)} %join.3.near_ref.rest_0_) | copy-start | bytes 786436
  9.1 34.0 %collective-permute-start.2 = (bf16[128,256]{1,0:T(8,128)(2,1)S(1)}, bf16[128,256]{1,0:T(8,128)(2,1)S(1)}, u32[]{:S(2)}, u32[]{:S(2)}) collective-permute-start(bf16[128,256]{1,0:T(8,128)(2,1)S(1)} %join.2), channel_id=1, source_target_pairs={{0,64},{16,80},{32,96},{48,112},{64,128},{80,144},{96,160},{112,17... | collective-permute-start | bytes 196616 | tf_op jit(solution)/shard_map/ppermute | solution.py:444
  18.7 24.4 %collective-permute-start.3 = (bf16[128,256]{1,0:T(8,128)(2,1)S(1)}, bf16[128,256]{1,0:T(8,128)(2,1)S(1)}, u32[]{:S(2)}, u32[]{:S(2)}) collective-permute-start(bf16[128,256]{1,0:T(8,128)(2,1)S(1)} %join.2), channel_id=1, source_target_pairs={{0,192},{16,208},{32,224},{48,240},{64,0},{80,16},{96,32},{112,48}... | collective-permute-start | bytes 196616 | tf_op jit(solution)/shard_map/ppermute | solution.py:444
  24.3 25.1 %collective-permute-start.5 = (bf16[128,256]{1,0:T(8,128)(2,1)S(1)}, bf16[128,256]{1,0:T(8,128)(2,1)S(1)}, u32[]{:S(2)}, u32[]{:S(2)}) collective-permute-start(bf16[128,256]{1,0:T(8,128)(2,1)S(1)} %join.2), channel_id=1, source_target_pairs={{0,128},{16,144},{32,160},{48,176},{64,192},{80,208},{96,224},{112... | collective-permute-start | bytes 196616 | tf_op jit(solution)/shard_map/ppermute | solution.py:444
  34.5 17.5 %collective-permute-start = (bf16[512,256]{1,0:T(8,128)(2,1)S(1)}, bf16[512,256]{1,0:T(8,128)(2,1)S(1)}, u32[]{:S(2)}, u32[]{:S(2)}) collective-permute-start(bf16[512,256]{1,0:T(8,128)(2,1)S(1)} %join.3.near_ref.rest_0_), channel_id=1, source_target_pairs={{0,256},{256,0},{1,257},{257,1},{2,258},{258,2},{3,259},{259,3},{4... | collective-permute-start | bytes 786440 | tf_op jit(solution)/shard_map/ppermute | solution.py:444
  39.2 17.1 %collective-permute-start.1 = (bf16[512,256]{1,0:T(8,128)(2,1)S(1)}, bf16[512,256]{1,0:T(8,128)(2,1)S(1)}, u32[]{:S(2)}, u32[]{:S(2)}) collective-permute-start(bf16[512,256]{1,0:T(8,128)(2,1)S(1)} %join.3.near_ref.rest_0_), channel_id=1, source_target_pairs={{0,16},{16,0},{1,17},{17,1},{2,18},{18,2},{3,19},{19,3},{4,20},{20... | collective-permute-start | bytes 786440 | tf_op jit(solution)/shard_map/ppermute | solution.py:444
  42.6 23.7 %copy-start.8 = (s32[8]{0:T(128)}, s32[8]{0:T(128)S(1)}, u32[]{:S(2)}) copy-start(s32[8]{0:T(128)S(1)} %and_select_fusion.places) | copy-start | bytes 100
  43.1 23.1 %copy-start.9 = (s32[128]{0:T(128)}, s32[128]{0:T(128)S(1)}, u32[]{:S(2)}) copy-start(s32[128]{0:T(128)S(1)} %reshape.24.member) | copy-start | bytes 1540
  43.2 11.3 %collective-permute-start.6 = (bf16[256,256]{1,0:T(8,128)(2,1)S(1)}, bf16[256,256]{1,0:T(8,128)(2,1)S(1)}, u32[]{:S(2)}, u32[]{:S(2)}) collective-permute-start(bf16[256,256]{1,0:T(8,128)(2,1)S(1)} %get-tuple-element.57), channel_id=1, source_target_pairs={{0,224},{16,240},{32,0},{48,16},{64,32},{80,48},{96,64},{112,80},{... | collective-permute-start | bytes 393224 | tf_op jit(solution)/shard_map/ppermute | solution.py:444
  45.4 11.0 %collective-permute-start.7 = (bf16[256,256]{1,0:T(8,128)(2,1)S(1)}, bf16[256,256]{1,0:T(8,128)(2,1)S(1)}, u32[]{:S(2)}, u32[]{:S(2)}) collective-permute-start(bf16[256,256]{1,0:T(8,128)(2,1)S(1)} %get-tuple-element.56), channel_id=1, source_target_pairs={{0,32},{16,48},{32,64},{48,80},{64,96},{80,112},{96,128},{112,144}... | collective-permute-start | bytes 393224 | tf_op jit(solution)/shard_map/ppermute | solution.py:444
  49.4 10.2 %collective-permute-start.4 = (bf16[512,256]{1,0:T(8,128)(2,1)S(1)}, bf16[512,256]{1,0:T(8,128)(2,1)S(1)}, u32[]{:S(2)}, u32[]{:S(2)}) collective-permute-start(bf16[512,256]{1,0:T(8,128)(2,1)S(1)} %join.3.near_ref.rest_0_), channel_id=1, source_target_pairs={{0,272},{16,256},{256,16},{272,0},{1,273},{17,257},{257,17},{273,1... | collective-permute-start | bytes 786440 | tf_op jit(solution)/shard_map/ppermute | solution.py:465
  52.0 14.2 %copy-start.3 = (bf16[512,256]{1,0:T(8,128)(2,1)}, bf16[512,256]{1,0:T(8,128)(2,1)S(1)}, u32[]{:S(2)}) copy-start(bf16[512,256]{1,0:T(8,128)(2,1)S(1)} %constant_dynamic-update-slice_fusion.piece.rest_4_.rest_0_) | copy-start | bytes 786436
  52.0 14.2 %copy-start.10 = (bf16[512,256]{1,0:T(8,128)(2,1)}, bf16[512,256]{1,0:T(8,128)(2,1)S(1)}, u32[]{:S(2)}) copy-start(bf16[512,256]{1,0:T(8,128)(2,1)S(1)} %collective-permute-done.side_ref.rest_1_) | copy-start | bytes 786436
  54.5 11.8 %copy-start.5 = (bf16[256,256]{1,0:T(8,128)(2,1)}, bf16[256,256]{1,0:T(8,128)(2,1)S(1)}, u32[]{:S(2)}) copy-start(bf16[256,256]{1,0:T(8,128)(2,1)S(1)} %collective-permute-done.6.rest_5_.rest_1_) | copy-start | bytes 393220
  56.3 9.9 %copy-start.6 = (bf16[256,256]{1,0:T(8,128)(2,1)}, bf16[256,256]{1,0:T(8,128)(2,1)S(1)}, u32[]{:S(2)}) copy-start(bf16[256,256]{1,0:T(8,128)(2,1)S(1)} %collective-permute-done.7.rest_6_.rest_2_) | copy-start | bytes 393220
  56.3 9.9 %copy-start.11 = (bf16[512,256]{1,0:T(8,128)(2,1)}, bf16[512,256]{1,0:T(8,128)(2,1)S(1)}, u32[]{:S(2)}) copy-start(bf16[512,256]{1,0:T(8,128)(2,1)S(1)} %collective-permute-done.1.rest_2_) | copy-start | bytes 786436
  59.6 6.7 %copy-start.12 = (bf16[512,256]{1,0:T(8,128)(2,1)}, bf16[512,256]{1,0:T(8,128)(2,1)S(1)}, u32[]{:S(2)}) copy-start(bf16[512,256]{1,0:T(8,128)(2,1)S(1)} %collective-permute-done.4.rest_3_) | copy-start | bytes 786436
  66.3 0.6 copy-start.7
  66.9 19.0 %all-to-all-start = ((bf16[8,48,128]{2,1,0:T(8,128)(2,1)}), bf16[8,48,128]{2,1,0:T(8,128)(2,1)S(1)}, u32[]{:S(2)}, u32[]{:S(2)}) async-start(bf16[8,48,128]{2,1,0:T(8,128)(2,1)} %get-tuple-element.34), calls=%async_computation | async-start | bytes 196608 | tf_op jit(solution)/shard_map/all_to_all | solution.py:484
  73.4 70.8 %reduce-scatter.3.cloned.1.call-start = ((), (), s32[]{:S(2)}) async-start(), calls=%async_computation.4 | async-start | bytes 655360 | tf_op jit(solution)/shard_map/reduce_scatter | solution.py:489
  95.4 11.8 %collective-permute-start.9 = (bf16[512,256]{1,0:T(8,128)(2,1)S(1)}, bf16[512,256]{1,0:T(8,128)(2,1)S(1)}, u32[]{:S(2)}, u32[]{:S(2)}) collective-permute-start(bf16[512,256]{1,0:T(8,128)(2,1)S(1)} %get-tuple-element.48), channel_id=1, source_target_pairs={{0,16},{16,0},{1,17},{17,1},{2,18},{18,2},{3,19},{19,3},{4,20},{20... | collective-permute-start | bytes 786440 | tf_op jit(solution)/shard_map/ppermute | solution.py:444
  100.0 11.9 %copy-start.1 = (bf16[2048,128]{1,0:T(8,128)(2,1)S(1)}, bf16[2048,128]{1,0:T(8,128)(2,1)}, u32[]{:S(2)}) copy-start(bf16[2048,128]{1,0:T(8,128)(2,1)} %kw) | copy-start | bytes 1572868
  100.0 17.4 %copy-start.2 = (bf16[2048,128]{1,0:T(8,128)(2,1)S(1)}, bf16[2048,128]{1,0:T(8,128)(2,1)}, u32[]{:S(2)}) copy-start(bf16[2048,128]{1,0:T(8,128)(2,1)} %vw) | copy-start | bytes 1572868
  105.3 14.1 %collective-permute-start.8 = (bf16[512,256]{1,0:T(8,128)(2,1)S(1)}, bf16[512,256]{1,0:T(8,128)(2,1)S(1)}, u32[]{:S(2)}, u32[]{:S(2)}) collective-permute-start(bf16[512,256]{1,0:T(8,128)(2,1)S(1)} %get-tuple-element.46), channel_id=1, source_target_pairs={{0,16},{16,0},{1,17},{17,1},{2,18},{18,2},{3,19},{19,3},{4,20},{20... | collective-permute-start | bytes 786440 | tf_op jit(solution)/shard_map/ppermute | solution.py:444
  108.0 11.5 %collective-permute-start.10 = (bf16[512,256]{1,0:T(8,128)(2,1)}, bf16[512,256]{1,0:T(8,128)(2,1)S(1)}, u32[]{:S(2)}, u32[]{:S(2)}) collective-permute-start(bf16[512,256]{1,0:T(8,128)(2,1)} %add_convert_fusion.1), channel_id=1, source_target_pairs={{0,256},{256,0},{1,257},{257,1},{2,258},{258,2},{3,259},{259,3},{4... | collective-permute-start | bytes 786440 | tf_op jit(solution)/shard_map/ppermute | solution.py:444
  111.9 32.3 %collective-permute-start.12 = (bf16[2048,128]{1,0:T(8,128)(2,1)S(1)}, bf16[2048,128]{1,0:T(8,128)(2,1)S(1)}, u32[]{:S(2)}, u32[]{:S(2)}) collective-permute-start(bf16[2048,128]{1,0:T(8,128)(2,1)S(1)} %copy-done.1), channel_id=1, source_target_pairs={{0,1},{1,0},{2,3},{3,2},{4,5},{5,4},{6,7},{7,6},{8,9},{9,8},{10,11... | collective-permute-start | bytes 1572872 | tf_op jit(solution)/shard_map/ppermute | solution.py:444
  117.5 26.7 %collective-permute-start.13 = (bf16[2048,128]{1,0:T(8,128)(2,1)S(1)}, bf16[2048,128]{1,0:T(8,128)(2,1)S(1)}, u32[]{:S(2)}, u32[]{:S(2)}) collective-permute-start(bf16[2048,128]{1,0:T(8,128)(2,1)S(1)} %copy-done.2), channel_id=1, source_target_pairs={{0,1},{1,0},{2,3},{3,2},{4,5},{5,4},{6,7},{7,6},{8,9},{9,8},{10,11... | collective-permute-start | bytes 1572872 | tf_op jit(solution)/shard_map/ppermute | solution.py:444
  119.6 4.4 %collective-permute-start.11 = (bf16[256,256]{1,0:T(8,128)(2,1)S(1)}, bf16[256,256]{1,0:T(8,128)(2,1)S(1)}, u32[]{:S(2)}, u32[]{:S(2)}) collective-permute-start(bf16[256,256]{1,0:T(8,128)(2,1)S(1)} %constant_dynamic-slice_fusion), channel_id=1, source_target_pairs={{0,1},{1,0},{2,3},{3,2},{4,5},{5,4},{6,7},{7,6},{8,9},{9,8},{10,11... | collective-permute-start | bytes 393224 | tf_op jit(solution)/shard_map/ppermute | solution.py:444
  146.5 42.5 %all-to-all-start.1 = ((bf16[16,256,128]{2,1,0:T(8,128)(2,1)}), bf16[16,256,128]{2,1,0:T(8,128)(2,1)S(1)}, u32[]{:S(2)}, u32[]{:S(2)}) async-start(bf16[16,256,128]{2,1,0:T(8,128)(2,1)} %project.1), calls=%async_computation.3 | async-start | bytes 2097152 | tf_op jit(solution)/shard_map/all_to_all | solution.py:505
  153.1 34.4 %reduce-scatter.5.cloned.1.call-start = ((), (), s32[]{:S(2)}) async-start(), calls=%async_computation.5 | async-start | bytes 196608 | tf_op jit(solution)/shard_map/reduce_scatter | solution.py:504
Sparse Core Ops, SparseCore 0:
  100.1 44.0 reduce-scatter.2
  156.7 30.7 reduce-scatter.4

commit v9 on v8

--- a/solution.py
+++ b/solution.py
@@ -9,11 +9,11 @@
 
 HEAD_DIM = 64
 BLOCK = 128
-AXES = ("xh", "z2", "z4", "par", "xl", "y", "core")
-SIZES = (2, 2, 4, 2, 2, 4, 2)
-ZH = ("z2", "z4")
-Z = ("z2", "z4", "par")
-CTX = ("xh", "z2", "z4", "par")
+AXES = ("xh", "zh", "par", "xl", "y", "core")
+SIZES = (2, 8, 2, 2, 4, 2)
+ZH = "zh"
+Z = ("zh", "par")
+CTX = ("xh", "zh", "par")
 HEAD = ("xl", "y", "core")
 BIG = 1e30
 
@@ -67,22 +67,37 @@
     return pairs
 
 
-def join_kernel(left, right, out, sems):
-    width = left.shape[1]
-    for copy in fetch([(left, out.at[:, pl.ds(0, width)]), (right, out.at[:, pl.ds(width, width)])], sems):
+def join_kernel(*refs):
+    *given, first, second, sems = refs
+    pairs = []
+    for i, source in enumerate(given):
+        width = source.shape[1]
+        pairs.append((source, (first, second)[i // 2].at[:, pl.ds(i % 2 * width, width)]))
+    for copy in fetch(pairs, sems):
         copy.wait()
 
 
-def join(left, right):
+def join(*given):
     return pl.pallas_call(
         join_kernel,
-        out_shape=jax.ShapeDtypeStruct((left.shape[0], 2 * left.shape[1]), left.dtype),
-        in_specs=[ANY] * 2,
-        out_specs=VMEM,
-        scratch_shapes=[pltpu.SemaphoreType.DMA((2,))],
+        out_shape=[jax.ShapeDtypeStruct((x.shape[0], 2 * x.shape[1]), x.dtype) for x in given[::2]],
+        in_specs=[ANY] * 4,
+        out_specs=[VMEM] * 2,
+        scratch_shapes=[pltpu.SemaphoreType.DMA((4,))],
         compiler_params=room(4),
         name="join",
-    )(*in_hbm(left, right))
+    )(*in_hbm(*given))
+
+
+def pair_places(p):
+    here, count = lax.axis_index("zh"), lax.axis_size("zh")
+    found = []
+    for steps in (SLOTS[::2], SLOTS[1::2]):
+        step = jnp.int32(steps[-1])
+        for i, other in enumerate(steps[:-1]):
+            step = jnp.where(p == i, other, step)
+        found.append(lax.rem(here + step + count, count))
+    return found
 
 
 def load_targets(pieces, held):
@@ -142,13 +157,13 @@
                 stats[pl.ds(start + 2 * place + h, 1), :] = row[:, (2 * h + s) * BLOCK : (2 * h + s + 1) * BLOCK]
 
 
-def early_kernel(places, member, near_ref, side_ref, piece, stats, kv):
+def early_kernel(member, near_ref, side_ref, piece, stats, kv):
     load_targets((near_ref, side_ref), kv)
     blocks = 2 * kv.shape[0] // BLOCK
 
     def step(p, carry):
         rows = pl.ds(pl.multiple_of(p * 2 * BLOCK, 2 * BLOCK), 2 * BLOCK)
-        first, second = places[2 * p], places[2 * p + 1]
+        first, second = pair_places(p)
         query, out = split_heads(piece[rows, :BLOCK]), split_heads(piece[rows, BLOCK:])
         store_stats(stats, first, second, part_stats(kv, query, out, member, first, second, 0, blocks))
         return carry
@@ -156,7 +171,7 @@
     lax.fori_loop(0, piece.shape[0] // (2 * BLOCK), step, 0)
 
 
-def forward_kernel(places, member, *rest):
+def forward_kernel(member, *rest):
     tables, pieces = rest[:4], rest[4:7]
     before, result, stats, held, kv = rest[7:]
     load_targets(pieces, held)
@@ -169,7 +184,7 @@
 
     def step(p, done):
         rows = pl.ds(pl.multiple_of(p * 2 * BLOCK, 2 * BLOCK), 2 * BLOCK)
-        first, second = places[2 * p], places[2 * p + 1]
+        first, second = pair_places(p)
         query, out = split_heads(held[rows, :BLOCK]), split_heads(held[rows, BLOCK:])
         if done:
             one = lanes_of(before, first, second, 0), lanes_of(before, first, second, half)
@@ -195,26 +210,26 @@
         result[peer] = message
 
 
-def forward(places, member, tables, pieces, before):
-    count = places.shape[0]
+def forward(member, tables, pieces, before):
+    count = len(SLOTS)
     rows = sum(p.shape[0] for p in pieces)
     enc = sum(t.shape[0] for t in tables)
     local = jax.ShapeDtypeStruct((4 * count, BLOCK), jnp.float32)
     if before is None:
         kernel, shapes = early_kernel, local
         scratch = [pltpu.VMEM((enc, 2 * BLOCK), jnp.bfloat16)]
-        given = [places, member, *tables, *pieces]
+        given = [member, *tables, *pieces]
     else:
         kernel, shapes = forward_kernel, [jax.ShapeDtypeStruct((count, 6 * count, BLOCK), jnp.bfloat16), local]
         scratch = [
             pltpu.VMEM((rows, 2 * BLOCK), jnp.bfloat16),
             pltpu.VMEM((2, enc // 2, 2 * BLOCK), jnp.bfloat16),
         ]
-        given = [places, member, *tables, *pieces, before]
+        given = [member, *tables, *pieces, before]
     return pl.pallas_call(
         kernel,
         out_shape=shapes,
-        in_specs=[SMEM] * 2 + [VMEM] * (len(given) - 2),
+        in_specs=[SMEM] + [VMEM] * (len(given) - 1),
         out_specs=VMEM if before is None else [VMEM] * 2,
         scratch_shapes=scratch,
         compiler_params=room(20),
@@ -237,7 +252,7 @@
     return jnp.concatenate([stats[pl.ds(s, 1), :] for s in spots], axis=1)
 
 
-def local_kernel(places, member, stats_ref, *rest):
+def local_kernel(member, stats_ref, *rest):
     tables, pieces = rest[:4], rest[4:7]
     sums, chances, slopes, kv, held, stats, turned, sems = rest[7:]
     side, p = pl.program_id(0), pl.program_id(1)
@@ -257,7 +272,7 @@
     blocks = enc // BLOCK
     half = stats.shape[0] // 2
     rows = pl.ds(pl.multiple_of(p * 2 * BLOCK, 2 * BLOCK), 2 * BLOCK)
-    first, second = places[2 * p], places[2 * p + 1]
+    first, second = pair_places(p)
     log_total = lanes_of(stats, first, second, 0)
     log_total = jnp.where(log_total > -0.5 * BIG, log_total, BIG)
     mean = lanes_of(stats, first, second, half)
@@ -276,17 +291,17 @@
             sums[0, i, dims, :] = dot_nn(turned[dims, :], table[0, :, lanes])
 
 
-def local(places, member, stats, tables, pieces):
+def local(member, stats, tables, pieces):
     rows = sum(p.shape[0] for p in pieces)
     enc = sum(t.shape[0] for t in tables) // 2
     pairs = rows // (2 * BLOCK)
     table = pltpu.HBM((2 * pairs, enc, 4 * BLOCK), jnp.bfloat16)
-    given = in_hbm(places, member, stats, *tables, *pieces)
+    given = in_hbm(member, stats, *tables, *pieces)
     return pl.pallas_call(
         local_kernel,
         grid=(2, pairs),
         out_shape=[pltpu.HBM((2 * pairs, 2, BLOCK, 2 * BLOCK), jnp.float32)] + [table] * 2,
-        in_specs=[SMEM] * 2 + [ANY] * (len(given) - 2),
+        in_specs=[SMEM] + [ANY] * (len(given) - 1),
         out_specs=[pl.BlockSpec((1, 2, BLOCK, 2 * BLOCK), lambda side, p: (side * pairs + p, 0, 0, 0))]
         + [pl.BlockSpec((1, enc, 4 * BLOCK), lambda side, p: (side * pairs + p, 0, 0))] * 2,
         scratch_shapes=[
@@ -294,7 +309,7 @@
             pltpu.VMEM((rows, 2 * BLOCK), jnp.bfloat16),
             pltpu.VMEM(stats.shape, stats.dtype),
             pltpu.VMEM((BLOCK, enc), jnp.bfloat16),
-            pltpu.SemaphoreType.DMA((len(given) - 2,)),
+            pltpu.SemaphoreType.DMA((len(given) - 1,)),
         ],
         compiler_params=room(20),
         cost_estimate=cost(3 * rows * 2 * enc * 4 * BLOCK, rows * enc * 4),
@@ -302,7 +317,7 @@
     )(*given)
 
 
-def scale_kernel(places, parts, stats_ref, sums_ref, *rest):
+def scale_kernel(parts, stats_ref, sums_ref, *rest):
     pieces = rest[:3]
     d_query, scaled, held, whole, stats, sums, sems = rest[3:]
     copies = fetch(stacked(pieces, held) + [(stats_ref, stats), (sums_ref, sums)], sems)
@@ -314,7 +329,7 @@
 
     def step(p, carry):
         rows = pl.ds(pl.multiple_of(p * 2 * BLOCK, 2 * BLOCK), 2 * BLOCK)
-        first, second = places[2 * p], places[2 * p + 1]
+        first, second = pair_places(p)
         share = jnp.exp(lanes_of(stats, first, second, 0) - lanes_of(whole, first, second, 0))
         shift = lanes_of(whole, first, second, half) - lanes_of(stats, first, second, half)
 
@@ -327,10 +342,9 @@
         share, shift = by_dim(share), by_dim(shift)
         slope = sums[p, 0] + sums[pairs + p, 0]
         chance = sums[p, 1] + sums[pairs + p, 1]
-        grad = (share * (slope - shift * chance)).T
-        far = d_query.shape[0] // 2
-        for place, part in ((first, grad[:BLOCK]), (second, grad[BLOCK:])):
-            d_query[2 * (place % far) + place // far] = part
+        grad = (share * (slope - shift * chance)).T.astype(jnp.bfloat16)
+        d_query[first] = grad[:BLOCK]
+        d_query[second] = grad[BLOCK:]
         share, shift = share.T, shift.T
         query = held[rows, :BLOCK].astype(jnp.float32) * share
         out = held[rows, BLOCK:].astype(jnp.float32) * share
@@ -342,24 +356,24 @@
     lax.fori_loop(0, pairs, step, 0)
 
 
-def scale(places, parts, stats, sums, pieces):
-    count = places.shape[0]
+def scale(parts, stats, sums, pieces):
+    count = len(SLOTS)
     rows = sum(p.shape[0] for p in pieces)
-    given = [*in_hbm(places), parts, *in_hbm(stats, sums, *pieces)]
+    given = [parts, *in_hbm(stats, sums, *pieces)]
     return pl.pallas_call(
         scale_kernel,
         out_shape=[
-            pltpu.HBM((count, BLOCK, BLOCK), jnp.float32),
+            pltpu.HBM((count, BLOCK, BLOCK), jnp.bfloat16),
             pltpu.HBM((rows, 3 * BLOCK), jnp.bfloat16),
         ],
-        in_specs=[SMEM, VMEM] + [ANY] * (len(given) - 2),
+        in_specs=[VMEM] + [ANY] * (len(given) - 1),
         out_specs=[VMEM] * 2,
         scratch_shapes=[
             pltpu.VMEM((rows, 2 * BLOCK), jnp.bfloat16),
             pltpu.VMEM((4 * count, BLOCK), jnp.float32),
             pltpu.VMEM(stats.shape, stats.dtype),
             pltpu.VMEM(sums.shape, sums.dtype),
-            pltpu.SemaphoreType.DMA((len(given) - 2,)),
+            pltpu.SemaphoreType.DMA((len(given) - 1,)),
         ],
         compiler_params=room(16),
         cost_estimate=cost(1 << 27, 1 << 16),
@@ -399,7 +413,7 @@
 
 def gather(scaled, chance, slope, side, kind):
     pairs, enc, lanes = chance.shape
-    pairs, step = pairs // 2, 2
+    pairs, step = pairs // 2, 1
     steps = pairs // step
     table = pl.BlockSpec((step, enc, lanes), lambda p: (side * steps + p, 0, 0))
     given = in_hbm(scaled, chance, slope)
@@ -454,10 +468,9 @@
     enc_rows = keys.shape[0]
     enc_blocks = enc_rows // BLOCK
 
-    own = join(keys, values)
+    near, own = join(queries, d_out, keys, values)
     side = moved(own, "xh", 1)
     next_ = moved(own, "par", 1)
-    near, own = lax.optimization_barrier((join(queries, d_out), own))
     ahead = moved(near, Z, 4)
     behind = moved(near, Z, -4)
     across = moved(near, Z, 8)
@@ -465,7 +478,6 @@
     tables = [own, side, next_, lax.ppermute(late, ("xh", "par"), [(0, 3), (1, 2), (2, 1), (3, 0)])]
 
     count = lax.axis_size(ZH)
-    places = (place + jnp.asarray(SLOTS, jnp.int32)) % count
     listed = lax.dynamic_slice_in_dim(block_lists, half * depth, depth, 0).reshape(count, depth // count, -1)
     listed = lax.dynamic_index_in_dim(listed, parity, 1, keepdims=False)
     step = jnp.arange(enc_blocks, dtype=jnp.int32)
@@ -478,18 +490,18 @@
     above = moved(bundle[: 2 * BLOCK], Z, -2)
     below = moved(bundle[BLOCK : 3 * BLOCK], Z, 2)
 
-    early = forward(places, member, tables[:2], [bundle], None)
+    early = forward(member, tables[:2], [bundle], None)
     pieces = [bundle, above, below]
-    parts, stats = forward(places, member, tables, pieces, early)
+    parts, stats = forward(member, tables, pieces, early)
     parts = lax.all_to_all(parts, ZH, 0, 0, tiled=True)
-    sums, chances, slopes = local(places, member, stats, tables, pieces)
+    sums, chances, slopes = local(member, stats, tables, pieces)
     parts, sums, chances, slopes = lax.optimization_barrier((parts, sums, chances, slopes))
 
-    d_query, scaled = scale(places, parts, stats, sums, pieces)
-    d_query = lax.psum_scatter(d_query.reshape(-1, BLOCK), "z4", scatter_dimension=0, tiled=True)
+    d_query, scaled = scale(parts, stats, sums, pieces)
+    d_query = lax.all_to_all(d_query, ZH, 0, 0, tiled=True)
     onward, next_ = (moved(part, "par", 1) for part in reversed(gather(scaled, chances, slopes, 1, bf16)))
     grads, side = gather(scaled, chances, slopes, 0, f32)
-    side, onward = lax.optimization_barrier((side, onward))
+    side, onward, d_query = lax.optimization_barrier((side, onward, d_query))
     from_half = moved((side + onward.astype(f32)).astype(bf16), "xh", 1)
     grads, key_weight, value_weight = lax.optimization_barrier((grads, key_weight, value_weight))
     far_key_weight = moved(key_weight, "core", 1)
@@ -499,13 +511,11 @@
 
     cores = lax.axis_size("core")
     weights = (key_weight, value_weight, far_key_weight, far_value_weight)
-    from_core, d_query = lax.optimization_barrier((from_core, d_query))
     memory = project(core[None], grads, from_core, *weights)
-    d_query = lax.psum_scatter(d_query, "z2", scatter_dimension=0, tiled=True)
     memory = lax.all_to_all(memory, HEAD, 0, 0, tiled=True)
     memory = memory.reshape(-1, cores, *memory.shape[1:]).astype(f32)
     d_memory = jnp.sum(memory, axis=0).reshape(keys.shape).astype(bf16)
-    d_queries = d_query.astype(bf16)
+    d_queries = jnp.sum(d_query.astype(f32), axis=0).astype(bf16)
     return d_queries, d_memory
 
 

time: 198 us -> 155 us (0.78)
  waiting for transfers between devices: 60.9 us -> 19.4 us
  starting transfers between devices: 76.1 us -> 89.6 us
  between operations: 14.5 us -> 1.13 us
    reduce_scatter x2 -> x0, waiting for transfers between devices: 53.9 us -> none  [the longest x1 33.6 us: body(): d_query = lax.psum_scatter(d_query, 'z2', scatter_dimension=0, tiled=True)]
    all_to_all x1, waiting for transfers between devices: 0.01 us -> 15.2 us  [body(): memory = lax.all_to_all(memory, HEAD, 0, 0, tiled=True)]
    all_to_all x0 -> x1, starting transfers between devices: none -> 11.3 us  [body(): d_query = lax.all_to_all(d_query, ZH, 0, 0, tiled=True)]
    all_to_all x1, starting transfers between devices: 6.51 us -> 9.94 us  [body(): parts = lax.all_to_all(parts, ZH, 0, 0, tiled=True)]
    ppermute x1, waiting for transfers between devices: 3.25 us -> 1.14 us  [body(): lax.ppermute(late, ('xh', 'par'), [(0, 3), (1, 2), (2, 1), (3, 0)])]
    pallas_call x4 -> x3, Pallas kernels: 10.9 us -> 10.1 us  [the longest x2 9.09 us: forward(): pl.pallas_call(kernel, out_shape=shapes, in_specs=[SMEM] + [VMEM] * (len(...]
  transfers between devices with their start and end apart: 18 -> 17, of which waited for: 6 -> 5; matrix products, arithmetic and copies ran while one was open for 2% -> 2% of each run, Pallas kernels for 10% -> 17%
where the time goes in v9:
time: 155 us; the launch traced here: 154 us
  starting transfers between devices  89.6 us (58%)
  Pallas kernels  40 us (26%)
  waiting for transfers between devices  19.4 us (13%)
  other arithmetic  3.65 us (2%)
    ppermute x13, starting transfers between devices, moved(): lax.ppermute(value, axis, [(i, (i + steps) % count) for i in range(count)])  60.9 us
    all_to_all x1, waiting for transfers between devices, body(): memory = lax.all_to_all(memory, HEAD, 0, 0, tiled=True)  15.2 us
    pallas_call x1, Pallas kernels, local(): pl.pallas_call(local_kernel, grid=(2, pairs), out_shape=[pltpu.HBM((2 * p...  12.2 us
    pallas_call x2, Pallas kernels, gather(): pl.pallas_call(gather_kernel, grid=(steps,), out_shape=[jax.ShapeDtypeStr...  11.8 us
    all_to_all x1, starting transfers between devices, body(): d_query = lax.all_to_all(d_query, ZH, 0, 0, tiled=True)  11.3 us
    all_to_all x1, starting transfers between devices, body(): parts = lax.all_to_all(parts, ZH, 0, 0, tiled=True)  9.94 us
    pallas_call x2, Pallas kernels, forward(): pl.pallas_call(kernel, out_shape=shapes, in_specs=[SMEM] + [VMEM] * (len(...  9.09 us
    all_to_all x1, starting transfers between devices, body(): memory = lax.all_to_all(memory, HEAD, 0, 0, tiled=True)  4.85 us
  transfers between devices with their start and end apart: 17, of which 5 were waited for; matrix products, arithmetic and copies ran while one was open for 2% of the time, Pallas kernels for 17%

profile of v9, /device:TPU:1, one launch (start us, length us, event | category | flops | bytes accessed | tf_op | source)
XLA Modules:
  0.0 153.9 jit_solution(16475638445074811545)
XLA Ops:
  0.6 0.0 copy-start
  0.6 1.0 join.1
  1.7 0.0 copy-start.8
  1.7 5.5 %collective-permute-start = (bf16[512,256]{1,0:T(8,128)(2,1)S(1)}, bf16[512,256]{1,0:T(8,128)(2,1)S(1)}, u32[]{:S(2)}, u32[]{:S(2)}) collective-permute-start(bf16[512,256]{1,0:T(8,128)(2,1)S(1)} %get-tuple-element.30.near_ref.rest_0_), channel_id=1, source_target_pairs={{0,256},{256,0},{1,257},{257,1},{2,258},{258,2},{3,259},{259,3},{4... | collective-permute-start | bytes 786440 | tf_op jit(solution)/shard_map/ppermute | solution.py:458
  7.2 3.5 %collective-permute-start.1 = (bf16[512,256]{1,0:T(8,128)(2,1)S(1)}, bf16[512,256]{1,0:T(8,128)(2,1)S(1)}, u32[]{:S(2)}, u32[]{:S(2)}) collective-permute-start(bf16[512,256]{1,0:T(8,128)(2,1)S(1)} %get-tuple-element.30.near_ref.rest_0_), channel_id=1, source_target_pairs={{0,16},{16,0},{1,17},{17,1},{2,18},{18,2},{3,19},{19,3},{4,20},{20... | collective-permute-start | bytes 786440 | tf_op jit(solution)/shard_map/ppermute | solution.py:458
  10.8 8.8 %collective-permute-start.2 = (bf16[128,256]{1,0:T(8,128)(2,1)S(1)}, bf16[128,256]{1,0:T(8,128)(2,1)S(1)}, u32[]{:S(2)}, u32[]{:S(2)}) collective-permute-start(bf16[128,256]{1,0:T(8,128)(2,1)S(1)} %get-tuple-element.29), channel_id=1, source_target_pairs={{0,64},{16,80},{32,96},{48,112},{64,128},{80,144},{96,160},{112,17... | collective-permute-start | bytes 196616 | tf_op jit(solution)/shard_map/ppermute | solution.py:458
  19.6 4.7 %collective-permute-start.3 = (bf16[128,256]{1,0:T(8,128)(2,1)S(1)}, bf16[128,256]{1,0:T(8,128)(2,1)S(1)}, u32[]{:S(2)}, u32[]{:S(2)}) collective-permute-start(bf16[128,256]{1,0:T(8,128)(2,1)S(1)} %get-tuple-element.29), channel_id=1, source_target_pairs={{0,192},{16,208},{32,224},{48,240},{64,0},{80,16},{96,32},{112,48}... | collective-permute-start | bytes 196616 | tf_op jit(solution)/shard_map/ppermute | solution.py:458
  24.2 10.3 %collective-permute-start.5 = (bf16[128,256]{1,0:T(8,128)(2,1)S(1)}, bf16[128,256]{1,0:T(8,128)(2,1)S(1)}, u32[]{:S(2)}, u32[]{:S(2)}) collective-permute-start(bf16[128,256]{1,0:T(8,128)(2,1)S(1)} %get-tuple-element.29), channel_id=1, source_target_pairs={{0,128},{16,144},{32,160},{48,176},{64,192},{80,208},{96,224},{112... | collective-permute-start | bytes 196616 | tf_op jit(solution)/shard_map/ppermute | solution.py:458
  34.5 0.0 copy-done
  34.6 0.1 pad_add_fusion
  34.7 0.3 compare_reduce_fusion
  35.0 0.1 reshape.20.member
  35.1 0.0 collective-permute-done.2
  35.1 0.0 collective-permute-done.3
  35.1 2.6 %collective-permute-start.4 = (bf16[512,256]{1,0:T(8,128)(2,1)S(1)}, bf16[512,256]{1,0:T(8,128)(2,1)S(1)}, u32[]{:S(2)}, u32[]{:S(2)}) collective-permute-start(bf16[512,256]{1,0:T(8,128)(2,1)S(1)} %get-tuple-element.30.near_ref.rest_0_), channel_id=1, source_target_pairs={{0,272},{16,256},{256,16},{272,0},{1,273},{17,257},{257,17},{273,1... | collective-permute-start | bytes 786440 | tf_op jit(solution)/shard_map/ppermute | solution.py:478
  37.7 1.9 %collective-permute-start.6 = (bf16[256,256]{1,0:T(8,128)(2,1)S(1)}, bf16[256,256]{1,0:T(8,128)(2,1)S(1)}, u32[]{:S(2)}, u32[]{:S(2)}) collective-permute-start(bf16[256,256]{1,0:T(8,128)(2,1)S(1)} %get-tuple-element.55), channel_id=1, source_target_pairs={{0,224},{16,240},{32,0},{48,16},{64,32},{80,48},{96,64},{112,80},{... | collective-permute-start | bytes 393224 | tf_op jit(solution)/shard_map/ppermute | solution.py:458
  39.7 0.0 collective-permute-done.5
  39.7 4.3 %collective-permute-start.7 = (bf16[256,256]{1,0:T(8,128)(2,1)S(1)}, bf16[256,256]{1,0:T(8,128)(2,1)S(1)}, u32[]{:S(2)}, u32[]{:S(2)}) collective-permute-start(bf16[256,256]{1,0:T(8,128)(2,1)S(1)} %get-tuple-element.54), channel_id=1, source_target_pairs={{0,32},{16,48},{32,64},{48,80},{64,96},{80,112},{96,128},{112,144}... | collective-permute-start | bytes 393224 | tf_op jit(solution)/shard_map/ppermute | solution.py:458
  44.0 0.0 copy-start.3
  44.0 0.0 collective-permute-done.side_ref.rest_1_
  44.0 0.0 copy-start.9
  44.0 2.5 %forward.2.rest_7_ = f32[32,128]{1,0:T(8,128)S(1)} custom-call(s32[128]{0:T(128)S(1)} %reshape.20.member, bf16[512,256]{1,0:T(8,128)(2,1)S(1)} %get-tuple-element.30.near_ref.rest_0_, bf16[512,256]{1,0:T(8,128)(2,1)S(1)} %collective-permute-done.side_ref.rest_1_, bf16[512,256]{1,0:T(8,128)(2,1)S(1)} %constant_dynamic-update-slice_fusion.piece.rest_4_.rest_0_), custom_call_target="tpu_custom_call" | custom-call | flops 2147483648 | bytes 1048576 | tf_op jit(solution)/shard_map/forward/pallas_call | solution.py:229
  46.5 0.0 collective-permute-done.6.rest_5_.rest_1_
  46.5 0.0 copy-start.4
  46.5 1.9 %collective-permute-done.7.rest_6_.rest_2_ = bf16[256,256]{1,0:T(8,128)(2,1)S(1)} collective-permute-done((bf16[256,256]{1,0:T(8,128)(2,1)S(1)}, bf16[256,256]{1,0:T(8,128)(2,1)S(1)}, u32[]{:S(2)}, u32[]{:S(2)}) %collective-permute-start.7) | collective-permute-done | bytes 131104 | tf_op jit(solution)/shard_map/ppermute | solution.py:458
  48.4 0.0 collective-permute-done.1.rest_2_
  48.4 1.1 collective-permute-done.4.rest_3_
  49.5 6.6 %forward.3 = (bf16[8,48,128]{2,1,0:T(8,128)(2,1)}, f32[32,128]{1,0:T(8,128)S(1)}) custom-call(s32[128]{0:T(128)S(1)} %reshape.20.member, bf16[512,256]{1,0:T(8,128)(2,1)S(1)} %get-tuple-element.30.near_ref.rest_0_, bf16[512,256]{1,0:T(8,128)(2,1)S(1)} %collective-permute-done.side_ref.rest_1_, bf16[512,256]{1,0:T(8,128)(2,1)S(1)} %collective-permute-done.1.rest_2_, ...), custom_call_target="tpu_custom_call" | custom-call | flops 8589934592 | bytes 1048576 | tf_op jit(solution)/shard_map/forward/pallas_call | solution.py:229
  56.2 0.0 copy-done.8
  56.2 0.0 copy-done.9
  56.2 0.0 copy-done.4
  56.2 0.0 copy-done.5
  56.2 0.0 copy-done.10
  56.2 0.0 copy-done.11
  56.2 0.0 copy-start.6
  56.2 9.9 %all-to-all-start = ((bf16[8,48,128]{2,1,0:T(8,128)(2,1)}), bf16[8,48,128]{2,1,0:T(8,128)(2,1)S(1)}, u32[]{:S(2)}, u32[]{:S(2)}) async-start(bf16[8,48,128]{2,1,0:T(8,128)(2,1)} %get-tuple-element.33), calls=%async_computation | async-start | bytes 196608 | tf_op jit(solution)/shard_map/all_to_all | solution.py:496
  66.2 12.2 %local.1 = (f32[8,2,128,256]{3,2,1,0:T(8,128)}, bf16[8,1024,512]{2,1,0:T(8,128)(2,1)}, bf16[8,1024,512]{2,1,0:T(8,128)(2,1)}) custom-call(s32[128]{0:T(128)} %copy-done.7, f32[32,128]{1,0:T(8,128)} %copy-done.6, bf16[512,256]{1,0:T(8,128)(2,1)} %copy-done.8, bf16[512,256]{1,0:T(8,128)(2,1)} %copy-done.9, bf16[512,256]{1,0:T(8,128)(2,1)} %copy-done.10, ...), custom_call_target="tpu_custom_call" | custom-call | flops 12884901888 | bytes 1048576 | tf_op jit(solution)/shard_map/local/pallas_call | solution.py:300
  78.4 0.2 all-to-all-done.parts
  78.6 3.6 %scale.1 = (bf16[8,128,128]{2,1,0:T(8,128)(2,1)}, bf16[1024,384]{1,0:T(8,128)(2,1)}) custom-call(bf16[8,48,128]{2,1,0:T(8,128)(2,1)S(1)} %all-to-all-done.parts, f32[32,128]{1,0:T(8,128)} %copy-done.6, f32[8,2,128,256]{3,2,1,0:T(8,128)} %get-tuple-element.39.sums_ref, bf16[512,256]{1,0:T(8,128)(2,1)} %copy-done.3, bf16[256,256]{1,0:T(8,128)(2,1)} %copy-done.4, ...), custom_call_target="tpu_custom_call" | custom-call | flops 536870912 | bytes 1048576 | tf_op jit(solution)/shard_map/scale/pallas_call | solution.py:363
  82.1 11.3 %all-to-all-start.1 = ((bf16[8,128,128]{2,1,0:T(8,128)(2,1)}), bf16[8,128,128]{2,1,0:T(8,128)(2,1)S(1)}, u32[]{:S(2)}, u32[]{:S(2)}) async-start(bf16[8,128,128]{2,1,0:T(8,128)(2,1)} %get-tuple-element.45), calls=%async_computation.1 | async-start | bytes 524288 | tf_op jit(solution)/shard_map/all_to_all | solution.py:501
  93.4 5.9 %gather.3 = (bf16[512,256]{1,0:T(8,128)(2,1)S(1)}, bf16[512,256]{1,0:T(8,128)(2,1)S(1)}) custom-call(bf16[1024,384]{1,0:T(8,128)(2,1)} %get-tuple-element.40.scaled, bf16[8,1024,512]{2,1,0:T(8,128)(2,1)} %get-tuple-element.41.chance, bf16[8,1024,512]{2,1,0:T(8,128)(2,1)} %get-tuple-element.42.slope), custom_call_target="tpu_custom_call" | custom-call | flops 3221225472 | bytes 1048576 | tf_op jit(solution)/shard_map/gather/pallas_call | solution.py:420
  99.4 1.9 %collective-permute-start.8 = (bf16[512,256]{1,0:T(8,128)(2,1)S(1)}, bf16[512,256]{1,0:T(8,128)(2,1)S(1)}, u32[]{:S(2)}, u32[]{:S(2)}) collective-permute-start(bf16[512,256]{1,0:T(8,128)(2,1)S(1)} %get-tuple-element.44), channel_id=1, source_target_pairs={{0,16},{16,0},{1,17},{17,1},{2,18},{18,2},{3,19},{19,3},{4,20},{20... | collective-permute-start | bytes 786440 | tf_op jit(solution)/shard_map/ppermute | solution.py:458
  101.3 0.0 copy-start.1
  101.3 0.0 copy-start.2
  101.3 3.5 %collective-permute-start.9 = (bf16[512,256]{1,0:T(8,128)(2,1)S(1)}, bf16[512,256]{1,0:T(8,128)(2,1)S(1)}, u32[]{:S(2)}, u32[]{:S(2)}) collective-permute-start(bf16[512,256]{1,0:T(8,128)(2,1)S(1)} %get-tuple-element.49), channel_id=1, source_target_pairs={{0,16},{16,0},{1,17},{17,1},{2,18},{18,2},{3,19},{19,3},{4,20},{20... | collective-permute-start | bytes 786440 | tf_op jit(solution)/shard_map/ppermute | solution.py:458
  104.8 5.9 %gather.2 = (f32[512,256]{1,0:T(8,128)S(1)}, f32[512,256]{1,0:T(8,128)S(1)}) custom-call(bf16[1024,384]{1,0:T(8,128)(2,1)} %get-tuple-element.40.scaled, bf16[8,1024,512]{2,1,0:T(8,128)(2,1)} %get-tuple-element.41.chance, bf16[8,1024,512]{2,1,0:T(8,128)(2,1)} %get-tuple-element.42.slope), custom_call_target="tpu_custom_call" | custom-call | flops 3221225472 | bytes 1048576 | tf_op jit(solution)/shard_map/gather/pallas_call | solution.py:420
  110.8 0.0 collective-permute-done.8
  110.8 0.0 all-to-all-done.1
  110.8 0.8 add_convert_fusion.1
  111.5 2.6 %collective-permute-start.10 = (bf16[512,256]{1,0:T(8,128)(2,1)}, bf16[512,256]{1,0:T(8,128)(2,1)}, u32[]{:S(2)}, u32[]{:S(2)}) collective-permute-start(bf16[512,256]{1,0:T(8,128)(2,1)} %add_convert_fusion.1), channel_id=1, source_target_pairs={{0,256},{256,0},{1,257},{257,1},{2,258},{258,2},{3,259},{259,3},{4... | collective-permute-start | bytes 786440 | tf_op jit(solution)/shard_map/ppermute | solution.py:458
  114.1 7.2 %collective-permute-start.12 = (bf16[2048,128]{1,0:T(8,128)(2,1)S(1)}, bf16[2048,128]{1,0:T(8,128)(2,1)S(1)}, u32[]{:S(2)}, u32[]{:S(2)}) collective-permute-start(bf16[2048,128]{1,0:T(8,128)(2,1)S(1)} %copy-done.1), channel_id=1, source_target_pairs={{0,1},{1,0},{2,3},{3,2},{4,5},{5,4},{6,7},{7,6},{8,9},{9,8},{10,11... | collective-permute-start | bytes 1572872 | tf_op jit(solution)/shard_map/ppermute | solution.py:458
  121.3 1.9 %collective-permute-start.13 = (bf16[2048,128]{1,0:T(8,128)(2,1)S(1)}, bf16[2048,128]{1,0:T(8,128)(2,1)S(1)}, u32[]{:S(2)}, u32[]{:S(2)}) collective-permute-start(bf16[2048,128]{1,0:T(8,128)(2,1)S(1)} %copy-done.2), channel_id=1, source_target_pairs={{0,1},{1,0},{2,3},{3,2},{4,5},{5,4},{6,7},{7,6},{8,9},{9,8},{10,11... | collective-permute-start | bytes 1572872 | tf_op jit(solution)/shard_map/ppermute | solution.py:458
  123.3 0.0 collective-permute-done.9
  123.3 0.0 collective-permute-done.10
  123.3 1.0 add_convert_fusion.grads
  124.3 4.9 %collective-permute-start.11 = (bf16[256,256]{1,0:T(8,128)(2,1)S(1)}, bf16[256,256]{1,0:T(8,128)(2,1)S(1)}, u32[]{:S(2)}, u32[]{:S(2)}) collective-permute-start(bf16[256,256]{1,0:T(8,128)(2,1)S(1)} %constant_dynamic-slice_fusion), channel_id=1, source_target_pairs={{0,1},{1,0},{2,3},{3,2},{4,5},{5,4},{6,7},{7,6},{8,9},{9,8},{10,11... | collective-permute-start | bytes 393224 | tf_op jit(solution)/shard_map/ppermute | solution.py:458
  129.2 0.0 collective-permute-done.12.far_kw
  129.3 0.0 collective-permute-done.13.far_vw
  129.3 0.9 collective-permute-done.11.from_core
  130.2 2.2 %project.1 = bf16[16,256,128]{2,1,0:T(8,128)(2,1)} custom-call(s32[1]{0:T(128)} %bitcast.2.core, bf16[512,256]{1,0:T(8,128)(2,1)S(1)} %add_convert_fusion.grads, bf16[256,256]{1,0:T(8,128)(2,1)S(1)} %collective-permute-done.11.from_core, bf16[2048,128]{1,0:T(8,128)(2,1)S(1)} %copy-done.1, bf16[2048,128]{1,0:T(8,128)(2,1)S(1)} %copy-done.2, ...), custom_call_target="tpu_custom_call" | custom-call | tf_op jit(solution)/shard_map/project/pallas_call | solution.py:446
  132.4 4.9 %all-to-all-start.2 = ((bf16[16,256,128]{2,1,0:T(8,128)(2,1)}), bf16[16,256,128]{2,1,0:T(8,128)(2,1)S(1)}, u32[]{:S(2)}, u32[]{:S(2)}) async-start(bf16[16,256,128]{2,1,0:T(8,128)(2,1)} %project.1), calls=%async_computation.2 | async-start | bytes 2097152 | tf_op jit(solution)/shard_map/all_to_all | solution.py:515
  137.3 0.7 reduce_sum.21
  137.9 15.2 %all-to-all-done.2 = bf16[16,256,128]{2,1,0:T(8,128)(2,1)S(1)} async-done(((bf16[16,256,128]{2,1,0:T(8,128)(2,1)}), bf16[16,256,128]{2,1,0:T(8,128)(2,1)S(1)}, u32[]{:S(2)}, u32[]{:S(2)}) %all-to-all-start.2) | async-done | bytes 1048608 | tf_op jit(solution)/shard_map/all_to_all | solution.py:515
  153.1 0.8 reduce.1
  (20 shorter events, 0.1 us)
Async XLA Ops:
  0.6 33.9 %copy-start = (s32[32,64]{1,0:T(8,128)S(1)}, s32[32,64]{1,0:T(8,128)}, u32[]{:S(2)}) copy-start(s32[32,64]{1,0:T(8,128)} %param.13) | copy-start | bytes 24580
  1.7 54.5 %copy-start.8 = (bf16[512,256]{1,0:T(8,128)(2,1)}, bf16[512,256]{1,0:T(8,128)(2,1)S(1)}, u32[]{:S(2)}) copy-start(bf16[512,256]{1,0:T(8,128)(2,1)S(1)} %get-tuple-element.30.near_ref.rest_0_) | copy-start | bytes 786436
  1.7 42.3 %collective-permute-start = (bf16[512,256]{1,0:T(8,128)(2,1)S(1)}, bf16[512,256]{1,0:T(8,128)(2,1)S(1)}, u32[]{:S(2)}, u32[]{:S(2)}) collective-permute-start(bf16[512,256]{1,0:T(8,128)(2,1)S(1)} %get-tuple-element.30.near_ref.rest_0_), channel_id=1, source_target_pairs={{0,256},{256,0},{1,257},{257,1},{2,258},{258,2},{3,259},{259,3},{4... | collective-permute-start | bytes 786440 | tf_op jit(solution)/shard_map/ppermute | solution.py:458
  7.2 41.2 %collective-permute-start.1 = (bf16[512,256]{1,0:T(8,128)(2,1)S(1)}, bf16[512,256]{1,0:T(8,128)(2,1)S(1)}, u32[]{:S(2)}, u32[]{:S(2)}) collective-permute-start(bf16[512,256]{1,0:T(8,128)(2,1)S(1)} %get-tuple-element.30.near_ref.rest_0_), channel_id=1, source_target_pairs={{0,16},{16,0},{1,17},{17,1},{2,18},{18,2},{3,19},{19,3},{4,20},{20... | collective-permute-start | bytes 786440 | tf_op jit(solution)/shard_map/ppermute | solution.py:458
  10.8 24.3 %collective-permute-start.2 = (bf16[128,256]{1,0:T(8,128)(2,1)S(1)}, bf16[128,256]{1,0:T(8,128)(2,1)S(1)}, u32[]{:S(2)}, u32[]{:S(2)}) collective-permute-start(bf16[128,256]{1,0:T(8,128)(2,1)S(1)} %get-tuple-element.29), channel_id=1, source_target_pairs={{0,64},{16,80},{32,96},{48,112},{64,128},{80,144},{96,160},{112,17... | collective-permute-start | bytes 196616 | tf_op jit(solution)/shard_map/ppermute | solution.py:458
  19.6 15.5 %collective-permute-start.3 = (bf16[128,256]{1,0:T(8,128)(2,1)S(1)}, bf16[128,256]{1,0:T(8,128)(2,1)S(1)}, u32[]{:S(2)}, u32[]{:S(2)}) collective-permute-start(bf16[128,256]{1,0:T(8,128)(2,1)S(1)} %get-tuple-element.29), channel_id=1, source_target_pairs={{0,192},{16,208},{32,224},{48,240},{64,0},{80,16},{96,32},{112,48}... | collective-permute-start | bytes 196616 | tf_op jit(solution)/shard_map/ppermute | solution.py:458
  24.2 15.4 %collective-permute-start.5 = (bf16[128,256]{1,0:T(8,128)(2,1)S(1)}, bf16[128,256]{1,0:T(8,128)(2,1)S(1)}, u32[]{:S(2)}, u32[]{:S(2)}) collective-permute-start(bf16[128,256]{1,0:T(8,128)(2,1)S(1)} %get-tuple-element.29), channel_id=1, source_target_pairs={{0,128},{16,144},{32,160},{48,176},{64,192},{80,208},{96,224},{112... | collective-permute-start | bytes 196616 | tf_op jit(solution)/shard_map/ppermute | solution.py:458
  35.1 21.1 %copy-start.7 = (s32[128]{0:T(128)}, s32[128]{0:T(128)S(1)}, u32[]{:S(2)}) copy-start(s32[128]{0:T(128)S(1)} %reshape.20.member) | copy-start | bytes 1540
  35.1 14.4 %collective-permute-start.4 = (bf16[512,256]{1,0:T(8,128)(2,1)S(1)}, bf16[512,256]{1,0:T(8,128)(2,1)S(1)}, u32[]{:S(2)}, u32[]{:S(2)}) collective-permute-start(bf16[512,256]{1,0:T(8,128)(2,1)S(1)} %get-tuple-element.30.near_ref.rest_0_), channel_id=1, source_target_pairs={{0,272},{16,256},{256,16},{272,0},{1,273},{17,257},{257,17},{273,1... | collective-permute-start | bytes 786440 | tf_op jit(solution)/shard_map/ppermute | solution.py:478
  37.7 8.7 %collective-permute-start.6 = (bf16[256,256]{1,0:T(8,128)(2,1)S(1)}, bf16[256,256]{1,0:T(8,128)(2,1)S(1)}, u32[]{:S(2)}, u32[]{:S(2)}) collective-permute-start(bf16[256,256]{1,0:T(8,128)(2,1)S(1)} %get-tuple-element.55), channel_id=1, source_target_pairs={{0,224},{16,240},{32,0},{48,16},{64,32},{80,48},{96,64},{112,80},{... | collective-permute-start | bytes 393224 | tf_op jit(solution)/shard_map/ppermute | solution.py:458
  39.7 8.7 %collective-permute-start.7 = (bf16[256,256]{1,0:T(8,128)(2,1)S(1)}, bf16[256,256]{1,0:T(8,128)(2,1)S(1)}, u32[]{:S(2)}, u32[]{:S(2)}) collective-permute-start(bf16[256,256]{1,0:T(8,128)(2,1)S(1)} %get-tuple-element.54), channel_id=1, source_target_pairs={{0,32},{16,48},{32,64},{48,80},{64,96},{80,112},{96,128},{112,144}... | collective-permute-start | bytes 393224 | tf_op jit(solution)/shard_map/ppermute | solution.py:458
  44.0 12.2 %copy-start.3 = (bf16[512,256]{1,0:T(8,128)(2,1)}, bf16[512,256]{1,0:T(8,128)(2,1)S(1)}, u32[]{:S(2)}) copy-start(bf16[512,256]{1,0:T(8,128)(2,1)S(1)} %constant_dynamic-update-slice_fusion.piece.rest_4_.rest_0_) | copy-start | bytes 786436
  44.0 12.2 %copy-start.9 = (bf16[512,256]{1,0:T(8,128)(2,1)}, bf16[512,256]{1,0:T(8,128)(2,1)S(1)}, u32[]{:S(2)}) copy-start(bf16[512,256]{1,0:T(8,128)(2,1)S(1)} %collective-permute-done.side_ref.rest_1_) | copy-start | bytes 786436
  46.5 9.7 %copy-start.4 = (bf16[256,256]{1,0:T(8,128)(2,1)}, bf16[256,256]{1,0:T(8,128)(2,1)S(1)}, u32[]{:S(2)}) copy-start(bf16[256,256]{1,0:T(8,128)(2,1)S(1)} %collective-permute-done.6.rest_5_.rest_1_) | copy-start | bytes 393220
  48.4 7.8 %copy-start.5 = (bf16[256,256]{1,0:T(8,128)(2,1)}, bf16[256,256]{1,0:T(8,128)(2,1)S(1)}, u32[]{:S(2)}) copy-start(bf16[256,256]{1,0:T(8,128)(2,1)S(1)} %collective-permute-done.7.rest_6_.rest_2_) | copy-start | bytes 393220
  48.4 7.8 %copy-start.10 = (bf16[512,256]{1,0:T(8,128)(2,1)}, bf16[512,256]{1,0:T(8,128)(2,1)S(1)}, u32[]{:S(2)}) copy-start(bf16[512,256]{1,0:T(8,128)(2,1)S(1)} %collective-permute-done.1.rest_2_) | copy-start | bytes 786436
  49.5 6.7 %copy-start.11 = (bf16[512,256]{1,0:T(8,128)(2,1)}, bf16[512,256]{1,0:T(8,128)(2,1)S(1)}, u32[]{:S(2)}) copy-start(bf16[512,256]{1,0:T(8,128)(2,1)S(1)} %collective-permute-done.4.rest_3_) | copy-start | bytes 786436
  56.2 10.0 %copy-start.6 = (f32[32,128]{1,0:T(8,128)}, f32[32,128]{1,0:T(8,128)S(1)}, u32[]{:S(2)}) copy-start(f32[32,128]{1,0:T(8,128)S(1)} %get-tuple-element.34.stats_ref) | copy-start | bytes 49156
  56.2 22.3 %all-to-all-start = ((bf16[8,48,128]{2,1,0:T(8,128)(2,1)}), bf16[8,48,128]{2,1,0:T(8,128)(2,1)S(1)}, u32[]{:S(2)}, u32[]{:S(2)}) async-start(bf16[8,48,128]{2,1,0:T(8,128)(2,1)} %get-tuple-element.33), calls=%async_computation | async-start | bytes 196608 | tf_op jit(solution)/shard_map/all_to_all | solution.py:496
  82.1 28.6 %all-to-all-start.1 = ((bf16[8,128,128]{2,1,0:T(8,128)(2,1)}), bf16[8,128,128]{2,1,0:T(8,128)(2,1)S(1)}, u32[]{:S(2)}, u32[]{:S(2)}) async-start(bf16[8,128,128]{2,1,0:T(8,128)(2,1)} %get-tuple-element.45), calls=%async_computation.1 | async-start | bytes 524288 | tf_op jit(solution)/shard_map/all_to_all | solution.py:501
  99.4 11.4 %collective-permute-start.8 = (bf16[512,256]{1,0:T(8,128)(2,1)S(1)}, bf16[512,256]{1,0:T(8,128)(2,1)S(1)}, u32[]{:S(2)}, u32[]{:S(2)}) collective-permute-start(bf16[512,256]{1,0:T(8,128)(2,1)S(1)} %get-tuple-element.44), channel_id=1, source_target_pairs={{0,16},{16,0},{1,17},{17,1},{2,18},{18,2},{3,19},{19,3},{4,20},{20... | collective-permute-start | bytes 786440 | tf_op jit(solution)/shard_map/ppermute | solution.py:458
  101.3 12.8 %copy-start.1 = (bf16[2048,128]{1,0:T(8,128)(2,1)S(1)}, bf16[2048,128]{1,0:T(8,128)(2,1)}, u32[]{:S(2)}) copy-start(bf16[2048,128]{1,0:T(8,128)(2,1)} %kw) | copy-start | bytes 1572868
  101.3 20.0 %copy-start.2 = (bf16[2048,128]{1,0:T(8,128)(2,1)S(1)}, bf16[2048,128]{1,0:T(8,128)(2,1)}, u32[]{:S(2)}) copy-start(bf16[2048,128]{1,0:T(8,128)(2,1)} %vw) | copy-start | bytes 1572868
  101.3 21.9 %collective-permute-start.9 = (bf16[512,256]{1,0:T(8,128)(2,1)S(1)}, bf16[512,256]{1,0:T(8,128)(2,1)S(1)}, u32[]{:S(2)}, u32[]{:S(2)}) collective-permute-start(bf16[512,256]{1,0:T(8,128)(2,1)S(1)} %get-tuple-element.49), channel_id=1, source_target_pairs={{0,16},{16,0},{1,17},{17,1},{2,18},{18,2},{3,19},{19,3},{4,20},{20... | collective-permute-start | bytes 786440 | tf_op jit(solution)/shard_map/ppermute | solution.py:458
  111.5 11.7 %collective-permute-start.10 = (bf16[512,256]{1,0:T(8,128)(2,1)}, bf16[512,256]{1,0:T(8,128)(2,1)}, u32[]{:S(2)}, u32[]{:S(2)}) collective-permute-start(bf16[512,256]{1,0:T(8,128)(2,1)} %add_convert_fusion.1), channel_id=1, source_target_pairs={{0,256},{256,0},{1,257},{257,1},{2,258},{258,2},{3,259},{259,3},{4... | collective-permute-start | bytes 786440 | tf_op jit(solution)/shard_map/ppermute | solution.py:458
  114.1 15.1 %collective-permute-start.12 = (bf16[2048,128]{1,0:T(8,128)(2,1)S(1)}, bf16[2048,128]{1,0:T(8,128)(2,1)S(1)}, u32[]{:S(2)}, u32[]{:S(2)}) collective-permute-start(bf16[2048,128]{1,0:T(8,128)(2,1)S(1)} %copy-done.1), channel_id=1, source_target_pairs={{0,1},{1,0},{2,3},{3,2},{4,5},{5,4},{6,7},{7,6},{8,9},{9,8},{10,11... | collective-permute-start | bytes 1572872 | tf_op jit(solution)/shard_map/ppermute | solution.py:458
  121.3 7.9 %collective-permute-start.13 = (bf16[2048,128]{1,0:T(8,128)(2,1)S(1)}, bf16[2048,128]{1,0:T(8,128)(2,1)S(1)}, u32[]{:S(2)}, u32[]{:S(2)}) collective-permute-start(bf16[2048,128]{1,0:T(8,128)(2,1)S(1)} %copy-done.2), channel_id=1, source_target_pairs={{0,1},{1,0},{2,3},{3,2},{4,5},{5,4},{6,7},{7,6},{8,9},{9,8},{10,11... | collective-permute-start | bytes 1572872 | tf_op jit(solution)/shard_map/ppermute | solution.py:458
  124.3 5.9 %collective-permute-start.11 = (bf16[256,256]{1,0:T(8,128)(2,1)S(1)}, bf16[256,256]{1,0:T(8,128)(2,1)S(1)}, u32[]{:S(2)}, u32[]{:S(2)}) collective-permute-start(bf16[256,256]{1,0:T(8,128)(2,1)S(1)} %constant_dynamic-slice_fusion), channel_id=1, source_target_pairs={{0,1},{1,0},{2,3},{3,2},{4,5},{5,4},{6,7},{7,6},{8,9},{9,8},{10,11... | collective-permute-start | bytes 393224 | tf_op jit(solution)/shard_map/ppermute | solution.py:458
  132.4 20.7 %all-to-all-start.2 = ((bf16[16,256,128]{2,1,0:T(8,128)(2,1)}), bf16[16,256,128]{2,1,0:T(8,128)(2,1)S(1)}, u32[]{:S(2)}, u32[]{:S(2)}) async-start(bf16[16,256,128]{2,1,0:T(8,128)(2,1)} %project.1), calls=%async_computation.2 | async-start | bytes 2097152 | tf_op jit(solution)/shard_map/all_to_all | solution.py:515

commit v10 on v9

--- a/solution.py
+++ b/solution.py
@@ -404,25 +404,25 @@
 
     @pl.when(p == pl.num_programs(0) - 1)
     def _():
-        half = d_key.shape[0] // 2
+        size = sent[0].shape[0]
         for i, target in enumerate(sent):
-            rows = slice(i * half, (i + 1) * half)
+            rows = slice(i * size, (i + 1) * size)
             target[:, :BLOCK] = d_key[rows, :].astype(target.dtype)
             target[:, BLOCK:] = d_value[rows, :].astype(target.dtype)
 
 
-def gather(scaled, chance, slope, side, kind):
+def gather(scaled, chance, slope, side, kind, parts):
     pairs, enc, lanes = chance.shape
-    pairs, step = pairs // 2, 1
+    pairs, step = pairs // 2, 2
     steps = pairs // step
     table = pl.BlockSpec((step, enc, lanes), lambda p: (side * steps + p, 0, 0))
     given = in_hbm(scaled, chance, slope)
     return pl.pallas_call(
         gather_kernel,
         grid=(steps,),
-        out_shape=[jax.ShapeDtypeStruct((enc // 2, 2 * BLOCK), kind)] * 2,
+        out_shape=[jax.ShapeDtypeStruct((enc // parts, 2 * BLOCK), kind)] * parts,
         in_specs=[pl.BlockSpec((step * 2 * BLOCK, scaled.shape[1]), lambda p: (p, 0)), table, table],
-        out_specs=[VMEM] * 2,
+        out_specs=[VMEM] * parts,
         scratch_shapes=[pltpu.VMEM((enc, BLOCK), jnp.float32)] * 2,
         compiler_params=room(20),
         cost_estimate=cost(3 * pairs * enc * lanes * BLOCK, 0),
@@ -473,7 +473,8 @@
     next_ = moved(own, "par", 1)
     ahead = moved(near, Z, 4)
     behind = moved(near, Z, -4)
-    across = moved(near, Z, 8)
+    middle = ahead.shape[0] // 2
+    across = jnp.concatenate([moved(ahead[:middle], Z, 4), moved(behind[middle:], Z, -4)], axis=0)
     late, ahead, behind = lax.optimization_barrier((own, ahead, behind))
     tables = [own, side, next_, lax.ppermute(late, ("xh", "par"), [(0, 3), (1, 2), (2, 1), (3, 0)])]
 
@@ -498,20 +499,23 @@
     parts, sums, chances, slopes = lax.optimization_barrier((parts, sums, chances, slopes))
 
     d_query, scaled = scale(parts, stats, sums, pieces)
+    from_next = moved(gather(scaled, chances, slopes, 1, bf16, 1)[0], "par", 1)
+    grads, side = gather(scaled, chances, slopes, 0, f32, 2)
+    d_query, grads = lax.optimization_barrier((d_query, grads))
     d_query = lax.all_to_all(d_query, ZH, 0, 0, tiled=True)
-    onward, next_ = (moved(part, "par", 1) for part in reversed(gather(scaled, chances, slopes, 1, bf16)))
-    grads, side = gather(scaled, chances, slopes, 0, f32)
-    side, onward, d_query = lax.optimization_barrier((side, onward, d_query))
-    from_half = moved((side + onward.astype(f32)).astype(bf16), "xh", 1)
-    grads, key_weight, value_weight = lax.optimization_barrier((grads, key_weight, value_weight))
+    grads, side, from_next, key_weight, value_weight = lax.optimization_barrier(
+        (grads, side, from_next, key_weight, value_weight)
+    )
     far_key_weight = moved(key_weight, "core", 1)
     far_value_weight = moved(value_weight, "core", 1)
-    grads = (grads + next_.astype(f32) + from_half.astype(f32)).astype(bf16)
+    from_half = moved((side + from_next[enc_rows:].astype(f32)).astype(bf16), "xh", 1)
+    grads = (grads + from_next[:enc_rows].astype(f32) + from_half.astype(f32)).astype(bf16)
     from_core = moved(lax.dynamic_slice_in_dim(grads, (1 - core) * (enc_rows // 2), enc_rows // 2, 0), "core", 1)
 
     cores = lax.axis_size("core")
     weights = (key_weight, value_weight, far_key_weight, far_value_weight)
     memory = project(core[None], grads, from_core, *weights)
+    memory, d_query = lax.optimization_barrier((memory, d_query))
     memory = lax.all_to_all(memory, HEAD, 0, 0, tiled=True)
     memory = memory.reshape(-1, cores, *memory.shape[1:]).astype(f32)
     d_memory = jnp.sum(memory, axis=0).reshape(keys.shape).astype(bf16)

time: 155 us -> 160 us (1.032)
  waiting for transfers between devices: 19.4 us -> 29 us
  starting transfers between devices: 89.6 us -> 86.2 us
  Pallas kernels: 40 us -> 38.4 us
    ppermute x13, waiting for transfers between devices: 2.87 us -> 13.1 us  [moved(): lax.ppermute(value, axis, [(i, (i + steps) % count) for i in range(count)])]
    all_to_all x1, starting transfers between devices: 9.94 us -> 7.03 us  [body(): parts = lax.all_to_all(parts, ZH, 0, 0, tiled=True)]
  transfers between devices with their start and end apart: 17 -> 17, of which waited for: 5 -> 7; matrix products, arithmetic and copies ran while one was open for 2% -> 2% of each run, Pallas kernels for 17% -> 14%
where the time goes in v10:
time: 160 us; the launch traced here: 159 us
  starting transfers between devices  86.2 us (54%)
  Pallas kernels  38.4 us (24%)
  waiting for transfers between devices  29 us (18%)
  other arithmetic  3.66 us (2%)
    ppermute x13, starting transfers between devices, moved(): lax.ppermute(value, axis, [(i, (i + steps) % count) for i in range(count)])  60.6 us
    all_to_all x1, waiting for transfers between devices, body(): memory = lax.all_to_all(memory, HEAD, 0, 0, tiled=True)  15.2 us
    ppermute x13, waiting for transfers between devices, moved(): lax.ppermute(value, axis, [(i, (i + steps) % count) for i in range(count)])  13.1 us
    pallas_call x1, Pallas kernels, local(): pl.pallas_call(local_kernel, grid=(2, pairs), out_shape=[pltpu.HBM((2 * p...  12.2 us
    all_to_all x1, starting transfers between devices, body(): d_query = lax.all_to_all(d_query, ZH, 0, 0, tiled=True)  11.2 us
    pallas_call x2, Pallas kernels, gather(): pl.pallas_call(gather_kernel, grid=(steps,), out_shape=[jax.ShapeDtypeStr...  10.3 us
    pallas_call x2, Pallas kernels, forward(): pl.pallas_call(kernel, out_shape=shapes, in_specs=[SMEM] + [VMEM] * (len(...  9.07 us
    all_to_all x1, starting transfers between devices, body(): parts = lax.all_to_all(parts, ZH, 0, 0, tiled=True)  7.03 us
  transfers between devices with their start and end apart: 17, of which 7 were waited for; matrix products, arithmetic and copies ran while one was open for 2% of the time, Pallas kernels for 14%

profile of v10, /device:TPU:1, one launch (start us, length us, event | category | flops | bytes accessed | tf_op | source)
XLA Modules:
  0.0 159.2 jit_solution(15861744472158350356)
XLA Ops:
  0.6 0.0 copy-start
  0.6 1.0 join.1
  1.7 0.0 copy-start.8
  1.7 5.5 %collective-permute-start = (bf16[512,256]{1,0:T(8,128)(2,1)S(1)}, bf16[512,256]{1,0:T(8,128)(2,1)S(1)}, u32[]{:S(2)}, u32[]{:S(2)}) collective-permute-start(bf16[512,256]{1,0:T(8,128)(2,1)S(1)} %get-tuple-element.31.near_ref.rest_0_), channel_id=1, source_target_pairs={{0,256},{256,0},{1,257},{257,1},{2,258},{258,2},{3,259},{259,3},{4... | collective-permute-start | bytes 786440 | tf_op jit(solution)/shard_map/ppermute | solution.py:458
  7.2 3.5 %collective-permute-start.1 = (bf16[512,256]{1,0:T(8,128)(2,1)S(1)}, bf16[512,256]{1,0:T(8,128)(2,1)S(1)}, u32[]{:S(2)}, u32[]{:S(2)}) collective-permute-start(bf16[512,256]{1,0:T(8,128)(2,1)S(1)} %get-tuple-element.31.near_ref.rest_0_), channel_id=1, source_target_pairs={{0,16},{16,0},{1,17},{17,1},{2,18},{18,2},{3,19},{19,3},{4,20},{20... | collective-permute-start | bytes 786440 | tf_op jit(solution)/shard_map/ppermute | solution.py:458
  10.8 8.8 %collective-permute-start.2 = (bf16[128,256]{1,0:T(8,128)(2,1)S(1)}, bf16[128,256]{1,0:T(8,128)(2,1)S(1)}, u32[]{:S(2)}, u32[]{:S(2)}) collective-permute-start(bf16[128,256]{1,0:T(8,128)(2,1)S(1)} %get-tuple-element.30), channel_id=1, source_target_pairs={{0,64},{16,80},{32,96},{48,112},{64,128},{80,144},{96,160},{112,17... | collective-permute-start | bytes 196616 | tf_op jit(solution)/shard_map/ppermute | solution.py:458
  19.6 4.7 %collective-permute-start.3 = (bf16[128,256]{1,0:T(8,128)(2,1)S(1)}, bf16[128,256]{1,0:T(8,128)(2,1)S(1)}, u32[]{:S(2)}, u32[]{:S(2)}) collective-permute-start(bf16[128,256]{1,0:T(8,128)(2,1)S(1)} %get-tuple-element.30), channel_id=1, source_target_pairs={{0,192},{16,208},{32,224},{48,240},{64,0},{80,16},{96,32},{112,48}... | collective-permute-start | bytes 196616 | tf_op jit(solution)/shard_map/ppermute | solution.py:458
  24.3 0.0 copy-done
  24.3 0.1 pad_add_fusion
  24.4 0.3 compare_reduce_fusion
  24.7 0.1 reshape.20.member
  24.8 2.1 %collective-permute-done.2 = bf16[128,256]{1,0:T(8,128)(2,1)S(1)} collective-permute-done((bf16[128,256]{1,0:T(8,128)(2,1)S(1)}, bf16[128,256]{1,0:T(8,128)(2,1)S(1)}, u32[]{:S(2)}, u32[]{:S(2)}) %collective-permute-start.2) | collective-permute-done | bytes 65568 | tf_op jit(solution)/shard_map/ppermute | solution.py:458
  26.9 3.3 %collective-permute-done.3 = bf16[128,256]{1,0:T(8,128)(2,1)S(1)} collective-permute-done((bf16[128,256]{1,0:T(8,128)(2,1)S(1)}, bf16[128,256]{1,0:T(8,128)(2,1)S(1)}, u32[]{:S(2)}, u32[]{:S(2)}) %collective-permute-start.3) | collective-permute-done | bytes 65568 | tf_op jit(solution)/shard_map/ppermute | solution.py:458
  30.1 1.9 %collective-permute-start.4 = (bf16[512,256]{1,0:T(8,128)(2,1)S(1)}, bf16[512,256]{1,0:T(8,128)(2,1)S(1)}, u32[]{:S(2)}, u32[]{:S(2)}) collective-permute-start(bf16[512,256]{1,0:T(8,128)(2,1)S(1)} %get-tuple-element.31.near_ref.rest_0_), channel_id=1, source_target_pairs={{0,272},{16,256},{256,16},{272,0},{1,273},{17,257},{257,17},{273,1... | collective-permute-start | bytes 786440 | tf_op jit(solution)/shard_map/ppermute | solution.py:479
  32.1 8.9 %collective-permute-start.5 = (bf16[64,256]{1,0:T(8,128)(2,1)S(1)}, bf16[64,256]{1,0:T(8,128)(2,1)S(1)}, u32[]{:S(2)}, u32[]{:S(2)}) collective-permute-start(bf16[64,256]{1,0:T(8,128)(2,1)S(1)} %slice.20), channel_id=1, source_target_pairs={{0,64},{16,80},{32,96},{48,112},{64,128},{80,144},{96,160},{112,17... | collective-permute-start | bytes 98312 | tf_op jit(solution)/shard_map/ppermute | solution.py:458
  41.1 1.9 %collective-permute-start.6 = (bf16[64,256]{1,0:T(8,128)(2,1)S(1)}, bf16[64,256]{1,0:T(8,128)(2,1)S(1)}, u32[]{:S(2)}, u32[]{:S(2)}) collective-permute-start(bf16[64,256]{1,0:T(8,128)(2,1)S(1)} %slice.21), channel_id=1, source_target_pairs={{0,192},{16,208},{32,224},{48,240},{64,0},{80,16},{96,32},{112,48}... | collective-permute-start | bytes 98312 | tf_op jit(solution)/shard_map/ppermute | solution.py:458
  43.0 0.0 collective-permute-done.5
  43.0 2.4 %collective-permute-start.7 = (bf16[256,256]{1,0:T(8,128)(2,1)S(1)}, bf16[256,256]{1,0:T(8,128)(2,1)S(1)}, u32[]{:S(2)}, u32[]{:S(2)}) collective-permute-start(bf16[256,256]{1,0:T(8,128)(2,1)S(1)} %get-tuple-element.57), channel_id=1, source_target_pairs={{0,224},{16,240},{32,0},{48,16},{64,32},{80,48},{96,64},{112,80},{... | collective-permute-start | bytes 393224 | tf_op jit(solution)/shard_map/ppermute | solution.py:458
  45.5 4.4 %collective-permute-done.6 = bf16[64,256]{1,0:T(8,128)(2,1)S(1)} collective-permute-done((bf16[64,256]{1,0:T(8,128)(2,1)S(1)}, bf16[64,256]{1,0:T(8,128)(2,1)S(1)}, u32[]{:S(2)}, u32[]{:S(2)}) %collective-permute-start.6) | collective-permute-done | bytes 32800 | tf_op jit(solution)/shard_map/ppermute | solution.py:458
  49.9 3.0 %collective-permute-start.8 = (bf16[256,256]{1,0:T(8,128)(2,1)S(1)}, bf16[256,256]{1,0:T(8,128)(2,1)S(1)}, u32[]{:S(2)}, u32[]{:S(2)}) collective-permute-start(bf16[256,256]{1,0:T(8,128)(2,1)S(1)} %get-tuple-element.56), channel_id=1, source_target_pairs={{0,32},{16,48},{32,64},{48,80},{64,96},{80,112},{96,128},{112,144}... | collective-permute-start | bytes 393224 | tf_op jit(solution)/shard_map/ppermute | solution.py:458
  52.9 0.0 copy-start.3
  52.9 0.0 collective-permute-done.side_ref.rest_1_
  52.9 0.0 copy-start.9
  52.9 2.5 %forward.2.rest_7_ = f32[32,128]{1,0:T(8,128)S(1)} custom-call(s32[128]{0:T(128)S(1)} %reshape.20.member, bf16[512,256]{1,0:T(8,128)(2,1)S(1)} %get-tuple-element.31.near_ref.rest_0_, bf16[512,256]{1,0:T(8,128)(2,1)S(1)} %collective-permute-done.side_ref.rest_1_, bf16[512,256]{1,0:T(8,128)(2,1)S(1)} %constant_dynamic-update-slice_fusion.piece.rest_4_.rest_0_), custom_call_target="tpu_custom_call" | custom-call | flops 2147483648 | bytes 1048576 | tf_op jit(solution)/shard_map/forward/pallas_call | solution.py:229
  55.4 0.0 collective-permute-done.7.rest_5_.rest_1_
  55.4 0.0 copy-start.4
  55.4 2.3 %collective-permute-done.8.rest_6_.rest_2_ = bf16[256,256]{1,0:T(8,128)(2,1)S(1)} collective-permute-done((bf16[256,256]{1,0:T(8,128)(2,1)S(1)}, bf16[256,256]{1,0:T(8,128)(2,1)S(1)}, u32[]{:S(2)}, u32[]{:S(2)}) %collective-permute-start.8) | collective-permute-done | bytes 131104 | tf_op jit(solution)/shard_map/ppermute | solution.py:458
  57.8 0.0 collective-permute-done.1.rest_2_
  57.8 0.0 collective-permute-done.4.rest_3_
  57.8 0.0 copy-start.11
  57.8 6.6 %forward.3 = (bf16[8,48,128]{2,1,0:T(8,128)(2,1)}, f32[32,128]{1,0:T(8,128)S(1)}) custom-call(s32[128]{0:T(128)S(1)} %reshape.20.member, bf16[512,256]{1,0:T(8,128)(2,1)S(1)} %get-tuple-element.31.near_ref.rest_0_, bf16[512,256]{1,0:T(8,128)(2,1)S(1)} %collective-permute-done.side_ref.rest_1_, bf16[512,256]{1,0:T(8,128)(2,1)S(1)} %collective-permute-done.1.rest_2_, ...), custom_call_target="tpu_custom_call" | custom-call | flops 8589934592 | bytes 1048576 | tf_op jit(solution)/shard_map/forward/pallas_call | solution.py:229
  64.4 0.0 copy-done.8
  64.4 0.0 copy-done.7
  64.4 0.0 copy-done.3
  64.4 0.0 copy-done.9
  64.5 0.0 copy-start.6
  64.5 0.6 copy-done.6
  65.1 7.0 %all-to-all-start = ((bf16[8,48,128]{2,1,0:T(8,128)(2,1)}), bf16[8,48,128]{2,1,0:T(8,128)(2,1)S(1)}, u32[]{:S(2)}, u32[]{:S(2)}) async-start(bf16[8,48,128]{2,1,0:T(8,128)(2,1)} %get-tuple-element.34), calls=%async_computation | async-start | bytes 196608 | tf_op jit(solution)/shard_map/all_to_all | solution.py:497
  72.1 12.2 %local.1 = (f32[8,2,128,256]{3,2,1,0:T(8,128)}, bf16[8,1024,512]{2,1,0:T(8,128)(2,1)}, bf16[8,1024,512]{2,1,0:T(8,128)(2,1)}) custom-call(s32[128]{0:T(128)} %copy-done.7, f32[32,128]{1,0:T(8,128)} %copy-done.6, bf16[512,256]{1,0:T(8,128)(2,1)} %copy-done.8, bf16[512,256]{1,0:T(8,128)(2,1)} %copy-done.9, bf16[512,256]{1,0:T(8,128)(2,1)} %copy-done.10, ...), custom_call_target="tpu_custom_call" | custom-call | flops 12884901888 | bytes 1048576 | tf_op jit(solution)/shard_map/local/pallas_call | solution.py:300
  84.3 0.7 all-to-all-done.parts
  85.0 3.6 %scale.1 = (bf16[8,128,128]{2,1,0:T(8,128)(2,1)}, bf16[1024,384]{1,0:T(8,128)(2,1)}) custom-call(bf16[8,48,128]{2,1,0:T(8,128)(2,1)S(1)} %all-to-all-done.parts, f32[32,128]{1,0:T(8,128)} %copy-done.6, f32[8,2,128,256]{3,2,1,0:T(8,128)} %get-tuple-element.40.sums_ref, bf16[512,256]{1,0:T(8,128)(2,1)} %copy-done.3, bf16[256,256]{1,0:T(8,128)(2,1)} %copy-done.4, ...), custom_call_target="tpu_custom_call" | custom-call | flops 536870912 | bytes 1048576 | tf_op jit(solution)/shard_map/scale/pallas_call | solution.py:363
  88.6 5.2 %gather.3 = bf16[1024,256]{1,0:T(8,128)(2,1)S(1)} custom-call(bf16[1024,384]{1,0:T(8,128)(2,1)} %get-tuple-element.42.scaled, bf16[8,1024,512]{2,1,0:T(8,128)(2,1)} %get-tuple-element.43.chance, bf16[8,1024,512]{2,1,0:T(8,128)(2,1)} %get-tuple-element.44.slope), custom_call_target="tpu_custom_call" | custom-call | flops 3221225472 | bytes 1048576 | tf_op jit(solution)/shard_map/gather/pallas_call | solution.py:420
  93.8 0.0 copy-start.1
  93.8 0.0 copy-start.2
  93.8 2.3 %collective-permute-start.9 = (bf16[1024,256]{1,0:T(8,128)(2,1)S(1)}, bf16[1024,256]{1,0:T(8,128)(2,1)S(1)}, u32[]{:S(2)}, u32[]{:S(2)}) collective-permute-start(bf16[1024,256]{1,0:T(8,128)(2,1)S(1)} %gather.3), channel_id=1, source_target_pairs={{0,16},{16,0},{1,17},{17,1},{2,18},{18,2},{3,19},{19,3},{4,20},{20... | collective-permute-start | bytes 1572872 | tf_op jit(solution)/shard_map/ppermute | solution.py:458
  96.1 5.2 %gather.2 = (f32[512,256]{1,0:T(8,128)S(1)}, f32[512,256]{1,0:T(8,128)S(1)}) custom-call(bf16[1024,384]{1,0:T(8,128)(2,1)} %get-tuple-element.42.scaled, bf16[8,1024,512]{2,1,0:T(8,128)(2,1)} %get-tuple-element.43.chance, bf16[8,1024,512]{2,1,0:T(8,128)(2,1)} %get-tuple-element.44.slope), custom_call_target="tpu_custom_call" | custom-call | flops 3221225472 | bytes 1048576 | tf_op jit(solution)/shard_map/gather/pallas_call | solution.py:420
  101.3 11.2 %all-to-all-start.1 = ((bf16[8,128,128]{2,1,0:T(8,128)(2,1)}), bf16[8,128,128]{2,1,0:T(8,128)(2,1)S(1)}, u32[]{:S(2)}, u32[]{:S(2)}) async-start(bf16[8,128,128]{2,1,0:T(8,128)(2,1)} %get-tuple-element.53), calls=%async_computation.1 | async-start | bytes 524288 | tf_op jit(solution)/shard_map/all_to_all | solution.py:505
  112.5 0.0 collective-permute-done.9
  112.5 0.8 add_convert_fusion.1
  113.3 4.6 %collective-permute-start.10 = (bf16[512,256]{1,0:T(8,128)(2,1)}, bf16[512,256]{1,0:T(8,128)(2,1)}, u32[]{:S(2)}, u32[]{:S(2)}) collective-permute-start(bf16[512,256]{1,0:T(8,128)(2,1)} %add_convert_fusion.1), channel_id=1, source_target_pairs={{0,256},{256,0},{1,257},{257,1},{2,258},{258,2},{3,259},{259,3},{4... | collective-permute-start | bytes 786440 | tf_op jit(solution)/shard_map/ppermute | solution.py:458
  118.0 9.4 %collective-permute-start.12 = (bf16[2048,128]{1,0:T(8,128)(2,1)S(1)}, bf16[2048,128]{1,0:T(8,128)(2,1)S(1)}, u32[]{:S(2)}, u32[]{:S(2)}) collective-permute-start(bf16[2048,128]{1,0:T(8,128)(2,1)S(1)} %copy-done.1), channel_id=1, source_target_pairs={{0,1},{1,0},{2,3},{3,2},{4,5},{5,4},{6,7},{7,6},{8,9},{9,8},{10,11... | collective-permute-start | bytes 1572872 | tf_op jit(solution)/shard_map/ppermute | solution.py:458
  127.4 1.9 %collective-permute-start.13 = (bf16[2048,128]{1,0:T(8,128)(2,1)S(1)}, bf16[2048,128]{1,0:T(8,128)(2,1)S(1)}, u32[]{:S(2)}, u32[]{:S(2)}) collective-permute-start(bf16[2048,128]{1,0:T(8,128)(2,1)S(1)} %copy-done.2), channel_id=1, source_target_pairs={{0,1},{1,0},{2,3},{3,2},{4,5},{5,4},{6,7},{7,6},{8,9},{9,8},{10,11... | collective-permute-start | bytes 1572872 | tf_op jit(solution)/shard_map/ppermute | solution.py:458
  129.3 0.0 collective-permute-done.10
  129.3 1.0 add_convert_fusion.grads
  130.4 3.5 %collective-permute-start.11 = (bf16[256,256]{1,0:T(8,128)(2,1)S(1)}, bf16[256,256]{1,0:T(8,128)(2,1)S(1)}, u32[]{:S(2)}, u32[]{:S(2)}) collective-permute-start(bf16[256,256]{1,0:T(8,128)(2,1)S(1)} %constant_dynamic-slice_fusion), channel_id=1, source_target_pairs={{0,1},{1,0},{2,3},{3,2},{4,5},{5,4},{6,7},{7,6},{8,9},{9,8},{10,11... | collective-permute-start | bytes 393224 | tf_op jit(solution)/shard_map/ppermute | solution.py:458
  133.9 1.0 collective-permute-done.11.from_core
  134.8 0.0 collective-permute-done.12.far_kw
  134.8 0.0 collective-permute-done.13.far_vw
  134.8 2.2 %project.1 = bf16[16,256,128]{2,1,0:T(8,128)(2,1)} custom-call(s32[1]{0:T(128)} %bitcast.core, bf16[512,256]{1,0:T(8,128)(2,1)S(1)} %add_convert_fusion.grads, bf16[256,256]{1,0:T(8,128)(2,1)S(1)} %collective-permute-done.11.from_core, bf16[2048,128]{1,0:T(8,128)(2,1)S(1)} %copy-done.1, bf16[2048,128]{1,0:T(8,128)(2,1)S(1)} %copy-done.2, ...), custom_call_target="tpu_custom_call" | custom-call | tf_op jit(solution)/shard_map/project/pallas_call | solution.py:446
  137.1 0.0 all-to-all-done.1
  137.1 5.5 %all-to-all-start.2 = ((bf16[16,256,128]{2,1,0:T(8,128)(2,1)}), bf16[16,256,128]{2,1,0:T(8,128)(2,1)S(1)}, u32[]{:S(2)}, u32[]{:S(2)}) async-start(bf16[16,256,128]{2,1,0:T(8,128)(2,1)} %project.1), calls=%async_computation.2 | async-start | bytes 2097152 | tf_op jit(solution)/shard_map/all_to_all | solution.py:519
  142.6 0.7 reduce_sum.21
  143.2 15.2 %all-to-all-done.2 = bf16[16,256,128]{2,1,0:T(8,128)(2,1)S(1)} async-done(((bf16[16,256,128]{2,1,0:T(8,128)(2,1)}), bf16[16,256,128]{2,1,0:T(8,128)(2,1)S(1)}, u32[]{:S(2)}, u32[]{:S(2)}) %all-to-all-start.2) | async-done | bytes 1048608 | tf_op jit(solution)/shard_map/all_to_all | solution.py:519
  158.4 0.8 reduce.1
  (23 shorter events, 0.1 us)
Async XLA Ops:
  0.6 23.6 %copy-start = (s32[32,64]{1,0:T(8,128)S(1)}, s32[32,64]{1,0:T(8,128)}, u32[]{:S(2)}) copy-start(s32[32,64]{1,0:T(8,128)} %param.13) | copy-start | bytes 24580
  1.7 62.7 %copy-start.8 = (bf16[512,256]{1,0:T(8,128)(2,1)}, bf16[512,256]{1,0:T(8,128)(2,1)S(1)}, u32[]{:S(2)}) copy-start(bf16[512,256]{1,0:T(8,128)(2,1)S(1)} %get-tuple-element.31.near_ref.rest_0_) | copy-start | bytes 786436
  1.7 51.2 %collective-permute-start = (bf16[512,256]{1,0:T(8,128)(2,1)S(1)}, bf16[512,256]{1,0:T(8,128)(2,1)S(1)}, u32[]{:S(2)}, u32[]{:S(2)}) collective-permute-start(bf16[512,256]{1,0:T(8,128)(2,1)S(1)} %get-tuple-element.31.near_ref.rest_0_), channel_id=1, source_target_pairs={{0,256},{256,0},{1,257},{257,1},{2,258},{258,2},{3,259},{259,3},{4... | collective-permute-start | bytes 786440 | tf_op jit(solution)/shard_map/ppermute | solution.py:458
  7.2 50.6 %collective-permute-start.1 = (bf16[512,256]{1,0:T(8,128)(2,1)S(1)}, bf16[512,256]{1,0:T(8,128)(2,1)S(1)}, u32[]{:S(2)}, u32[]{:S(2)}) collective-permute-start(bf16[512,256]{1,0:T(8,128)(2,1)S(1)} %get-tuple-element.31.near_ref.rest_0_), channel_id=1, source_target_pairs={{0,16},{16,0},{1,17},{17,1},{2,18},{18,2},{3,19},{19,3},{4,20},{20... | collective-permute-start | bytes 786440 | tf_op jit(solution)/shard_map/ppermute | solution.py:458
  10.8 16.1 %collective-permute-start.2 = (bf16[128,256]{1,0:T(8,128)(2,1)S(1)}, bf16[128,256]{1,0:T(8,128)(2,1)S(1)}, u32[]{:S(2)}, u32[]{:S(2)}) collective-permute-start(bf16[128,256]{1,0:T(8,128)(2,1)S(1)} %get-tuple-element.30), channel_id=1, source_target_pairs={{0,64},{16,80},{32,96},{48,112},{64,128},{80,144},{96,160},{112,17... | collective-permute-start | bytes 196616 | tf_op jit(solution)/shard_map/ppermute | solution.py:458
  19.6 10.6 %collective-permute-start.3 = (bf16[128,256]{1,0:T(8,128)(2,1)S(1)}, bf16[128,256]{1,0:T(8,128)(2,1)S(1)}, u32[]{:S(2)}, u32[]{:S(2)}) collective-permute-start(bf16[128,256]{1,0:T(8,128)(2,1)S(1)} %get-tuple-element.30), channel_id=1, source_target_pairs={{0,192},{16,208},{32,224},{48,240},{64,0},{80,16},{96,32},{112,48}... | collective-permute-start | bytes 196616 | tf_op jit(solution)/shard_map/ppermute | solution.py:458
  24.8 39.6 %copy-start.7 = (s32[128]{0:T(128)}, s32[128]{0:T(128)S(1)}, u32[]{:S(2)}) copy-start(s32[128]{0:T(128)S(1)} %reshape.20.member) | copy-start | bytes 1540
  30.1 27.6 %collective-permute-start.4 = (bf16[512,256]{1,0:T(8,128)(2,1)S(1)}, bf16[512,256]{1,0:T(8,128)(2,1)S(1)}, u32[]{:S(2)}, u32[]{:S(2)}) collective-permute-start(bf16[512,256]{1,0:T(8,128)(2,1)S(1)} %get-tuple-element.31.near_ref.rest_0_), channel_id=1, source_target_pairs={{0,272},{16,256},{256,16},{272,0},{1,273},{17,257},{257,17},{273,1... | collective-permute-start | bytes 786440 | tf_op jit(solution)/shard_map/ppermute | solution.py:479
  32.1 10.9 %collective-permute-start.5 = (bf16[64,256]{1,0:T(8,128)(2,1)S(1)}, bf16[64,256]{1,0:T(8,128)(2,1)S(1)}, u32[]{:S(2)}, u32[]{:S(2)}) collective-permute-start(bf16[64,256]{1,0:T(8,128)(2,1)S(1)} %slice.20), channel_id=1, source_target_pairs={{0,64},{16,80},{32,96},{48,112},{64,128},{80,144},{96,160},{112,17... | collective-permute-start | bytes 98312 | tf_op jit(solution)/shard_map/ppermute | solution.py:458
  41.1 8.8 %collective-permute-start.6 = (bf16[64,256]{1,0:T(8,128)(2,1)S(1)}, bf16[64,256]{1,0:T(8,128)(2,1)S(1)}, u32[]{:S(2)}, u32[]{:S(2)}) collective-permute-start(bf16[64,256]{1,0:T(8,128)(2,1)S(1)} %slice.21), channel_id=1, source_target_pairs={{0,192},{16,208},{32,224},{48,240},{64,0},{80,16},{96,32},{112,48}... | collective-permute-start | bytes 98312 | tf_op jit(solution)/shard_map/ppermute | solution.py:458
  43.0 12.4 %collective-permute-start.7 = (bf16[256,256]{1,0:T(8,128)(2,1)S(1)}, bf16[256,256]{1,0:T(8,128)(2,1)S(1)}, u32[]{:S(2)}, u32[]{:S(2)}) collective-permute-start(bf16[256,256]{1,0:T(8,128)(2,1)S(1)} %get-tuple-element.57), channel_id=1, source_target_pairs={{0,224},{16,240},{32,0},{48,16},{64,32},{80,48},{96,64},{112,80},{... | collective-permute-start | bytes 393224 | tf_op jit(solution)/shard_map/ppermute | solution.py:458
  49.9 7.9 %collective-permute-start.8 = (bf16[256,256]{1,0:T(8,128)(2,1)S(1)}, bf16[256,256]{1,0:T(8,128)(2,1)S(1)}, u32[]{:S(2)}, u32[]{:S(2)}) collective-permute-start(bf16[256,256]{1,0:T(8,128)(2,1)S(1)} %get-tuple-element.56), channel_id=1, source_target_pairs={{0,32},{16,48},{32,64},{48,80},{64,96},{80,112},{96,128},{112,144}... | collective-permute-start | bytes 393224 | tf_op jit(solution)/shard_map/ppermute | solution.py:458
  52.9 11.5 %copy-start.3 = (bf16[512,256]{1,0:T(8,128)(2,1)}, bf16[512,256]{1,0:T(8,128)(2,1)S(1)}, u32[]{:S(2)}) copy-start(bf16[512,256]{1,0:T(8,128)(2,1)S(1)} %constant_dynamic-update-slice_fusion.piece.rest_4_.rest_0_) | copy-start | bytes 786436
  52.9 11.5 %copy-start.9 = (bf16[512,256]{1,0:T(8,128)(2,1)}, bf16[512,256]{1,0:T(8,128)(2,1)S(1)}, u32[]{:S(2)}) copy-start(bf16[512,256]{1,0:T(8,128)(2,1)S(1)} %collective-permute-done.side_ref.rest_1_) | copy-start | bytes 786436
  55.4 9.0 %copy-start.4 = (bf16[256,256]{1,0:T(8,128)(2,1)}, bf16[256,256]{1,0:T(8,128)(2,1)S(1)}, u32[]{:S(2)}) copy-start(bf16[256,256]{1,0:T(8,128)(2,1)S(1)} %collective-permute-done.7.rest_5_.rest_1_) | copy-start | bytes 393220
  57.8 6.7 %copy-start.5 = (bf16[256,256]{1,0:T(8,128)(2,1)}, bf16[256,256]{1,0:T(8,128)(2,1)S(1)}, u32[]{:S(2)}) copy-start(bf16[256,256]{1,0:T(8,128)(2,1)S(1)} %collective-permute-done.8.rest_6_.rest_2_) | copy-start | bytes 393220
  57.8 6.7 %copy-start.10 = (bf16[512,256]{1,0:T(8,128)(2,1)}, bf16[512,256]{1,0:T(8,128)(2,1)S(1)}, u32[]{:S(2)}) copy-start(bf16[512,256]{1,0:T(8,128)(2,1)S(1)} %collective-permute-done.1.rest_2_) | copy-start | bytes 786436
  57.8 6.7 %copy-start.11 = (bf16[512,256]{1,0:T(8,128)(2,1)}, bf16[512,256]{1,0:T(8,128)(2,1)S(1)}, u32[]{:S(2)}) copy-start(bf16[512,256]{1,0:T(8,128)(2,1)S(1)} %collective-permute-done.4.rest_3_) | copy-start | bytes 786436
  64.5 0.6 copy-start.6
  65.1 20.0 %all-to-all-start = ((bf16[8,48,128]{2,1,0:T(8,128)(2,1)}), bf16[8,48,128]{2,1,0:T(8,128)(2,1)S(1)}, u32[]{:S(2)}, u32[]{:S(2)}) async-start(bf16[8,48,128]{2,1,0:T(8,128)(2,1)} %get-tuple-element.34), calls=%async_computation | async-start | bytes 196608 | tf_op jit(solution)/shard_map/all_to_all | solution.py:497
  93.8 24.2 %copy-start.1 = (bf16[2048,128]{1,0:T(8,128)(2,1)S(1)}, bf16[2048,128]{1,0:T(8,128)(2,1)}, u32[]{:S(2)}) copy-start(bf16[2048,128]{1,0:T(8,128)(2,1)} %kw) | copy-start | bytes 1572868
  93.8 33.6 %copy-start.2 = (bf16[2048,128]{1,0:T(8,128)(2,1)S(1)}, bf16[2048,128]{1,0:T(8,128)(2,1)}, u32[]{:S(2)}) copy-start(bf16[2048,128]{1,0:T(8,128)(2,1)} %vw) | copy-start | bytes 1572868
  93.8 18.7 %collective-permute-start.9 = (bf16[1024,256]{1,0:T(8,128)(2,1)S(1)}, bf16[1024,256]{1,0:T(8,128)(2,1)S(1)}, u32[]{:S(2)}, u32[]{:S(2)}) collective-permute-start(bf16[1024,256]{1,0:T(8,128)(2,1)S(1)} %gather.3), channel_id=1, source_target_pairs={{0,16},{16,0},{1,17},{17,1},{2,18},{18,2},{3,19},{19,3},{4,20},{20... | collective-permute-start | bytes 1572872 | tf_op jit(solution)/shard_map/ppermute | solution.py:458
  101.3 35.8 %all-to-all-start.1 = ((bf16[8,128,128]{2,1,0:T(8,128)(2,1)}), bf16[8,128,128]{2,1,0:T(8,128)(2,1)S(1)}, u32[]{:S(2)}, u32[]{:S(2)}) async-start(bf16[8,128,128]{2,1,0:T(8,128)(2,1)} %get-tuple-element.53), calls=%async_computation.1 | async-start | bytes 524288 | tf_op jit(solution)/shard_map/all_to_all | solution.py:505
  113.3 16.0 %collective-permute-start.10 = (bf16[512,256]{1,0:T(8,128)(2,1)}, bf16[512,256]{1,0:T(8,128)(2,1)}, u32[]{:S(2)}, u32[]{:S(2)}) collective-permute-start(bf16[512,256]{1,0:T(8,128)(2,1)} %add_convert_fusion.1), channel_id=1, source_target_pairs={{0,256},{256,0},{1,257},{257,1},{2,258},{258,2},{3,259},{259,3},{4... | collective-permute-start | bytes 786440 | tf_op jit(solution)/shard_map/ppermute | solution.py:458
  118.0 16.9 %collective-permute-start.12 = (bf16[2048,128]{1,0:T(8,128)(2,1)S(1)}, bf16[2048,128]{1,0:T(8,128)(2,1)S(1)}, u32[]{:S(2)}, u32[]{:S(2)}) collective-permute-start(bf16[2048,128]{1,0:T(8,128)(2,1)S(1)} %copy-done.1), channel_id=1, source_target_pairs={{0,1},{1,0},{2,3},{3,2},{4,5},{5,4},{6,7},{7,6},{8,9},{9,8},{10,11... | collective-permute-start | bytes 1572872 | tf_op jit(solution)/shard_map/ppermute | solution.py:458
  127.4 7.4 %collective-permute-start.13 = (bf16[2048,128]{1,0:T(8,128)(2,1)S(1)}, bf16[2048,128]{1,0:T(8,128)(2,1)S(1)}, u32[]{:S(2)}, u32[]{:S(2)}) collective-permute-start(bf16[2048,128]{1,0:T(8,128)(2,1)S(1)} %copy-done.2), channel_id=1, source_target_pairs={{0,1},{1,0},{2,3},{3,2},{4,5},{5,4},{6,7},{7,6},{8,9},{9,8},{10,11... | collective-permute-start | bytes 1572872 | tf_op jit(solution)/shard_map/ppermute | solution.py:458
  130.4 4.4 %collective-permute-start.11 = (bf16[256,256]{1,0:T(8,128)(2,1)S(1)}, bf16[256,256]{1,0:T(8,128)(2,1)S(1)}, u32[]{:S(2)}, u32[]{:S(2)}) collective-permute-start(bf16[256,256]{1,0:T(8,128)(2,1)S(1)} %constant_dynamic-slice_fusion), channel_id=1, source_target_pairs={{0,1},{1,0},{2,3},{3,2},{4,5},{5,4},{6,7},{7,6},{8,9},{9,8},{10,11... | collective-permute-start | bytes 393224 | tf_op jit(solution)/shard_map/ppermute | solution.py:458
  137.1 21.3 %all-to-all-start.2 = ((bf16[16,256,128]{2,1,0:T(8,128)(2,1)}), bf16[16,256,128]{2,1,0:T(8,128)(2,1)S(1)}, u32[]{:S(2)}, u32[]{:S(2)}) async-start(bf16[16,256,128]{2,1,0:T(8,128)(2,1)} %project.1), calls=%async_computation.2 | async-start | bytes 2097152 | tf_op jit(solution)/shard_map/all_to_all | solution.py:519

commit v11 on v7

--- a/solution.py
+++ b/solution.py
@@ -82,6 +82,17 @@
         compiler_params=room(4),
         name="join",
     )(*in_hbm(left, right))
+
+
+def pair_places(p):
+    here, count = lax.axis_index("zh"), lax.axis_size("zh")
+    found = []
+    for steps in (SLOTS[::2], SLOTS[1::2]):
+        step = jnp.int32(steps[-1])
+        for i, other in enumerate(steps[:-1]):
+            step = jnp.where(p == i, other, step)
+        found.append(lax.rem(here + step + count, count))
+    return found
 
 
 def load_targets(pieces, held):
@@ -133,7 +144,7 @@
     return top + jnp.log(total), mean / total
 
 
-def forward_kernel(base, places, member, *rest):
+def forward_kernel(base, member, *rest):
     tables = rest[:4]
     *pieces, before, result, stats, held, kv = rest[4:]
     load_targets(pieces, held)
@@ -147,7 +158,7 @@
 
     def step(p, carry):
         rows = pl.ds(pl.multiple_of(p * 2 * BLOCK, 2 * BLOCK), 2 * BLOCK)
-        first, second = places[base + 2 * p], places[base + 2 * p + 1]
+        first, second = pair_places(base // 2 + p)
         query = split_heads(held[rows, :BLOCK])
         out = split_heads(held[rows, BLOCK:])
         log_total, mean = union(
@@ -172,11 +183,11 @@
             result[peer] = message
 
 
-def forward(base, places, member, tables, pieces, before):
-    count = places.shape[0]
+def forward(base, member, tables, pieces, before):
+    count = len(SLOTS)
     rows = sum(p.shape[0] for p in pieces)
     enc = sum(t.shape[0] for t in tables)
-    given = [places, member, *tables, *pieces]
+    given = [member, *tables, *pieces]
     local = jax.ShapeDtypeStruct((4 * count, BLOCK), jnp.float32)
     if before is None:
         shapes = [local]
@@ -190,7 +201,7 @@
     return pl.pallas_call(
         kernel,
         out_shape=shapes,
-        in_specs=[SMEM] * 2 + [VMEM] * (len(given) - 2),
+        in_specs=[SMEM] + [VMEM] * (len(given) - 1),
         out_specs=[VMEM] * len(shapes),
         scratch_shapes=[
             pltpu.VMEM((rows, 2 * BLOCK), jnp.bfloat16),
@@ -216,7 +227,7 @@
     return jnp.concatenate([stats[pl.ds(s, 1), :] for s in spots], axis=1)
 
 
-def local_kernel(places, member, stats_ref, *rest):
+def local_kernel(member, stats_ref, *rest):
     tables, pieces = rest[:4], rest[4:7]
     sums, chances, slopes, kv, held, stats, turned, sems = rest[7:]
     side, p = pl.program_id(0), pl.program_id(1)
@@ -236,7 +247,7 @@
     blocks = enc // BLOCK
     half = stats.shape[0] // 2
     rows = pl.ds(pl.multiple_of(p * 2 * BLOCK, 2 * BLOCK), 2 * BLOCK)
-    first, second = places[2 * p], places[2 * p + 1]
+    first, second = pair_places(p)
     log_total = lanes_of(stats, first, second, 0)
     log_total = jnp.where(log_total > -0.5 * BIG, log_total, BIG)
     mean = lanes_of(stats, first, second, half)
@@ -255,17 +266,17 @@
             sums[0, i, dims, :] = dot_nn(turned[dims, :], table[0, :, lanes])
 
 
-def local(places, member, stats, tables, pieces):
+def local(member, stats, tables, pieces):
     rows = sum(p.shape[0] for p in pieces)
     enc = sum(t.shape[0] for t in tables) // 2
     pairs = rows // (2 * BLOCK)
     table = pltpu.HBM((2 * pairs, enc, 4 * BLOCK), jnp.bfloat16)
-    given = in_hbm(places, member, stats, *tables, *pieces)
+    given = in_hbm(member, stats, *tables, *pieces)
     return pl.pallas_call(
         local_kernel,
         grid=(2, pairs),
         out_shape=[pltpu.HBM((2 * pairs, 2, BLOCK, 2 * BLOCK), jnp.float32)] + [table] * 2,
-        in_specs=[SMEM] * 2 + [ANY] * (len(given) - 2),
+        in_specs=[SMEM] + [ANY] * (len(given) - 1),
         out_specs=[pl.BlockSpec((1, 2, BLOCK, 2 * BLOCK), lambda side, p: (side * pairs + p, 0, 0, 0))]
         + [pl.BlockSpec((1, enc, 4 * BLOCK), lambda side, p: (side * pairs + p, 0, 0))] * 2,
         scratch_shapes=[
@@ -273,7 +284,7 @@
             pltpu.VMEM((rows, 2 * BLOCK), jnp.bfloat16),
             pltpu.VMEM(stats.shape, stats.dtype),
             pltpu.VMEM((BLOCK, enc), jnp.bfloat16),
-            pltpu.SemaphoreType.DMA((len(given) - 2,)),
+            pltpu.SemaphoreType.DMA((len(given) - 1,)),
         ],
         compiler_params=room(20),
         cost_estimate=cost(3 * rows * 2 * enc * 4 * BLOCK, rows * enc * 4),
@@ -281,11 +292,12 @@
     )(*given)
 
 
-def scale_kernel(places, parts, stats_ref, sums_ref, *rest):
+def scale_kernel(parts, stats_ref, sums_ref, *rest):
     pieces = rest[:3]
     d_query, scaled, held, whole, stats, sums, sems = rest[3:]
     copies = fetch(stacked(pieces, held) + [(stats_ref, stats), (sums_ref, sums)], sems)
     merge_stats(parts, whole)
+    parity = lax.axis_index("par")
     for copy in copies:
         copy.wait()
     half = stats.shape[0] // 2
@@ -293,7 +305,7 @@
 
     def step(p, carry):
         rows = pl.ds(pl.multiple_of(p * 2 * BLOCK, 2 * BLOCK), 2 * BLOCK)
-        first, second = places[2 * p], places[2 * p + 1]
+        first, second = pair_places(p)
         share = jnp.exp(lanes_of(stats, first, second, 0) - lanes_of(whole, first, second, 0))
         shift = lanes_of(whole, first, second, half) - lanes_of(stats, first, second, half)
 
@@ -307,8 +319,10 @@
         slope = sums[p, 0] + sums[pairs + p, 0]
         chance = sums[p, 1] + sums[pairs + p, 1]
         grad = (share * (slope - shift * chance)).T.astype(jnp.bfloat16)
-        d_query[first] = grad[:BLOCK]
-        d_query[second] = grad[BLOCK:]
+        part = BLOCK // 2
+        for i, place in enumerate((first, second)):
+            for j, to in enumerate((parity, 1 - parity)):
+                d_query[2 * place + to] = grad[(2 * i + j) * part : (2 * i + j + 1) * part]
         share, shift = share.T, shift.T
         query = held[rows, :BLOCK].astype(jnp.float32) * share
         out = held[rows, BLOCK:].astype(jnp.float32) * share
@@ -320,24 +334,24 @@
     lax.fori_loop(0, pairs, step, 0)
 
 
-def scale(places, parts, stats, sums, pieces):
-    count = places.shape[0]
+def scale(parts, stats, sums, pieces):
+    count = len(SLOTS)
     rows = sum(p.shape[0] for p in pieces)
-    given = [*in_hbm(places), parts, *in_hbm(stats, sums, *pieces)]
+    given = [parts, *in_hbm(stats, sums, *pieces)]
     return pl.pallas_call(
         scale_kernel,
         out_shape=[
-            pltpu.HBM((count, BLOCK, BLOCK), jnp.bfloat16),
+            pltpu.HBM((2 * count, BLOCK // 2, BLOCK), jnp.bfloat16),
             pltpu.HBM((rows, 3 * BLOCK), jnp.bfloat16),
         ],
-        in_specs=[SMEM, VMEM] + [ANY] * (len(given) - 2),
+        in_specs=[VMEM] + [ANY] * (len(given) - 1),
         out_specs=[VMEM] * 2,
         scratch_shapes=[
             pltpu.VMEM((rows, 2 * BLOCK), jnp.bfloat16),
             pltpu.VMEM((4 * count, BLOCK), jnp.float32),
             pltpu.VMEM(stats.shape, stats.dtype),
             pltpu.VMEM(sums.shape, sums.dtype),
-            pltpu.SemaphoreType.DMA((len(given) - 2,)),
+            pltpu.SemaphoreType.DMA((len(given) - 1,)),
         ],
         compiler_params=room(16),
         cost_estimate=cost(1 << 27, 1 << 16),
@@ -390,26 +404,27 @@
     )(*given)
 
 
-def project_kernel(core, chunk, grads, from_core, kw, vw, far_kw, far_vw, memory):
+def project_kernel(core, grads, from_core, kw, vw, far_kw, far_vw, memory):
     rows = from_core.shape[0]
     mine = grads[pl.ds(pl.multiple_of(core[0] * rows, rows), rows), :]
     other = from_core[...]
-    for j in range(memory.shape[0]):
-        part = pl.ds(pl.multiple_of(chunk[j] * BLOCK, BLOCK), BLOCK)
+    for j in range(0, memory.shape[0], 2):
+        part = slice(j * BLOCK, (j + 2) * BLOCK)
         total = dot_nt(mine[:, :BLOCK], kw[part, :]) + dot_nt(mine[:, BLOCK:], vw[part, :])
         total = total + dot_nt(other[:, :BLOCK], far_kw[part, :]) + dot_nt(other[:, BLOCK:], far_vw[part, :])
-        memory[j] = total.astype(jnp.bfloat16)
-
-
-def project(core, chunk, *given):
+        memory[j] = total[:, :BLOCK].astype(jnp.bfloat16)
+        memory[j + 1] = total[:, BLOCK:].astype(jnp.bfloat16)
+
+
+def project(core, *given):
     return pl.pallas_call(
         project_kernel,
-        out_shape=jax.ShapeDtypeStruct((chunk.shape[0], given[1].shape[0], BLOCK), jnp.bfloat16),
-        in_specs=[SMEM] * 2 + [VMEM] * len(given),
+        out_shape=jax.ShapeDtypeStruct((given[2].shape[0] // BLOCK, given[1].shape[0], BLOCK), jnp.bfloat16),
+        in_specs=[SMEM] + [VMEM] * len(given),
         out_specs=VMEM,
         compiler_params=room(8),
         name="project",
-    )(core, chunk, *given)
+    )(core, *given)
 
 
 def moved(value, axis, steps):
@@ -441,7 +456,6 @@
     ]
 
     count = lax.axis_size("zh")
-    places = (place + jnp.asarray(SLOTS, jnp.int32)) % count
     listed = lax.dynamic_slice_in_dim(block_lists, half * depth, depth, 0).reshape(count, depth // count, -1)
     listed = lax.dynamic_index_in_dim(listed, parity, 1, keepdims=False)
     step = jnp.arange(enc_blocks, dtype=jnp.int32)
@@ -454,18 +468,18 @@
     above = moved(bundle[: 2 * BLOCK], Z, -2)
     below = moved(bundle[BLOCK : 3 * BLOCK], Z, 2)
 
-    (early,) = forward(0, places, member, tables, [bundle], None)
-    parts, stats = forward(len(OWN), places, member, tables, [above, below], early)
+    (early,) = forward(0, member, tables, [bundle], None)
+    parts, stats = forward(len(OWN), member, tables, [above, below], early)
     pieces = [bundle, above, below]
     parts = lax.all_to_all(parts, "zh", 0, 0, tiled=True)
-    sums, chances, slopes = local(places, member, stats, tables, pieces)
+    sums, chances, slopes = local(member, stats, tables, pieces)
     parts, sums, chances, slopes = lax.optimization_barrier((parts, sums, chances, slopes))
 
-    d_query, scaled = scale(places, parts, stats, sums, pieces)
+    d_query, scaled = scale(parts, stats, sums, pieces)
     from_next = moved(gather(scaled, chances, slopes, 1, bf16), "par", 1)
     grads = gather(scaled, chances, slopes, 0, f32)
     d_query, grads = lax.optimization_barrier((d_query, grads))
-    d_query = lax.all_to_all(d_query, "zh", 0, 0, tiled=True)
+    d_query = lax.all_to_all(d_query, Z, 0, 0, tiled=True)
     grads, from_next, key_weight, value_weight = lax.optimization_barrier(
         (grads, from_next, key_weight, value_weight)
     )
@@ -477,14 +491,16 @@
     from_core = moved(lax.dynamic_slice_in_dim(grads, (1 - core) * (enc_rows // 2), enc_rows // 2, 0), "core", 1)
 
     cores = lax.axis_size("core")
-    chunk = jnp.arange(key_weight.shape[0] // BLOCK, dtype=jnp.int32)
     weights = (key_weight, value_weight, far_key_weight, far_value_weight)
-    memory = project(core[None], chunk, grads, from_core, *weights)
+    memory = project(core[None], grads, from_core, *weights)
     memory, d_query = lax.optimization_barrier((memory, d_query))
     memory = lax.all_to_all(memory, HEAD, 0, 0, tiled=True)
     memory = memory.reshape(-1, cores, *memory.shape[1:]).astype(f32)
     d_memory = jnp.sum(memory, axis=0).reshape(keys.shape).astype(bf16)
-    d_queries = jnp.sum(d_query.astype(f32), axis=0).astype(bf16)
+    d_query = jnp.sum(d_query.reshape(count, 2, *d_query.shape[1:]).astype(f32), axis=0).astype(bf16)
+    first = lax.dynamic_index_in_dim(d_query, parity, 0, keepdims=False)
+    second = moved(lax.dynamic_index_in_dim(d_query, 1 - parity, 0, keepdims=False), "par", 1)
+    d_queries = jnp.concatenate([first, second], axis=0)
     return d_queries, d_memory
 
 

time: 150 us -> 148 us (0.987)
  waiting for transfers between devices: 20 us -> 13.3 us
  starting transfers between devices: 83.3 us -> 89.8 us
    ppermute x12 -> x13, starting transfers between devices: 56.9 us -> 64.8 us  [moved(): lax.ppermute(value, axis, [(i, (i + steps) % count) for i in range(count)])]
    all_to_all x1, waiting for transfers between devices: 15.2 us -> 10.2 us  [body(): memory = lax.all_to_all(memory, HEAD, 0, 0, tiled=True)]
    ppermute x1, waiting for transfers between devices: 3.49 us -> 0.01 us  [body(): lax.ppermute(late, ('xh', 'par'), [(0, 3), (1, 2), (2, 1), (3, 0)])]
    ppermute x12 -> x13, waiting for transfers between devices: 0.99 us -> 2.8 us  [moved(): lax.ppermute(value, axis, [(i, (i + steps) % count) for i in range(count)])]
  transfers between devices with their start and end apart: 16 -> 17, of which waited for: 4 -> 6; matrix products, arithmetic and copies ran while one was open for 3% -> 2% of each run, Pallas kernels for 17% -> 17%
where the time goes in v11:
time: 148 us; the launch traced here: 147 us
  starting transfers between devices  89.8 us (61%)
  Pallas kernels  39 us (26%)
  waiting for transfers between devices  13.3 us (9%)
  other arithmetic  3.85 us (3%)
    ppermute x13, starting transfers between devices, moved(): lax.ppermute(value, axis, [(i, (i + steps) % count) for i in range(count)])  64.8 us
    pallas_call x1, Pallas kernels, local(): pl.pallas_call(local_kernel, grid=(2, pairs), out_shape=[pltpu.HBM((2 * p...  12.2 us
    all_to_all x1, starting transfers between devices, body(): d_query = lax.all_to_all(d_query, Z, 0, 0, tiled=True)  10.9 us
    pallas_call x2, Pallas kernels, gather(): pl.pallas_call(gather_kernel, grid=(steps,), out_shape=jax.ShapeDtypeStru...  10.3 us
    all_to_all x1, waiting for transfers between devices, body(): memory = lax.all_to_all(memory, HEAD, 0, 0, tiled=True)  10.2 us
    pallas_call x2, Pallas kernels, forward(): pl.pallas_call(kernel, out_shape=shapes, in_specs=[SMEM] + [VMEM] * (len(...  8.89 us
    all_to_all x1, starting transfers between devices, body(): parts = lax.all_to_all(parts, 'zh', 0, 0, tiled=True)  6.65 us
    all_to_all x1, starting transfers between devices, body(): memory = lax.all_to_all(memory, HEAD, 0, 0, tiled=True)  4.85 us
  transfers between devices with their start and end apart: 17, of which 6 were waited for; matrix products, arithmetic and copies ran while one was open for 2% of the time, Pallas kernels for 17%

profile of v11, /device:TPU:1, one launch (start us, length us, event | category | flops | bytes accessed | tf_op | source)
XLA Modules:
  0.0 147.2 jit_solution(7562987160029439324)
XLA Ops:
  0.6 0.0 copy-start
  0.6 0.8 join.3
  1.4 16.3 %collective-permute-start.7 = (bf16[128,256]{1,0:T(8,128)(2,1)S(1)}, bf16[128,256]{1,0:T(8,128)(2,1)S(1)}, u32[]{:S(2)}, u32[]{:S(2)}) collective-permute-start(bf16[128,256]{1,0:T(8,128)(2,1)S(1)} %join.3), channel_id=1, source_target_pairs={{0,128},{16,144},{32,160},{48,176},{64,192},{80,208},{96,224},{112... | collective-permute-start | bytes 196616 | tf_op jit(solution)/shard_map/ppermute | solution.py:432
  17.7 1.9 %collective-permute-start.3 = (bf16[128,256]{1,0:T(8,128)(2,1)S(1)}, bf16[128,256]{1,0:T(8,128)(2,1)S(1)}, u32[]{:S(2)}, u32[]{:S(2)}) collective-permute-start(bf16[128,256]{1,0:T(8,128)(2,1)S(1)} %join.3), channel_id=1, source_target_pairs={{0,192},{16,208},{32,224},{48,240},{64,0},{80,16},{96,32},{112,48}... | collective-permute-start | bytes 196616 | tf_op jit(solution)/shard_map/ppermute | solution.py:432
  19.7 7.3 %collective-permute-start.2 = (bf16[128,256]{1,0:T(8,128)(2,1)S(1)}, bf16[128,256]{1,0:T(8,128)(2,1)S(1)}, u32[]{:S(2)}, u32[]{:S(2)}) collective-permute-start(bf16[128,256]{1,0:T(8,128)(2,1)S(1)} %join.3), channel_id=1, source_target_pairs={{0,64},{16,80},{32,96},{48,112},{64,128},{80,144},{96,160},{112,17... | collective-permute-start | bytes 196616 | tf_op jit(solution)/shard_map/ppermute | solution.py:432
  26.9 1.0 join.2.refs_1_.rest_0_
  27.9 0.0 copy-start.4
  27.9 2.6 %collective-permute-start.1 = (bf16[512,256]{1,0:T(8,128)(2,1)S(1)}, bf16[512,256]{1,0:T(8,128)(2,1)S(1)}, u32[]{:S(2)}, u32[]{:S(2)}) collective-permute-start(bf16[512,256]{1,0:T(8,128)(2,1)S(1)} %join.2.refs_1_.rest_0_), channel_id=1, source_target_pairs={{0,16},{16,0},{1,17},{17,1},{2,18},{18,2},{3,19},{19,3},{4,20},{20... | collective-permute-start | bytes 786440 | tf_op jit(solution)/shard_map/ppermute | solution.py:432
  30.6 4.7 %collective-permute-start = (bf16[512,256]{1,0:T(8,128)(2,1)S(1)}, bf16[512,256]{1,0:T(8,128)(2,1)S(1)}, u32[]{:S(2)}, u32[]{:S(2)}) collective-permute-start(bf16[512,256]{1,0:T(8,128)(2,1)S(1)} %join.2.refs_1_.rest_0_), channel_id=1, source_target_pairs={{0,256},{256,0},{1,257},{257,1},{2,258},{258,2},{3,259},{259,3},{4... | collective-permute-start | bytes 786440 | tf_op jit(solution)/shard_map/ppermute | solution.py:432
  35.3 0.0 copy-done
  35.4 0.1 pad_add_fusion
  35.4 0.0 collective-permute-done.3
  35.4 0.0 collective-permute-done.2
  35.4 2.6 %collective-permute-start.4 = (bf16[512,256]{1,0:T(8,128)(2,1)S(1)}, bf16[512,256]{1,0:T(8,128)(2,1)S(1)}, u32[]{:S(2)}, u32[]{:S(2)}) collective-permute-start(bf16[512,256]{1,0:T(8,128)(2,1)S(1)} %join.2.refs_1_.rest_0_), channel_id=1, source_target_pairs={{0,272},{16,256},{256,16},{272,0},{1,273},{17,257},{257,17},{273,1... | collective-permute-start | bytes 786440 | tf_op jit(solution)/shard_map/ppermute | solution.py:455
  38.0 0.3 compare_reduce_fusion
  38.3 0.1 reshape.24.refs_0_.member
  38.4 4.1 %collective-permute-start.6 = (bf16[256,256]{1,0:T(8,128)(2,1)S(1)}, bf16[256,256]{1,0:T(8,128)(2,1)S(1)}, u32[]{:S(2)}, u32[]{:S(2)}) collective-permute-start(bf16[256,256]{1,0:T(8,128)(2,1)S(1)} %get-tuple-element.46), channel_id=1, source_target_pairs={{0,32},{16,48},{32,64},{48,80},{64,96},{80,112},{96,128},{112,144}... | collective-permute-start | bytes 393224 | tf_op jit(solution)/shard_map/ppermute | solution.py:432
  42.5 0.0 collective-permute-done.7
  42.5 3.3 %collective-permute-start.5 = (bf16[256,256]{1,0:T(8,128)(2,1)S(1)}, bf16[256,256]{1,0:T(8,128)(2,1)S(1)}, u32[]{:S(2)}, u32[]{:S(2)}) collective-permute-start(bf16[256,256]{1,0:T(8,128)(2,1)S(1)} %get-tuple-element.47), channel_id=1, source_target_pairs={{0,224},{16,240},{32,0},{48,16},{64,32},{80,48},{96,64},{112,80},{... | collective-permute-start | bytes 393224 | tf_op jit(solution)/shard_map/ppermute | solution.py:432
  45.9 0.0 copy-start.1
  45.9 0.0 collective-permute-done.1.refs_3_.rest_2_
  45.9 0.0 copy-start.9
  45.9 0.0 collective-permute-done.refs_2_.rest_1_
  45.9 0.0 collective-permute-done.4.refs_4_.rest_3_
  45.9 0.0 copy-start.11
  46.0 4.1 %forward.2.rest_6_ = f32[32,128]{1,0:T(8,128)S(1)} custom-call(s32[128]{0:T(128)S(1)} %reshape.24.refs_0_.member, bf16[512,256]{1,0:T(8,128)(2,1)S(1)} %join.2.refs_1_.rest_0_, bf16[512,256]{1,0:T(8,128)(2,1)S(1)} %collective-permute-done.refs_2_.rest_1_, bf16[512,256]{1,0:T(8,128)(2,1)S(1)} %collective-permute-done.1.refs_3_.rest_2_, ...), custom_call_target="tpu_custom_call" | custom-call | flops 4294967296 | bytes 1048576 | tf_op jit(solution)/shard_map/forward/pallas_call | solution.py:201
  50.1 0.2 collective-permute-done.6.rest_5_.rest_6_.rest_2_
  50.2 0.3 collective-permute-done.5.rest_4_.rest_5_.rest_1_
  50.5 4.8 %forward.3 = (bf16[8,48,128]{2,1,0:T(8,128)(2,1)}, f32[32,128]{1,0:T(8,128)S(1)}) custom-call(s32[128]{0:T(128)S(1)} %reshape.24.refs_0_.member, bf16[512,256]{1,0:T(8,128)(2,1)S(1)} %join.2.refs_1_.rest_0_, bf16[512,256]{1,0:T(8,128)(2,1)S(1)} %collective-permute-done.refs_2_.rest_1_, bf16[512,256]{1,0:T(8,128)(2,1)S(1)} %collective-permute-done.1.refs_3_.rest_2_, ...), custom_call_target="tpu_custom_call" | custom-call | flops 4294967296 | bytes 1048576 | tf_op jit(solution)/shard_map/forward/pallas_call | solution.py:201
  55.3 0.0 copy-done.1
  55.3 0.0 copy-start.7
  55.3 6.7 %all-to-all-start = ((bf16[8,48,128]{2,1,0:T(8,128)(2,1)}), bf16[8,48,128]{2,1,0:T(8,128)(2,1)S(1)}, u32[]{:S(2)}, u32[]{:S(2)}) async-start(bf16[8,48,128]{2,1,0:T(8,128)(2,1)} %get-tuple-element.27), calls=%async_computation | async-start | bytes 196608 | tf_op jit(solution)/shard_map/all_to_all | solution.py:474
  62.0 0.0 copy-done.6
  62.0 0.0 copy-done.7
  62.0 12.2 %local.1 = (f32[8,2,128,256]{3,2,1,0:T(8,128)}, bf16[8,1024,512]{2,1,0:T(8,128)(2,1)}, bf16[8,1024,512]{2,1,0:T(8,128)(2,1)}) custom-call(s32[128]{0:T(128)} %copy-done.8, f32[32,128]{1,0:T(8,128)} %copy-done.7, bf16[512,256]{1,0:T(8,128)(2,1)} %copy-done.4, bf16[512,256]{1,0:T(8,128)(2,1)} %copy-done.10, bf16[512,256]{1,0:T(8,128)(2,1)} %copy-done.9, ...), custom_call_target="tpu_custom_call" | custom-call | flops 12884901888 | bytes 1048576 | tf_op jit(solution)/shard_map/local/pallas_call | solution.py:275
  74.2 0.3 all-to-all-done.parts
  74.5 3.6 %scale.1 = (bf16[16,64,128]{2,1,0:T(8,128)(2,1)}, bf16[1024,384]{1,0:T(8,128)(2,1)}) custom-call(bf16[8,48,128]{2,1,0:T(8,128)(2,1)S(1)} %all-to-all-done.parts, f32[32,128]{1,0:T(8,128)} %copy-done.7, f32[8,2,128,256]{3,2,1,0:T(8,128)} %get-tuple-element.33.sums_ref, bf16[512,256]{1,0:T(8,128)(2,1)} %copy-done.1, bf16[256,256]{1,0:T(8,128)(2,1)} %copy-done.6, ...), custom_call_target="tpu_custom_call" | custom-call | flops 536870912 | bytes 1048576 | tf_op jit(solution)/shard_map/scale/pallas_call | solution.py:341
  78.1 5.2 %gather.3 = bf16[1024,256]{1,0:T(8,128)(2,1)S(1)} custom-call(bf16[1024,384]{1,0:T(8,128)(2,1)} %get-tuple-element.35.scaled, bf16[8,1024,512]{2,1,0:T(8,128)(2,1)} %get-tuple-element.36.chance, bf16[8,1024,512]{2,1,0:T(8,128)(2,1)} %get-tuple-element.37.slope), custom_call_target="tpu_custom_call" | custom-call | flops 3221225472 | bytes 1048576 | tf_op jit(solution)/shard_map/gather/pallas_call | solution.py:394
  83.2 0.0 copy-start.2
  83.3 0.0 copy-start.3
  83.3 5.7 %collective-permute-start.8 = (bf16[1024,256]{1,0:T(8,128)(2,1)S(1)}, bf16[1024,256]{1,0:T(8,128)(2,1)S(1)}, u32[]{:S(2)}, u32[]{:S(2)}) collective-permute-start(bf16[1024,256]{1,0:T(8,128)(2,1)S(1)} %gather.3), channel_id=1, source_target_pairs={{0,16},{16,0},{1,17},{17,1},{2,18},{18,2},{3,19},{19,3},{4,20},{20... | collective-permute-start | bytes 1572872 | tf_op jit(solution)/shard_map/ppermute | solution.py:432
  89.0 5.2 %gather.2 = f32[1024,256]{1,0:T(8,128)S(1)} custom-call(bf16[1024,384]{1,0:T(8,128)(2,1)} %get-tuple-element.35.scaled, bf16[8,1024,512]{2,1,0:T(8,128)(2,1)} %get-tuple-element.36.chance, bf16[8,1024,512]{2,1,0:T(8,128)(2,1)} %get-tuple-element.37.slope), custom_call_target="tpu_custom_call" | custom-call | flops 3221225472 | bytes 1048576 | tf_op jit(solution)/shard_map/gather/pallas_call | solution.py:394
  94.1 10.9 %all-to-all-start.1 = ((bf16[16,64,128]{2,1,0:T(8,128)(2,1)}), bf16[16,64,128]{2,1,0:T(8,128)(2,1)S(1)}, u32[]{:S(2)}, u32[]{:S(2)}) async-start(bf16[16,64,128]{2,1,0:T(8,128)(2,1)} %get-tuple-element.43), calls=%async_computation.1 | async-start | bytes 524288 | tf_op jit(solution)/shard_map/all_to_all | solution.py:482
  105.1 0.0 collective-permute-done.8
  105.1 0.8 add_convert_fusion.1
  105.9 1.9 %collective-permute-start.9 = (bf16[512,256]{1,0:T(8,128)(2,1)}, bf16[512,256]{1,0:T(8,128)(2,1)}, u32[]{:S(2)}, u32[]{:S(2)}) collective-permute-start(bf16[512,256]{1,0:T(8,128)(2,1)} %add_convert_fusion.1), channel_id=1, source_target_pairs={{0,256},{256,0},{1,257},{257,1},{2,258},{258,2},{3,259},{259,3},{4... | collective-permute-start | bytes 786440 | tf_op jit(solution)/shard_map/ppermute | solution.py:432
  107.8 0.0 copy-done.12
  107.8 0.0 copy-done.2
  107.8 6.5 %collective-permute-start.11 = (bf16[2048,128]{1,0:T(8,128)(2,1)S(1)}, bf16[2048,128]{1,0:T(8,128)(2,1)S(1)}, u32[]{:S(2)}, u32[]{:S(2)}) collective-permute-start(bf16[2048,128]{1,0:T(8,128)(2,1)S(1)} %copy-done.2), channel_id=1, source_target_pairs={{0,1},{1,0},{2,3},{3,2},{4,5},{5,4},{6,7},{7,6},{8,9},{9,8},{10,11... | collective-permute-start | bytes 1572872 | tf_op jit(solution)/shard_map/ppermute | solution.py:432
  114.4 1.9 %collective-permute-start.12 = (bf16[2048,128]{1,0:T(8,128)(2,1)S(1)}, bf16[2048,128]{1,0:T(8,128)(2,1)S(1)}, u32[]{:S(2)}, u32[]{:S(2)}) collective-permute-start(bf16[2048,128]{1,0:T(8,128)(2,1)S(1)} %copy-done.3), channel_id=1, source_target_pairs={{0,1},{1,0},{2,3},{3,2},{4,5},{5,4},{6,7},{7,6},{8,9},{9,8},{10,11... | collective-permute-start | bytes 1572872 | tf_op jit(solution)/shard_map/ppermute | solution.py:432
  116.3 0.0 collective-permute-done.9
  116.3 1.1 add_convert_fusion.grads
  117.5 5.1 %collective-permute-start.10 = (bf16[256,256]{1,0:T(8,128)(2,1)S(1)}, bf16[256,256]{1,0:T(8,128)(2,1)S(1)}, u32[]{:S(2)}, u32[]{:S(2)}) collective-permute-start(bf16[256,256]{1,0:T(8,128)(2,1)S(1)} %constant_dynamic-slice_fusion), channel_id=1, source_target_pairs={{0,1},{1,0},{2,3},{3,2},{4,5},{5,4},{6,7},{7,6},{8,9},{9,8},{10,11... | collective-permute-start | bytes 393224 | tf_op jit(solution)/shard_map/ppermute | solution.py:432
  122.5 1.0 collective-permute-done.10.from_core
  123.5 0.0 collective-permute-done.11.far_kw
  123.5 0.0 collective-permute-done.12.far_vw
  123.5 2.2 %project.1 = bf16[16,256,128]{2,1,0:T(8,128)(2,1)} custom-call(s32[1]{0:T(128)} %bitcast.core, bf16[512,256]{1,0:T(8,128)(2,1)S(1)} %add_convert_fusion.grads, bf16[256,256]{1,0:T(8,128)(2,1)S(1)} %collective-permute-done.10.from_core, bf16[2048,128]{1,0:T(8,128)(2,1)S(1)} %copy-done.2, bf16[2048,128]{1,0:T(8,128)(2,1)S(1)} %copy-done.3, ...), custom_call_target="tpu_custom_call" | custom-call | tf_op jit(solution)/shard_map/project/pallas_call | solution.py:420
  125.7 0.0 all-to-all-done.1
  125.7 4.8 %all-to-all-start.2 = ((bf16[16,256,128]{2,1,0:T(8,128)(2,1)}), bf16[16,256,128]{2,1,0:T(8,128)(2,1)S(1)}, u32[]{:S(2)}, u32[]{:S(2)}) async-start(bf16[16,256,128]{2,1,0:T(8,128)(2,1)} %project.1), calls=%async_computation.2 | async-start | bytes 2097152 | tf_op jit(solution)/shard_map/all_to_all | solution.py:497
  130.6 3.6 %collective-permute-start.13 = (bf16[64,128]{1,0:T(8,128)(2,1)S(1)}, bf16[64,128]{1,0:T(8,128)(2,1)S(1)}, u32[]{:S(2)}, u32[]{:S(2)}) collective-permute-start(bf16[64,128]{1,0:T(8,128)(2,1)S(1)} %get-tuple-element.49), channel_id=1, source_target_pairs={{0,16},{16,0},{1,17},{17,1},{2,18},{18,2},{3,19},{19,3},{4,20},{20... | collective-permute-start | bytes 49160 | tf_op jit(solution)/shard_map/ppermute | solution.py:432
  134.2 1.4 collective-permute-done.13
  135.6 0.6 pad_maximum_fusion.3
  136.2 10.2 %all-to-all-done.2 = bf16[16,256,128]{2,1,0:T(8,128)(2,1)S(1)} async-done(((bf16[16,256,128]{2,1,0:T(8,128)(2,1)}), bf16[16,256,128]{2,1,0:T(8,128)(2,1)S(1)}, u32[]{:S(2)}, u32[]{:S(2)}) %all-to-all-start.2) | async-done | bytes 1048608 | tf_op jit(solution)/shard_map/all_to_all | solution.py:497
  146.4 0.8 reduce.1
  (22 shorter events, 0.2 us)
Async XLA Ops:
  0.6 34.7 %copy-start = (s32[32,64]{1,0:T(8,128)S(1)}, s32[32,64]{1,0:T(8,128)}, u32[]{:S(2)}) copy-start(s32[32,64]{1,0:T(8,128)} %param.13) | copy-start | bytes 24580
  1.4 41.1 %collective-permute-start.7 = (bf16[128,256]{1,0:T(8,128)(2,1)S(1)}, bf16[128,256]{1,0:T(8,128)(2,1)S(1)}, u32[]{:S(2)}, u32[]{:S(2)}) collective-permute-start(bf16[128,256]{1,0:T(8,128)(2,1)S(1)} %join.3), channel_id=1, source_target_pairs={{0,128},{16,144},{32,160},{48,176},{64,192},{80,208},{96,224},{112... | collective-permute-start | bytes 196616 | tf_op jit(solution)/shard_map/ppermute | solution.py:432
  17.7 17.7 %collective-permute-start.3 = (bf16[128,256]{1,0:T(8,128)(2,1)S(1)}, bf16[128,256]{1,0:T(8,128)(2,1)S(1)}, u32[]{:S(2)}, u32[]{:S(2)}) collective-permute-start(bf16[128,256]{1,0:T(8,128)(2,1)S(1)} %join.3), channel_id=1, source_target_pairs={{0,192},{16,208},{32,224},{48,240},{64,0},{80,16},{96,32},{112,48}... | collective-permute-start | bytes 196616 | tf_op jit(solution)/shard_map/ppermute | solution.py:432
  19.7 15.8 %collective-permute-start.2 = (bf16[128,256]{1,0:T(8,128)(2,1)S(1)}, bf16[128,256]{1,0:T(8,128)(2,1)S(1)}, u32[]{:S(2)}, u32[]{:S(2)}) collective-permute-start(bf16[128,256]{1,0:T(8,128)(2,1)S(1)} %join.3), channel_id=1, source_target_pairs={{0,64},{16,80},{32,96},{48,112},{64,128},{80,144},{96,160},{112,17... | collective-permute-start | bytes 196616 | tf_op jit(solution)/shard_map/ppermute | solution.py:432
  27.9 22.6 %copy-start.4 = (bf16[512,256]{1,0:T(8,128)(2,1)}, bf16[512,256]{1,0:T(8,128)(2,1)S(1)}, u32[]{:S(2)}) copy-start(bf16[512,256]{1,0:T(8,128)(2,1)S(1)} %join.2.refs_1_.rest_0_) | copy-start | bytes 786436
  27.9 18.0 %collective-permute-start.1 = (bf16[512,256]{1,0:T(8,128)(2,1)S(1)}, bf16[512,256]{1,0:T(8,128)(2,1)S(1)}, u32[]{:S(2)}, u32[]{:S(2)}) collective-permute-start(bf16[512,256]{1,0:T(8,128)(2,1)S(1)} %join.2.refs_1_.rest_0_), channel_id=1, source_target_pairs={{0,16},{16,0},{1,17},{17,1},{2,18},{18,2},{3,19},{19,3},{4,20},{20... | collective-permute-start | bytes 786440 | tf_op jit(solution)/shard_map/ppermute | solution.py:432
  30.6 15.3 %collective-permute-start = (bf16[512,256]{1,0:T(8,128)(2,1)S(1)}, bf16[512,256]{1,0:T(8,128)(2,1)S(1)}, u32[]{:S(2)}, u32[]{:S(2)}) collective-permute-start(bf16[512,256]{1,0:T(8,128)(2,1)S(1)} %join.2.refs_1_.rest_0_), channel_id=1, source_target_pairs={{0,256},{256,0},{1,257},{257,1},{2,258},{258,2},{3,259},{259,3},{4... | collective-permute-start | bytes 786440 | tf_op jit(solution)/shard_map/ppermute | solution.py:432
  35.4 10.5 %collective-permute-start.4 = (bf16[512,256]{1,0:T(8,128)(2,1)S(1)}, bf16[512,256]{1,0:T(8,128)(2,1)S(1)}, u32[]{:S(2)}, u32[]{:S(2)}) collective-permute-start(bf16[512,256]{1,0:T(8,128)(2,1)S(1)} %join.2.refs_1_.rest_0_), channel_id=1, source_target_pairs={{0,272},{16,256},{256,16},{272,0},{1,273},{17,257},{257,17},{273,1... | collective-permute-start | bytes 786440 | tf_op jit(solution)/shard_map/ppermute | solution.py:455
  38.4 12.1 %copy-start.8 = (s32[128]{0:T(128)}, s32[128]{0:T(128)S(1)}, u32[]{:S(2)}) copy-start(s32[128]{0:T(128)S(1)} %reshape.24.refs_0_.member) | copy-start | bytes 1540
  38.4 11.8 %collective-permute-start.6 = (bf16[256,256]{1,0:T(8,128)(2,1)S(1)}, bf16[256,256]{1,0:T(8,128)(2,1)S(1)}, u32[]{:S(2)}, u32[]{:S(2)}) collective-permute-start(bf16[256,256]{1,0:T(8,128)(2,1)S(1)} %get-tuple-element.46), channel_id=1, source_target_pairs={{0,32},{16,48},{32,64},{48,80},{64,96},{80,112},{96,128},{112,144}... | collective-permute-start | bytes 393224 | tf_op jit(solution)/shard_map/ppermute | solution.py:432
  42.5 8.0 %collective-permute-start.5 = (bf16[256,256]{1,0:T(8,128)(2,1)S(1)}, bf16[256,256]{1,0:T(8,128)(2,1)S(1)}, u32[]{:S(2)}, u32[]{:S(2)}) collective-permute-start(bf16[256,256]{1,0:T(8,128)(2,1)S(1)} %get-tuple-element.47), channel_id=1, source_target_pairs={{0,224},{16,240},{32,0},{48,16},{64,32},{80,48},{96,64},{112,80},{... | collective-permute-start | bytes 393224 | tf_op jit(solution)/shard_map/ppermute | solution.py:432
  45.9 9.4 %copy-start.1 = (bf16[512,256]{1,0:T(8,128)(2,1)}, bf16[512,256]{1,0:T(8,128)(2,1)S(1)}, u32[]{:S(2)}) copy-start(bf16[512,256]{1,0:T(8,128)(2,1)S(1)} %pad_maximum_fusion.refs_5_.rest_4_.rest_0_) | copy-start | bytes 786436
  45.9 9.4 %copy-start.9 = (bf16[512,256]{1,0:T(8,128)(2,1)}, bf16[512,256]{1,0:T(8,128)(2,1)S(1)}, u32[]{:S(2)}) copy-start(bf16[512,256]{1,0:T(8,128)(2,1)S(1)} %collective-permute-done.1.refs_3_.rest_2_) | copy-start | bytes 786436
  45.9 9.4 %copy-start.10 = (bf16[512,256]{1,0:T(8,128)(2,1)}, bf16[512,256]{1,0:T(8,128)(2,1)S(1)}, u32[]{:S(2)}) copy-start(bf16[512,256]{1,0:T(8,128)(2,1)S(1)} %collective-permute-done.refs_2_.rest_1_) | copy-start | bytes 786436
  45.9 9.4 %copy-start.11 = (bf16[512,256]{1,0:T(8,128)(2,1)}, bf16[512,256]{1,0:T(8,128)(2,1)S(1)}, u32[]{:S(2)}) copy-start(bf16[512,256]{1,0:T(8,128)(2,1)S(1)} %collective-permute-done.4.refs_4_.rest_3_) | copy-start | bytes 786436
  50.2 11.7 %copy-start.5 = (bf16[256,256]{1,0:T(8,128)(2,1)}, bf16[256,256]{1,0:T(8,128)(2,1)S(1)}, u32[]{:S(2)}) copy-start(bf16[256,256]{1,0:T(8,128)(2,1)S(1)} %collective-permute-done.6.rest_5_.rest_6_.rest_2_) | copy-start | bytes 393220
  50.5 11.5 %copy-start.6 = (bf16[256,256]{1,0:T(8,128)(2,1)}, bf16[256,256]{1,0:T(8,128)(2,1)S(1)}, u32[]{:S(2)}) copy-start(bf16[256,256]{1,0:T(8,128)(2,1)S(1)} %collective-permute-done.5.rest_4_.rest_5_.rest_1_) | copy-start | bytes 393220
  55.3 6.7 %copy-start.7 = (f32[32,128]{1,0:T(8,128)}, f32[32,128]{1,0:T(8,128)S(1)}, u32[]{:S(2)}) copy-start(f32[32,128]{1,0:T(8,128)S(1)} %get-tuple-element.28.stats_ref) | copy-start | bytes 49156
  55.3 19.2 %all-to-all-start = ((bf16[8,48,128]{2,1,0:T(8,128)(2,1)}), bf16[8,48,128]{2,1,0:T(8,128)(2,1)S(1)}, u32[]{:S(2)}, u32[]{:S(2)}) async-start(bf16[8,48,128]{2,1,0:T(8,128)(2,1)} %get-tuple-element.27), calls=%async_computation | async-start | bytes 196608 | tf_op jit(solution)/shard_map/all_to_all | solution.py:474
  83.2 24.6 %copy-start.2 = (bf16[2048,128]{1,0:T(8,128)(2,1)S(1)}, bf16[2048,128]{1,0:T(8,128)(2,1)}, u32[]{:S(2)}) copy-start(bf16[2048,128]{1,0:T(8,128)(2,1)} %kw) | copy-start | bytes 1572868
  83.3 31.1 %copy-start.3 = (bf16[2048,128]{1,0:T(8,128)(2,1)S(1)}, bf16[2048,128]{1,0:T(8,128)(2,1)}, u32[]{:S(2)}) copy-start(bf16[2048,128]{1,0:T(8,128)(2,1)} %vw) | copy-start | bytes 1572868
  83.3 21.8 %collective-permute-start.8 = (bf16[1024,256]{1,0:T(8,128)(2,1)S(1)}, bf16[1024,256]{1,0:T(8,128)(2,1)S(1)}, u32[]{:S(2)}, u32[]{:S(2)}) collective-permute-start(bf16[1024,256]{1,0:T(8,128)(2,1)S(1)} %gather.3), channel_id=1, source_target_pairs={{0,16},{16,0},{1,17},{17,1},{2,18},{18,2},{3,19},{19,3},{4,20},{20... | collective-permute-start | bytes 1572872 | tf_op jit(solution)/shard_map/ppermute | solution.py:432
  94.1 31.6 %all-to-all-start.1 = ((bf16[16,64,128]{2,1,0:T(8,128)(2,1)}), bf16[16,64,128]{2,1,0:T(8,128)(2,1)S(1)}, u32[]{:S(2)}, u32[]{:S(2)}) async-start(bf16[16,64,128]{2,1,0:T(8,128)(2,1)} %get-tuple-element.43), calls=%async_computation.1 | async-start | bytes 524288 | tf_op jit(solution)/shard_map/all_to_all | solution.py:482
  105.1 2.8 %copy-start.12 = (bf16[1024,256]{1,0:T(8,128)(2,1)}, bf16[1024,256]{1,0:T(8,128)(2,1)S(1)}, u32[]{:S(2)}) copy-start(bf16[1024,256]{1,0:T(8,128)(2,1)S(1)} %collective-permute-done.8) | copy-start | bytes 1572868
  105.9 10.4 %collective-permute-start.9 = (bf16[512,256]{1,0:T(8,128)(2,1)}, bf16[512,256]{1,0:T(8,128)(2,1)}, u32[]{:S(2)}, u32[]{:S(2)}) collective-permute-start(bf16[512,256]{1,0:T(8,128)(2,1)} %add_convert_fusion.1), channel_id=1, source_target_pairs={{0,256},{256,0},{1,257},{257,1},{2,258},{258,2},{3,259},{259,3},{4... | collective-permute-start | bytes 786440 | tf_op jit(solution)/shard_map/ppermute | solution.py:432
  107.8 15.6 %collective-permute-start.11 = (bf16[2048,128]{1,0:T(8,128)(2,1)S(1)}, bf16[2048,128]{1,0:T(8,128)(2,1)S(1)}, u32[]{:S(2)}, u32[]{:S(2)}) collective-permute-start(bf16[2048,128]{1,0:T(8,128)(2,1)S(1)} %copy-done.2), channel_id=1, source_target_pairs={{0,1},{1,0},{2,3},{3,2},{4,5},{5,4},{6,7},{7,6},{8,9},{9,8},{10,11... | collective-permute-start | bytes 1572872 | tf_op jit(solution)/shard_map/ppermute | solution.py:432
  114.4 9.1 %collective-permute-start.12 = (bf16[2048,128]{1,0:T(8,128)(2,1)S(1)}, bf16[2048,128]{1,0:T(8,128)(2,1)S(1)}, u32[]{:S(2)}, u32[]{:S(2)}) collective-permute-start(bf16[2048,128]{1,0:T(8,128)(2,1)S(1)} %copy-done.3), channel_id=1, source_target_pairs={{0,1},{1,0},{2,3},{3,2},{4,5},{5,4},{6,7},{7,6},{8,9},{9,8},{10,11... | collective-permute-start | bytes 1572872 | tf_op jit(solution)/shard_map/ppermute | solution.py:432
  117.5 6.0 %collective-permute-start.10 = (bf16[256,256]{1,0:T(8,128)(2,1)S(1)}, bf16[256,256]{1,0:T(8,128)(2,1)S(1)}, u32[]{:S(2)}, u32[]{:S(2)}) collective-permute-start(bf16[256,256]{1,0:T(8,128)(2,1)S(1)} %constant_dynamic-slice_fusion), channel_id=1, source_target_pairs={{0,1},{1,0},{2,3},{3,2},{4,5},{5,4},{6,7},{7,6},{8,9},{9,8},{10,11... | collective-permute-start | bytes 393224 | tf_op jit(solution)/shard_map/ppermute | solution.py:432
  125.7 20.7 %all-to-all-start.2 = ((bf16[16,256,128]{2,1,0:T(8,128)(2,1)}), bf16[16,256,128]{2,1,0:T(8,128)(2,1)S(1)}, u32[]{:S(2)}, u32[]{:S(2)}) async-start(bf16[16,256,128]{2,1,0:T(8,128)(2,1)} %project.1), calls=%async_computation.2 | async-start | bytes 2097152 | tf_op jit(solution)/shard_map/all_to_all | solution.py:497
  130.6 5.0 %collective-permute-start.13 = (bf16[64,128]{1,0:T(8,128)(2,1)S(1)}, bf16[64,128]{1,0:T(8,128)(2,1)S(1)}, u32[]{:S(2)}, u32[]{:S(2)}) collective-permute-start(bf16[64,128]{1,0:T(8,128)(2,1)S(1)} %get-tuple-element.49), channel_id=1, source_target_pairs={{0,16},{16,0},{1,17},{17,1},{2,18},{18,2},{3,19},{19,3},{4,20},{20... | collective-permute-start | bytes 49160 | tf_op jit(solution)/shard_map/ppermute | solution.py:432

commit v12 on v11

--- a/solution.py
+++ b/solution.py
@@ -174,7 +174,8 @@
                 stats[pl.ds(half + 2 * place + h, 1), :] = mean[:, lanes]
         return carry
 
-    lax.fori_loop(0, pairs, step, 0)
+    for p in range(pairs):
+        step(p, 0)
     if result is not None:
         high = stats[:half, :].astype(jnp.bfloat16)
         low = (stats[:half, :] - high.astype(jnp.float32)).astype(jnp.bfloat16)
@@ -207,7 +208,7 @@
             pltpu.VMEM((rows, 2 * BLOCK), jnp.bfloat16),
             pltpu.VMEM((2, enc // 2, 2 * BLOCK), jnp.bfloat16),
         ],
-        compiler_params=room(20),
+        compiler_params=room(32),
         cost_estimate=cost(2 * rows * enc * 4 * BLOCK, rows * enc * 2),
         name="forward",
     )(*given)
@@ -331,7 +332,8 @@
         scaled[rows, 2 * BLOCK :] = query.astype(jnp.bfloat16)
         return carry
 
-    lax.fori_loop(0, pairs, step, 0)
+    for p in range(pairs):
+        step(p, 0)
 
 
 def scale(parts, stats, sums, pieces):

time: 148 us -> 147 us (level)
  no operation moved by 1% of the time
where the time goes in v12:
time: 147 us; the launch traced here: 146 us
  starting transfers between devices  89.5 us (61%)
  Pallas kernels  38.1 us (26%)
  waiting for transfers between devices  13.5 us (9%)
  other arithmetic  3.85 us (3%)
    ppermute x13, starting transfers between devices, moved(): lax.ppermute(value, axis, [(i, (i + steps) % count) for i in range(count)])  64.5 us
    pallas_call x1, Pallas kernels, local(): pl.pallas_call(local_kernel, grid=(2, pairs), out_shape=[pltpu.HBM((2 * p...  12.2 us
    all_to_all x1, starting transfers between devices, body(): d_query = lax.all_to_all(d_query, Z, 0, 0, tiled=True)  10.9 us
    pallas_call x2, Pallas kernels, gather(): pl.pallas_call(gather_kernel, grid=(steps,), out_shape=jax.ShapeDtypeStru...  10.3 us
    all_to_all x1, waiting for transfers between devices, body(): memory = lax.all_to_all(memory, HEAD, 0, 0, tiled=True)  10.2 us
    pallas_call x2, Pallas kernels, forward(): pl.pallas_call(kernel, out_shape=shapes, in_specs=[SMEM] + [VMEM] * (len(...  8.36 us
    all_to_all x1, starting transfers between devices, body(): parts = lax.all_to_all(parts, 'zh', 0, 0, tiled=True)  6.65 us
    all_to_all x1, starting transfers between devices, body(): memory = lax.all_to_all(memory, HEAD, 0, 0, tiled=True)  4.85 us
  transfers between devices with their start and end apart: 17, of which 6 were waited for; matrix products, arithmetic and copies ran while one was open for 2% of the time, Pallas kernels for 17%

profile of v12, /device:TPU:1, one launch (start us, length us, event | category | flops | bytes accessed | tf_op | source)
XLA Modules:
  0.0 146.3 jit_solution(8048155192213301354)
XLA Ops:
  0.6 0.0 copy-start
  0.6 0.8 join.3
  1.4 16.3 %collective-permute-start.7 = (bf16[128,256]{1,0:T(8,128)(2,1)S(1)}, bf16[128,256]{1,0:T(8,128)(2,1)S(1)}, u32[]{:S(2)}, u32[]{:S(2)}) collective-permute-start(bf16[128,256]{1,0:T(8,128)(2,1)S(1)} %join.3), channel_id=1, source_target_pairs={{0,128},{16,144},{32,160},{48,176},{64,192},{80,208},{96,224},{112... | collective-permute-start | bytes 196616 | tf_op jit(solution)/shard_map/ppermute | solution.py:434
  17.7 1.9 %collective-permute-start.3 = (bf16[128,256]{1,0:T(8,128)(2,1)S(1)}, bf16[128,256]{1,0:T(8,128)(2,1)S(1)}, u32[]{:S(2)}, u32[]{:S(2)}) collective-permute-start(bf16[128,256]{1,0:T(8,128)(2,1)S(1)} %join.3), channel_id=1, source_target_pairs={{0,192},{16,208},{32,224},{48,240},{64,0},{80,16},{96,32},{112,48}... | collective-permute-start | bytes 196616 | tf_op jit(solution)/shard_map/ppermute | solution.py:434
  19.7 7.3 %collective-permute-start.2 = (bf16[128,256]{1,0:T(8,128)(2,1)S(1)}, bf16[128,256]{1,0:T(8,128)(2,1)S(1)}, u32[]{:S(2)}, u32[]{:S(2)}) collective-permute-start(bf16[128,256]{1,0:T(8,128)(2,1)S(1)} %join.3), channel_id=1, source_target_pairs={{0,64},{16,80},{32,96},{48,112},{64,128},{80,144},{96,160},{112,17... | collective-permute-start | bytes 196616 | tf_op jit(solution)/shard_map/ppermute | solution.py:434
  26.9 1.0 join.2.refs_1_.rest_0_
  27.9 0.0 copy-start.4
  27.9 2.6 %collective-permute-start.1 = (bf16[512,256]{1,0:T(8,128)(2,1)S(1)}, bf16[512,256]{1,0:T(8,128)(2,1)S(1)}, u32[]{:S(2)}, u32[]{:S(2)}) collective-permute-start(bf16[512,256]{1,0:T(8,128)(2,1)S(1)} %join.2.refs_1_.rest_0_), channel_id=1, source_target_pairs={{0,16},{16,0},{1,17},{17,1},{2,18},{18,2},{3,19},{19,3},{4,20},{20... | collective-permute-start | bytes 786440 | tf_op jit(solution)/shard_map/ppermute | solution.py:434
  30.6 4.7 %collective-permute-start = (bf16[512,256]{1,0:T(8,128)(2,1)S(1)}, bf16[512,256]{1,0:T(8,128)(2,1)S(1)}, u32[]{:S(2)}, u32[]{:S(2)}) collective-permute-start(bf16[512,256]{1,0:T(8,128)(2,1)S(1)} %join.2.refs_1_.rest_0_), channel_id=1, source_target_pairs={{0,256},{256,0},{1,257},{257,1},{2,258},{258,2},{3,259},{259,3},{4... | collective-permute-start | bytes 786440 | tf_op jit(solution)/shard_map/ppermute | solution.py:434
  35.3 0.0 copy-done
  35.4 0.1 pad_add_fusion
  35.4 0.0 collective-permute-done.3
  35.4 0.0 collective-permute-done.2
  35.4 2.6 %collective-permute-start.4 = (bf16[512,256]{1,0:T(8,128)(2,1)S(1)}, bf16[512,256]{1,0:T(8,128)(2,1)S(1)}, u32[]{:S(2)}, u32[]{:S(2)}) collective-permute-start(bf16[512,256]{1,0:T(8,128)(2,1)S(1)} %join.2.refs_1_.rest_0_), channel_id=1, source_target_pairs={{0,272},{16,256},{256,16},{272,0},{1,273},{17,257},{257,17},{273,1... | collective-permute-start | bytes 786440 | tf_op jit(solution)/shard_map/ppermute | solution.py:457
  38.0 0.3 compare_reduce_fusion
  38.3 0.1 reshape.24.refs_0_.member
  38.4 4.1 %collective-permute-start.6 = (bf16[256,256]{1,0:T(8,128)(2,1)S(1)}, bf16[256,256]{1,0:T(8,128)(2,1)S(1)}, u32[]{:S(2)}, u32[]{:S(2)}) collective-permute-start(bf16[256,256]{1,0:T(8,128)(2,1)S(1)} %get-tuple-element.46), channel_id=1, source_target_pairs={{0,32},{16,48},{32,64},{48,80},{64,96},{80,112},{96,128},{112,144}... | collective-permute-start | bytes 393224 | tf_op jit(solution)/shard_map/ppermute | solution.py:434
  42.5 0.0 collective-permute-done.7
  42.5 3.3 %collective-permute-start.5 = (bf16[256,256]{1,0:T(8,128)(2,1)S(1)}, bf16[256,256]{1,0:T(8,128)(2,1)S(1)}, u32[]{:S(2)}, u32[]{:S(2)}) collective-permute-start(bf16[256,256]{1,0:T(8,128)(2,1)S(1)} %get-tuple-element.47), channel_id=1, source_target_pairs={{0,224},{16,240},{32,0},{48,16},{64,32},{80,48},{96,64},{112,80},{... | collective-permute-start | bytes 393224 | tf_op jit(solution)/shard_map/ppermute | solution.py:434
  45.9 0.0 copy-start.1
  45.9 0.0 collective-permute-done.1.refs_3_.rest_2_
  45.9 0.0 copy-start.9
  45.9 0.0 collective-permute-done.refs_2_.rest_1_
  45.9 0.0 copy-start.10
  45.9 0.0 collective-permute-done.4.refs_4_.rest_3_
  45.9 0.0 copy-start.11
  46.0 3.9 %forward.2.rest_6_ = f32[32,128]{1,0:T(8,128)S(1)} custom-call(s32[128]{0:T(128)S(1)} %reshape.24.refs_0_.member, bf16[512,256]{1,0:T(8,128)(2,1)S(1)} %join.2.refs_1_.rest_0_, bf16[512,256]{1,0:T(8,128)(2,1)S(1)} %collective-permute-done.refs_2_.rest_1_, bf16[512,256]{1,0:T(8,128)(2,1)S(1)} %collective-permute-done.1.refs_3_.rest_2_, ...), custom_call_target="tpu_custom_call" | custom-call | flops 4294967296 | bytes 1048576 | tf_op jit(solution)/shard_map/forward/pallas_call | solution.py:202
  49.8 0.4 collective-permute-done.6.rest_5_.rest_6_.rest_2_
  50.2 0.3 collective-permute-done.5.rest_4_.rest_5_.rest_1_
  50.5 0.0 copy-done.4
  50.5 0.0 copy-done.8
  50.5 4.5 %forward.3 = (bf16[8,48,128]{2,1,0:T(8,128)(2,1)}, f32[32,128]{1,0:T(8,128)S(1)}) custom-call(s32[128]{0:T(128)S(1)} %reshape.24.refs_0_.member, bf16[512,256]{1,0:T(8,128)(2,1)S(1)} %join.2.refs_1_.rest_0_, bf16[512,256]{1,0:T(8,128)(2,1)S(1)} %collective-permute-done.refs_2_.rest_1_, bf16[512,256]{1,0:T(8,128)(2,1)S(1)} %collective-permute-done.1.refs_3_.rest_2_, ...), custom_call_target="tpu_custom_call" | custom-call | flops 4294967296 | bytes 1048576 | tf_op jit(solution)/shard_map/forward/pallas_call | solution.py:202
  55.1 0.0 copy-start.7
  55.1 6.7 %all-to-all-start = ((bf16[8,48,128]{2,1,0:T(8,128)(2,1)}), bf16[8,48,128]{2,1,0:T(8,128)(2,1)S(1)}, u32[]{:S(2)}, u32[]{:S(2)}) async-start(bf16[8,48,128]{2,1,0:T(8,128)(2,1)} %get-tuple-element.27), calls=%async_computation | async-start | bytes 196608 | tf_op jit(solution)/shard_map/all_to_all | solution.py:476
  61.7 0.0 copy-done.6
  61.7 0.0 copy-done.7
  61.7 12.2 %local.1 = (f32[8,2,128,256]{3,2,1,0:T(8,128)}, bf16[8,1024,512]{2,1,0:T(8,128)(2,1)}, bf16[8,1024,512]{2,1,0:T(8,128)(2,1)}) custom-call(s32[128]{0:T(128)} %copy-done.8, f32[32,128]{1,0:T(8,128)} %copy-done.7, bf16[512,256]{1,0:T(8,128)(2,1)} %copy-done.4, bf16[512,256]{1,0:T(8,128)(2,1)} %copy-done.10, bf16[512,256]{1,0:T(8,128)(2,1)} %copy-done.9, ...), custom_call_target="tpu_custom_call" | custom-call | flops 12884901888 | bytes 1048576 | tf_op jit(solution)/shard_map/local/pallas_call | solution.py:276
  74.0 0.3 all-to-all-done.parts
  74.2 3.2 %scale.1 = (bf16[16,64,128]{2,1,0:T(8,128)(2,1)}, bf16[1024,384]{1,0:T(8,128)(2,1)}) custom-call(bf16[8,48,128]{2,1,0:T(8,128)(2,1)S(1)} %all-to-all-done.parts, f32[32,128]{1,0:T(8,128)} %copy-done.7, f32[8,2,128,256]{3,2,1,0:T(8,128)} %get-tuple-element.33.sums_ref, bf16[512,256]{1,0:T(8,128)(2,1)} %copy-done.1, bf16[256,256]{1,0:T(8,128)(2,1)} %copy-done.6, ...), custom_call_target="tpu_custom_call" | custom-call | flops 536870912 | bytes 1048576 | tf_op jit(solution)/shard_map/scale/pallas_call | solution.py:343
  77.5 5.2 %gather.3 = bf16[1024,256]{1,0:T(8,128)(2,1)S(1)} custom-call(bf16[1024,384]{1,0:T(8,128)(2,1)} %get-tuple-element.35.scaled, bf16[8,1024,512]{2,1,0:T(8,128)(2,1)} %get-tuple-element.36.chance, bf16[8,1024,512]{2,1,0:T(8,128)(2,1)} %get-tuple-element.37.slope), custom_call_target="tpu_custom_call" | custom-call | flops 3221225472 | bytes 1048576 | tf_op jit(solution)/shard_map/gather/pallas_call | solution.py:396
  82.6 0.0 copy-start.2
  82.7 0.0 copy-start.3
  82.7 5.7 %collective-permute-start.8 = (bf16[1024,256]{1,0:T(8,128)(2,1)S(1)}, bf16[1024,256]{1,0:T(8,128)(2,1)S(1)}, u32[]{:S(2)}, u32[]{:S(2)}) collective-permute-start(bf16[1024,256]{1,0:T(8,128)(2,1)S(1)} %gather.3), channel_id=1, source_target_pairs={{0,16},{16,0},{1,17},{17,1},{2,18},{18,2},{3,19},{19,3},{4,20},{20... | collective-permute-start | bytes 1572872 | tf_op jit(solution)/shard_map/ppermute | solution.py:434
  88.3 5.2 %gather.2 = f32[1024,256]{1,0:T(8,128)S(1)} custom-call(bf16[1024,384]{1,0:T(8,128)(2,1)} %get-tuple-element.35.scaled, bf16[8,1024,512]{2,1,0:T(8,128)(2,1)} %get-tuple-element.36.chance, bf16[8,1024,512]{2,1,0:T(8,128)(2,1)} %get-tuple-element.37.slope), custom_call_target="tpu_custom_call" | custom-call | flops 3221225472 | bytes 1048576 | tf_op jit(solution)/shard_map/gather/pallas_call | solution.py:396
  93.5 10.9 %all-to-all-start.1 = ((bf16[16,64,128]{2,1,0:T(8,128)(2,1)}), bf16[16,64,128]{2,1,0:T(8,128)(2,1)S(1)}, u32[]{:S(2)}, u32[]{:S(2)}) async-start(bf16[16,64,128]{2,1,0:T(8,128)(2,1)} %get-tuple-element.43), calls=%async_computation.1 | async-start | bytes 524288 | tf_op jit(solution)/shard_map/all_to_all | solution.py:484
  104.4 0.0 collective-permute-done.8
  104.5 0.8 add_convert_fusion.1
  105.3 1.9 %collective-permute-start.9 = (bf16[512,256]{1,0:T(8,128)(2,1)}, bf16[512,256]{1,0:T(8,128)(2,1)}, u32[]{:S(2)}, u32[]{:S(2)}) collective-permute-start(bf16[512,256]{1,0:T(8,128)(2,1)} %add_convert_fusion.1), channel_id=1, source_target_pairs={{0,256},{256,0},{1,257},{257,1},{2,258},{258,2},{3,259},{259,3},{4... | collective-permute-start | bytes 786440 | tf_op jit(solution)/shard_map/ppermute | solution.py:434
  107.2 6.2 %collective-permute-start.11 = (bf16[2048,128]{1,0:T(8,128)(2,1)S(1)}, bf16[2048,128]{1,0:T(8,128)(2,1)S(1)}, u32[]{:S(2)}, u32[]{:S(2)}) collective-permute-start(bf16[2048,128]{1,0:T(8,128)(2,1)S(1)} %copy-done.2), channel_id=1, source_target_pairs={{0,1},{1,0},{2,3},{3,2},{4,5},{5,4},{6,7},{7,6},{8,9},{9,8},{10,11... | collective-permute-start | bytes 1572872 | tf_op jit(solution)/shard_map/ppermute | solution.py:434
  113.5 1.9 %collective-permute-start.12 = (bf16[2048,128]{1,0:T(8,128)(2,1)S(1)}, bf16[2048,128]{1,0:T(8,128)(2,1)S(1)}, u32[]{:S(2)}, u32[]{:S(2)}) collective-permute-start(bf16[2048,128]{1,0:T(8,128)(2,1)S(1)} %copy-done.3), channel_id=1, source_target_pairs={{0,1},{1,0},{2,3},{3,2},{4,5},{5,4},{6,7},{7,6},{8,9},{9,8},{10,11... | collective-permute-start | bytes 1572872 | tf_op jit(solution)/shard_map/ppermute | solution.py:434
  115.4 0.0 collective-permute-done.9
  115.4 1.1 add_convert_fusion.grads
  116.6 5.1 %collective-permute-start.10 = (bf16[256,256]{1,0:T(8,128)(2,1)S(1)}, bf16[256,256]{1,0:T(8,128)(2,1)S(1)}, u32[]{:S(2)}, u32[]{:S(2)}) collective-permute-start(bf16[256,256]{1,0:T(8,128)(2,1)S(1)} %constant_dynamic-slice_fusion), channel_id=1, source_target_pairs={{0,1},{1,0},{2,3},{3,2},{4,5},{5,4},{6,7},{7,6},{8,9},{9,8},{10,11... | collective-permute-start | bytes 393224 | tf_op jit(solution)/shard_map/ppermute | solution.py:434
  121.6 1.0 collective-permute-done.10.from_core
  122.6 0.0 collective-permute-done.11.far_kw
  122.6 0.0 collective-permute-done.12.far_vw
  122.6 2.2 %project.1 = bf16[16,256,128]{2,1,0:T(8,128)(2,1)} custom-call(s32[1]{0:T(128)} %bitcast.core, bf16[512,256]{1,0:T(8,128)(2,1)S(1)} %add_convert_fusion.grads, bf16[256,256]{1,0:T(8,128)(2,1)S(1)} %collective-permute-done.10.from_core, bf16[2048,128]{1,0:T(8,128)(2,1)S(1)} %copy-done.2, bf16[2048,128]{1,0:T(8,128)(2,1)S(1)} %copy-done.3, ...), custom_call_target="tpu_custom_call" | custom-call | tf_op jit(solution)/shard_map/project/pallas_call | solution.py:422
  124.8 0.0 all-to-all-done.1
  124.8 4.8 %all-to-all-start.2 = ((bf16[16,256,128]{2,1,0:T(8,128)(2,1)}), bf16[16,256,128]{2,1,0:T(8,128)(2,1)S(1)}, u32[]{:S(2)}, u32[]{:S(2)}) async-start(bf16[16,256,128]{2,1,0:T(8,128)(2,1)} %project.1), calls=%async_computation.2 | async-start | bytes 2097152 | tf_op jit(solution)/shard_map/all_to_all | solution.py:499
  129.8 3.6 %collective-permute-start.13 = (bf16[64,128]{1,0:T(8,128)(2,1)S(1)}, bf16[64,128]{1,0:T(8,128)(2,1)S(1)}, u32[]{:S(2)}, u32[]{:S(2)}) collective-permute-start(bf16[64,128]{1,0:T(8,128)(2,1)S(1)} %get-tuple-element.49), channel_id=1, source_target_pairs={{0,16},{16,0},{1,17},{17,1},{2,18},{18,2},{3,19},{19,3},{4,20},{20... | collective-permute-start | bytes 49160 | tf_op jit(solution)/shard_map/ppermute | solution.py:434
  133.3 1.4 collective-permute-done.13
  134.7 0.6 pad_maximum_fusion.3
  135.3 10.2 %all-to-all-done.2 = bf16[16,256,128]{2,1,0:T(8,128)(2,1)S(1)} async-done(((bf16[16,256,128]{2,1,0:T(8,128)(2,1)}), bf16[16,256,128]{2,1,0:T(8,128)(2,1)S(1)}, u32[]{:S(2)}, u32[]{:S(2)}) %all-to-all-start.2) | async-done | bytes 1048608 | tf_op jit(solution)/shard_map/all_to_all | solution.py:499
  145.5 0.8 reduce.1
  (22 shorter events, 0.2 us)
Async XLA Ops:
  0.6 34.7 %copy-start = (s32[32,64]{1,0:T(8,128)S(1)}, s32[32,64]{1,0:T(8,128)}, u32[]{:S(2)}) copy-start(s32[32,64]{1,0:T(8,128)} %param.13) | copy-start | bytes 24580
  1.4 41.1 %collective-permute-start.7 = (bf16[128,256]{1,0:T(8,128)(2,1)S(1)}, bf16[128,256]{1,0:T(8,128)(2,1)S(1)}, u32[]{:S(2)}, u32[]{:S(2)}) collective-permute-start(bf16[128,256]{1,0:T(8,128)(2,1)S(1)} %join.3), channel_id=1, source_target_pairs={{0,128},{16,144},{32,160},{48,176},{64,192},{80,208},{96,224},{112... | collective-permute-start | bytes 196616 | tf_op jit(solution)/shard_map/ppermute | solution.py:434
  17.7 17.7 %collective-permute-start.3 = (bf16[128,256]{1,0:T(8,128)(2,1)S(1)}, bf16[128,256]{1,0:T(8,128)(2,1)S(1)}, u32[]{:S(2)}, u32[]{:S(2)}) collective-permute-start(bf16[128,256]{1,0:T(8,128)(2,1)S(1)} %join.3), channel_id=1, source_target_pairs={{0,192},{16,208},{32,224},{48,240},{64,0},{80,16},{96,32},{112,48}... | collective-permute-start | bytes 196616 | tf_op jit(solution)/shard_map/ppermute | solution.py:434
  19.7 15.8 %collective-permute-start.2 = (bf16[128,256]{1,0:T(8,128)(2,1)S(1)}, bf16[128,256]{1,0:T(8,128)(2,1)S(1)}, u32[]{:S(2)}, u32[]{:S(2)}) collective-permute-start(bf16[128,256]{1,0:T(8,128)(2,1)S(1)} %join.3), channel_id=1, source_target_pairs={{0,64},{16,80},{32,96},{48,112},{64,128},{80,144},{96,160},{112,17... | collective-permute-start | bytes 196616 | tf_op jit(solution)/shard_map/ppermute | solution.py:434
  27.9 22.6 %copy-start.4 = (bf16[512,256]{1,0:T(8,128)(2,1)}, bf16[512,256]{1,0:T(8,128)(2,1)S(1)}, u32[]{:S(2)}) copy-start(bf16[512,256]{1,0:T(8,128)(2,1)S(1)} %join.2.refs_1_.rest_0_) | copy-start | bytes 786436
  27.9 18.0 %collective-permute-start.1 = (bf16[512,256]{1,0:T(8,128)(2,1)S(1)}, bf16[512,256]{1,0:T(8,128)(2,1)S(1)}, u32[]{:S(2)}, u32[]{:S(2)}) collective-permute-start(bf16[512,256]{1,0:T(8,128)(2,1)S(1)} %join.2.refs_1_.rest_0_), channel_id=1, source_target_pairs={{0,16},{16,0},{1,17},{17,1},{2,18},{18,2},{3,19},{19,3},{4,20},{20... | collective-permute-start | bytes 786440 | tf_op jit(solution)/shard_map/ppermute | solution.py:434
  30.6 15.3 %collective-permute-start = (bf16[512,256]{1,0:T(8,128)(2,1)S(1)}, bf16[512,256]{1,0:T(8,128)(2,1)S(1)}, u32[]{:S(2)}, u32[]{:S(2)}) collective-permute-start(bf16[512,256]{1,0:T(8,128)(2,1)S(1)} %join.2.refs_1_.rest_0_), channel_id=1, source_target_pairs={{0,256},{256,0},{1,257},{257,1},{2,258},{258,2},{3,259},{259,3},{4... | collective-permute-start | bytes 786440 | tf_op jit(solution)/shard_map/ppermute | solution.py:434
  35.4 10.5 %collective-permute-start.4 = (bf16[512,256]{1,0:T(8,128)(2,1)S(1)}, bf16[512,256]{1,0:T(8,128)(2,1)S(1)}, u32[]{:S(2)}, u32[]{:S(2)}) collective-permute-start(bf16[512,256]{1,0:T(8,128)(2,1)S(1)} %join.2.refs_1_.rest_0_), channel_id=1, source_target_pairs={{0,272},{16,256},{256,16},{272,0},{1,273},{17,257},{257,17},{273,1... | collective-permute-start | bytes 786440 | tf_op jit(solution)/shard_map/ppermute | solution.py:457
  38.4 12.1 %copy-start.8 = (s32[128]{0:T(128)}, s32[128]{0:T(128)S(1)}, u32[]{:S(2)}) copy-start(s32[128]{0:T(128)S(1)} %reshape.24.refs_0_.member) | copy-start | bytes 1540
  38.4 11.8 %collective-permute-start.6 = (bf16[256,256]{1,0:T(8,128)(2,1)S(1)}, bf16[256,256]{1,0:T(8,128)(2,1)S(1)}, u32[]{:S(2)}, u32[]{:S(2)}) collective-permute-start(bf16[256,256]{1,0:T(8,128)(2,1)S(1)} %get-tuple-element.46), channel_id=1, source_target_pairs={{0,32},{16,48},{32,64},{48,80},{64,96},{80,112},{96,128},{112,144}... | collective-permute-start | bytes 393224 | tf_op jit(solution)/shard_map/ppermute | solution.py:434
  42.5 8.0 %collective-permute-start.5 = (bf16[256,256]{1,0:T(8,128)(2,1)S(1)}, bf16[256,256]{1,0:T(8,128)(2,1)S(1)}, u32[]{:S(2)}, u32[]{:S(2)}) collective-permute-start(bf16[256,256]{1,0:T(8,128)(2,1)S(1)} %get-tuple-element.47), channel_id=1, source_target_pairs={{0,224},{16,240},{32,0},{48,16},{64,32},{80,48},{96,64},{112,80},{... | collective-permute-start | bytes 393224 | tf_op jit(solution)/shard_map/ppermute | solution.py:434
  45.9 9.2 %copy-start.1 = (bf16[512,256]{1,0:T(8,128)(2,1)}, bf16[512,256]{1,0:T(8,128)(2,1)S(1)}, u32[]{:S(2)}) copy-start(bf16[512,256]{1,0:T(8,128)(2,1)S(1)} %pad_maximum_fusion.refs_5_.rest_4_.rest_0_) | copy-start | bytes 786436
  45.9 9.1 %copy-start.9 = (bf16[512,256]{1,0:T(8,128)(2,1)}, bf16[512,256]{1,0:T(8,128)(2,1)S(1)}, u32[]{:S(2)}) copy-start(bf16[512,256]{1,0:T(8,128)(2,1)S(1)} %collective-permute-done.1.refs_3_.rest_2_) | copy-start | bytes 786436
  45.9 9.1 %copy-start.10 = (bf16[512,256]{1,0:T(8,128)(2,1)}, bf16[512,256]{1,0:T(8,128)(2,1)S(1)}, u32[]{:S(2)}) copy-start(bf16[512,256]{1,0:T(8,128)(2,1)S(1)} %collective-permute-done.refs_2_.rest_1_) | copy-start | bytes 786436
  45.9 9.1 %copy-start.11 = (bf16[512,256]{1,0:T(8,128)(2,1)}, bf16[512,256]{1,0:T(8,128)(2,1)S(1)}, u32[]{:S(2)}) copy-start(bf16[512,256]{1,0:T(8,128)(2,1)S(1)} %collective-permute-done.4.refs_4_.rest_3_) | copy-start | bytes 786436
  50.2 11.5 %copy-start.5 = (bf16[256,256]{1,0:T(8,128)(2,1)}, bf16[256,256]{1,0:T(8,128)(2,1)S(1)}, u32[]{:S(2)}) copy-start(bf16[256,256]{1,0:T(8,128)(2,1)S(1)} %collective-permute-done.6.rest_5_.rest_6_.rest_2_) | copy-start | bytes 393220
  50.5 11.2 %copy-start.6 = (bf16[256,256]{1,0:T(8,128)(2,1)}, bf16[256,256]{1,0:T(8,128)(2,1)S(1)}, u32[]{:S(2)}) copy-start(bf16[256,256]{1,0:T(8,128)(2,1)S(1)} %collective-permute-done.5.rest_4_.rest_5_.rest_1_) | copy-start | bytes 393220
  55.1 6.7 %copy-start.7 = (f32[32,128]{1,0:T(8,128)}, f32[32,128]{1,0:T(8,128)S(1)}, u32[]{:S(2)}) copy-start(f32[32,128]{1,0:T(8,128)S(1)} %get-tuple-element.28.stats_ref) | copy-start | bytes 49156
  55.1 19.2 %all-to-all-start = ((bf16[8,48,128]{2,1,0:T(8,128)(2,1)}), bf16[8,48,128]{2,1,0:T(8,128)(2,1)S(1)}, u32[]{:S(2)}, u32[]{:S(2)}) async-start(bf16[8,48,128]{2,1,0:T(8,128)(2,1)} %get-tuple-element.27), calls=%async_computation | async-start | bytes 196608 | tf_op jit(solution)/shard_map/all_to_all | solution.py:476
  82.6 24.6 %copy-start.2 = (bf16[2048,128]{1,0:T(8,128)(2,1)S(1)}, bf16[2048,128]{1,0:T(8,128)(2,1)}, u32[]{:S(2)}) copy-start(bf16[2048,128]{1,0:T(8,128)(2,1)} %kw) | copy-start | bytes 1572868
  82.7 30.8 %copy-start.3 = (bf16[2048,128]{1,0:T(8,128)(2,1)S(1)}, bf16[2048,128]{1,0:T(8,128)(2,1)}, u32[]{:S(2)}) copy-start(bf16[2048,128]{1,0:T(8,128)(2,1)} %vw) | copy-start | bytes 1572868
  82.7 21.8 %collective-permute-start.8 = (bf16[1024,256]{1,0:T(8,128)(2,1)S(1)}, bf16[1024,256]{1,0:T(8,128)(2,1)S(1)}, u32[]{:S(2)}, u32[]{:S(2)}) collective-permute-start(bf16[1024,256]{1,0:T(8,128)(2,1)S(1)} %gather.3), channel_id=1, source_target_pairs={{0,16},{16,0},{1,17},{17,1},{2,18},{18,2},{3,19},{19,3},{4,20},{20... | collective-permute-start | bytes 1572872 | tf_op jit(solution)/shard_map/ppermute | solution.py:434
  93.5 31.3 %all-to-all-start.1 = ((bf16[16,64,128]{2,1,0:T(8,128)(2,1)}), bf16[16,64,128]{2,1,0:T(8,128)(2,1)S(1)}, u32[]{:S(2)}, u32[]{:S(2)}) async-start(bf16[16,64,128]{2,1,0:T(8,128)(2,1)} %get-tuple-element.43), calls=%async_computation.1 | async-start | bytes 524288 | tf_op jit(solution)/shard_map/all_to_all | solution.py:484
  104.4 2.8 %copy-start.12 = (bf16[1024,256]{1,0:T(8,128)(2,1)}, bf16[1024,256]{1,0:T(8,128)(2,1)S(1)}, u32[]{:S(2)}) copy-start(bf16[1024,256]{1,0:T(8,128)(2,1)S(1)} %collective-permute-done.8) | copy-start | bytes 1572868
  105.3 10.1 %collective-permute-start.9 = (bf16[512,256]{1,0:T(8,128)(2,1)}, bf16[512,256]{1,0:T(8,128)(2,1)}, u32[]{:S(2)}, u32[]{:S(2)}) collective-permute-start(bf16[512,256]{1,0:T(8,128)(2,1)} %add_convert_fusion.1), channel_id=1, source_target_pairs={{0,256},{256,0},{1,257},{257,1},{2,258},{258,2},{3,259},{259,3},{4... | collective-permute-start | bytes 786440 | tf_op jit(solution)/shard_map/ppermute | solution.py:434
  107.2 15.4 %collective-permute-start.11 = (bf16[2048,128]{1,0:T(8,128)(2,1)S(1)}, bf16[2048,128]{1,0:T(8,128)(2,1)S(1)}, u32[]{:S(2)}, u32[]{:S(2)}) collective-permute-start(bf16[2048,128]{1,0:T(8,128)(2,1)S(1)} %copy-done.2), channel_id=1, source_target_pairs={{0,1},{1,0},{2,3},{3,2},{4,5},{5,4},{6,7},{7,6},{8,9},{9,8},{10,11... | collective-permute-start | bytes 1572872 | tf_op jit(solution)/shard_map/ppermute | solution.py:434
  113.5 9.1 %collective-permute-start.12 = (bf16[2048,128]{1,0:T(8,128)(2,1)S(1)}, bf16[2048,128]{1,0:T(8,128)(2,1)S(1)}, u32[]{:S(2)}, u32[]{:S(2)}) collective-permute-start(bf16[2048,128]{1,0:T(8,128)(2,1)S(1)} %copy-done.3), channel_id=1, source_target_pairs={{0,1},{1,0},{2,3},{3,2},{4,5},{5,4},{6,7},{7,6},{8,9},{9,8},{10,11... | collective-permute-start | bytes 1572872 | tf_op jit(solution)/shard_map/ppermute | solution.py:434
  116.6 6.0 %collective-permute-start.10 = (bf16[256,256]{1,0:T(8,128)(2,1)S(1)}, bf16[256,256]{1,0:T(8,128)(2,1)S(1)}, u32[]{:S(2)}, u32[]{:S(2)}) collective-permute-start(bf16[256,256]{1,0:T(8,128)(2,1)S(1)} %constant_dynamic-slice_fusion), channel_id=1, source_target_pairs={{0,1},{1,0},{2,3},{3,2},{4,5},{5,4},{6,7},{7,6},{8,9},{9,8},{10,11... | collective-permute-start | bytes 393224 | tf_op jit(solution)/shard_map/ppermute | solution.py:434
  124.8 20.7 %all-to-all-start.2 = ((bf16[16,256,128]{2,1,0:T(8,128)(2,1)}), bf16[16,256,128]{2,1,0:T(8,128)(2,1)S(1)}, u32[]{:S(2)}, u32[]{:S(2)}) async-start(bf16[16,256,128]{2,1,0:T(8,128)(2,1)} %project.1), calls=%async_computation.2 | async-start | bytes 2097152 | tf_op jit(solution)/shard_map/all_to_all | solution.py:499
  129.8 5.0 %collective-permute-start.13 = (bf16[64,128]{1,0:T(8,128)(2,1)S(1)}, bf16[64,128]{1,0:T(8,128)(2,1)S(1)}, u32[]{:S(2)}, u32[]{:S(2)}) collective-permute-start(bf16[64,128]{1,0:T(8,128)(2,1)S(1)} %get-tuple-element.49), channel_id=1, source_target_pairs={{0,16},{16,0},{1,17},{17,1},{2,18},{18,2},{3,19},{19,3},{4,20},{20... | collective-permute-start | bytes 49160 | tf_op jit(solution)/shard_map/ppermute | solution.py:434
